TPU v7x, 32 devices: a whole 2x2x4 slice. The times are simulated.
32 devices in a mesh: diamond: 2 (over x), tile: 16 (over z, y, core).
Axes of the slice: x: 2, y: 2, z: 4, core: 2. Of those that a mesh axis runs over, the one named last changes fastest.
Arguments:
- adjoint_temp: float32 [2, 16, 256, 128], P('diamond', 'tile'), may hold values from -6 to 6
- misfit: float32 [2, 16, 256, 128], P('diamond', 'tile'), may hold values from -4 to 4
- viscosity: float32 [2, 16, 256, 128], P('diamond', 'tile'), may hold values from 0.1 to 10
- velocity: float32 [3, 2, 16, 256, 128], P(None, 'diamond', 'tile'), may hold values from -6 to 6
- forcing: float32 [3, 2, 16, 256, 128], P(None, 'diamond', 'tile'), may hold values from -9 to 9
- edge_table: int32 [2, 256], replicated, may hold values from 0 to 255, as said below
- pole_table: int32 [2, 256], replicated, may hold values from 0 to 255, as said below
Outputs:
- solution: float32 [3, 2, 16, 256, 128], P(None, 'diamond', 'tile')
- residual: float32 [3, 2, 16, 256, 128], P(None, 'diamond', 'tile')
- adjoint_next: float32 [2, 16, 256, 128], P('diamond', 'tile')
Inputs may be any that keep to these rules, and one draw needn't show every extreme that they name: `edge_table`: each row of the table is a permutation of the 256 nodes, and row 1 is the inverse permutation of row 0. `pole_table`: each row of the table is a permutation of the 256 nodes, and row 1 is the inverse permutation of row 0.
All inputs are finite; a program needn't handle non-finite values.
Results may differ from a plain program's by a relative error of at most 0.008.
Values sent between devices are 32-bit elements; how exact they have to be, the bound alone decides.
No kernel may reach another device: no remote copies, remote signals or barrier semaphores. Data moves between devices by JAX's collectives and lax.ppermute only.
A program may use at most 64 MiB of HBM per device.

v0:
```python
import jax
import jax.numpy as jnp
from jax import lax
from jax.sharding import PartitionSpec as P

ITERS = 3


TIME_STEP = 0.1
DIFFUSION = 1.0
MASS_TERM = 0.5
BUOYANCY = 1.0


def extended_2(shard, sides, width):
    for axis, dim in sides:
        size, length = (lax.axis_size(axis), shard.shape[dim])
        up = [(i, (i + 1) % size) for i in range(size - 1)]
        down = [(j, i) for i, j in up]
        last = lax.slice_in_dim(shard, length - width, length, axis=dim)
        leading = lax.slice_in_dim(shard, 0, width, axis=dim)
        before = lax.ppermute(last, axis, up)
        after = lax.ppermute(leading, axis, down)
        shard = jnp.concatenate([before, shard, after], axis=dim)
    return shard


def from_partner(value, axis, apart):
    mask = 2**apart
    pairs = [(source, source ^ mask) for source in range(lax.axis_size(axis))]
    return lax.ppermute(value, axis, pairs)


def outer_rows(field):
    return jnp.stack([field[:, :, 0], field[:, :, -1]], axis=2)


def assemble(field, extended, received, edge_table, pole_table):
    group = lax.axis_index("diamond")
    tile_index = lax.axis_index("tile")
    final = lax.axis_size("tile") - 1
    pole_line = lax.dynamic_index_in_dim(pole_table, group, 0, keepdims=False)
    edge_line = lax.dynamic_index_in_dim(edge_table, group, 0, keepdims=False)
    from_pole = jnp.take(received[:, :, 0], pole_line, axis=2)
    from_edge = jnp.take(received[:, :, 1], edge_line, axis=2)
    width = field.shape[2]
    first_row = jnp.where(tile_index == 0, from_pole, extended[:, :, 0])
    last_row = jnp.where(tile_index == final, from_edge, extended[:, :, width + 1])
    x_after = jnp.concatenate([extended[:, :, 2 : width + 1], last_row[:, :, None]], axis=2)
    x_before = jnp.concatenate([first_row[:, :, None], extended[:, :, 1:width]], axis=2)
    zeros_y = jnp.zeros_like(field[:, :, :, :1])
    y_after = jnp.concatenate([field[:, :, :, 1:], zeros_y], axis=3)
    y_before = jnp.concatenate([zeros_y, field[:, :, :, :-1]], axis=3)
    zeros_r = jnp.zeros_like(field[:, :, :, :, :1])
    r_after = jnp.concatenate([field[:, :, :, :, 1:], zeros_r], axis=4)
    r_before = jnp.concatenate([zeros_r, field[:, :, :, :, :-1]], axis=4)
    return [x_after, x_before, y_after, y_before, r_after, r_before]


def face_masks(count_y, count_r):
    y_place = jnp.arange(count_y)[:, None]
    r_place = jnp.arange(count_r)
    unity = jnp.ones((1, 1), jnp.float32)
    return [
        unity,
        unity,
        (y_place < count_y - 1).astype(jnp.float32),
        (y_place > 0).astype(jnp.float32),
        (r_place < count_r - 1).astype(jnp.float32),
        (r_place > 0).astype(jnp.float32),
    ]


def body(adjoint_temp, misfit, viscosity, velocity, forcing, edge_table, pole_table):
    paired = jnp.stack([adjoint_temp, viscosity])
    extended = extended_2(paired, (("tile", 2),), 1)
    received = from_partner(outer_rows(paired), "diamond", 0)
    near_both = assemble(paired, extended, received, edge_table, pole_table)
    temp_near = [entry[0] for entry in near_both]
    visc_near = [entry[1] for entry in near_both]
    laplace = sum(temp_near) - 6.0 * adjoint_temp
    transport = 0.5 * (
        velocity[0] * (temp_near[0] - temp_near[1])
        + velocity[1] * (temp_near[2] - temp_near[3])
        + velocity[2] * (temp_near[4] - temp_near[5])
    )
    adjoint_next = adjoint_temp + TIME_STEP * (DIFFUSION * laplace + transport) + misfit
    inside = face_masks(adjoint_temp.shape[2], adjoint_temp.shape[3])
    weights = [0.5 * (viscosity + visc_near[k]) * inside[k] for k in range(6)]
    diagonal = MASS_TERM + sum(weights)

    def combine(vector, near):
        total = diagonal * vector
        for k in range(6):
            total = total - weights[k] * near[k]
        return total

    def apply(vector):
        whole_ext = extended_2(vector, (("tile", 2),), 1)
        whole_got = from_partner(outer_rows(vector), "diamond", 0)
        near = assemble(vector, whole_ext, whole_got, edge_table, pole_table)
        return combine(vector, near)

    def products(residual, precond, image):
        return lax.psum(
            (jnp.sum(residual * precond), jnp.sum(precond * image)), ("diamond", "tile")
        )

    right = forcing.at[2].add(BUOYANCY * adjoint_next)
    solution = jnp.zeros_like(right)
    residual = right
    precond = residual / diagonal
    image = apply(precond)
    product_now, curvature = products(residual, precond, image)
    step_size = product_now / curvature
    direction, along = (precond, image)
    for step in range(ITERS):
        solution = solution + step_size * direction
        residual = residual - step_size * along
        if step + 1 < ITERS:
            precond = residual / diagonal
            image = apply(precond)
            product_next, curvature = products(residual, precond, image)
            ratio = product_next / product_now
            step_size = product_next / (curvature - ratio * product_next / step_size)
            direction = precond + ratio * direction
            along = image + ratio * along
            product_now = product_next
    return (solution, residual, adjoint_next)


def solution(mesh):
    placed = (
        P("diamond", "tile", None, None),
        P("diamond", "tile", None, None),
        P("diamond", "tile", None, None),
        P(None, "diamond", "tile", None, None),
        P(None, "diamond", "tile", None, None),
        P(),
        P(),
    )
    return jax.shard_map(
        body,
        mesh=mesh,
        in_specs=placed,
        out_specs=(
            P(None, "diamond", "tile", None, None),
            P(None, "diamond", "tile", None, None),
            P("diamond", "tile", None, None),
        ),
        check_vma=False,
    )
```

profile of v0, /device:TPU:0, one launch (start us, length us, event | category | flops | bytes accessed | tf_op | source)
XLA Modules:
  0.0 261.3 jit_solution(14619953274183823548)
XLA Ops:
  0.6 1.7 fusion.40
  2.4 3.0 %collective-permute-start.2 = (f32[2,1,1,256,128]{4,3,0,2,1:T(8,128)}, f32[2,1,1,256,128]{4,3,0,2,1:T(8,128)}, u32[]{:S(2)}, u32[]{:S(2)}) collective-permute-start(f32[2,1,1,256,128]{4,3,0,2,1:T(8,128)} %fusion.40), channel_id=1, source_target_pairs={{0,1},{1,2},{2,3},{3,4},{4,5},{5,6},{6,7},{7,8},{8,9},{9,10},{10,1... | collective-permute-start | bytes 786440 | tf_op jit(solution)/shard_map/ppermute | solution.py:22
  5.4 1.3 collective-permute-start.1
  6.8 2.4 collective-permute-start
  11.6 9.2 %collective-permute-done = f32[2,1,2,256,128]{4,3,2,1,0:T(8,128)S(1)} collective-permute-done((f32[2,1,2,256,128]{4,3,2,1,0:T(8,128)S(1)}, f32[2,1,2,256,128]{4,3,2,1,0:T(8,128)S(1)}, u32[]{:S(2)}, u32[]{:S(2)}) %collective-permute-start) | collective-permute-done | bytes 524320 | tf_op jit(solution)/shard_map/ppermute | solution.py:31
  21.2 1.0 gather_fusion.1
  22.2 1.0 gather_fusion
  23.2 1.1 fusion.41
  24.3 1.1 fusion.42
  25.4 0.8 bitcast_add_fusion
  26.2 2.9 %scatter-add.4 = f32[3,1,1,256,128]{4,0,3,2,1:T(4,128)S(1)} dynamic-update-slice(f32[3,1,1,256,128]{4,0,3,2,1:T(4,128)S(1)} %copy.92, f32[1,1,1,256,128]{4,0,3,2,1:T(1,128)S(1)} %bitcast.376, s32[]{:T(128)} %constant.94.clone.1, s32[]{:T(128)} %constant.93.clone.1, s32[]{:T(128)} %constant.93.clone.1, s32[]{:T(128)} %constant.93.clone.1, s32[]{:T(128)} %constant.93.clone.1) | dynamic-update-slice | bytes 262148 | tf_op jit(solution)/shard_map/scatter-add | solution.py:109
  30.4 2.5 collective-permute-start.3
  33.0 3.0 %collective-permute-start.5 = (f32[3,1,1,256,128]{4,0,3,2,1:T(4,128)S(1)}, f32[3,1,1,256,128]{4,0,3,2,1:T(4,128)}, u32[]{:S(2)}, u32[]{:S(2)}) collective-permute-start(f32[3,1,1,256,128]{4,0,3,2,1:T(4,128)S(1)} %broadcast_divide_fusion.2), channel_id=1, source_target_pairs={{0,1},{1,2},{2,3},{3,4},{4,5},{5,6},{6,7},{7,8},{8,9},{9,10},{10,1... | collective-permute-start | bytes 1179656 | tf_op jit(solution)/shard_map/ppermute | solution.py:22
  36.0 1.3 collective-permute-start.4
  37.6 0.9 fusion.85
  38.5 12.7 %collective-permute-done.3 = f32[3,1,2,256,128]{4,3,2,1,0:T(8,128)S(1)} collective-permute-done((f32[3,1,2,256,128]{4,3,2,1,0:T(8,128)S(1)}, f32[3,1,2,256,128]{4,3,2,1,0:T(8,128)S(1)}, u32[]{:S(2)}, u32[]{:S(2)}) %collective-permute-start.3) | collective-permute-done | bytes 786464 | tf_op jit(solution)/shard_map/ppermute | solution.py:31
  51.2 0.8 fusion.80
  52.0 1.1 copy.124
  53.1 2.8 %gather_fusion.2 = f32[256,3,128]{2,1,0:T(4,128)} fusion(f32[3,256,128]{2,0,1:T(4,128)} %bitcast.372, s32[1024]{0:T(1024)S(1)} %pad_clamp_fusion.1), kind=kCustom, calls=%fused_computation.1.clone | custom fusion | bytes 787456 | tf_op jit(solution)/shard_map/jit(_take)/gather | solution.py:45
  55.9 2.1 copy.123
  58.0 2.8 %gather_fusion.3 = f32[256,3,128]{2,1,0:T(4,128)} fusion(f32[3,256,128]{2,0,1:T(4,128)} %bitcast.373, s32[1024]{0:T(1024)S(1)} %pad_clamp_fusion), kind=kCustom, calls=%fused_computation.3.clone | custom fusion | bytes 787456 | tf_op jit(solution)/shard_map/jit(_take)/gather | solution.py:44
  60.8 4.2 %multiply_reduce_fusion.4 = (f32[]{:T(128)}, f32[]{:T(128)}, f32[3,1,1,256,128]{4,0,3,2,1:T(4,128)S(1)}) fusion(f32[3,1,1,256,128]{4,0,3,2,1:T(4,128)S(1)} %scatter-add.4, f32[3,1,1,256,127]{4,0,3,2,1:T(4,128)S(1)} %get-tuple-element.64, f32[256,128]{1,0:T(8,128)S(1)} %get-tuple-element.70, f32[3,1,1,256,127]{4,0,3,2,1:T(4,128)S(1)} %get-tuple-element.63, ...), kind=kLoop, calls=%fused_computation.69 | loop fusion | flops 2162686 | bytes 4840970 | tf_op jit(solution)/shard_map/reduce_sum | solution.py:106
  65.0 41.0 %all-reduce.18 = (f32[]{:T(128)}, f32[]{:T(128)}) all-reduce(f32[]{:T(128)} %get-tuple-element.31, f32[]{:T(128)} %get-tuple-element.30), channel_id=1, replica_groups=mesh['diamond'=2,'tile'=16] {'diamond','tile'}, use_global_device_ids=true, to_apply=%region_1.3 | all-reduce | flops 2 | bytes 16 | tf_op jit(solution)/shard_map/psum | solution.py:105
  107.8 2.3 collective-permute-start.6
  110.1 2.1 collective-permute-start.8
  112.2 1.3 collective-permute-start.7
  113.5 1.4 fusion.84
  114.9 1.1 fusion.83
  116.0 10.6 %collective-permute-done.6 = f32[3,1,2,256,128]{4,3,2,1,0:T(8,128)S(1)} collective-permute-done((f32[3,1,2,256,128]{4,3,2,1,0:T(8,128)S(1)}, f32[3,1,2,256,128]{4,3,2,1,0:T(8,128)S(1)}, u32[]{:S(2)}, u32[]{:S(2)}) %collective-permute-start.6) | collective-permute-done | bytes 786464 | tf_op jit(solution)/shard_map/ppermute | solution.py:31
  126.6 0.8 fusion.79
  127.7 1.8 gather_fusion.4
  129.4 1.3 copy.121
  130.7 1.8 gather_fusion.5
  132.5 4.5 %multiply_reduce_fusion.2 = (f32[]{:T(128)}, f32[]{:T(128)}, f32[3,1,1,256,128]{4,0,3,2,1:T(4,128)S(1)}) fusion(f32[3,1,1,256,128]{4,0,3,2,1:T(4,128)S(1)} %get-tuple-element.42, f32[3,1,1,256,128]{4,0,3,2,1:T(4,128)S(1)} %get-tuple-element.43, f32[3,1,1,256,127]{4,0,3,2,1:T(4,128)} %get-tuple-element.60, f32[256,128]{1,0:T(8,128)S(1)} %get-tuple-element.70, ...), kind=kLoop, calls=%fused_computation.66 | loop fusion | flops 2064382 | bytes 5234186 | tf_op jit(solution)/shard_map/reduce_sum | solution.py:106
  137.0 39.5 %all-reduce.17 = (f32[]{:T(128)}, f32[]{:T(128)}) all-reduce(f32[]{:T(128)} %get-tuple-element.29, f32[]{:T(128)} %get-tuple-element.28), channel_id=1, replica_groups=mesh['diamond'=2,'tile'=16] {'diamond','tile'}, use_global_device_ids=true, to_apply=%region_5.8 | all-reduce | flops 2 | bytes 16 | tf_op jit(solution)/shard_map/psum | solution.py:105
  181.1 1.1 broadcast_divide_fusion
  182.3 2.3 collective-permute-start.9
  184.7 2.1 collective-permute-start.11
  186.8 1.3 collective-permute-start.10
  188.1 1.4 fusion.82
  189.4 1.1 fusion.81
  190.6 10.5 %collective-permute-done.9 = f32[3,1,2,256,128]{4,3,2,1,0:T(8,128)S(1)} collective-permute-done((f32[3,1,2,256,128]{4,3,2,1,0:T(8,128)S(1)}, f32[3,1,2,256,128]{4,3,2,1,0:T(8,128)S(1)}, u32[]{:S(2)}, u32[]{:S(2)}) %collective-permute-start.9) | collective-permute-done | bytes 786464 | tf_op jit(solution)/shard_map/ppermute | solution.py:31
  201.1 0.8 fusion.78
  202.1 1.8 gather_fusion.6
  203.9 2.1 copy.119
  206.0 2.9 %gather_fusion.7 = f32[256,3,128]{2,1,0:T(4,128)} fusion(f32[3,256,128]{2,0,1:T(4,128)} %bitcast.371, s32[1024]{0:T(1024)S(1)} %pad_clamp_fusion), kind=kCustom, calls=%fused_computation.7.clone | custom fusion | bytes 787456 | tf_op jit(solution)/shard_map/jit(_take)/gather | solution.py:44
  208.8 5.4 %multiply_reduce_fusion = (f32[]{:T(128)}, f32[]{:T(128)}, f32[3,1,1,256,128]{4,0,3,2,1:T(4,128)}) fusion(f32[3,1,1,256,128]{4,0,3,2,1:T(4,128)S(1)} %get-tuple-element.39, f32[3,1,1,256,128]{4,0,3,2,1:T(4,128)S(1)} %copy-done, f32[3,1,1,256,127]{4,0,3,2,1:T(4,128)} %get-tuple-element.56, f32[256,128]{1,0:T(8,128)} %copy-done.3, ...), kind=kLoop, calls=%fused_computation.62 | loop fusion | flops 2064382 | bytes 5234186 | tf_op jit(solution)/shard_map/reduce_sum | solution.py:106
  214.2 40.3 %all-reduce.16 = (f32[]{:T(128)}, f32[]{:T(128)}) all-reduce(f32[]{:T(128)} %get-tuple-element.27, f32[]{:T(128)} %get-tuple-element.26), channel_id=1, replica_groups=mesh['diamond'=2,'tile'=16] {'diamond','tile'}, use_global_device_ids=true, to_apply=%region_9.12 | all-reduce | flops 2 | bytes 16 | tf_op jit(solution)/shard_map/psum | solution.py:105
  (74 shorter events, 8.4 us)
Async XLA Ops:
  0.6 6.1 %copy-start.1 = (f32[1,1,256,128]{3,2,1,0:T(8,128)S(1)}, f32[1,1,256,128]{3,2,1,0:T(8,128)}, u32[]{:S(2)}) copy-start(f32[1,1,256,128]{3,2,1,0:T(8,128)} %param.13) | copy-start | bytes 393220
  0.6 6.1 %copy-start.2 = (f32[1,1,256,128]{3,2,1,0:T(8,128)S(1)}, f32[1,1,256,128]{3,2,1,0:T(8,128)}, u32[]{:S(2)}) copy-start(f32[1,1,256,128]{3,2,1,0:T(8,128)} %param.15) | copy-start | bytes 393220
  2.4 20.8 %collective-permute-start.2 = (f32[2,1,1,256,128]{4,3,0,2,1:T(8,128)}, f32[2,1,1,256,128]{4,3,0,2,1:T(8,128)}, u32[]{:S(2)}, u32[]{:S(2)}) collective-permute-start(f32[2,1,1,256,128]{4,3,0,2,1:T(8,128)} %fusion.40), channel_id=1, source_target_pairs={{0,1},{1,2},{2,3},{3,4},{4,5},{5,6},{6,7},{7,8},{8,9},{9,10},{10,1... | collective-permute-start | bytes 786440 | tf_op jit(solution)/shard_map/ppermute | solution.py:22
  5.4 18.8 %collective-permute-start.1 = (f32[2,1,1,256,128]{4,3,0,2,1:T(8,128)}, f32[2,1,1,256,128]{4,3,0,2,1:T(8,128)}, u32[]{:S(2)}, u32[]{:S(2)}) collective-permute-start(f32[2,1,1,256,128]{4,3,0,2,1:T(8,128)} %fusion.40), channel_id=1, source_target_pairs={{1,0},{2,1},{3,2},{4,3},{5,4},{6,5},{7,6},{8,7},{9,8},{10,9},{11,1... | collective-permute-start | bytes 786440 | tf_op jit(solution)/shard_map/ppermute | solution.py:23
  6.8 14.0 %collective-permute-start = (f32[2,1,2,256,128]{4,3,2,1,0:T(8,128)S(1)}, f32[2,1,2,256,128]{4,3,2,1,0:T(8,128)S(1)}, u32[]{:S(2)}, u32[]{:S(2)}) collective-permute-start(f32[2,1,2,256,128]{4,3,2,1,0:T(8,128)S(1)} %maximum_maximum_fusion), channel_id=1, source_target_pairs={{0,16},{16,0},{1,17},{17,1},{2,18},{18,2},{3,19},{19,3},{4,20},{20... | collective-permute-start | bytes 1572872 | tf_op jit(solution)/shard_map/ppermute | solution.py:31
  9.9 1.4 copy-start.8
  9.9 0.7 copy-start.16
  10.0 0.7 copy-start.15
  24.2 1.1 copy-start.9
  24.2 1.1 copy-start.10
  26.2 2.9 %copy-start.12 = (f32[256]{0:T(256)S(1)}, f32[256]{0:T(256)}, u32[]{:S(2)}) copy-start(f32[256]{0:T(256)} %get-tuple-element.83) | copy-start | bytes 3076
  26.2 2.9 %copy-start.14 = (f32[128]{0:T(128)S(1)}, f32[128]{0:T(128)}, u32[]{:S(2)}) copy-start(f32[128]{0:T(128)} %get-tuple-element.81) | copy-start | bytes 1540
  29.1 0.7 copy-start.11
  29.1 0.7 copy-start.13
  30.0 102.4 %copy-start.3 = (f32[256,128]{1,0:T(8,128)}, f32[256,128]{1,0:T(8,128)S(1)}, u32[]{:S(2)}) copy-start(f32[256,128]{1,0:T(8,128)S(1)} %get-tuple-element.70) | copy-start | bytes 393220
  30.0 102.4 %copy-start.4 = (f32[256,128]{1,0:T(8,128)}, f32[256,128]{1,0:T(8,128)S(1)}, u32[]{:S(2)}) copy-start(f32[256,128]{1,0:T(8,128)S(1)} %get-tuple-element.71) | copy-start | bytes 393220
  30.0 102.4 %copy-start.5 = (f32[256,128]{1,0:T(8,128)}, f32[256,128]{1,0:T(8,128)S(1)}, u32[]{:S(2)}) copy-start(f32[256,128]{1,0:T(8,128)S(1)} %get-tuple-element.72) | copy-start | bytes 393220
  30.0 102.4 %copy-start.6 = (f32[256,128]{1,0:T(8,128)}, f32[256,128]{1,0:T(8,128)S(1)}, u32[]{:S(2)}) copy-start(f32[256,128]{1,0:T(8,128)S(1)} %get-tuple-element.73) | copy-start | bytes 393220
  30.4 20.8 %collective-permute-start.3 = (f32[3,1,2,256,128]{4,3,2,1,0:T(8,128)S(1)}, f32[3,1,2,256,128]{4,3,2,1,0:T(8,128)S(1)}, u32[]{:S(2)}, u32[]{:S(2)}) collective-permute-start(f32[3,1,2,256,128]{4,3,2,1,0:T(8,128)S(1)} %copy.94), channel_id=1, source_target_pairs={{0,16},{16,0},{1,17},{17,1},{2,18},{18,2},{3,19},{19,3},{4,20},{20... | collective-permute-start | bytes 2359304 | tf_op jit(solution)/shard_map/ppermute | solution.py:31
  33.0 27.8 %collective-permute-start.5 = (f32[3,1,1,256,128]{4,0,3,2,1:T(4,128)S(1)}, f32[3,1,1,256,128]{4,0,3,2,1:T(4,128)}, u32[]{:S(2)}, u32[]{:S(2)}) collective-permute-start(f32[3,1,1,256,128]{4,0,3,2,1:T(4,128)S(1)} %broadcast_divide_fusion.2), channel_id=1, source_target_pairs={{0,1},{1,2},{2,3},{3,4},{4,5},{5,6},{6,7},{7,8},{8,9},{9,10},{10,1... | collective-permute-start | bytes 1179656 | tf_op jit(solution)/shard_map/ppermute | solution.py:22
  36.0 24.8 %collective-permute-start.4 = (f32[3,1,1,256,128]{4,0,3,2,1:T(4,128)S(1)}, f32[3,1,1,256,128]{4,0,3,2,1:T(4,128)}, u32[]{:S(2)}, u32[]{:S(2)}) collective-permute-start(f32[3,1,1,256,128]{4,0,3,2,1:T(4,128)S(1)} %broadcast_divide_fusion.2), channel_id=1, source_target_pairs={{1,0},{2,1},{3,2},{4,3},{5,4},{6,5},{7,6},{8,7},{9,8},{10,9},{11,1... | collective-permute-start | bytes 1179656 | tf_op jit(solution)/shard_map/ppermute | solution.py:23
  107.8 18.8 %collective-permute-start.6 = (f32[3,1,2,256,128]{4,3,2,1,0:T(8,128)S(1)}, f32[3,1,2,256,128]{4,3,2,1,0:T(8,128)S(1)}, u32[]{:S(2)}, u32[]{:S(2)}) collective-permute-start(f32[3,1,2,256,128]{4,3,2,1,0:T(8,128)S(1)} %copy.97), channel_id=1, source_target_pairs={{0,16},{16,0},{1,17},{17,1},{2,18},{18,2},{3,19},{19,3},{4,20},{20... | collective-permute-start | bytes 2359304 | tf_op jit(solution)/shard_map/ppermute | solution.py:31
  110.1 22.3 %collective-permute-start.8 = (f32[3,1,1,256,128]{4,0,3,2,1:T(4,128)S(1)}, f32[3,1,1,256,128]{4,0,3,2,1:T(4,128)}, u32[]{:S(2)}, u32[]{:S(2)}) collective-permute-start(f32[3,1,1,256,128]{4,0,3,2,1:T(4,128)S(1)} %get-tuple-element.42), channel_id=1, source_target_pairs={{0,1},{1,2},{2,3},{3,4},{4,5},{5,6},{6,7},{7,8},{8,9},{9,10},{10,1... | collective-permute-start | bytes 1179656 | tf_op jit(solution)/shard_map/ppermute | solution.py:22
  112.2 20.2 %collective-permute-start.7 = (f32[3,1,1,256,128]{4,0,3,2,1:T(4,128)S(1)}, f32[3,1,1,256,128]{4,0,3,2,1:T(4,128)}, u32[]{:S(2)}, u32[]{:S(2)}) collective-permute-start(f32[3,1,1,256,128]{4,0,3,2,1:T(4,128)S(1)} %get-tuple-element.42), channel_id=1, source_target_pairs={{1,0},{2,1},{3,2},{4,3},{5,4},{6,5},{7,6},{8,7},{9,8},{10,9},{11,1... | collective-permute-start | bytes 1179656 | tf_op jit(solution)/shard_map/ppermute | solution.py:23
  182.3 18.7 %collective-permute-start.9 = (f32[3,1,2,256,128]{4,3,2,1,0:T(8,128)S(1)}, f32[3,1,2,256,128]{4,3,2,1,0:T(8,128)S(1)}, u32[]{:S(2)}, u32[]{:S(2)}) collective-permute-start(f32[3,1,2,256,128]{4,3,2,1,0:T(8,128)S(1)} %copy.100), channel_id=1, source_target_pairs={{0,16},{16,0},{1,17},{17,1},{2,18},{18,2},{3,19},{19,3},{4,20},{20... | collective-permute-start | bytes 2359304 | tf_op jit(solution)/shard_map/ppermute | solution.py:31
  184.7 24.1 %collective-permute-start.11 = (f32[3,1,1,256,128]{4,0,3,2,1:T(4,128)S(1)}, f32[3,1,1,256,128]{4,0,3,2,1:T(4,128)}, u32[]{:S(2)}, u32[]{:S(2)}) collective-permute-start(f32[3,1,1,256,128]{4,0,3,2,1:T(4,128)S(1)} %get-tuple-element.39), channel_id=1, source_target_pairs={{0,1},{1,2},{2,3},{3,4},{4,5},{5,6},{6,7},{7,8},{8,9},{9,10},{10,1... | collective-permute-start | bytes 1179656 | tf_op jit(solution)/shard_map/ppermute | solution.py:22
  186.8 22.1 %collective-permute-start.10 = (f32[3,1,1,256,128]{4,0,3,2,1:T(4,128)S(1)}, f32[3,1,1,256,128]{4,0,3,2,1:T(4,128)}, u32[]{:S(2)}, u32[]{:S(2)}) collective-permute-start(f32[3,1,1,256,128]{4,0,3,2,1:T(4,128)S(1)} %get-tuple-element.39), channel_id=1, source_target_pairs={{1,0},{2,1},{3,2},{4,3},{5,4},{6,5},{7,6},{8,7},{9,8},{10,9},{11,1... | collective-permute-start | bytes 1179656 | tf_op jit(solution)/shard_map/ppermute | solution.py:23
  206.0 2.9 %copy-start = (f32[3,1,1,256,128]{4,0,3,2,1:T(4,128)S(1)}, f32[3,1,1,256,128]{4,0,3,2,1:T(4,128)}, u32[]{:S(2)}) copy-start(f32[3,1,1,256,128]{4,0,3,2,1:T(4,128)} %get-tuple-element.40) | copy-start | bytes 1179652
  258.5 1.0 copy-start.7
where the time goes:
time: 263 us; the launch traced here: 261 us
  blocking collectives  121 us (46%)
  waiting for transfers between devices  43 us (16%)
  local copies, waits for them, and re-layouts  38.7 us (15%)
  starting transfers between devices  25 us (10%)
  other arithmetic  23 us (9%)
  between operations  10.8 us (4%)
    psum x3, blocking collectives, products(): lax.psum((jnp.sum(residual * precond), jnp.sum(precond * image)), ('diamo...  121 us
    ppermute x4, waiting for transfers between devices, from_partner(): return lax.ppermute(value, axis, pairs)  43 us
    reduce_sum x3, other arithmetic, products(): jnp.sum(precond * image)  14.2 us
    unnamed x43, local copies, waits for them, and re-layouts  10.8 us
    ppermute x4, starting transfers between devices, extended_2(): before = lax.ppermute(last, axis, up)  10.2 us
    ppermute x4, starting transfers between devices, from_partner(): return lax.ppermute(value, axis, pairs)  9.61 us
    gather x4, local copies, waits for them, and re-layouts, assemble(): from_pole = jnp.take(received[:, :, 0], pole_line, axis=2)  8.4 us
    gather x4, local copies, waits for them, and re-layouts, assemble(): from_edge = jnp.take(received[:, :, 1], edge_line, axis=2)  7.31 us
  transfers between devices with their start and end apart: 12, of which 4 were waited for; matrix products, arithmetic and copies ran while one was open for 13% of the time, Pallas kernels for 0%

commit v1 on v0

v1 whole, which is shorter than its diff:
```python
import functools

import jax
import jax.numpy as jnp
from jax import lax
from jax.experimental import pallas as pl
from jax.experimental.pallas import tpu as pltpu
from jax.sharding import PartitionSpec as P

ITERS = 3
TIME_STEP = 0.1
DIFFUSION = 1.0
MASS_TERM = 0.5
BUOYANCY = 1.0
CENTERS = (0.0, 0.45, -0.45, 0.75, -0.75, 0.95, -0.95)
CHUNK = 32
SPLITS = ((0, 1), (1, 2), (2, 3))


def rows_around(load, start, total):
    low, high = max(start - 8, 0), min(start + CHUNK + 8, total)
    block = load(low, high)
    at = start - low
    after = pltpu.roll(block, high - low - 1, 0)[at : at + CHUNK]
    before = pltpu.roll(block, 1, 0)[at : at + CHUNK]
    return block[at : at + CHUNK], after, before


def layers_around(block):
    count = block.shape[1]
    return pltpu.roll(block, count - 1, 1), pltpu.roll(block, 1, 1)


def split3(value):
    top = value.astype(jnp.bfloat16)
    rest = value - top.astype(jnp.float32)
    middle = rest.astype(jnp.bfloat16)
    bottom = (rest - middle.astype(jnp.float32)).astype(jnp.bfloat16)
    return [top, middle, bottom]


def fold_matrix(edge_ref, pole_ref):
    group, tile = lax.axis_index("diamond"), lax.axis_index("tile")
    final = lax.axis_size("tile") - 1
    count = edge_ref.shape[1]
    rows = lax.broadcasted_iota(jnp.int32, (count, count), 0)
    same = lax.broadcasted_iota(jnp.int32, (1, count), 1)
    edge = jnp.where(group == 0, edge_ref[1:2], edge_ref[0:1])
    pole = jnp.where(group == 0, pole_ref[1:2], pole_ref[0:1])
    line = jnp.where(tile == 0, pole, jnp.where(tile == final, edge, same))
    return (rows == line).astype(jnp.bfloat16)


def unfold(matrix_ref, far_ref, out_ref):
    layers = far_ref.shape[2]
    for at in range(far_ref.shape[0]):
        pieces = jnp.concatenate(split3(far_ref[at]), axis=1)
        moved = jnp.dot(matrix_ref[...], pieces, preferred_element_type=jnp.float32)
        out_ref[at] = (
            moved[:, :layers] + moved[:, layers : 2 * layers] + moved[:, 2 * layers :]
        )


def local_kernel(
    temp_hbm, misfit_hbm, visc_hbm, velocity_hbm, forcing_hbm, edge_hbm, pole_hbm,
    half_ref, side_ref, base_ref, right_ref, part_ref, speed_ref, matrix_ref,
    temp_ref, misfit_ref, visc_ref, velocity_ref, edge_ref, pole_ref, sems,
):
    sources = [visc_hbm, temp_hbm, edge_hbm, pole_hbm, velocity_hbm, misfit_hbm, forcing_hbm]
    targets = [visc_ref, temp_ref, edge_ref, pole_ref, velocity_ref, misfit_ref, right_ref]
    copies = [pltpu.make_async_copy(s, t, sems.at[i]) for i, (s, t) in enumerate(zip(sources, targets))]
    for copy in copies:
        copy.start()
    odd = lax.rem(lax.axis_index("tile"), 2)
    half = jnp.where(odd == 0, 0.5, -0.5).astype(jnp.float32)
    total, layers = temp_ref.shape
    for copy in copies:
        copy.wait()
    matrix_ref[...] = fold_matrix(edge_ref, pole_ref)
    for start in range(0, total, CHUNK):
        here = slice(start, start + CHUNK)
        visc, visc_after, visc_before = rows_around(lambda a, b: visc_ref[a:b], start, total)
        temp, temp_after, temp_before = rows_around(lambda a, b: temp_ref[a:b], start, total)
        place = start + lax.broadcasted_iota(jnp.int32, (CHUNK, layers), 0)
        layer = lax.broadcasted_iota(jnp.int32, (CHUNK, layers), 1)
        inside = [place < total - 1, place > 0, layer < layers - 1, layer > 0]
        visc_near = [visc_after, visc_before, *layers_around(visc)]
        temp_near = [temp_after, temp_before, *layers_around(temp)]
        zero = jnp.zeros_like(visc)
        weights = [jnp.where(m, 0.5 * (visc + v), zero) for m, v in zip(inside, visc_near)]
        temps = [jnp.where(m, t, zero) for m, t in zip(inside, temp_near)]
        half_ref[here] = 0.5 * visc
        for k in range(4):
            side_ref[k, here] = weights[k]
        base_ref[here] = MASS_TERM + sum(weights)
        transport = 0.5 * (
            velocity_ref[1, here] * (temps[0] - temps[1]) + velocity_ref[2, here] * (temps[2] - temps[3])
        )
        laplace = sum(temps) - 6.0 * temp
        part_ref[here] = temp + TIME_STEP * (DIFFUSION * laplace + transport) + misfit_ref[here]
        speed_ref[here] = half * velocity_ref[0, here]


def prepare_kernel(
    half_ref, side_ref, base_ref, right_ref, part_ref, speed_ref, matrix_ref,
    visc_near_ref, temp_near_ref, visc_far_ref, temp_far_ref,
    next_ref, weights_ref, diagonal_ref, *refs,
):
    *first_refs, moved_visc_ref, moved_temp_ref = refs
    unfold(matrix_ref, visc_far_ref, moved_visc_ref)
    unfold(matrix_ref, temp_far_ref, moved_temp_ref)
    for start in range(0, half_ref.shape[0], CHUNK):
        here = slice(start, start + CHUNK)
        near, far = temp_near_ref[0, here], moved_temp_ref[0, here]
        adjoint_next = part_ref[here] + TIME_STEP * (
            DIFFUSION * (near + far) + speed_ref[here] * (near - far)
        )
        next_ref[here] = adjoint_next
        visc = half_ref[here]
        weights = [visc + 0.5 * visc_near_ref[0, here], visc + 0.5 * moved_visc_ref[0, here]]
        diagonal = base_ref[here] + weights[0] + weights[1]
        diagonal_ref[here] = diagonal
        inverse = 1.0 / diagonal
        weights += [side_ref[k, here] for k in range(4)]
        for k in range(6):
            weights_ref[k, here] = weights[k] * inverse
        for (low, high), first_ref in zip(SPLITS, first_refs):
            for at in range(low, high):
                right = right_ref[at, here]
                if at == 2:
                    right = right + BUOYANCY * adjoint_next
                first_ref[at - low, here] = right * inverse


def average(start, at, field_ref, near_ref, moved_ref, weights):
    here = slice(start, start + CHUNK)
    mid, after, before = rows_around(lambda a, b: field_ref[at, a:b], start, field_ref.shape[1])
    around = [near_ref[at, here], moved_ref[at, here], after, before, *layers_around(mid)]
    return sum(w * v for w, v in zip(weights, around))


def apply_kernel(far_ref, near_ref, field_ref, weights_ref, matrix_ref, after_ref, out_ref, moved_ref):
    unfold(matrix_ref, far_ref, moved_ref)
    for start in range(0, field_ref.shape[1], CHUNK):
        here = slice(start, start + CHUNK)
        weights = [weights_ref[k, here] for k in range(6)]
        for at in range(field_ref.shape[0]):
            out_ref[at, here] = average(start, at, field_ref, near_ref, moved_ref, weights)


def fold8(value):
    return jnp.sum(value.reshape(value.shape[0] // 8, 8, value.shape[1]), axis=0)


def moment_lanes(k):
    row = lax.broadcasted_iota(jnp.int32, (8, 128), 0)
    lane = lax.broadcasted_iota(jnp.int32, (8, 128), 1)
    return lane == row + 8 * k


def place_moment(k, sums):
    rows = [jnp.sum(s, axis=0, keepdims=True) for s in sums]
    rows += [rows[0]] * (8 - len(rows))
    column = jnp.sum(jnp.concatenate(rows, axis=0), axis=1, keepdims=True)
    return jnp.where(moment_lanes(k), column, 0.0)


def early_kernel(diagonal_ref, *refs):
    moments_ref, left_ref, shift_ref = refs[-3:]
    total, layers = diagonal_ref.shape
    sums = [[jnp.zeros((8, layers), jnp.float32) for _ in CENTERS] for _ in range(5)]
    for i, (low, high) in enumerate(SPLITS):
        y0_ref, y1_ref, y2_ref = refs[3 * i : 3 * i + 3]
        for start in range(0, total, CHUNK):
            here = slice(start, start + CHUNK)
            diagonal = diagonal_ref[here]
            for at in range(high - low):
                y0, y1, y2 = y0_ref[at, here], y1_ref[at, here], y2_ref[at, here]
                d0 = diagonal * y0
                m0 = fold8(d0 * y0)
                for j, center in enumerate(CENTERS):
                    q1 = y1 - center * y0
                    t2 = y2 - center * y1
                    q2 = t2 - center * q1
                    d1, d2 = diagonal * q1, diagonal * q2
                    left_ref[j, low + at, here] = d2
                    shift_ref[j, low + at, here] = center * (y2 + t2 + q2)
                    sums[0][j] += m0
                    sums[1][j] += fold8(d0 * q1)
                    sums[2][j] += fold8(d1 * q1)
                    sums[3][j] += fold8(d1 * q2)
                    sums[4][j] += fold8(d2 * q2)
    moments_ref[...] = sum(place_moment(k, sums[k]) for k in range(5))


def powers(center, y0, y1, y2, y3):
    q1 = y1 - center * y0
    t2 = y2 - center * y1
    q2 = t2 - center * q1
    q3 = (y3 - center * y2 - center * t2) - center * q2
    return q1, q2, q3


def last_kernel(
    low, far_ref, near_ref, field_ref, weights_ref, matrix_ref, earlier_ref, left_ref, shift_ref,
    out_ref, moments_ref, moved_ref,
):
    unfold(matrix_ref, far_ref, moved_ref)
    total, layers = field_ref.shape[1:]
    sums = [jnp.zeros((8, layers), jnp.float32) for _ in CENTERS]
    for start in range(0, total, CHUNK):
        here = slice(start, start + CHUNK)
        weights = [weights_ref[k, here] for k in range(6)]
        for at in range(field_ref.shape[0]):
            y3 = average(start, at, field_ref, near_ref, moved_ref, weights)
            out_ref[at, here] = y3
            for j in range(len(CENTERS)):
                sums[j] += fold8(left_ref[j, low + at, here] * (y3 - shift_ref[j, low + at, here]))
    message = earlier_ref[...] + place_moment(5, sums)
    if len(moments_ref.shape) == 2:
        moments_ref[...] = message
    else:
        row = jnp.sum(message, axis=0, keepdims=True)
        for device in range(moments_ref.shape[0]):
            moments_ref[device] = row


def inner(left, right, moments, shift=0):
    total = 0.0
    for i, a in enumerate(left):
        for j, b in enumerate(right):
            total = total + (a * b) * moments[i + j + shift]
    return total


def axpy(scale, left, right):
    count = max(len(left), len(right))
    result = []
    for i in range(count):
        if i >= len(left):
            result.append(right[i])
        elif i >= len(right):
            result.append(scale * left[i])
        else:
            result.append(scale * left[i] + right[i])
    return result


def recurrence(moments, centers):
    def operator(poly):
        result = [(1.0 - centers) * a for a in poly] + [jnp.zeros_like(centers)]
        for i, a in enumerate(poly):
            result[i + 1] = result[i + 1] - a
        return result

    one = jnp.ones_like(centers)
    residual, direction, answer = [one], [one], []
    product_now = moments[0]
    for step in range(ITERS):
        image = operator(direction)
        step_size = product_now / inner(direction, image, moments)
        answer = axpy(step_size, direction, answer)
        residual = axpy(-step_size, image, residual)
        if step + 1 < ITERS:
            product_next = inner(residual, residual, moments)
            direction = axpy(product_next / product_now, direction, residual)
            product_now = product_next
    return answer, residual


def finish_kernel(moments_ref, diagonal_ref, *refs):
    solution_ref, residual_ref = refs[-2:]
    streams = [refs[4 * i : 4 * i + 4] for i in range(len(SPLITS))]
    rows = [moments_ref[device] for device in range(moments_ref.shape[0])]
    while len(rows) > 1:
        rows = [a + b for a, b in zip(rows[::2], rows[1::2])]
    row = jnp.broadcast_to(rows[0], (8, 128))
    moments = [jnp.sum(jnp.where(moment_lanes(k), row, 0.0), axis=1, keepdims=True) for k in range(6)]
    place = lax.broadcasted_iota(jnp.int32, (8, 1), 0)
    centers = jnp.zeros((8, 1), jnp.float32)
    for j, center in enumerate(CENTERS):
        centers = jnp.where(place == j, center, centers)
    answer, residual = recurrence(moments, centers)
    packed = [centers, *answer, *residual]
    mean = centers[0:1] + moments[1][0:1] / moments[0][0:1]
    best = jnp.abs(mean - centers[0:1])
    chosen = [p[0:1] for p in packed]
    for j in range(1, len(CENTERS)):
        away = jnp.abs(mean - centers[j : j + 1])
        better = away < best
        best = jnp.where(better, away, best)
        chosen = [jnp.where(better, p[j : j + 1], c) for p, c in zip(packed, chosen)]
    total, layers = diagonal_ref.shape
    chosen = [jnp.broadcast_to(c, (CHUNK, layers)) for c in chosen]
    center, answer, residual = chosen[0], chosen[1:4], chosen[4:8]
    for start in range(0, total, CHUNK):
        here = slice(start, start + CHUNK)
        diagonal = diagonal_ref[here]
        for (low, high), stream in zip(SPLITS, streams):
            for at in range(high - low):
                values = [ref[at, here] for ref in stream]
                q1, q2, q3 = powers(center, *values)
                solution_ref[low + at, here] = answer[0] * values[0] + answer[1] * q1 + answer[2] * q2
                residual_ref[low + at, here] = diagonal * (
                    residual[0] * values[0] + residual[1] * q1 + residual[2] * q2 + residual[3] * q3
                )


def call(kernel, out_shapes, *args, scratch=(), place=pltpu.VMEM):
    whole = pl.BlockSpec(memory_space=pltpu.VMEM)
    if place is pltpu.HBM:
        args = [pltpu.with_memory_space_constraint(a, place) for a in args]
    outs = [o if isinstance(o, jax.ShapeDtypeStruct) else jax.ShapeDtypeStruct(o, jnp.float32) for o in out_shapes]
    return pl.pallas_call(
        kernel,
        out_shape=outs,
        in_specs=[pl.BlockSpec(memory_space=place)] * len(args),
        out_specs=[whole] * len(out_shapes),
        scratch_shapes=[pltpu.VMEM(s, jnp.float32) if isinstance(s, tuple) else s for s in scratch],
        compiler_params=pltpu.CompilerParams(vmem_limit_bytes=24 * 2**20),
    )(*args)


def ring_pairs(groups, tiles):
    beside = [(g * tiles + i, g * tiles + (i ^ 1)) for g in range(groups) for i in range(tiles)]
    across = []
    for g in range(groups):
        for i in range(tiles):
            j = i - 1 if i % 2 == 0 else i + 1
            if j < 0 or j >= tiles:
                across.append((g * tiles + i, (1 - g) * tiles + i))
            else:
                across.append((g * tiles + i, g * tiles + j))
    return beside, across


NAMES = ("diamond", "tile")


def exchange(value):
    beside, across = ring_pairs(lax.axis_size("diamond"), lax.axis_size("tile"))
    far = lax.ppermute(value, NAMES, across)
    near = lax.ppermute(value, NAMES, beside)
    return near, far


def body(adjoint_temp, misfit, viscosity, velocity, forcing, edge_table, pole_table):
    rows, layers = adjoint_temp.shape[2:]
    devices = lax.axis_size("diamond") * lax.axis_size("tile")
    flat, triple = (rows, layers), (3, rows, layers)
    temp, source, visc = (v.reshape(flat) for v in (adjoint_temp, misfit, viscosity))
    visc_near, visc_far = exchange(visc[None])
    temp_near, temp_far = exchange(temp[None])
    table = pltpu.VMEM(edge_table.shape, edge_table.dtype)
    half, side, base, right, part, speed, matrix = call(
        local_kernel,
        [flat, (4, *flat), flat, triple, flat, flat, jax.ShapeDtypeStruct((rows, rows), jnp.bfloat16)],
        temp, source, visc, velocity.reshape(triple), forcing.reshape(triple), edge_table, pole_table,
        scratch=[flat, flat, flat, triple, table, table, pltpu.SemaphoreType.DMA((7,))],
        place=pltpu.HBM,
    )
    shapes = [(high - low, rows, layers) for low, high in SPLITS]
    adjoint_next, weights, diagonal, *first = call(
        prepare_kernel, [flat, (6, *flat), flat, *shapes],
        half, side, base, right, part, speed, matrix, visc_near, temp_near, visc_far, temp_far,
        scratch=[(1, *flat), (1, *flat)],
    )
    streams = [[field] for field in first]
    swapped = [exchange(field) for field in first]
    latest = first[-1]
    for step in range(ITERS - 1):
        for i, shape in enumerate(shapes):
            near, far = swapped[i]
            (latest,) = call(
                apply_kernel, [shape], far, near, streams[i][-1], weights, matrix, latest, scratch=[shape]
            )
            swapped[i] = exchange(latest)
            streams[i].append(latest)
    many = (len(CENTERS), *triple)
    moments, left, shift = call(
        early_kernel, [(8, 128), many, many], diagonal, *[field for stream in streams for field in stream]
    )
    for i, shape in enumerate(shapes):
        near, far = swapped[i]
        sums = (8, 128) if i + 1 < len(shapes) else (devices, 1, 128)
        field, moments = call(
            functools.partial(last_kernel, SPLITS[i][0]), [shape, sums],
            far, near, streams[i][-1], weights, matrix, moments, left, shift, scratch=[shape],
        )
        streams[i].append(field)
    moments = lax.all_to_all(moments, NAMES, 0, 0)
    fields = [field for stream in streams for field in stream]
    answer, residual = call(finish_kernel, [triple, triple], moments, diagonal, *fields)
    whole = (3, 1, 1, rows, layers)
    return answer.reshape(whole), residual.reshape(whole), adjoint_next.reshape(adjoint_temp.shape)


def solution(mesh):
    flat = P("diamond", "tile", None, None)
    triple = P(None, "diamond", "tile", None, None)
    return jax.shard_map(
        body,
        mesh=mesh,
        in_specs=(flat, flat, flat, triple, triple, P(), P()),
        out_specs=(triple, triple, flat),
        check_vma=False,
    )
```

time: 263 us -> 54.5 us (0.21)
  blocking collectives: 121 us -> 14.4 us
  waiting for transfers between devices: 43 us -> 3.51 us
  local copies, waits for them, and re-layouts: 38.7 us -> 0 us
  other arithmetic: 23 us -> 0 us
  between operations: 10.8 us -> 0.73 us
  Pallas kernels: 0 us -> 8.97 us
    psum x3 -> x0, blocking collectives: 121 us -> none  [products(): lax.psum((jnp.sum(residual * precond), jnp.sum(precond * image)), ('diamo...]
    ppermute x12 -> x22, waiting for transfers between devices: 43 us -> 3.51 us  [the longest x11 3.49 us: exchange(): far = lax.ppermute(value, NAMES, across)]
    gather x8 -> x0, local copies, waits for them, and re-layouts: 15.7 us -> none  [the longest x4 8.4 us: assemble(): from_pole = jnp.take(received[:, :, 0], pole_line, axis=2)]
    all_to_all x0 -> x1, blocking collectives: none -> 14.4 us  [body(): moments = lax.all_to_all(moments, NAMES, 0, 0)]
    reduce_sum x3 -> x0, other arithmetic: 14.2 us -> none  [products(): jnp.sum(precond * image)]
    unnamed x43 -> x0, local copies, waits for them, and re-layouts: 10.8 us -> none
    pallas_call x0 -> x13, Pallas kernels: none -> 8.97 us  [call(): pl.pallas_call(kernel, out_shape=outs, in_specs=[pl.BlockSpec(memory_spac...]
    slice x9 -> x0, local copies, waits for them, and re-layouts: 8.62 us -> none  [the longest x3 3.16 us: assemble(): y_after = jnp.concatenate([field[:, :, :, 1:], zeros_y], axis=3)]
  transfers between devices with their start and end apart: 12 -> 22, of which waited for: 4 -> 2; matrix products, arithmetic and copies ran while one was open for 13% -> 0% of each run, Pallas kernels for 0% -> 11%
where the time goes in v1:
time: 54.5 us; the launch traced here: 54.4 us
  starting transfers between devices  26.8 us (49%)
  blocking collectives  14.4 us (26%)
  Pallas kernels  8.97 us (16%)
  waiting for transfers between devices  3.51 us (6%)
  between operations  0.73 us (1%)
    ppermute x11, starting transfers between devices, exchange(): far = lax.ppermute(value, NAMES, across)  15.3 us
    all_to_all x1, blocking collectives, body(): moments = lax.all_to_all(moments, NAMES, 0, 0)  14.4 us
    ppermute x11, starting transfers between devices, exchange(): near = lax.ppermute(value, NAMES, beside)  11.4 us
    pallas_call x13, Pallas kernels, call(): pl.pallas_call(kernel, out_shape=outs, in_specs=[pl.BlockSpec(memory_spac...  8.97 us
    ppermute x11, waiting for transfers between devices, exchange(): far = lax.ppermute(value, NAMES, across)  3.49 us
  transfers between devices with their start and end apart: 22, of which 2 were waited for; matrix products, arithmetic and copies ran while one was open for 0% of the time, Pallas kernels for 11%

profile of v1, /device:TPU:0, one launch (start us, length us, event | category | flops | bytes accessed | tf_op | source)
XLA Modules:
  0.0 54.4 jit_solution(5754253587409965444)
XLA Ops:
  0.6 0.5 collective-permute-start
  1.2 0.1 collective-permute-start.1
  1.2 2.9 %collective-permute-start.2 = (f32[1,256,128]{2,1,0:T(8,128)}, f32[1,256,128]{2,1,0:T(8,128)S(1)}, u32[]{:S(2)}, u32[]{:S(2)}) collective-permute-start(f32[1,256,128]{2,1,0:T(8,128)} %bitcast.18), channel_id=1, source_target_pairs={{0,16},{1,2},{2,1},{3,4},{4,3},{5,6},{6,5},{7,8},{8,7},{9,10},{10,... | collective-permute-start | bytes 393224 | tf_op jit(solution)/shard_map/ppermute | solution.py:342
  4.1 0.0 collective-permute-start.3
  4.2 1.7 %shard_map.94 = (f32[256,128]{1,0:T(8,128)S(1)}, f32[4,256,128]{2,1,0:T(8,128)S(1)}, f32[256,128]{1,0:T(8,128)S(1)}, f32[3,256,128]{2,1,0:T(8,128)S(1)}, f32[256...) custom-call(f32[256,128]{1,0:T(8,128)} %bitcast.22, f32[256,128]{1,0:T(8,128)} %bitcast.16, ...), custom_call_target="tpu_custom_call" | custom-call | tf_op jit(solution)/shard_map/pallas_call | solution.py:314
  5.9 0.0 collective-permute-done.1.temp_near_ref
  5.9 1.4 %collective-permute-done.2.visc_far_ref = f32[1,256,128]{2,1,0:T(8,128)S(1)} collective-permute-done((f32[1,256,128]{2,1,0:T(8,128)}, f32[1,256,128]{2,1,0:T(8,128)S(1)}, u32[]{:S(2)}, u32[]{:S(2)}) %collective-permute-start.2) | collective-permute-done | bytes 131104 | tf_op jit(solution)/shard_map/ppermute | solution.py:342
  7.3 2.0 %collective-permute-done.3.temp_far_ref = f32[1,256,128]{2,1,0:T(8,128)S(1)} collective-permute-done((f32[1,256,128]{2,1,0:T(8,128)}, f32[1,256,128]{2,1,0:T(8,128)S(1)}, u32[]{:S(2)}, u32[]{:S(2)}) %collective-permute-start.3) | collective-permute-done | bytes 131104 | tf_op jit(solution)/shard_map/ppermute | solution.py:342
  9.3 1.0 %shard_map.95 = (f32[256,128]{1,0:T(8,128)}, f32[6,256,128]{2,1,0:T(8,128)S(1)}, f32[256,128]{1,0:T(8,128)S(1)}, f32[1,256,128]{2,1,0:T(8,128)S(1)}, f32[1,256,1...) custom-call(f32[256,128]{1,0:T(8,128)S(1)} %get-tuple-element.27.half_ref, f32[4,256,128]{2,1,0:T(8,128)S(1)} %get-tuple-element.28.side_ref, ...), custom_call_target="tpu_custom_call" | custom-call | tf_op jit(solution)/shard_map/pallas_call | solution.py:314
  10.3 1.4 %collective-permute-start.8 = (f32[1,256,128]{2,1,0:T(8,128)S(1)}, f32[1,256,128]{2,1,0:T(8,128)S(1)}, u32[]{:S(2)}, u32[]{:S(2)}) collective-permute-start(f32[1,256,128]{2,1,0:T(8,128)S(1)} %get-tuple-element.37.field_ref.refs_0_), channel_id=1, source_target_pairs={{0,16},{1,2},{2,1},{3,4},{4,3},{5,6},{6,5},{7,8},{8,7},{9,10},{10,... | collective-permute-start | bytes 393224 | tf_op jit(solution)/shard_map/ppermute | solution.py:342
  11.7 2.4 %collective-permute-start.9 = (f32[1,256,128]{2,1,0:T(8,128)S(1)}, f32[1,256,128]{2,1,0:T(8,128)S(1)}, u32[]{:S(2)}, u32[]{:S(2)}) collective-permute-start(f32[1,256,128]{2,1,0:T(8,128)S(1)} %get-tuple-element.37.field_ref.refs_0_), channel_id=1, source_target_pairs={{0,1},{1,0},{2,3},{3,2},{4,5},{5,4},{6,7},{7,6},{8,9},{9,8},{10,11... | collective-permute-start | bytes 393224 | tf_op jit(solution)/shard_map/ppermute | solution.py:343
  14.1 1.5 %collective-permute-start.6 = (f32[1,256,128]{2,1,0:T(8,128)S(1)}, f32[1,256,128]{2,1,0:T(8,128)S(1)}, u32[]{:S(2)}, u32[]{:S(2)}) collective-permute-start(f32[1,256,128]{2,1,0:T(8,128)S(1)} %get-tuple-element.36.field_ref.refs_3_.refs_4_), channel_id=1, source_target_pairs={{0,16},{1,2},{2,1},{3,4},{4,3},{5,6},{6,5},{7,8},{8,7},{9,10},{10,... | collective-permute-start | bytes 393224 | tf_op jit(solution)/shard_map/ppermute | solution.py:342
  15.6 0.0 collective-permute-start.7
  15.6 0.5 collective-permute-start.4
  16.1 0.0 collective-permute-done.8.far_ref
  16.1 2.1 %collective-permute-start.5 = (f32[1,256,128]{2,1,0:T(8,128)S(1)}, f32[1,256,128]{2,1,0:T(8,128)S(1)}, u32[]{:S(2)}, u32[]{:S(2)}) collective-permute-start(f32[1,256,128]{2,1,0:T(8,128)S(1)} %get-tuple-element.34.after_ref.field_ref.refs_6_.refs_8_), channel_id=1, source_target_pairs={{0,1},{1,0},{2,3},{3,2},{4,5},{5,4},{6,7},{7,6},{8,9},{9,8},{10,11... | collective-permute-start | bytes 393224 | tf_op jit(solution)/shard_map/ppermute | solution.py:343
  18.3 0.3 shard_map.96.after_ref.field_ref.refs_1_
  18.5 1.6 %collective-permute-start.14 = (f32[1,256,128]{2,1,0:T(8,128)S(1)}, f32[1,256,128]{2,1,0:T(8,128)S(1)}, u32[]{:S(2)}, u32[]{:S(2)}) collective-permute-start(f32[1,256,128]{2,1,0:T(8,128)S(1)} %shard_map.96.after_ref.field_ref.refs_1_), channel_id=1, source_target_pairs={{0,16},{1,2},{2,1},{3,4},{4,3},{5,6},{6,5},{7,8},{8,7},{9,10},{10,... | collective-permute-start | bytes 393224 | tf_op jit(solution)/shard_map/ppermute | solution.py:342
  20.1 0.0 collective-permute-done.6.far_ref
  20.1 1.0 %collective-permute-start.15 = (f32[1,256,128]{2,1,0:T(8,128)S(1)}, f32[1,256,128]{2,1,0:T(8,128)S(1)}, u32[]{:S(2)}, u32[]{:S(2)}) collective-permute-start(f32[1,256,128]{2,1,0:T(8,128)S(1)} %shard_map.96.after_ref.field_ref.refs_1_), channel_id=1, source_target_pairs={{0,1},{1,0},{2,3},{3,2},{4,5},{5,4},{6,7},{7,6},{8,9},{9,8},{10,11... | collective-permute-start | bytes 393224 | tf_op jit(solution)/shard_map/ppermute | solution.py:343
  21.1 0.0 collective-permute-done.7.near_ref
  21.1 0.3 shard_map.97.after_ref.field_ref.refs_4_.refs_5_
  21.3 1.6 %collective-permute-start.12 = (f32[1,256,128]{2,1,0:T(8,128)S(1)}, f32[1,256,128]{2,1,0:T(8,128)S(1)}, u32[]{:S(2)}, u32[]{:S(2)}) collective-permute-start(f32[1,256,128]{2,1,0:T(8,128)S(1)} %shard_map.97.after_ref.field_ref.refs_4_.refs_5_), channel_id=1, source_target_pairs={{0,16},{1,2},{2,1},{3,4},{4,3},{5,6},{6,5},{7,8},{8,7},{9,10},{10,... | collective-permute-start | bytes 393224 | tf_op jit(solution)/shard_map/ppermute | solution.py:342
  22.9 0.0 collective-permute-done.4.far_ref
  22.9 1.0 %collective-permute-start.13 = (f32[1,256,128]{2,1,0:T(8,128)S(1)}, f32[1,256,128]{2,1,0:T(8,128)S(1)}, u32[]{:S(2)}, u32[]{:S(2)}) collective-permute-start(f32[1,256,128]{2,1,0:T(8,128)S(1)} %shard_map.97.after_ref.field_ref.refs_4_.refs_5_), channel_id=1, source_target_pairs={{0,1},{1,0},{2,3},{3,2},{4,5},{5,4},{6,7},{7,6},{8,9},{9,8},{10,11... | collective-permute-start | bytes 393224 | tf_op jit(solution)/shard_map/ppermute | solution.py:343
  23.9 0.0 collective-permute-done.5.near_ref
  23.9 0.3 shard_map.98.after_ref.field_ref.refs_7_.refs_9_
  24.1 1.6 %collective-permute-start.10 = (f32[1,256,128]{2,1,0:T(8,128)S(1)}, f32[1,256,128]{2,1,0:T(8,128)S(1)}, u32[]{:S(2)}, u32[]{:S(2)}) collective-permute-start(f32[1,256,128]{2,1,0:T(8,128)S(1)} %shard_map.98.after_ref.field_ref.refs_7_.refs_9_), channel_id=1, source_target_pairs={{0,16},{1,2},{2,1},{3,4},{4,3},{5,6},{6,5},{7,8},{8,7},{9,10},{10,... | collective-permute-start | bytes 393224 | tf_op jit(solution)/shard_map/ppermute | solution.py:342
  25.7 0.0 collective-permute-done.14.far_ref
  25.7 0.0 collective-permute-start.11
  25.7 0.0 collective-permute-done.15.near_ref
  25.7 0.3 shard_map.99.after_ref.refs_2_.field_ref
  26.0 1.2 %collective-permute-start.20 = (f32[1,256,128]{2,1,0:T(8,128)S(1)}, f32[1,256,128]{2,1,0:T(8,128)S(1)}, u32[]{:S(2)}, u32[]{:S(2)}) collective-permute-start(f32[1,256,128]{2,1,0:T(8,128)S(1)} %shard_map.99.after_ref.refs_2_.field_ref), channel_id=1, source_target_pairs={{0,16},{1,2},{2,1},{3,4},{4,3},{5,6},{6,5},{7,8},{8,7},{9,10},{10,... | collective-permute-start | bytes 393224 | tf_op jit(solution)/shard_map/ppermute | solution.py:342
  27.1 2.4 %collective-permute-start.21 = (f32[1,256,128]{2,1,0:T(8,128)S(1)}, f32[1,256,128]{2,1,0:T(8,128)S(1)}, u32[]{:S(2)}, u32[]{:S(2)}) collective-permute-start(f32[1,256,128]{2,1,0:T(8,128)S(1)} %shard_map.99.after_ref.refs_2_.field_ref), channel_id=1, source_target_pairs={{0,1},{1,0},{2,3},{3,2},{4,5},{5,4},{6,7},{7,6},{8,9},{9,8},{10,11... | collective-permute-start | bytes 393224 | tf_op jit(solution)/shard_map/ppermute | solution.py:343
  29.5 0.3 shard_map.100.after_ref.refs_5_.field_ref.refs_6_
  29.8 1.6 %collective-permute-start.18 = (f32[1,256,128]{2,1,0:T(8,128)S(1)}, f32[1,256,128]{2,1,0:T(8,128)S(1)}, u32[]{:S(2)}, u32[]{:S(2)}) collective-permute-start(f32[1,256,128]{2,1,0:T(8,128)S(1)} %shard_map.100.after_ref.refs_5_.field_ref.refs_6_), channel_id=1, source_target_pairs={{0,16},{1,2},{2,1},{3,4},{4,3},{5,6},{6,5},{7,8},{8,7},{9,10},{10,... | collective-permute-start | bytes 393224 | tf_op jit(solution)/shard_map/ppermute | solution.py:342
  31.3 0.0 collective-permute-done.10.far_ref
  31.3 1.0 %collective-permute-start.19 = (f32[1,256,128]{2,1,0:T(8,128)S(1)}, f32[1,256,128]{2,1,0:T(8,128)S(1)}, u32[]{:S(2)}, u32[]{:S(2)}) collective-permute-start(f32[1,256,128]{2,1,0:T(8,128)S(1)} %shard_map.100.after_ref.refs_5_.field_ref.refs_6_), channel_id=1, source_target_pairs={{0,1},{1,0},{2,3},{3,2},{4,5},{5,4},{6,7},{7,6},{8,9},{9,8},{10,11... | collective-permute-start | bytes 393224 | tf_op jit(solution)/shard_map/ppermute | solution.py:343
  32.3 0.0 collective-permute-done.11.near_ref
  32.3 0.3 shard_map.101.refs_8_.field_ref.refs_10_
  32.6 1.6 %collective-permute-start.16 = (f32[1,256,128]{2,1,0:T(8,128)S(1)}, f32[1,256,128]{2,1,0:T(8,128)S(1)}, u32[]{:S(2)}, u32[]{:S(2)}) collective-permute-start(f32[1,256,128]{2,1,0:T(8,128)S(1)} %shard_map.101.refs_8_.field_ref.refs_10_), channel_id=1, source_target_pairs={{0,16},{1,2},{2,1},{3,4},{4,3},{5,6},{6,5},{7,8},{8,7},{9,10},{10,... | collective-permute-start | bytes 393224 | tf_op jit(solution)/shard_map/ppermute | solution.py:342
  34.1 1.0 %collective-permute-start.17 = (f32[1,256,128]{2,1,0:T(8,128)S(1)}, f32[1,256,128]{2,1,0:T(8,128)S(1)}, u32[]{:S(2)}, u32[]{:S(2)}) collective-permute-start(f32[1,256,128]{2,1,0:T(8,128)S(1)} %shard_map.101.refs_8_.field_ref.refs_10_), channel_id=1, source_target_pairs={{0,1},{1,0},{2,3},{3,2},{4,5},{5,4},{6,7},{7,6},{8,9},{9,8},{10,11... | collective-permute-start | bytes 393224 | tf_op jit(solution)/shard_map/ppermute | solution.py:343
  35.1 2.0 %shard_map.102 = (f32[8,128]{1,0:T(8,128)S(1)}, f32[7,3,256,128]{3,2,1,0:T(8,128)S(1)}, f32[7,3,256,128]{3,2,1,0:T(8,128)S(1)}) custom-call(f32[256,128]{1,0:T(8,128)S(1)} %get-tuple-element.38.diagonal_ref, f32[1,256,128]{2,1,0:T(8,128)S(1)} %get-tuple-element.37.field_ref.refs_0_, f32[1,256,128]{2,1,0:T(8,128)S(1)} %shard_map.96.after_ref.field_ref.refs_1_, ...), custom_call_target="tpu_custom_call" | custom-call | tf_op jit(solution)/shard_map/pallas_call | solution.py:314
  37.2 0.5 shard_map.103
  37.6 0.5 shard_map.104
  38.1 0.5 shard_map.105
  38.6 14.4 %all_to_all.5.moments_ref = f32[32,1,128]{2,1,0:T(1,128)S(1)} all-to-all(f32[32,1,128]{2,1,0:T(1,128)S(1)} %get-tuple-element.44), channel_id=1, replica_groups=mesh['diamond'=2,'tile'=16] {'diamond','tile'}, dimensions={0} | all-to-all | bytes 32768 | tf_op jit(solution)/shard_map/all_to_all | solution.py:391
  53.0 1.4 %shard_map.106 = (f32[3,256,128]{2,1,0:T(8,128)}, f32[3,256,128]{2,1,0:T(8,128)}) custom-call(f32[32,1,128]{2,1,0:T(1,128)S(1)} %all_to_all.5.moments_ref, f32[256,128]{1,0:T(8,128)S(1)} %get-tuple-element.38.diagonal_ref, f32[1,256,128]{2,1,0:T(8,128)S(1)} %get-tuple-element.37.field_ref.refs_0_, f32[1,256,128]{2,1,0:T(8,128)S(1)} %shard_map.96.after_ref.field_ref.refs_1_, ...), custom_call_target="tpu_custom_call" | custom-call | tf_op jit(solution)/shard_map/pallas_call | solution.py:314
  (10 shorter events, 0.0 us)
Async XLA Ops:
  0.6 5.2 %collective-permute-start = (f32[1,256,128]{2,1,0:T(8,128)}, f32[1,256,128]{2,1,0:T(8,128)S(1)}, u32[]{:S(2)}, u32[]{:S(2)}) collective-permute-start(f32[1,256,128]{2,1,0:T(8,128)} %bitcast.17), channel_id=1, source_target_pairs={{0,1},{1,0},{2,3},{3,2},{4,5},{5,4},{6,7},{7,6},{8,9},{9,8},{10,11... | collective-permute-start | bytes 393224 | tf_op jit(solution)/shard_map/ppermute | solution.py:343
  1.2 4.7 %collective-permute-start.1 = (f32[1,256,128]{2,1,0:T(8,128)}, f32[1,256,128]{2,1,0:T(8,128)S(1)}, u32[]{:S(2)}, u32[]{:S(2)}) collective-permute-start(f32[1,256,128]{2,1,0:T(8,128)} %bitcast.20), channel_id=1, source_target_pairs={{0,1},{1,0},{2,3},{3,2},{4,5},{5,4},{6,7},{7,6},{8,9},{9,8},{10,11... | collective-permute-start | bytes 393224 | tf_op jit(solution)/shard_map/ppermute | solution.py:343
  1.2 6.1 %collective-permute-start.2 = (f32[1,256,128]{2,1,0:T(8,128)}, f32[1,256,128]{2,1,0:T(8,128)S(1)}, u32[]{:S(2)}, u32[]{:S(2)}) collective-permute-start(f32[1,256,128]{2,1,0:T(8,128)} %bitcast.18), channel_id=1, source_target_pairs={{0,16},{1,2},{2,1},{3,4},{4,3},{5,6},{6,5},{7,8},{8,7},{9,10},{10,... | collective-permute-start | bytes 393224 | tf_op jit(solution)/shard_map/ppermute | solution.py:342
  4.1 5.2 %collective-permute-start.3 = (f32[1,256,128]{2,1,0:T(8,128)}, f32[1,256,128]{2,1,0:T(8,128)S(1)}, u32[]{:S(2)}, u32[]{:S(2)}) collective-permute-start(f32[1,256,128]{2,1,0:T(8,128)} %bitcast.21), channel_id=1, source_target_pairs={{0,16},{1,2},{2,1},{3,4},{4,3},{5,6},{6,5},{7,8},{8,7},{9,10},{10,... | collective-permute-start | bytes 393224 | tf_op jit(solution)/shard_map/ppermute | solution.py:342
  10.3 5.8 %collective-permute-start.8 = (f32[1,256,128]{2,1,0:T(8,128)S(1)}, f32[1,256,128]{2,1,0:T(8,128)S(1)}, u32[]{:S(2)}, u32[]{:S(2)}) collective-permute-start(f32[1,256,128]{2,1,0:T(8,128)S(1)} %get-tuple-element.37.field_ref.refs_0_), channel_id=1, source_target_pairs={{0,16},{1,2},{2,1},{3,4},{4,3},{5,6},{6,5},{7,8},{8,7},{9,10},{10,... | collective-permute-start | bytes 393224 | tf_op jit(solution)/shard_map/ppermute | solution.py:342
  11.7 6.6 %collective-permute-start.9 = (f32[1,256,128]{2,1,0:T(8,128)S(1)}, f32[1,256,128]{2,1,0:T(8,128)S(1)}, u32[]{:S(2)}, u32[]{:S(2)}) collective-permute-start(f32[1,256,128]{2,1,0:T(8,128)S(1)} %get-tuple-element.37.field_ref.refs_0_), channel_id=1, source_target_pairs={{0,1},{1,0},{2,3},{3,2},{4,5},{5,4},{6,7},{7,6},{8,9},{9,8},{10,11... | collective-permute-start | bytes 393224 | tf_op jit(solution)/shard_map/ppermute | solution.py:343
  14.1 6.0 %collective-permute-start.6 = (f32[1,256,128]{2,1,0:T(8,128)S(1)}, f32[1,256,128]{2,1,0:T(8,128)S(1)}, u32[]{:S(2)}, u32[]{:S(2)}) collective-permute-start(f32[1,256,128]{2,1,0:T(8,128)S(1)} %get-tuple-element.36.field_ref.refs_3_.refs_4_), channel_id=1, source_target_pairs={{0,16},{1,2},{2,1},{3,4},{4,3},{5,6},{6,5},{7,8},{8,7},{9,10},{10,... | collective-permute-start | bytes 393224 | tf_op jit(solution)/shard_map/ppermute | solution.py:342
  15.6 5.5 %collective-permute-start.7 = (f32[1,256,128]{2,1,0:T(8,128)S(1)}, f32[1,256,128]{2,1,0:T(8,128)S(1)}, u32[]{:S(2)}, u32[]{:S(2)}) collective-permute-start(f32[1,256,128]{2,1,0:T(8,128)S(1)} %get-tuple-element.36.field_ref.refs_3_.refs_4_), channel_id=1, source_target_pairs={{0,1},{1,0},{2,3},{3,2},{4,5},{5,4},{6,7},{7,6},{8,9},{9,8},{10,11... | collective-permute-start | bytes 393224 | tf_op jit(solution)/shard_map/ppermute | solution.py:343
  15.6 7.3 %collective-permute-start.4 = (f32[1,256,128]{2,1,0:T(8,128)S(1)}, f32[1,256,128]{2,1,0:T(8,128)S(1)}, u32[]{:S(2)}, u32[]{:S(2)}) collective-permute-start(f32[1,256,128]{2,1,0:T(8,128)S(1)} %get-tuple-element.34.after_ref.field_ref.refs_6_.refs_8_), channel_id=1, source_target_pairs={{0,16},{1,2},{2,1},{3,4},{4,3},{5,6},{6,5},{7,8},{8,7},{9,10},{10,... | collective-permute-start | bytes 393224 | tf_op jit(solution)/shard_map/ppermute | solution.py:342
  16.1 7.8 %collective-permute-start.5 = (f32[1,256,128]{2,1,0:T(8,128)S(1)}, f32[1,256,128]{2,1,0:T(8,128)S(1)}, u32[]{:S(2)}, u32[]{:S(2)}) collective-permute-start(f32[1,256,128]{2,1,0:T(8,128)S(1)} %get-tuple-element.34.after_ref.field_ref.refs_6_.refs_8_), channel_id=1, source_target_pairs={{0,1},{1,0},{2,3},{3,2},{4,5},{5,4},{6,7},{7,6},{8,9},{9,8},{10,11... | collective-permute-start | bytes 393224 | tf_op jit(solution)/shard_map/ppermute | solution.py:343
  18.5 7.2 %collective-permute-start.14 = (f32[1,256,128]{2,1,0:T(8,128)S(1)}, f32[1,256,128]{2,1,0:T(8,128)S(1)}, u32[]{:S(2)}, u32[]{:S(2)}) collective-permute-start(f32[1,256,128]{2,1,0:T(8,128)S(1)} %shard_map.96.after_ref.field_ref.refs_1_), channel_id=1, source_target_pairs={{0,16},{1,2},{2,1},{3,4},{4,3},{5,6},{6,5},{7,8},{8,7},{9,10},{10,... | collective-permute-start | bytes 393224 | tf_op jit(solution)/shard_map/ppermute | solution.py:342
  20.1 5.6 %collective-permute-start.15 = (f32[1,256,128]{2,1,0:T(8,128)S(1)}, f32[1,256,128]{2,1,0:T(8,128)S(1)}, u32[]{:S(2)}, u32[]{:S(2)}) collective-permute-start(f32[1,256,128]{2,1,0:T(8,128)S(1)} %shard_map.96.after_ref.field_ref.refs_1_), channel_id=1, source_target_pairs={{0,1},{1,0},{2,3},{3,2},{4,5},{5,4},{6,7},{7,6},{8,9},{9,8},{10,11... | collective-permute-start | bytes 393224 | tf_op jit(solution)/shard_map/ppermute | solution.py:343
  21.3 5.8 %collective-permute-start.12 = (f32[1,256,128]{2,1,0:T(8,128)S(1)}, f32[1,256,128]{2,1,0:T(8,128)S(1)}, u32[]{:S(2)}, u32[]{:S(2)}) collective-permute-start(f32[1,256,128]{2,1,0:T(8,128)S(1)} %shard_map.97.after_ref.field_ref.refs_4_.refs_5_), channel_id=1, source_target_pairs={{0,16},{1,2},{2,1},{3,4},{4,3},{5,6},{6,5},{7,8},{8,7},{9,10},{10,... | collective-permute-start | bytes 393224 | tf_op jit(solution)/shard_map/ppermute | solution.py:342
  22.9 6.6 %collective-permute-start.13 = (f32[1,256,128]{2,1,0:T(8,128)S(1)}, f32[1,256,128]{2,1,0:T(8,128)S(1)}, u32[]{:S(2)}, u32[]{:S(2)}) collective-permute-start(f32[1,256,128]{2,1,0:T(8,128)S(1)} %shard_map.97.after_ref.field_ref.refs_4_.refs_5_), channel_id=1, source_target_pairs={{0,1},{1,0},{2,3},{3,2},{4,5},{5,4},{6,7},{7,6},{8,9},{9,8},{10,11... | collective-permute-start | bytes 393224 | tf_op jit(solution)/shard_map/ppermute | solution.py:343
  24.1 7.2 %collective-permute-start.10 = (f32[1,256,128]{2,1,0:T(8,128)S(1)}, f32[1,256,128]{2,1,0:T(8,128)S(1)}, u32[]{:S(2)}, u32[]{:S(2)}) collective-permute-start(f32[1,256,128]{2,1,0:T(8,128)S(1)} %shard_map.98.after_ref.field_ref.refs_7_.refs_9_), channel_id=1, source_target_pairs={{0,16},{1,2},{2,1},{3,4},{4,3},{5,6},{6,5},{7,8},{8,7},{9,10},{10,... | collective-permute-start | bytes 393224 | tf_op jit(solution)/shard_map/ppermute | solution.py:342
  25.7 6.6 %collective-permute-start.11 = (f32[1,256,128]{2,1,0:T(8,128)S(1)}, f32[1,256,128]{2,1,0:T(8,128)S(1)}, u32[]{:S(2)}, u32[]{:S(2)}) collective-permute-start(f32[1,256,128]{2,1,0:T(8,128)S(1)} %shard_map.98.after_ref.field_ref.refs_7_.refs_9_), channel_id=1, source_target_pairs={{0,1},{1,0},{2,3},{3,2},{4,5},{5,4},{6,7},{7,6},{8,9},{9,8},{10,11... | collective-permute-start | bytes 393224 | tf_op jit(solution)/shard_map/ppermute | solution.py:343
  26.0 8.2 %collective-permute-start.20 = (f32[1,256,128]{2,1,0:T(8,128)S(1)}, f32[1,256,128]{2,1,0:T(8,128)S(1)}, u32[]{:S(2)}, u32[]{:S(2)}) collective-permute-start(f32[1,256,128]{2,1,0:T(8,128)S(1)} %shard_map.99.after_ref.refs_2_.field_ref), channel_id=1, source_target_pairs={{0,16},{1,2},{2,1},{3,4},{4,3},{5,6},{6,5},{7,8},{8,7},{9,10},{10,... | collective-permute-start | bytes 393224 | tf_op jit(solution)/shard_map/ppermute | solution.py:342
  27.1 10.0 %collective-permute-start.21 = (f32[1,256,128]{2,1,0:T(8,128)S(1)}, f32[1,256,128]{2,1,0:T(8,128)S(1)}, u32[]{:S(2)}, u32[]{:S(2)}) collective-permute-start(f32[1,256,128]{2,1,0:T(8,128)S(1)} %shard_map.99.after_ref.refs_2_.field_ref), channel_id=1, source_target_pairs={{0,1},{1,0},{2,3},{3,2},{4,5},{5,4},{6,7},{7,6},{8,9},{9,8},{10,11... | collective-permute-start | bytes 393224 | tf_op jit(solution)/shard_map/ppermute | solution.py:343
  29.8 7.9 %collective-permute-start.18 = (f32[1,256,128]{2,1,0:T(8,128)S(1)}, f32[1,256,128]{2,1,0:T(8,128)S(1)}, u32[]{:S(2)}, u32[]{:S(2)}) collective-permute-start(f32[1,256,128]{2,1,0:T(8,128)S(1)} %shard_map.100.after_ref.refs_5_.field_ref.refs_6_), channel_id=1, source_target_pairs={{0,16},{1,2},{2,1},{3,4},{4,3},{5,6},{6,5},{7,8},{8,7},{9,10},{10,... | collective-permute-start | bytes 393224 | tf_op jit(solution)/shard_map/ppermute | solution.py:342
  31.3 6.3 %collective-permute-start.19 = (f32[1,256,128]{2,1,0:T(8,128)S(1)}, f32[1,256,128]{2,1,0:T(8,128)S(1)}, u32[]{:S(2)}, u32[]{:S(2)}) collective-permute-start(f32[1,256,128]{2,1,0:T(8,128)S(1)} %shard_map.100.after_ref.refs_5_.field_ref.refs_6_), channel_id=1, source_target_pairs={{0,1},{1,0},{2,3},{3,2},{4,5},{5,4},{6,7},{7,6},{8,9},{9,8},{10,11... | collective-permute-start | bytes 393224 | tf_op jit(solution)/shard_map/ppermute | solution.py:343
  32.6 5.5 %collective-permute-start.16 = (f32[1,256,128]{2,1,0:T(8,128)S(1)}, f32[1,256,128]{2,1,0:T(8,128)S(1)}, u32[]{:S(2)}, u32[]{:S(2)}) collective-permute-start(f32[1,256,128]{2,1,0:T(8,128)S(1)} %shard_map.101.refs_8_.field_ref.refs_10_), channel_id=1, source_target_pairs={{0,16},{1,2},{2,1},{3,4},{4,3},{5,6},{6,5},{7,8},{8,7},{9,10},{10,... | collective-permute-start | bytes 393224 | tf_op jit(solution)/shard_map/ppermute | solution.py:342
  34.1 4.0 %collective-permute-start.17 = (f32[1,256,128]{2,1,0:T(8,128)S(1)}, f32[1,256,128]{2,1,0:T(8,128)S(1)}, u32[]{:S(2)}, u32[]{:S(2)}) collective-permute-start(f32[1,256,128]{2,1,0:T(8,128)S(1)} %shard_map.101.refs_8_.field_ref.refs_10_), channel_id=1, source_target_pairs={{0,1},{1,0},{2,3},{3,2},{4,5},{5,4},{6,7},{7,6},{8,9},{9,8},{10,11... | collective-permute-start | bytes 393224 | tf_op jit(solution)/shard_map/ppermute | solution.py:343

commit v2 on v1

--- a/solution.py
+++ b/solution.py
@@ -101,35 +101,40 @@
         speed_ref[here] = half * velocity_ref[0, here]
 
 
-def prepare_kernel(
-    half_ref, side_ref, base_ref, right_ref, part_ref, speed_ref, matrix_ref,
-    visc_near_ref, temp_near_ref, visc_far_ref, temp_far_ref,
-    next_ref, weights_ref, diagonal_ref, *refs,
+def weigh_kernel(
+    far_ref, near_ref, half_ref, side_ref, base_ref, right_ref, matrix_ref,
+    weights_ref, diagonal_ref, inverse_ref, *refs,
 ):
-    *first_refs, moved_visc_ref, moved_temp_ref = refs
-    unfold(matrix_ref, visc_far_ref, moved_visc_ref)
-    unfold(matrix_ref, temp_far_ref, moved_temp_ref)
+    *first_refs, moved_ref = refs
+    unfold(matrix_ref, far_ref, moved_ref)
     for start in range(0, half_ref.shape[0], CHUNK):
         here = slice(start, start + CHUNK)
-        near, far = temp_near_ref[0, here], moved_temp_ref[0, here]
+        visc = half_ref[here]
+        weights = [visc + 0.5 * near_ref[0, here], visc + 0.5 * moved_ref[0, here]]
+        diagonal = base_ref[here] + weights[0] + weights[1]
+        diagonal_ref[here] = diagonal
+        inverse = 1.0 / diagonal
+        inverse_ref[here] = inverse
+        for (low, high), first_ref in zip(SPLITS, first_refs):
+            for at in range(low, high):
+                first_ref[at - low, here] = right_ref[at, here] * inverse
+        weights += [side_ref[k, here] for k in range(4)]
+        for k in range(6):
+            weights_ref[k, here] = weights[k] * inverse
+
+
+def step_kernel(
+    far_ref, near_ref, right_ref, part_ref, speed_ref, inverse_ref, matrix_ref, next_ref, first_ref, moved_ref
+):
+    unfold(matrix_ref, far_ref, moved_ref)
+    for start in range(0, part_ref.shape[0], CHUNK):
+        here = slice(start, start + CHUNK)
+        near, far = near_ref[0, here], moved_ref[0, here]
         adjoint_next = part_ref[here] + TIME_STEP * (
             DIFFUSION * (near + far) + speed_ref[here] * (near - far)
         )
         next_ref[here] = adjoint_next
-        visc = half_ref[here]
-        weights = [visc + 0.5 * visc_near_ref[0, here], visc + 0.5 * moved_visc_ref[0, here]]
-        diagonal = base_ref[here] + weights[0] + weights[1]
-        diagonal_ref[here] = diagonal
-        inverse = 1.0 / diagonal
-        weights += [side_ref[k, here] for k in range(4)]
-        for k in range(6):
-            weights_ref[k, here] = weights[k] * inverse
-        for (low, high), first_ref in zip(SPLITS, first_refs):
-            for at in range(low, high):
-                right = right_ref[at, here]
-                if at == 2:
-                    right = right + BUOYANCY * adjoint_next
-                first_ref[at - low, here] = right * inverse
+        first_ref[0, here] = (right_ref[2, here] + BUOYANCY * adjoint_next) * inverse_ref[here]
 
 
 def average(start, at, field_ref, near_ref, moved_ref, weights):
@@ -139,7 +144,7 @@
     return sum(w * v for w, v in zip(weights, around))
 
 
-def apply_kernel(far_ref, near_ref, field_ref, weights_ref, matrix_ref, after_ref, out_ref, moved_ref):
+def apply_kernel(far_ref, near_ref, field_ref, weights_ref, matrix_ref, out_ref, moved_ref):
     unfold(matrix_ref, far_ref, moved_ref)
     for start in range(0, field_ref.shape[1], CHUNK):
         here = slice(start, start + CHUNK)
@@ -360,22 +365,23 @@
         place=pltpu.HBM,
     )
     shapes = [(high - low, rows, layers) for low, high in SPLITS]
-    adjoint_next, weights, diagonal, *first = call(
-        prepare_kernel, [flat, (6, *flat), flat, *shapes],
-        half, side, base, right, part, speed, matrix, visc_near, temp_near, visc_far, temp_far,
-        scratch=[(1, *flat), (1, *flat)],
+    weights, diagonal, inverse, *first = call(
+        weigh_kernel, [(6, *flat), flat, flat, *shapes[:-1]],
+        visc_far, visc_near, half, side, base, right, matrix, scratch=[(1, *flat)],
     )
+    adjoint_next, *rest = call(
+        step_kernel, [flat, shapes[-1]],
+        temp_far, temp_near, right, part, speed, inverse, matrix, scratch=[(1, *flat)],
+    )
+    first += rest
     streams = [[field] for field in first]
     swapped = [exchange(field) for field in first]
-    latest = first[-1]
     for step in range(ITERS - 1):
         for i, shape in enumerate(shapes):
             near, far = swapped[i]
-            (latest,) = call(
-                apply_kernel, [shape], far, near, streams[i][-1], weights, matrix, latest, scratch=[shape]
-            )
-            swapped[i] = exchange(latest)
-            streams[i].append(latest)
+            (field,) = call(apply_kernel, [shape], far, near, streams[i][-1], weights, matrix, scratch=[shape])
+            swapped[i] = exchange(field)
+            streams[i].append(field)
     many = (len(CENTERS), *triple)
     moments, left, shift = call(
         early_kernel, [(8, 128), many, many], diagonal, *[field for stream in streams for field in stream]

time: 54.5 us -> 51.1 us (0.938)
  waiting for transfers between devices: 3.51 us -> 0.44 us
  starting transfers between devices: 26.8 us -> 26.2 us
    ppermute x11, waiting for transfers between devices: 3.49 us -> 0.41 us  [exchange(): far = lax.ppermute(value, NAMES, across)]
    ppermute x11, starting transfers between devices: 11.4 us -> 8.97 us  [exchange(): near = lax.ppermute(value, NAMES, beside)]
    ppermute x11, starting transfers between devices: 15.3 us -> 17.3 us  [exchange(): far = lax.ppermute(value, NAMES, across)]
    pallas_call x13 -> x14, Pallas kernels: 8.97 us -> 9.17 us  [call(): pl.pallas_call(kernel, out_shape=outs, in_specs=[pl.BlockSpec(memory_spac...]
  transfers between devices with their start and end apart: 22 -> 22, of which waited for: 2 -> 1; matrix products, arithmetic and copies ran while one was open for 0% -> 0% of each run, Pallas kernels for 11% -> 14%
where the time goes in v2:
time: 51.1 us; the launch traced here: 50.9 us
  starting transfers between devices  26.2 us (51%)
  blocking collectives  14.4 us (28%)
  Pallas kernels  9.17 us (18%)
  between operations  0.74 us (1%)
    ppermute x11, starting transfers between devices, exchange(): far = lax.ppermute(value, NAMES, across)  17.3 us
    all_to_all x1, blocking collectives, body(): moments = lax.all_to_all(moments, NAMES, 0, 0)  14.4 us
    pallas_call x14, Pallas kernels, call(): pl.pallas_call(kernel, out_shape=outs, in_specs=[pl.BlockSpec(memory_spac...  9.17 us
    ppermute x11, starting transfers between devices, exchange(): near = lax.ppermute(value, NAMES, beside)  8.97 us
  transfers between devices with their start and end apart: 22, of which 1 were waited for; matrix products, arithmetic and copies ran while one was open for 0% of the time, Pallas kernels for 14%

profile of v2, /device:TPU:0, one launch (start us, length us, event | category | flops | bytes accessed | tf_op | source)
XLA Modules:
  0.0 50.9 jit_solution(14160488530786467491)
XLA Ops:
  0.6 3.0 %collective-permute-start.2 = (f32[1,256,128]{2,1,0:T(8,128)}, f32[1,256,128]{2,1,0:T(8,128)S(1)}, u32[]{:S(2)}, u32[]{:S(2)}) collective-permute-start(f32[1,256,128]{2,1,0:T(8,128)} %bitcast.17), channel_id=1, source_target_pairs={{0,16},{1,2},{2,1},{3,4},{4,3},{5,6},{6,5},{7,8},{8,7},{9,10},{10,... | collective-permute-start | bytes 393224 | tf_op jit(solution)/shard_map/ppermute | solution.py:347
  3.6 0.1 collective-permute-start.3
  3.8 1.5 %collective-permute-start = (f32[1,256,128]{2,1,0:T(8,128)}, f32[1,256,128]{2,1,0:T(8,128)S(1)}, u32[]{:S(2)}, u32[]{:S(2)}) collective-permute-start(f32[1,256,128]{2,1,0:T(8,128)} %bitcast.20), channel_id=1, source_target_pairs={{0,16},{1,2},{2,1},{3,4},{4,3},{5,6},{6,5},{7,8},{8,7},{9,10},{10,... | collective-permute-start | bytes 393224 | tf_op jit(solution)/shard_map/ppermute | solution.py:347
  5.3 0.1 collective-permute-start.1
  5.4 1.7 %shard_map.94 = (f32[256,128]{1,0:T(8,128)S(1)}, f32[4,256,128]{2,1,0:T(8,128)S(1)}, f32[256,128]{1,0:T(8,128)S(1)}, f32[3,256,128]{2,1,0:T(8,128)S(1)}, f32[256...) custom-call(f32[256,128]{1,0:T(8,128)} %bitcast.22, f32[256,128]{1,0:T(8,128)} %bitcast.16, ...), custom_call_target="tpu_custom_call" | custom-call | tf_op jit(solution)/shard_map/pallas_call | solution.py:319
  7.1 0.0 collective-permute-done.2.far_ref
  7.1 0.0 collective-permute-done.3.near_ref
  7.1 0.3 shard_map.95
  7.4 1.8 %collective-permute-start.16 = (f32[1,256,128]{2,1,0:T(8,128)S(1)}, f32[1,256,128]{2,1,0:T(8,128)S(1)}, u32[]{:S(2)}, u32[]{:S(2)}) collective-permute-start(f32[1,256,128]{2,1,0:T(8,128)S(1)} %get-tuple-element.39.field_ref.refs_0_), channel_id=1, source_target_pairs={{0,16},{1,2},{2,1},{3,4},{4,3},{5,6},{6,5},{7,8},{8,7},{9,10},{10,... | collective-permute-start | bytes 393224 | tf_op jit(solution)/shard_map/ppermute | solution.py:347
  9.2 2.4 %collective-permute-start.17 = (f32[1,256,128]{2,1,0:T(8,128)S(1)}, f32[1,256,128]{2,1,0:T(8,128)S(1)}, u32[]{:S(2)}, u32[]{:S(2)}) collective-permute-start(f32[1,256,128]{2,1,0:T(8,128)S(1)} %get-tuple-element.39.field_ref.refs_0_), channel_id=1, source_target_pairs={{0,1},{1,0},{2,3},{3,2},{4,5},{5,4},{6,7},{7,6},{8,9},{9,8},{10,11... | collective-permute-start | bytes 393224 | tf_op jit(solution)/shard_map/ppermute | solution.py:348
  11.5 1.5 %collective-permute-start.10 = (f32[1,256,128]{2,1,0:T(8,128)S(1)}, f32[1,256,128]{2,1,0:T(8,128)S(1)}, u32[]{:S(2)}, u32[]{:S(2)}) collective-permute-start(f32[1,256,128]{2,1,0:T(8,128)S(1)} %get-tuple-element.38.field_ref.refs_3_.refs_4_), channel_id=1, source_target_pairs={{0,16},{1,2},{2,1},{3,4},{4,3},{5,6},{6,5},{7,8},{8,7},{9,10},{10,... | collective-permute-start | bytes 393224 | tf_op jit(solution)/shard_map/ppermute | solution.py:347
  13.0 0.0 collective-permute-done.1.near_ref
  13.0 0.9 %shard_map.96 = (f32[256,128]{1,0:T(8,128)}, f32[1,256,128]{2,1,0:T(8,128)S(1)}) custom-call(f32[1,256,128]{2,1,0:T(8,128)S(1)} %collective-permute-done.far_ref, f32[1,256,128]{2,1,0:T(8,128)S(1)} %collective-permute-done.1.near_ref, f32[3,256,128]{2,1,0:T(8,128)S(1)} %get-tuple-element.28.right_ref, f32[256,128]{1,0:T(8,128)S(1)} %get-tuple-element.29.part_ref, ...), custom_call_target="tpu_custom_call" | custom-call | tf_op jit(solution)/shard_map/pallas_call | solution.py:319
  13.9 0.5 %collective-permute-start.4 = (f32[1,256,128]{2,1,0:T(8,128)S(1)}, f32[1,256,128]{2,1,0:T(8,128)S(1)}, u32[]{:S(2)}, u32[]{:S(2)}) collective-permute-start(f32[1,256,128]{2,1,0:T(8,128)S(1)} %get-tuple-element.36.field_ref.refs_6_.refs_8_), channel_id=1, source_target_pairs={{0,16},{1,2},{2,1},{3,4},{4,3},{5,6},{6,5},{7,8},{8,7},{9,10},{10,... | collective-permute-start | bytes 393224 | tf_op jit(solution)/shard_map/ppermute | solution.py:347
  14.5 1.2 %collective-permute-start.5 = (f32[1,256,128]{2,1,0:T(8,128)S(1)}, f32[1,256,128]{2,1,0:T(8,128)S(1)}, u32[]{:S(2)}, u32[]{:S(2)}) collective-permute-start(f32[1,256,128]{2,1,0:T(8,128)S(1)} %get-tuple-element.36.field_ref.refs_6_.refs_8_), channel_id=1, source_target_pairs={{0,1},{1,0},{2,3},{3,2},{4,5},{5,4},{6,7},{7,6},{8,9},{9,8},{10,11... | collective-permute-start | bytes 393224 | tf_op jit(solution)/shard_map/ppermute | solution.py:348
  15.7 0.0 collective-permute-done.17.near_ref
  15.7 0.3 shard_map.101.field_ref.refs_1_
  16.0 1.6 %collective-permute-start.18 = (f32[1,256,128]{2,1,0:T(8,128)S(1)}, f32[1,256,128]{2,1,0:T(8,128)S(1)}, u32[]{:S(2)}, u32[]{:S(2)}) collective-permute-start(f32[1,256,128]{2,1,0:T(8,128)S(1)} %shard_map.101.field_ref.refs_1_), channel_id=1, source_target_pairs={{0,16},{1,2},{2,1},{3,4},{4,3},{5,6},{6,5},{7,8},{8,7},{9,10},{10,... | collective-permute-start | bytes 393224 | tf_op jit(solution)/shard_map/ppermute | solution.py:347
  17.5 0.6 %collective-permute-start.19 = (f32[1,256,128]{2,1,0:T(8,128)S(1)}, f32[1,256,128]{2,1,0:T(8,128)S(1)}, u32[]{:S(2)}, u32[]{:S(2)}) collective-permute-start(f32[1,256,128]{2,1,0:T(8,128)S(1)} %shard_map.101.field_ref.refs_1_), channel_id=1, source_target_pairs={{0,1},{1,0},{2,3},{3,2},{4,5},{5,4},{6,7},{7,6},{8,9},{9,8},{10,11... | collective-permute-start | bytes 393224 | tf_op jit(solution)/shard_map/ppermute | solution.py:348
  18.2 0.0 collective-permute-done.11.near_ref
  18.2 0.3 shard_map.99.field_ref.refs_4_.refs_5_
  18.5 1.6 %collective-permute-start.12 = (f32[1,256,128]{2,1,0:T(8,128)S(1)}, f32[1,256,128]{2,1,0:T(8,128)S(1)}, u32[]{:S(2)}, u32[]{:S(2)}) collective-permute-start(f32[1,256,128]{2,1,0:T(8,128)S(1)} %shard_map.99.field_ref.refs_4_.refs_5_), channel_id=1, source_target_pairs={{0,16},{1,2},{2,1},{3,4},{4,3},{5,6},{6,5},{7,8},{8,7},{9,10},{10,... | collective-permute-start | bytes 393224 | tf_op jit(solution)/shard_map/ppermute | solution.py:347
  20.0 0.0 collective-permute-start.13
  20.0 0.0 collective-permute-done.5.near_ref
  20.0 0.3 shard_map.97.field_ref.refs_7_.refs_9_
  20.3 1.2 %collective-permute-start.6 = (f32[1,256,128]{2,1,0:T(8,128)S(1)}, f32[1,256,128]{2,1,0:T(8,128)S(1)}, u32[]{:S(2)}, u32[]{:S(2)}) collective-permute-start(f32[1,256,128]{2,1,0:T(8,128)S(1)} %shard_map.97.field_ref.refs_7_.refs_9_), channel_id=1, source_target_pairs={{0,16},{1,2},{2,1},{3,4},{4,3},{5,6},{6,5},{7,8},{8,7},{9,10},{10,... | collective-permute-start | bytes 393224 | tf_op jit(solution)/shard_map/ppermute | solution.py:347
  21.5 2.3 %collective-permute-start.7 = (f32[1,256,128]{2,1,0:T(8,128)S(1)}, f32[1,256,128]{2,1,0:T(8,128)S(1)}, u32[]{:S(2)}, u32[]{:S(2)}) collective-permute-start(f32[1,256,128]{2,1,0:T(8,128)S(1)} %shard_map.97.field_ref.refs_7_.refs_9_), channel_id=1, source_target_pairs={{0,1},{1,0},{2,3},{3,2},{4,5},{5,4},{6,7},{7,6},{8,9},{9,8},{10,11... | collective-permute-start | bytes 393224 | tf_op jit(solution)/shard_map/ppermute | solution.py:348
  23.8 0.3 shard_map.102.refs_2_.field_ref
  24.1 1.6 %collective-permute-start.20 = (f32[1,256,128]{2,1,0:T(8,128)S(1)}, f32[1,256,128]{2,1,0:T(8,128)S(1)}, u32[]{:S(2)}, u32[]{:S(2)}) collective-permute-start(f32[1,256,128]{2,1,0:T(8,128)S(1)} %shard_map.102.refs_2_.field_ref), channel_id=1, source_target_pairs={{0,16},{1,2},{2,1},{3,4},{4,3},{5,6},{6,5},{7,8},{8,7},{9,10},{10,... | collective-permute-start | bytes 393224 | tf_op jit(solution)/shard_map/ppermute | solution.py:347
  25.6 0.0 collective-permute-done.12.far_ref
  25.6 1.0 %collective-permute-start.21 = (f32[1,256,128]{2,1,0:T(8,128)S(1)}, f32[1,256,128]{2,1,0:T(8,128)S(1)}, u32[]{:S(2)}, u32[]{:S(2)}) collective-permute-start(f32[1,256,128]{2,1,0:T(8,128)S(1)} %shard_map.102.refs_2_.field_ref), channel_id=1, source_target_pairs={{0,1},{1,0},{2,3},{3,2},{4,5},{5,4},{6,7},{7,6},{8,9},{9,8},{10,11... | collective-permute-start | bytes 393224 | tf_op jit(solution)/shard_map/ppermute | solution.py:348
  26.6 0.3 shard_map.100.refs_5_.field_ref.refs_6_
  26.9 1.6 %collective-permute-start.14 = (f32[1,256,128]{2,1,0:T(8,128)S(1)}, f32[1,256,128]{2,1,0:T(8,128)S(1)}, u32[]{:S(2)}, u32[]{:S(2)}) collective-permute-start(f32[1,256,128]{2,1,0:T(8,128)S(1)} %shard_map.100.refs_5_.field_ref.refs_6_), channel_id=1, source_target_pairs={{0,16},{1,2},{2,1},{3,4},{4,3},{5,6},{6,5},{7,8},{8,7},{9,10},{10,... | collective-permute-start | bytes 393224 | tf_op jit(solution)/shard_map/ppermute | solution.py:347
  28.4 1.0 %collective-permute-start.15 = (f32[1,256,128]{2,1,0:T(8,128)S(1)}, f32[1,256,128]{2,1,0:T(8,128)S(1)}, u32[]{:S(2)}, u32[]{:S(2)}) collective-permute-start(f32[1,256,128]{2,1,0:T(8,128)S(1)} %shard_map.100.refs_5_.field_ref.refs_6_), channel_id=1, source_target_pairs={{0,1},{1,0},{2,3},{3,2},{4,5},{5,4},{6,7},{7,6},{8,9},{9,8},{10,11... | collective-permute-start | bytes 393224 | tf_op jit(solution)/shard_map/ppermute | solution.py:348
  29.4 0.0 collective-permute-done.7.near_ref
  29.4 0.3 shard_map.98.refs_8_.field_ref.refs_10_
  29.7 1.6 %collective-permute-start.8 = (f32[1,256,128]{2,1,0:T(8,128)S(1)}, f32[1,256,128]{2,1,0:T(8,128)S(1)}, u32[]{:S(2)}, u32[]{:S(2)}) collective-permute-start(f32[1,256,128]{2,1,0:T(8,128)S(1)} %shard_map.98.refs_8_.field_ref.refs_10_), channel_id=1, source_target_pairs={{0,16},{1,2},{2,1},{3,4},{4,3},{5,6},{6,5},{7,8},{8,7},{9,10},{10,... | collective-permute-start | bytes 393224 | tf_op jit(solution)/shard_map/ppermute | solution.py:347
  31.3 0.1 collective-permute-start.9
  31.4 2.0 %shard_map.103 = (f32[8,128]{1,0:T(8,128)S(1)}, f32[7,3,256,128]{3,2,1,0:T(8,128)S(1)}, f32[7,3,256,128]{3,2,1,0:T(8,128)S(1)}) custom-call(f32[256,128]{1,0:T(8,128)S(1)} %get-tuple-element.40.diagonal_ref, f32[1,256,128]{2,1,0:T(8,128)S(1)} %get-tuple-element.39.field_ref.refs_0_, f32[1,256,128]{2,1,0:T(8,128)S(1)} %shard_map.101.field_ref.refs_1_, ...), custom_call_target="tpu_custom_call" | custom-call | tf_op jit(solution)/shard_map/pallas_call | solution.py:319
  33.4 0.0 collective-permute-done.21.near_ref
  33.4 0.5 shard_map.104
  33.9 0.0 collective-permute-done.14.far_ref
  33.9 0.5 shard_map.105
  34.3 0.4 collective-permute-done.8.far_ref
  34.7 0.0 collective-permute-done.9.near_ref
  34.7 0.5 shard_map.106
  35.2 14.4 %all_to_all.5.moments_ref = f32[32,1,128]{2,1,0:T(1,128)S(1)} all-to-all(f32[32,1,128]{2,1,0:T(1,128)S(1)} %get-tuple-element.46), channel_id=1, replica_groups=mesh['diamond'=2,'tile'=16] {'diamond','tile'}, dimensions={0} | all-to-all | bytes 32768 | tf_op jit(solution)/shard_map/all_to_all | solution.py:397
  49.6 1.4 %shard_map.107 = (f32[3,256,128]{2,1,0:T(8,128)}, f32[3,256,128]{2,1,0:T(8,128)}) custom-call(f32[32,1,128]{2,1,0:T(1,128)S(1)} %all_to_all.5.moments_ref, f32[256,128]{1,0:T(8,128)S(1)} %get-tuple-element.40.diagonal_ref, f32[1,256,128]{2,1,0:T(8,128)S(1)} %get-tuple-element.39.field_ref.refs_0_, f32[1,256,128]{2,1,0:T(8,128)S(1)} %shard_map.101.field_ref.refs_1_, ...), custom_call_target="tpu_custom_call" | custom-call | tf_op jit(solution)/shard_map/pallas_call | solution.py:319
  (11 shorter events, 0.0 us)
Async XLA Ops:
  0.6 6.4 %collective-permute-start.2 = (f32[1,256,128]{2,1,0:T(8,128)}, f32[1,256,128]{2,1,0:T(8,128)S(1)}, u32[]{:S(2)}, u32[]{:S(2)}) collective-permute-start(f32[1,256,128]{2,1,0:T(8,128)} %bitcast.17), channel_id=1, source_target_pairs={{0,16},{1,2},{2,1},{3,4},{4,3},{5,6},{6,5},{7,8},{8,7},{9,10},{10,... | collective-permute-start | bytes 393224 | tf_op jit(solution)/shard_map/ppermute | solution.py:347
  3.6 3.5 %collective-permute-start.3 = (f32[1,256,128]{2,1,0:T(8,128)}, f32[1,256,128]{2,1,0:T(8,128)S(1)}, u32[]{:S(2)}, u32[]{:S(2)}) collective-permute-start(f32[1,256,128]{2,1,0:T(8,128)} %bitcast.18), channel_id=1, source_target_pairs={{0,1},{1,0},{2,3},{3,2},{4,5},{5,4},{6,7},{7,6},{8,9},{9,8},{10,11... | collective-permute-start | bytes 393224 | tf_op jit(solution)/shard_map/ppermute | solution.py:348
  3.8 9.3 %collective-permute-start = (f32[1,256,128]{2,1,0:T(8,128)}, f32[1,256,128]{2,1,0:T(8,128)S(1)}, u32[]{:S(2)}, u32[]{:S(2)}) collective-permute-start(f32[1,256,128]{2,1,0:T(8,128)} %bitcast.20), channel_id=1, source_target_pairs={{0,16},{1,2},{2,1},{3,4},{4,3},{5,6},{6,5},{7,8},{8,7},{9,10},{10,... | collective-permute-start | bytes 393224 | tf_op jit(solution)/shard_map/ppermute | solution.py:347
  5.3 7.8 %collective-permute-start.1 = (f32[1,256,128]{2,1,0:T(8,128)}, f32[1,256,128]{2,1,0:T(8,128)S(1)}, u32[]{:S(2)}, u32[]{:S(2)}) collective-permute-start(f32[1,256,128]{2,1,0:T(8,128)} %bitcast.21), channel_id=1, source_target_pairs={{0,1},{1,0},{2,3},{3,2},{4,5},{5,4},{6,7},{7,6},{8,9},{9,8},{10,11... | collective-permute-start | bytes 393224 | tf_op jit(solution)/shard_map/ppermute | solution.py:348
  7.4 7.1 %collective-permute-start.16 = (f32[1,256,128]{2,1,0:T(8,128)S(1)}, f32[1,256,128]{2,1,0:T(8,128)S(1)}, u32[]{:S(2)}, u32[]{:S(2)}) collective-permute-start(f32[1,256,128]{2,1,0:T(8,128)S(1)} %get-tuple-element.39.field_ref.refs_0_), channel_id=1, source_target_pairs={{0,16},{1,2},{2,1},{3,4},{4,3},{5,6},{6,5},{7,8},{8,7},{9,10},{10,... | collective-permute-start | bytes 393224 | tf_op jit(solution)/shard_map/ppermute | solution.py:347
  9.2 6.6 %collective-permute-start.17 = (f32[1,256,128]{2,1,0:T(8,128)S(1)}, f32[1,256,128]{2,1,0:T(8,128)S(1)}, u32[]{:S(2)}, u32[]{:S(2)}) collective-permute-start(f32[1,256,128]{2,1,0:T(8,128)S(1)} %get-tuple-element.39.field_ref.refs_0_), channel_id=1, source_target_pairs={{0,1},{1,0},{2,3},{3,2},{4,5},{5,4},{6,7},{7,6},{8,9},{9,8},{10,11... | collective-permute-start | bytes 393224 | tf_op jit(solution)/shard_map/ppermute | solution.py:348
  11.5 6.0 %collective-permute-start.10 = (f32[1,256,128]{2,1,0:T(8,128)S(1)}, f32[1,256,128]{2,1,0:T(8,128)S(1)}, u32[]{:S(2)}, u32[]{:S(2)}) collective-permute-start(f32[1,256,128]{2,1,0:T(8,128)S(1)} %get-tuple-element.38.field_ref.refs_3_.refs_4_), channel_id=1, source_target_pairs={{0,16},{1,2},{2,1},{3,4},{4,3},{5,6},{6,5},{7,8},{8,7},{9,10},{10,... | collective-permute-start | bytes 393224 | tf_op jit(solution)/shard_map/ppermute | solution.py:347
  13.0 5.2 %collective-permute-start.11 = (f32[1,256,128]{2,1,0:T(8,128)S(1)}, f32[1,256,128]{2,1,0:T(8,128)S(1)}, u32[]{:S(2)}, u32[]{:S(2)}) collective-permute-start(f32[1,256,128]{2,1,0:T(8,128)S(1)} %get-tuple-element.38.field_ref.refs_3_.refs_4_), channel_id=1, source_target_pairs={{0,1},{1,0},{2,3},{3,2},{4,5},{5,4},{6,7},{7,6},{8,9},{9,8},{10,11... | collective-permute-start | bytes 393224 | tf_op jit(solution)/shard_map/ppermute | solution.py:348
  13.9 6.1 %collective-permute-start.4 = (f32[1,256,128]{2,1,0:T(8,128)S(1)}, f32[1,256,128]{2,1,0:T(8,128)S(1)}, u32[]{:S(2)}, u32[]{:S(2)}) collective-permute-start(f32[1,256,128]{2,1,0:T(8,128)S(1)} %get-tuple-element.36.field_ref.refs_6_.refs_8_), channel_id=1, source_target_pairs={{0,16},{1,2},{2,1},{3,4},{4,3},{5,6},{6,5},{7,8},{8,7},{9,10},{10,... | collective-permute-start | bytes 393224 | tf_op jit(solution)/shard_map/ppermute | solution.py:347
  14.5 5.5 %collective-permute-start.5 = (f32[1,256,128]{2,1,0:T(8,128)S(1)}, f32[1,256,128]{2,1,0:T(8,128)S(1)}, u32[]{:S(2)}, u32[]{:S(2)}) collective-permute-start(f32[1,256,128]{2,1,0:T(8,128)S(1)} %get-tuple-element.36.field_ref.refs_6_.refs_8_), channel_id=1, source_target_pairs={{0,1},{1,0},{2,3},{3,2},{4,5},{5,4},{6,7},{7,6},{8,9},{9,8},{10,11... | collective-permute-start | bytes 393224 | tf_op jit(solution)/shard_map/ppermute | solution.py:348
  16.0 5.5 %collective-permute-start.18 = (f32[1,256,128]{2,1,0:T(8,128)S(1)}, f32[1,256,128]{2,1,0:T(8,128)S(1)}, u32[]{:S(2)}, u32[]{:S(2)}) collective-permute-start(f32[1,256,128]{2,1,0:T(8,128)S(1)} %shard_map.101.field_ref.refs_1_), channel_id=1, source_target_pairs={{0,16},{1,2},{2,1},{3,4},{4,3},{5,6},{6,5},{7,8},{8,7},{9,10},{10,... | collective-permute-start | bytes 393224 | tf_op jit(solution)/shard_map/ppermute | solution.py:347
  17.5 6.3 %collective-permute-start.19 = (f32[1,256,128]{2,1,0:T(8,128)S(1)}, f32[1,256,128]{2,1,0:T(8,128)S(1)}, u32[]{:S(2)}, u32[]{:S(2)}) collective-permute-start(f32[1,256,128]{2,1,0:T(8,128)S(1)} %shard_map.101.field_ref.refs_1_), channel_id=1, source_target_pairs={{0,1},{1,0},{2,3},{3,2},{4,5},{5,4},{6,7},{7,6},{8,9},{9,8},{10,11... | collective-permute-start | bytes 393224 | tf_op jit(solution)/shard_map/ppermute | solution.py:348
  18.5 7.2 %collective-permute-start.12 = (f32[1,256,128]{2,1,0:T(8,128)S(1)}, f32[1,256,128]{2,1,0:T(8,128)S(1)}, u32[]{:S(2)}, u32[]{:S(2)}) collective-permute-start(f32[1,256,128]{2,1,0:T(8,128)S(1)} %shard_map.99.field_ref.refs_4_.refs_5_), channel_id=1, source_target_pairs={{0,16},{1,2},{2,1},{3,4},{4,3},{5,6},{6,5},{7,8},{8,7},{9,10},{10,... | collective-permute-start | bytes 393224 | tf_op jit(solution)/shard_map/ppermute | solution.py:347
  20.0 6.6 %collective-permute-start.13 = (f32[1,256,128]{2,1,0:T(8,128)S(1)}, f32[1,256,128]{2,1,0:T(8,128)S(1)}, u32[]{:S(2)}, u32[]{:S(2)}) collective-permute-start(f32[1,256,128]{2,1,0:T(8,128)S(1)} %shard_map.99.field_ref.refs_4_.refs_5_), channel_id=1, source_target_pairs={{0,1},{1,0},{2,3},{3,2},{4,5},{5,4},{6,7},{7,6},{8,9},{9,8},{10,11... | collective-permute-start | bytes 393224 | tf_op jit(solution)/shard_map/ppermute | solution.py:348
  20.3 8.2 %collective-permute-start.6 = (f32[1,256,128]{2,1,0:T(8,128)S(1)}, f32[1,256,128]{2,1,0:T(8,128)S(1)}, u32[]{:S(2)}, u32[]{:S(2)}) collective-permute-start(f32[1,256,128]{2,1,0:T(8,128)S(1)} %shard_map.97.field_ref.refs_7_.refs_9_), channel_id=1, source_target_pairs={{0,16},{1,2},{2,1},{3,4},{4,3},{5,6},{6,5},{7,8},{8,7},{9,10},{10,... | collective-permute-start | bytes 393224 | tf_op jit(solution)/shard_map/ppermute | solution.py:347
  21.5 8.0 %collective-permute-start.7 = (f32[1,256,128]{2,1,0:T(8,128)S(1)}, f32[1,256,128]{2,1,0:T(8,128)S(1)}, u32[]{:S(2)}, u32[]{:S(2)}) collective-permute-start(f32[1,256,128]{2,1,0:T(8,128)S(1)} %shard_map.97.field_ref.refs_7_.refs_9_), channel_id=1, source_target_pairs={{0,1},{1,0},{2,3},{3,2},{4,5},{5,4},{6,7},{7,6},{8,9},{9,8},{10,11... | collective-permute-start | bytes 393224 | tf_op jit(solution)/shard_map/ppermute | solution.py:348
  24.1 7.2 %collective-permute-start.20 = (f32[1,256,128]{2,1,0:T(8,128)S(1)}, f32[1,256,128]{2,1,0:T(8,128)S(1)}, u32[]{:S(2)}, u32[]{:S(2)}) collective-permute-start(f32[1,256,128]{2,1,0:T(8,128)S(1)} %shard_map.102.refs_2_.field_ref), channel_id=1, source_target_pairs={{0,16},{1,2},{2,1},{3,4},{4,3},{5,6},{6,5},{7,8},{8,7},{9,10},{10,... | collective-permute-start | bytes 393224 | tf_op jit(solution)/shard_map/ppermute | solution.py:347
  25.6 7.8 %collective-permute-start.21 = (f32[1,256,128]{2,1,0:T(8,128)S(1)}, f32[1,256,128]{2,1,0:T(8,128)S(1)}, u32[]{:S(2)}, u32[]{:S(2)}) collective-permute-start(f32[1,256,128]{2,1,0:T(8,128)S(1)} %shard_map.102.refs_2_.field_ref), channel_id=1, source_target_pairs={{0,1},{1,0},{2,3},{3,2},{4,5},{5,4},{6,7},{7,6},{8,9},{9,8},{10,11... | collective-permute-start | bytes 393224 | tf_op jit(solution)/shard_map/ppermute | solution.py:348
  26.9 7.0 %collective-permute-start.14 = (f32[1,256,128]{2,1,0:T(8,128)S(1)}, f32[1,256,128]{2,1,0:T(8,128)S(1)}, u32[]{:S(2)}, u32[]{:S(2)}) collective-permute-start(f32[1,256,128]{2,1,0:T(8,128)S(1)} %shard_map.100.refs_5_.field_ref.refs_6_), channel_id=1, source_target_pairs={{0,16},{1,2},{2,1},{3,4},{4,3},{5,6},{6,5},{7,8},{8,7},{9,10},{10,... | collective-permute-start | bytes 393224 | tf_op jit(solution)/shard_map/ppermute | solution.py:347
  28.4 5.4 %collective-permute-start.15 = (f32[1,256,128]{2,1,0:T(8,128)S(1)}, f32[1,256,128]{2,1,0:T(8,128)S(1)}, u32[]{:S(2)}, u32[]{:S(2)}) collective-permute-start(f32[1,256,128]{2,1,0:T(8,128)S(1)} %shard_map.100.refs_5_.field_ref.refs_6_), channel_id=1, source_target_pairs={{0,1},{1,0},{2,3},{3,2},{4,5},{5,4},{6,7},{7,6},{8,9},{9,8},{10,11... | collective-permute-start | bytes 393224 | tf_op jit(solution)/shard_map/ppermute | solution.py:348
  29.7 5.0 %collective-permute-start.8 = (f32[1,256,128]{2,1,0:T(8,128)S(1)}, f32[1,256,128]{2,1,0:T(8,128)S(1)}, u32[]{:S(2)}, u32[]{:S(2)}) collective-permute-start(f32[1,256,128]{2,1,0:T(8,128)S(1)} %shard_map.98.refs_8_.field_ref.refs_10_), channel_id=1, source_target_pairs={{0,16},{1,2},{2,1},{3,4},{4,3},{5,6},{6,5},{7,8},{8,7},{9,10},{10,... | collective-permute-start | bytes 393224 | tf_op jit(solution)/shard_map/ppermute | solution.py:347
  31.3 3.5 %collective-permute-start.9 = (f32[1,256,128]{2,1,0:T(8,128)S(1)}, f32[1,256,128]{2,1,0:T(8,128)S(1)}, u32[]{:S(2)}, u32[]{:S(2)}) collective-permute-start(f32[1,256,128]{2,1,0:T(8,128)S(1)} %shard_map.98.refs_8_.field_ref.refs_10_), channel_id=1, source_target_pairs={{0,1},{1,0},{2,3},{3,2},{4,5},{5,4},{6,7},{7,6},{8,9},{9,8},{10,11... | collective-permute-start | bytes 393224 | tf_op jit(solution)/shard_map/ppermute | solution.py:348

commit v3 on v2

--- a/solution.py
+++ b/solution.py
@@ -63,8 +63,8 @@
 
 def local_kernel(
     temp_hbm, misfit_hbm, visc_hbm, velocity_hbm, forcing_hbm, edge_hbm, pole_hbm,
-    half_ref, side_ref, base_ref, right_ref, part_ref, speed_ref, matrix_ref,
-    temp_ref, misfit_ref, visc_ref, velocity_ref, edge_ref, pole_ref, sems,
+    half_ref, side_ref, base_ref, right_ref, part_ref, speed_ref, matrix_ref, temp_ref,
+    misfit_ref, visc_ref, velocity_ref, edge_ref, pole_ref, sems,
 ):
     sources = [visc_hbm, temp_hbm, edge_hbm, pole_hbm, velocity_hbm, misfit_hbm, forcing_hbm]
     targets = [visc_ref, temp_ref, edge_ref, pole_ref, velocity_ref, misfit_ref, right_ref]
@@ -274,7 +274,7 @@
 
 
 def finish_kernel(moments_ref, diagonal_ref, *refs):
-    solution_ref, residual_ref = refs[-2:]
+    *refs, solution_hbm, residual_hbm, solution_ref, residual_ref, sems = refs
     streams = [refs[4 * i : 4 * i + 4] for i in range(len(SPLITS))]
     rows = [moments_ref[device] for device in range(moments_ref.shape[0])]
     while len(rows) > 1:
@@ -298,21 +298,25 @@
     total, layers = diagonal_ref.shape
     chosen = [jnp.broadcast_to(c, (CHUNK, layers)) for c in chosen]
     center, answer, residual = chosen[0], chosen[1:4], chosen[4:8]
-    for start in range(0, total, CHUNK):
-        here = slice(start, start + CHUNK)
-        diagonal = diagonal_ref[here]
-        for (low, high), stream in zip(SPLITS, streams):
-            for at in range(high - low):
+    copies = []
+    for (low, high), stream in zip(SPLITS, streams):
+        for at in range(high - low):
+            for start in range(0, total, CHUNK):
+                here = slice(start, start + CHUNK)
                 values = [ref[at, here] for ref in stream]
                 q1, q2, q3 = powers(center, *values)
                 solution_ref[low + at, here] = answer[0] * values[0] + answer[1] * q1 + answer[2] * q2
-                residual_ref[low + at, here] = diagonal * (
+                residual_ref[low + at, here] = diagonal_ref[here] * (
                     residual[0] * values[0] + residual[1] * q1 + residual[2] * q2 + residual[3] * q3
                 )
-
-
-def call(kernel, out_shapes, *args, scratch=(), place=pltpu.VMEM):
-    whole = pl.BlockSpec(memory_space=pltpu.VMEM)
+            for k, (source, target) in enumerate(((solution_ref, solution_hbm), (residual_ref, residual_hbm))):
+                copies.append(pltpu.make_async_copy(source.at[low + at], target.at[low + at], sems.at[k, low + at]))
+                copies[-1].start()
+    for copy in copies:
+        copy.wait()
+
+
+def call(kernel, out_shapes, *args, scratch=(), place=pltpu.VMEM, out_place=pltpu.VMEM):
     if place is pltpu.HBM:
         args = [pltpu.with_memory_space_constraint(a, place) for a in args]
     outs = [o if isinstance(o, jax.ShapeDtypeStruct) else jax.ShapeDtypeStruct(o, jnp.float32) for o in out_shapes]
@@ -320,7 +324,7 @@
         kernel,
         out_shape=outs,
         in_specs=[pl.BlockSpec(memory_space=place)] * len(args),
-        out_specs=[whole] * len(out_shapes),
+        out_specs=[pl.BlockSpec(memory_space=out_place)] * len(out_shapes),
         scratch_shapes=[pltpu.VMEM(s, jnp.float32) if isinstance(s, tuple) else s for s in scratch],
         compiler_params=pltpu.CompilerParams(vmem_limit_bytes=24 * 2**20),
     )(*args)
@@ -355,15 +359,15 @@
     flat, triple = (rows, layers), (3, rows, layers)
     temp, source, visc = (v.reshape(flat) for v in (adjoint_temp, misfit, viscosity))
     visc_near, visc_far = exchange(visc[None])
-    temp_near, temp_far = exchange(temp[None])
     table = pltpu.VMEM(edge_table.shape, edge_table.dtype)
-    half, side, base, right, part, speed, matrix = call(
+    half, side, base, right, part, speed, matrix, sent = call(
         local_kernel,
-        [flat, (4, *flat), flat, triple, flat, flat, jax.ShapeDtypeStruct((rows, rows), jnp.bfloat16)],
+        [flat, (4, *flat), flat, triple, flat, flat, jax.ShapeDtypeStruct((rows, rows), jnp.bfloat16), flat],
         temp, source, visc, velocity.reshape(triple), forcing.reshape(triple), edge_table, pole_table,
-        scratch=[flat, flat, flat, triple, table, table, pltpu.SemaphoreType.DMA((7,))],
+        scratch=[flat, flat, triple, table, table, pltpu.SemaphoreType.DMA((7,))],
         place=pltpu.HBM,
     )
+    temp_near, temp_far = exchange(sent[None])
     shapes = [(high - low, rows, layers) for low, high in SPLITS]
     weights, diagonal, inverse, *first = call(
         weigh_kernel, [(6, *flat), flat, flat, *shapes[:-1]],
@@ -396,7 +400,10 @@
         streams[i].append(field)
     moments = lax.all_to_all(moments, NAMES, 0, 0)
     fields = [field for stream in streams for field in stream]
-    answer, residual = call(finish_kernel, [triple, triple], moments, diagonal, *fields)
+    answer, residual = call(
+        finish_kernel, [triple, triple], moments, diagonal, *fields,
+        scratch=[triple, triple, pltpu.SemaphoreType.DMA((2, 3))], out_place=pltpu.HBM,
+    )
     whole = (3, 1, 1, rows, layers)
     return answer.reshape(whole), residual.reshape(whole), adjoint_next.reshape(adjoint_temp.shape)
 

time: 51.1 us -> 50.5 us (0.988)
    ppermute x11, starting transfers between devices: 17.3 us -> 18.3 us  [exchange(): far = lax.ppermute(value, NAMES, across)]
    ppermute x11, starting transfers between devices: 8.97 us -> 8.28 us  [exchange(): near = lax.ppermute(value, NAMES, beside)]
  transfers between devices with their start and end apart: 22 -> 22, of which waited for: 1 -> 0; matrix products, arithmetic and copies ran while one was open for 0% -> 0% of each run, Pallas kernels for 14% -> 15%
where the time goes in v3:
time: 50.5 us; the launch traced here: 50.3 us
  starting transfers between devices  26.6 us (53%)
  blocking collectives  13.9 us (28%)
  Pallas kernels  9.04 us (18%)
  between operations  0.72 us (1%)
    ppermute x11, starting transfers between devices, exchange(): far = lax.ppermute(value, NAMES, across)  18.3 us
    all_to_all x1, blocking collectives, body(): moments = lax.all_to_all(moments, NAMES, 0, 0)  13.9 us
    pallas_call x14, Pallas kernels, call(): pl.pallas_call(kernel, out_shape=outs, in_specs=[pl.BlockSpec(memory_spac...  9.04 us
    ppermute x11, starting transfers between devices, exchange(): near = lax.ppermute(value, NAMES, beside)  8.28 us
  transfers between devices with their start and end apart: 22, of which 0 were waited for; matrix products, arithmetic and copies ran while one was open for 0% of the time, Pallas kernels for 15%

profile of v3, /device:TPU:0, one launch (start us, length us, event | category | flops | bytes accessed | tf_op | source)
XLA Modules:
  0.0 50.3 jit_solution(8121071953434882464)
XLA Ops:
  0.6 3.0 %collective-permute-start.2 = (f32[1,256,128]{2,1,0:T(8,128)}, f32[1,256,128]{2,1,0:T(8,128)S(1)}, u32[]{:S(2)}, u32[]{:S(2)}) collective-permute-start(f32[1,256,128]{2,1,0:T(8,128)} %bitcast.20), channel_id=1, source_target_pairs={{0,16},{1,2},{2,1},{3,4},{4,3},{5,6},{6,5},{7,8},{8,7},{9,10},{10,... | collective-permute-start | bytes 393224 | tf_op jit(solution)/shard_map/ppermute | solution.py:351
  3.6 0.1 collective-permute-start.3
  3.8 1.7 %shard_map.94 = (f32[256,128]{1,0:T(8,128)S(1)}, f32[4,256,128]{2,1,0:T(8,128)S(1)}, f32[256,128]{1,0:T(8,128)S(1)}, f32[3,256,128]{2,1,0:T(8,128)S(1)}, f32[256...) custom-call(f32[256,128]{1,0:T(8,128)} %bitcast.18, ...), custom_call_target="tpu_custom_call" | custom-call | tf_op jit(solution)/shard_map/pallas_call | solution.py:323
  5.4 1.6 %collective-permute-start = (f32[1,256,128]{2,1,0:T(8,128)S(1)}, f32[1,256,128]{2,1,0:T(8,128)S(1)}, u32[]{:S(2)}, u32[]{:S(2)}) collective-permute-start(f32[1,256,128]{2,1,0:T(8,128)S(1)} %bitcast.14), channel_id=1, source_target_pairs={{0,16},{1,2},{2,1},{3,4},{4,3},{5,6},{6,5},{7,8},{8,7},{9,10},{10,... | collective-permute-start | bytes 393224 | tf_op jit(solution)/shard_map/ppermute | solution.py:351
  7.0 0.1 collective-permute-start.1
  7.1 0.0 collective-permute-done.2.far_ref
  7.1 0.0 collective-permute-done.3.near_ref
  7.1 0.3 shard_map.95
  7.4 1.7 %collective-permute-start.16 = (f32[1,256,128]{2,1,0:T(8,128)S(1)}, f32[1,256,128]{2,1,0:T(8,128)S(1)}, u32[]{:S(2)}, u32[]{:S(2)}) collective-permute-start(f32[1,256,128]{2,1,0:T(8,128)S(1)} %get-tuple-element.41.field_ref.refs_0_), channel_id=1, source_target_pairs={{0,16},{1,2},{2,1},{3,4},{4,3},{5,6},{6,5},{7,8},{8,7},{9,10},{10,... | collective-permute-start | bytes 393224 | tf_op jit(solution)/shard_map/ppermute | solution.py:351
  9.2 1.0 %collective-permute-start.17 = (f32[1,256,128]{2,1,0:T(8,128)S(1)}, f32[1,256,128]{2,1,0:T(8,128)S(1)}, u32[]{:S(2)}, u32[]{:S(2)}) collective-permute-start(f32[1,256,128]{2,1,0:T(8,128)S(1)} %get-tuple-element.41.field_ref.refs_0_), channel_id=1, source_target_pairs={{0,1},{1,0},{2,3},{3,2},{4,5},{5,4},{6,7},{7,6},{8,9},{9,8},{10,11... | collective-permute-start | bytes 393224 | tf_op jit(solution)/shard_map/ppermute | solution.py:352
  10.1 1.5 %collective-permute-start.10 = (f32[1,256,128]{2,1,0:T(8,128)S(1)}, f32[1,256,128]{2,1,0:T(8,128)S(1)}, u32[]{:S(2)}, u32[]{:S(2)}) collective-permute-start(f32[1,256,128]{2,1,0:T(8,128)S(1)} %get-tuple-element.40.field_ref.refs_3_.refs_4_), channel_id=1, source_target_pairs={{0,16},{1,2},{2,1},{3,4},{4,3},{5,6},{6,5},{7,8},{8,7},{9,10},{10,... | collective-permute-start | bytes 393224 | tf_op jit(solution)/shard_map/ppermute | solution.py:351
  11.6 0.0 collective-permute-done.far_ref
  11.6 0.0 collective-permute-start.11
  11.6 0.0 collective-permute-done.1.near_ref
  11.6 0.9 %shard_map.96 = (f32[256,128]{1,0:T(8,128)}, f32[1,256,128]{2,1,0:T(8,128)S(1)}) custom-call(f32[1,256,128]{2,1,0:T(8,128)S(1)} %collective-permute-done.far_ref, f32[1,256,128]{2,1,0:T(8,128)S(1)} %collective-permute-done.1.near_ref, f32[3,256,128]{2,1,0:T(8,128)S(1)} %get-tuple-element.30.right_ref, f32[256,128]{1,0:T(8,128)S(1)} %get-tuple-element.31.part_ref, ...), custom_call_target="tpu_custom_call" | custom-call | tf_op jit(solution)/shard_map/pallas_call | solution.py:323
  12.5 1.2 %collective-permute-start.4 = (f32[1,256,128]{2,1,0:T(8,128)S(1)}, f32[1,256,128]{2,1,0:T(8,128)S(1)}, u32[]{:S(2)}, u32[]{:S(2)}) collective-permute-start(f32[1,256,128]{2,1,0:T(8,128)S(1)} %get-tuple-element.38.field_ref.refs_6_.refs_8_), channel_id=1, source_target_pairs={{0,16},{1,2},{2,1},{3,4},{4,3},{5,6},{6,5},{7,8},{8,7},{9,10},{10,... | collective-permute-start | bytes 393224 | tf_op jit(solution)/shard_map/ppermute | solution.py:351
  13.8 0.0 collective-permute-done.16.far_ref
  13.8 1.1 %collective-permute-start.5 = (f32[1,256,128]{2,1,0:T(8,128)S(1)}, f32[1,256,128]{2,1,0:T(8,128)S(1)}, u32[]{:S(2)}, u32[]{:S(2)}) collective-permute-start(f32[1,256,128]{2,1,0:T(8,128)S(1)} %get-tuple-element.38.field_ref.refs_6_.refs_8_), channel_id=1, source_target_pairs={{0,1},{1,0},{2,3},{3,2},{4,5},{5,4},{6,7},{7,6},{8,9},{9,8},{10,11... | collective-permute-start | bytes 393224 | tf_op jit(solution)/shard_map/ppermute | solution.py:352
  14.9 0.3 shard_map.101.field_ref.refs_1_
  15.1 1.6 %collective-permute-start.18 = (f32[1,256,128]{2,1,0:T(8,128)S(1)}, f32[1,256,128]{2,1,0:T(8,128)S(1)}, u32[]{:S(2)}, u32[]{:S(2)}) collective-permute-start(f32[1,256,128]{2,1,0:T(8,128)S(1)} %shard_map.101.field_ref.refs_1_), channel_id=1, source_target_pairs={{0,16},{1,2},{2,1},{3,4},{4,3},{5,6},{6,5},{7,8},{8,7},{9,10},{10,... | collective-permute-start | bytes 393224 | tf_op jit(solution)/shard_map/ppermute | solution.py:351
  16.7 1.0 %collective-permute-start.19 = (f32[1,256,128]{2,1,0:T(8,128)S(1)}, f32[1,256,128]{2,1,0:T(8,128)S(1)}, u32[]{:S(2)}, u32[]{:S(2)}) collective-permute-start(f32[1,256,128]{2,1,0:T(8,128)S(1)} %shard_map.101.field_ref.refs_1_), channel_id=1, source_target_pairs={{0,1},{1,0},{2,3},{3,2},{4,5},{5,4},{6,7},{7,6},{8,9},{9,8},{10,11... | collective-permute-start | bytes 393224 | tf_op jit(solution)/shard_map/ppermute | solution.py:352
  17.7 0.0 collective-permute-done.11.near_ref
  17.7 0.3 shard_map.99.field_ref.refs_4_.refs_5_
  17.9 1.6 %collective-permute-start.12 = (f32[1,256,128]{2,1,0:T(8,128)S(1)}, f32[1,256,128]{2,1,0:T(8,128)S(1)}, u32[]{:S(2)}, u32[]{:S(2)}) collective-permute-start(f32[1,256,128]{2,1,0:T(8,128)S(1)} %shard_map.99.field_ref.refs_4_.refs_5_), channel_id=1, source_target_pairs={{0,16},{1,2},{2,1},{3,4},{4,3},{5,6},{6,5},{7,8},{8,7},{9,10},{10,... | collective-permute-start | bytes 393224 | tf_op jit(solution)/shard_map/ppermute | solution.py:351
  19.5 0.0 collective-permute-done.4.far_ref
  19.5 1.0 %collective-permute-start.13 = (f32[1,256,128]{2,1,0:T(8,128)S(1)}, f32[1,256,128]{2,1,0:T(8,128)S(1)}, u32[]{:S(2)}, u32[]{:S(2)}) collective-permute-start(f32[1,256,128]{2,1,0:T(8,128)S(1)} %shard_map.99.field_ref.refs_4_.refs_5_), channel_id=1, source_target_pairs={{0,1},{1,0},{2,3},{3,2},{4,5},{5,4},{6,7},{7,6},{8,9},{9,8},{10,11... | collective-permute-start | bytes 393224 | tf_op jit(solution)/shard_map/ppermute | solution.py:352
  20.5 0.0 collective-permute-done.5.near_ref
  20.5 0.3 shard_map.97.field_ref.refs_7_.refs_9_
  20.7 1.6 %collective-permute-start.6 = (f32[1,256,128]{2,1,0:T(8,128)S(1)}, f32[1,256,128]{2,1,0:T(8,128)S(1)}, u32[]{:S(2)}, u32[]{:S(2)}) collective-permute-start(f32[1,256,128]{2,1,0:T(8,128)S(1)} %shard_map.97.field_ref.refs_7_.refs_9_), channel_id=1, source_target_pairs={{0,16},{1,2},{2,1},{3,4},{4,3},{5,6},{6,5},{7,8},{8,7},{9,10},{10,... | collective-permute-start | bytes 393224 | tf_op jit(solution)/shard_map/ppermute | solution.py:351
  22.3 0.0 collective-permute-done.18.far_ref
  22.3 0.0 collective-permute-start.7
  22.3 0.3 shard_map.102.refs_2_.field_ref
  22.6 1.6 %collective-permute-start.20 = (f32[1,256,128]{2,1,0:T(8,128)S(1)}, f32[1,256,128]{2,1,0:T(8,128)S(1)}, u32[]{:S(2)}, u32[]{:S(2)}) collective-permute-start(f32[1,256,128]{2,1,0:T(8,128)S(1)} %shard_map.102.refs_2_.field_ref), channel_id=1, source_target_pairs={{0,16},{1,2},{2,1},{3,4},{4,3},{5,6},{6,5},{7,8},{8,7},{9,10},{10,... | collective-permute-start | bytes 393224 | tf_op jit(solution)/shard_map/ppermute | solution.py:351
  24.2 0.0 collective-permute-done.12.far_ref
  24.2 1.9 %collective-permute-start.21 = (f32[1,256,128]{2,1,0:T(8,128)S(1)}, f32[1,256,128]{2,1,0:T(8,128)S(1)}, u32[]{:S(2)}, u32[]{:S(2)}) collective-permute-start(f32[1,256,128]{2,1,0:T(8,128)S(1)} %shard_map.102.refs_2_.field_ref), channel_id=1, source_target_pairs={{0,1},{1,0},{2,3},{3,2},{4,5},{5,4},{6,7},{7,6},{8,9},{9,8},{10,11... | collective-permute-start | bytes 393224 | tf_op jit(solution)/shard_map/ppermute | solution.py:352
  26.1 0.0 collective-permute-done.13.near_ref
  26.1 0.3 shard_map.100.refs_5_.field_ref.refs_6_
  26.4 1.6 %collective-permute-start.14 = (f32[1,256,128]{2,1,0:T(8,128)S(1)}, f32[1,256,128]{2,1,0:T(8,128)S(1)}, u32[]{:S(2)}, u32[]{:S(2)}) collective-permute-start(f32[1,256,128]{2,1,0:T(8,128)S(1)} %shard_map.100.refs_5_.field_ref.refs_6_), channel_id=1, source_target_pairs={{0,16},{1,2},{2,1},{3,4},{4,3},{5,6},{6,5},{7,8},{8,7},{9,10},{10,... | collective-permute-start | bytes 393224 | tf_op jit(solution)/shard_map/ppermute | solution.py:351
  27.9 1.0 %collective-permute-start.15 = (f32[1,256,128]{2,1,0:T(8,128)S(1)}, f32[1,256,128]{2,1,0:T(8,128)S(1)}, u32[]{:S(2)}, u32[]{:S(2)}) collective-permute-start(f32[1,256,128]{2,1,0:T(8,128)S(1)} %shard_map.100.refs_5_.field_ref.refs_6_), channel_id=1, source_target_pairs={{0,1},{1,0},{2,3},{3,2},{4,5},{5,4},{6,7},{7,6},{8,9},{9,8},{10,11... | collective-permute-start | bytes 393224 | tf_op jit(solution)/shard_map/ppermute | solution.py:352
  28.9 0.3 shard_map.98.refs_8_.field_ref.refs_10_
  29.2 1.6 %collective-permute-start.8 = (f32[1,256,128]{2,1,0:T(8,128)S(1)}, f32[1,256,128]{2,1,0:T(8,128)S(1)}, u32[]{:S(2)}, u32[]{:S(2)}) collective-permute-start(f32[1,256,128]{2,1,0:T(8,128)S(1)} %shard_map.98.refs_8_.field_ref.refs_10_), channel_id=1, source_target_pairs={{0,16},{1,2},{2,1},{3,4},{4,3},{5,6},{6,5},{7,8},{8,7},{9,10},{10,... | collective-permute-start | bytes 393224 | tf_op jit(solution)/shard_map/ppermute | solution.py:351
  30.7 1.0 %collective-permute-start.9 = (f32[1,256,128]{2,1,0:T(8,128)S(1)}, f32[1,256,128]{2,1,0:T(8,128)S(1)}, u32[]{:S(2)}, u32[]{:S(2)}) collective-permute-start(f32[1,256,128]{2,1,0:T(8,128)S(1)} %shard_map.98.refs_8_.field_ref.refs_10_), channel_id=1, source_target_pairs={{0,1},{1,0},{2,3},{3,2},{4,5},{5,4},{6,7},{7,6},{8,9},{9,8},{10,11... | collective-permute-start | bytes 393224 | tf_op jit(solution)/shard_map/ppermute | solution.py:352
  31.7 2.0 %shard_map.103 = (f32[8,128]{1,0:T(8,128)S(1)}, f32[7,3,256,128]{3,2,1,0:T(8,128)S(1)}, f32[7,3,256,128]{3,2,1,0:T(8,128)S(1)}) custom-call(f32[256,128]{1,0:T(8,128)S(1)} %get-tuple-element.42.diagonal_ref, f32[1,256,128]{2,1,0:T(8,128)S(1)} %get-tuple-element.41.field_ref.refs_0_, f32[1,256,128]{2,1,0:T(8,128)S(1)} %shard_map.101.field_ref.refs_1_, ...), custom_call_target="tpu_custom_call" | custom-call | tf_op jit(solution)/shard_map/pallas_call | solution.py:323
  33.8 0.5 shard_map.104
  34.2 0.5 shard_map.105
  34.7 0.5 shard_map.106
  35.2 13.9 %all_to_all.5.moments_ref = f32[32,1,128]{2,1,0:T(1,128)S(1)} all-to-all(f32[32,1,128]{2,1,0:T(1,128)S(1)} %get-tuple-element.48), channel_id=1, replica_groups=mesh['diamond'=2,'tile'=16] {'diamond','tile'}, dimensions={0} | all-to-all | bytes 32768 | tf_op jit(solution)/shard_map/all_to_all | solution.py:401
  49.0 1.2 %shard_map.107 = (f32[3,256,128]{2,1,0:T(8,128)}, f32[3,256,128]{2,1,0:T(8,128)}) custom-call(f32[32,1,128]{2,1,0:T(1,128)S(1)} %all_to_all.5.moments_ref, f32[256,128]{1,0:T(8,128)S(1)} %get-tuple-element.42.diagonal_ref, f32[1,256,128]{2,1,0:T(8,128)S(1)} %get-tuple-element.41.field_ref.refs_0_, f32[1,256,128]{2,1,0:T(8,128)S(1)} %shard_map.101.field_ref.refs_1_, ...), custom_call_target="tpu_custom_call" | custom-call | tf_op jit(solution)/shard_map/pallas_call | solution.py:323
  (11 shorter events, 0.0 us)
Async XLA Ops:
  0.6 6.5 %collective-permute-start.2 = (f32[1,256,128]{2,1,0:T(8,128)}, f32[1,256,128]{2,1,0:T(8,128)S(1)}, u32[]{:S(2)}, u32[]{:S(2)}) collective-permute-start(f32[1,256,128]{2,1,0:T(8,128)} %bitcast.20), channel_id=1, source_target_pairs={{0,16},{1,2},{2,1},{3,4},{4,3},{5,6},{6,5},{7,8},{8,7},{9,10},{10,... | collective-permute-start | bytes 393224 | tf_op jit(solution)/shard_map/ppermute | solution.py:351
  3.6 3.5 %collective-permute-start.3 = (f32[1,256,128]{2,1,0:T(8,128)}, f32[1,256,128]{2,1,0:T(8,128)S(1)}, u32[]{:S(2)}, u32[]{:S(2)}) collective-permute-start(f32[1,256,128]{2,1,0:T(8,128)} %bitcast.21), channel_id=1, source_target_pairs={{0,1},{1,0},{2,3},{3,2},{4,5},{5,4},{6,7},{7,6},{8,9},{9,8},{10,11... | collective-permute-start | bytes 393224 | tf_op jit(solution)/shard_map/ppermute | solution.py:352
  5.4 6.2 %collective-permute-start = (f32[1,256,128]{2,1,0:T(8,128)S(1)}, f32[1,256,128]{2,1,0:T(8,128)S(1)}, u32[]{:S(2)}, u32[]{:S(2)}) collective-permute-start(f32[1,256,128]{2,1,0:T(8,128)S(1)} %bitcast.14), channel_id=1, source_target_pairs={{0,16},{1,2},{2,1},{3,4},{4,3},{5,6},{6,5},{7,8},{8,7},{9,10},{10,... | collective-permute-start | bytes 393224 | tf_op jit(solution)/shard_map/ppermute | solution.py:351
  7.0 4.6 %collective-permute-start.1 = (f32[1,256,128]{2,1,0:T(8,128)S(1)}, f32[1,256,128]{2,1,0:T(8,128)S(1)}, u32[]{:S(2)}, u32[]{:S(2)}) collective-permute-start(f32[1,256,128]{2,1,0:T(8,128)S(1)} %bitcast.15), channel_id=1, source_target_pairs={{0,1},{1,0},{2,3},{3,2},{4,5},{5,4},{6,7},{7,6},{8,9},{9,8},{10,11... | collective-permute-start | bytes 393224 | tf_op jit(solution)/shard_map/ppermute | solution.py:352
  7.4 6.3 %collective-permute-start.16 = (f32[1,256,128]{2,1,0:T(8,128)S(1)}, f32[1,256,128]{2,1,0:T(8,128)S(1)}, u32[]{:S(2)}, u32[]{:S(2)}) collective-permute-start(f32[1,256,128]{2,1,0:T(8,128)S(1)} %get-tuple-element.41.field_ref.refs_0_), channel_id=1, source_target_pairs={{0,16},{1,2},{2,1},{3,4},{4,3},{5,6},{6,5},{7,8},{8,7},{9,10},{10,... | collective-permute-start | bytes 393224 | tf_op jit(solution)/shard_map/ppermute | solution.py:351
  9.2 5.7 %collective-permute-start.17 = (f32[1,256,128]{2,1,0:T(8,128)S(1)}, f32[1,256,128]{2,1,0:T(8,128)S(1)}, u32[]{:S(2)}, u32[]{:S(2)}) collective-permute-start(f32[1,256,128]{2,1,0:T(8,128)S(1)} %get-tuple-element.41.field_ref.refs_0_), channel_id=1, source_target_pairs={{0,1},{1,0},{2,3},{3,2},{4,5},{5,4},{6,7},{7,6},{8,9},{9,8},{10,11... | collective-permute-start | bytes 393224 | tf_op jit(solution)/shard_map/ppermute | solution.py:352
  10.1 6.5 %collective-permute-start.10 = (f32[1,256,128]{2,1,0:T(8,128)S(1)}, f32[1,256,128]{2,1,0:T(8,128)S(1)}, u32[]{:S(2)}, u32[]{:S(2)}) collective-permute-start(f32[1,256,128]{2,1,0:T(8,128)S(1)} %get-tuple-element.40.field_ref.refs_3_.refs_4_), channel_id=1, source_target_pairs={{0,16},{1,2},{2,1},{3,4},{4,3},{5,6},{6,5},{7,8},{8,7},{9,10},{10,... | collective-permute-start | bytes 393224 | tf_op jit(solution)/shard_map/ppermute | solution.py:351
  11.6 6.0 %collective-permute-start.11 = (f32[1,256,128]{2,1,0:T(8,128)S(1)}, f32[1,256,128]{2,1,0:T(8,128)S(1)}, u32[]{:S(2)}, u32[]{:S(2)}) collective-permute-start(f32[1,256,128]{2,1,0:T(8,128)S(1)} %get-tuple-element.40.field_ref.refs_3_.refs_4_), channel_id=1, source_target_pairs={{0,1},{1,0},{2,3},{3,2},{4,5},{5,4},{6,7},{7,6},{8,9},{9,8},{10,11... | collective-permute-start | bytes 393224 | tf_op jit(solution)/shard_map/ppermute | solution.py:352
  12.5 7.0 %collective-permute-start.4 = (f32[1,256,128]{2,1,0:T(8,128)S(1)}, f32[1,256,128]{2,1,0:T(8,128)S(1)}, u32[]{:S(2)}, u32[]{:S(2)}) collective-permute-start(f32[1,256,128]{2,1,0:T(8,128)S(1)} %get-tuple-element.38.field_ref.refs_6_.refs_8_), channel_id=1, source_target_pairs={{0,16},{1,2},{2,1},{3,4},{4,3},{5,6},{6,5},{7,8},{8,7},{9,10},{10,... | collective-permute-start | bytes 393224 | tf_op jit(solution)/shard_map/ppermute | solution.py:351
  13.8 6.7 %collective-permute-start.5 = (f32[1,256,128]{2,1,0:T(8,128)S(1)}, f32[1,256,128]{2,1,0:T(8,128)S(1)}, u32[]{:S(2)}, u32[]{:S(2)}) collective-permute-start(f32[1,256,128]{2,1,0:T(8,128)S(1)} %get-tuple-element.38.field_ref.refs_6_.refs_8_), channel_id=1, source_target_pairs={{0,1},{1,0},{2,3},{3,2},{4,5},{5,4},{6,7},{7,6},{8,9},{9,8},{10,11... | collective-permute-start | bytes 393224 | tf_op jit(solution)/shard_map/ppermute | solution.py:352
  15.1 7.2 %collective-permute-start.18 = (f32[1,256,128]{2,1,0:T(8,128)S(1)}, f32[1,256,128]{2,1,0:T(8,128)S(1)}, u32[]{:S(2)}, u32[]{:S(2)}) collective-permute-start(f32[1,256,128]{2,1,0:T(8,128)S(1)} %shard_map.101.field_ref.refs_1_), channel_id=1, source_target_pairs={{0,16},{1,2},{2,1},{3,4},{4,3},{5,6},{6,5},{7,8},{8,7},{9,10},{10,... | collective-permute-start | bytes 393224 | tf_op jit(solution)/shard_map/ppermute | solution.py:351
  16.7 5.7 %collective-permute-start.19 = (f32[1,256,128]{2,1,0:T(8,128)S(1)}, f32[1,256,128]{2,1,0:T(8,128)S(1)}, u32[]{:S(2)}, u32[]{:S(2)}) collective-permute-start(f32[1,256,128]{2,1,0:T(8,128)S(1)} %shard_map.101.field_ref.refs_1_), channel_id=1, source_target_pairs={{0,1},{1,0},{2,3},{3,2},{4,5},{5,4},{6,7},{7,6},{8,9},{9,8},{10,11... | collective-permute-start | bytes 393224 | tf_op jit(solution)/shard_map/ppermute | solution.py:352
  17.9 6.2 %collective-permute-start.12 = (f32[1,256,128]{2,1,0:T(8,128)S(1)}, f32[1,256,128]{2,1,0:T(8,128)S(1)}, u32[]{:S(2)}, u32[]{:S(2)}) collective-permute-start(f32[1,256,128]{2,1,0:T(8,128)S(1)} %shard_map.99.field_ref.refs_4_.refs_5_), channel_id=1, source_target_pairs={{0,16},{1,2},{2,1},{3,4},{4,3},{5,6},{6,5},{7,8},{8,7},{9,10},{10,... | collective-permute-start | bytes 393224 | tf_op jit(solution)/shard_map/ppermute | solution.py:351
  19.5 6.6 %collective-permute-start.13 = (f32[1,256,128]{2,1,0:T(8,128)S(1)}, f32[1,256,128]{2,1,0:T(8,128)S(1)}, u32[]{:S(2)}, u32[]{:S(2)}) collective-permute-start(f32[1,256,128]{2,1,0:T(8,128)S(1)} %shard_map.99.field_ref.refs_4_.refs_5_), channel_id=1, source_target_pairs={{0,1},{1,0},{2,3},{3,2},{4,5},{5,4},{6,7},{7,6},{8,9},{9,8},{10,11... | collective-permute-start | bytes 393224 | tf_op jit(solution)/shard_map/ppermute | solution.py:352
  20.7 7.2 %collective-permute-start.6 = (f32[1,256,128]{2,1,0:T(8,128)S(1)}, f32[1,256,128]{2,1,0:T(8,128)S(1)}, u32[]{:S(2)}, u32[]{:S(2)}) collective-permute-start(f32[1,256,128]{2,1,0:T(8,128)S(1)} %shard_map.97.field_ref.refs_7_.refs_9_), channel_id=1, source_target_pairs={{0,16},{1,2},{2,1},{3,4},{4,3},{5,6},{6,5},{7,8},{8,7},{9,10},{10,... | collective-permute-start | bytes 393224 | tf_op jit(solution)/shard_map/ppermute | solution.py:351
  22.3 6.6 %collective-permute-start.7 = (f32[1,256,128]{2,1,0:T(8,128)S(1)}, f32[1,256,128]{2,1,0:T(8,128)S(1)}, u32[]{:S(2)}, u32[]{:S(2)}) collective-permute-start(f32[1,256,128]{2,1,0:T(8,128)S(1)} %shard_map.97.field_ref.refs_7_.refs_9_), channel_id=1, source_target_pairs={{0,1},{1,0},{2,3},{3,2},{4,5},{5,4},{6,7},{7,6},{8,9},{9,8},{10,11... | collective-permute-start | bytes 393224 | tf_op jit(solution)/shard_map/ppermute | solution.py:352
  22.6 8.1 %collective-permute-start.20 = (f32[1,256,128]{2,1,0:T(8,128)S(1)}, f32[1,256,128]{2,1,0:T(8,128)S(1)}, u32[]{:S(2)}, u32[]{:S(2)}) collective-permute-start(f32[1,256,128]{2,1,0:T(8,128)S(1)} %shard_map.102.refs_2_.field_ref), channel_id=1, source_target_pairs={{0,16},{1,2},{2,1},{3,4},{4,3},{5,6},{6,5},{7,8},{8,7},{9,10},{10,... | collective-permute-start | bytes 393224 | tf_op jit(solution)/shard_map/ppermute | solution.py:351
  24.2 9.6 %collective-permute-start.21 = (f32[1,256,128]{2,1,0:T(8,128)S(1)}, f32[1,256,128]{2,1,0:T(8,128)S(1)}, u32[]{:S(2)}, u32[]{:S(2)}) collective-permute-start(f32[1,256,128]{2,1,0:T(8,128)S(1)} %shard_map.102.refs_2_.field_ref), channel_id=1, source_target_pairs={{0,1},{1,0},{2,3},{3,2},{4,5},{5,4},{6,7},{7,6},{8,9},{9,8},{10,11... | collective-permute-start | bytes 393224 | tf_op jit(solution)/shard_map/ppermute | solution.py:352
  26.4 7.9 %collective-permute-start.14 = (f32[1,256,128]{2,1,0:T(8,128)S(1)}, f32[1,256,128]{2,1,0:T(8,128)S(1)}, u32[]{:S(2)}, u32[]{:S(2)}) collective-permute-start(f32[1,256,128]{2,1,0:T(8,128)S(1)} %shard_map.100.refs_5_.field_ref.refs_6_), channel_id=1, source_target_pairs={{0,16},{1,2},{2,1},{3,4},{4,3},{5,6},{6,5},{7,8},{8,7},{9,10},{10,... | collective-permute-start | bytes 393224 | tf_op jit(solution)/shard_map/ppermute | solution.py:351
  27.9 6.3 %collective-permute-start.15 = (f32[1,256,128]{2,1,0:T(8,128)S(1)}, f32[1,256,128]{2,1,0:T(8,128)S(1)}, u32[]{:S(2)}, u32[]{:S(2)}) collective-permute-start(f32[1,256,128]{2,1,0:T(8,128)S(1)} %shard_map.100.refs_5_.field_ref.refs_6_), channel_id=1, source_target_pairs={{0,1},{1,0},{2,3},{3,2},{4,5},{5,4},{6,7},{7,6},{8,9},{9,8},{10,11... | collective-permute-start | bytes 393224 | tf_op jit(solution)/shard_map/ppermute | solution.py:352
  29.2 5.5 %collective-permute-start.8 = (f32[1,256,128]{2,1,0:T(8,128)S(1)}, f32[1,256,128]{2,1,0:T(8,128)S(1)}, u32[]{:S(2)}, u32[]{:S(2)}) collective-permute-start(f32[1,256,128]{2,1,0:T(8,128)S(1)} %shard_map.98.refs_8_.field_ref.refs_10_), channel_id=1, source_target_pairs={{0,16},{1,2},{2,1},{3,4},{4,3},{5,6},{6,5},{7,8},{8,7},{9,10},{10,... | collective-permute-start | bytes 393224 | tf_op jit(solution)/shard_map/ppermute | solution.py:351
  30.7 4.0 %collective-permute-start.9 = (f32[1,256,128]{2,1,0:T(8,128)S(1)}, f32[1,256,128]{2,1,0:T(8,128)S(1)}, u32[]{:S(2)}, u32[]{:S(2)}) collective-permute-start(f32[1,256,128]{2,1,0:T(8,128)S(1)} %shard_map.98.refs_8_.field_ref.refs_10_), channel_id=1, source_target_pairs={{0,1},{1,0},{2,3},{3,2},{4,5},{5,4},{6,7},{7,6},{8,9},{9,8},{10,11... | collective-permute-start | bytes 393224 | tf_op jit(solution)/shard_map/ppermute | solution.py:352

commit v4 on v3

--- a/solution.py
+++ b/solution.py
@@ -17,6 +17,14 @@
 SPLITS = ((0, 1), (1, 2), (2, 3))
 
 
+def tile_index():
+    return 2 * lax.axis_index("chip") + lax.axis_index("core")
+
+
+def tile_count():
+    return 2 * lax.axis_size("chip")
+
+
 def rows_around(load, start, total):
     low, high = max(start - 8, 0), min(start + CHUNK + 8, total)
     block = load(low, high)
@@ -40,8 +48,8 @@
 
 
 def fold_matrix(edge_ref, pole_ref):
-    group, tile = lax.axis_index("diamond"), lax.axis_index("tile")
-    final = lax.axis_size("tile") - 1
+    group, tile = lax.axis_index("diamond"), tile_index()
+    final = tile_count() - 1
     count = edge_ref.shape[1]
     rows = lax.broadcasted_iota(jnp.int32, (count, count), 0)
     same = lax.broadcasted_iota(jnp.int32, (1, count), 1)
@@ -71,7 +79,7 @@
     copies = [pltpu.make_async_copy(s, t, sems.at[i]) for i, (s, t) in enumerate(zip(sources, targets))]
     for copy in copies:
         copy.start()
-    odd = lax.rem(lax.axis_index("tile"), 2)
+    odd = lax.axis_index("core")
     half = jnp.where(odd == 0, 0.5, -0.5).astype(jnp.float32)
     total, layers = temp_ref.shape
     for copy in copies:
@@ -222,12 +230,7 @@
             for j in range(len(CENTERS)):
                 sums[j] += fold8(left_ref[j, low + at, here] * (y3 - shift_ref[j, low + at, here]))
     message = earlier_ref[...] + place_moment(5, sums)
-    if len(moments_ref.shape) == 2:
-        moments_ref[...] = message
-    else:
-        row = jnp.sum(message, axis=0, keepdims=True)
-        for device in range(moments_ref.shape[0]):
-            moments_ref[device] = row
+    moments_ref[...] = jnp.sum(message, axis=0, keepdims=True) if moments_ref.shape[0] == 1 else message
 
 
 def inner(left, right, moments, shift=0):
@@ -273,8 +276,10 @@
     return answer, residual
 
 
-def finish_kernel(moments_ref, diagonal_ref, *refs):
-    *refs, solution_hbm, residual_hbm, solution_ref, residual_ref, sems = refs
+def finish_kernel(moments_ref, diagonal_ref, next_ref, *refs):
+    *refs, solution_hbm, residual_hbm, next_hbm, solution_ref, residual_ref, sems, next_sem = refs
+    copies = [pltpu.make_async_copy(next_ref, next_hbm, next_sem)]
+    copies[0].start()
     streams = [refs[4 * i : 4 * i + 4] for i in range(len(SPLITS))]
     rows = [moments_ref[device] for device in range(moments_ref.shape[0])]
     while len(rows) > 1:
@@ -298,7 +303,6 @@
     total, layers = diagonal_ref.shape
     chosen = [jnp.broadcast_to(c, (CHUNK, layers)) for c in chosen]
     center, answer, residual = chosen[0], chosen[1:4], chosen[4:8]
-    copies = []
     for (low, high), stream in zip(SPLITS, streams):
         for at in range(high - low):
             for start in range(0, total, CHUNK):
@@ -343,11 +347,11 @@
     return beside, across
 
 
-NAMES = ("diamond", "tile")
+NAMES = ("diamond", "chip", "core")
 
 
 def exchange(value):
-    beside, across = ring_pairs(lax.axis_size("diamond"), lax.axis_size("tile"))
+    beside, across = ring_pairs(lax.axis_size("diamond"), tile_count())
     far = lax.ppermute(value, NAMES, across)
     near = lax.ppermute(value, NAMES, beside)
     return near, far
@@ -355,7 +359,7 @@
 
 def body(adjoint_temp, misfit, viscosity, velocity, forcing, edge_table, pole_table):
     rows, layers = adjoint_temp.shape[2:]
-    devices = lax.axis_size("diamond") * lax.axis_size("tile")
+    chips = lax.axis_size("diamond") * lax.axis_size("chip")
     flat, triple = (rows, layers), (3, rows, layers)
     temp, source, visc = (v.reshape(flat) for v in (adjoint_temp, misfit, viscosity))
     visc_near, visc_far = exchange(visc[None])
@@ -392,25 +396,28 @@
     )
     for i, shape in enumerate(shapes):
         near, far = swapped[i]
-        sums = (8, 128) if i + 1 < len(shapes) else (devices, 1, 128)
+        sums = (8 if i + 1 < len(shapes) else 1, 128)
         field, moments = call(
             functools.partial(last_kernel, SPLITS[i][0]), [shape, sums],
             far, near, streams[i][-1], weights, matrix, moments, left, shift, scratch=[shape],
         )
         streams[i].append(field)
-    moments = lax.all_to_all(moments, NAMES, 0, 0)
+    moments = moments + lax.ppermute(moments, "core", [(0, 1), (1, 0)])
+    moments = lax.all_to_all(jnp.broadcast_to(moments, (chips, 1, 128)), NAMES[:2], 0, 0)
     fields = [field for stream in streams for field in stream]
-    answer, residual = call(
-        finish_kernel, [triple, triple], moments, diagonal, *fields,
-        scratch=[triple, triple, pltpu.SemaphoreType.DMA((2, 3))], out_place=pltpu.HBM,
+    answer, residual, adjoint_next = call(
+        finish_kernel, [triple, triple, flat], moments, diagonal, adjoint_next, *fields,
+        scratch=[triple, triple, pltpu.SemaphoreType.DMA((2, 3)), pltpu.SemaphoreType.DMA], out_place=pltpu.HBM,
     )
     whole = (3, 1, 1, rows, layers)
     return answer.reshape(whole), residual.reshape(whole), adjoint_next.reshape(adjoint_temp.shape)
 
 
 def solution(mesh):
-    flat = P("diamond", "tile", None, None)
-    triple = P(None, "diamond", "tile", None, None)
+    groups, tiles = mesh.devices.shape
+    mesh = jax.sharding.Mesh(mesh.devices.reshape(groups, tiles // 2, 2), NAMES)
+    flat = P("diamond", ("chip", "core"), None, None)
+    triple = P(None, "diamond", ("chip", "core"), None, None)
     return jax.shard_map(
         body,
         mesh=mesh,

time: 50.5 us -> 54.3 us (1.075)
  starting transfers between devices: 26.6 us -> 28.4 us
  blocking collectives: 13.9 us -> 15.6 us
  waiting for transfers between devices: 0.06 us -> 0.88 us
  Pallas kernels: 9.04 us -> 8.49 us
    all_to_all x1, blocking collectives: 13.9 us -> 15.6 us  [body(): lax.all_to_all(jnp.broadcast_to(moments, (chips, 1, 128)), NAMES[:2], 0, 0)]
    ppermute x0 -> x1, starting transfers between devices: none -> 1.14 us  [body(): moments = moments + lax.ppermute(moments, 'core', [(0, 1), (1, 0)])]
    ppermute x11, starting transfers between devices: 8.28 us -> 9.37 us  [exchange(): near = lax.ppermute(value, NAMES, beside)]
    ppermute x0 -> x1, waiting for transfers between devices: none -> 0.82 us  [body(): moments = moments + lax.ppermute(moments, 'core', [(0, 1), (1, 0)])]
    pallas_call x14, Pallas kernels: 9.04 us -> 8.49 us  [call(): pl.pallas_call(kernel, out_shape=outs, in_specs=[pl.BlockSpec(memory_spac...]
  transfers between devices with their start and end apart: 22 -> 23, of which waited for: 0 -> 1; matrix products, arithmetic and copies ran while one was open for 0% -> 0% of each run, Pallas kernels for 15% -> 12%
where the time goes in v4:
time: 54.3 us; the launch traced here: 54.1 us
  starting transfers between devices  28.4 us (52%)
  blocking collectives  15.6 us (29%)
  Pallas kernels  8.49 us (16%)
  waiting for transfers between devices  0.88 us (2%)
  between operations  0.72 us (1%)
    ppermute x11, starting transfers between devices, exchange(): far = lax.ppermute(value, NAMES, across)  17.9 us
    all_to_all x1, blocking collectives, body(): lax.all_to_all(jnp.broadcast_to(moments, (chips, 1, 128)), NAMES[:2], 0, 0)  15.6 us
    ppermute x11, starting transfers between devices, exchange(): near = lax.ppermute(value, NAMES, beside)  9.37 us
    pallas_call x14, Pallas kernels, call(): pl.pallas_call(kernel, out_shape=outs, in_specs=[pl.BlockSpec(memory_spac...  8.49 us
    ppermute x1, starting transfers between devices, body(): moments = moments + lax.ppermute(moments, 'core', [(0, 1), (1, 0)])  1.14 us
  transfers between devices with their start and end apart: 23, of which 1 were waited for; matrix products, arithmetic and copies ran while one was open for 0% of the time, Pallas kernels for 12%

profile of v4, /device:TPU:0, one launch (start us, length us, event | category | flops | bytes accessed | tf_op | source)
XLA Modules:
  0.0 54.1 jit_solution(3665783863482064717)
XLA Ops:
  0.6 3.0 %collective-permute-start.2 = (f32[1,256,128]{2,1,0:T(8,128)}, f32[1,256,128]{2,1,0:T(8,128)S(1)}, u32[]{:S(2)}, u32[]{:S(2)}) collective-permute-start(f32[1,256,128]{2,1,0:T(8,128)} %bitcast.22), channel_id=1, source_target_pairs={{0,16},{1,2},{2,1},{3,4},{4,3},{5,6},{6,5},{7,8},{8,7},{9,10},{10,... | collective-permute-start | bytes 393224 | tf_op jit(solution)/shard_map/ppermute | solution.py:355
  3.6 0.1 collective-permute-start.3
  3.8 1.7 %shard_map.94 = (f32[256,128]{1,0:T(8,128)S(1)}, f32[4,256,128]{2,1,0:T(8,128)S(1)}, f32[256,128]{1,0:T(8,128)S(1)}, f32[3,256,128]{2,1,0:T(8,128)S(1)}, f32[256...) custom-call(f32[256,128]{1,0:T(8,128)} %bitcast.20, ...), custom_call_target="tpu_custom_call" | custom-call | tf_op jit(solution)/shard_map/pallas_call | solution.py:327
  5.4 1.6 %collective-permute-start = (f32[1,256,128]{2,1,0:T(8,128)S(1)}, f32[1,256,128]{2,1,0:T(8,128)S(1)}, u32[]{:S(2)}, u32[]{:S(2)}) collective-permute-start(f32[1,256,128]{2,1,0:T(8,128)S(1)} %bitcast.16), channel_id=1, source_target_pairs={{0,16},{1,2},{2,1},{3,4},{4,3},{5,6},{6,5},{7,8},{8,7},{9,10},{10,... | collective-permute-start | bytes 393224 | tf_op jit(solution)/shard_map/ppermute | solution.py:355
  7.0 0.1 collective-permute-start.1
  7.1 0.3 shard_map.95
  7.4 1.7 %collective-permute-start.16 = (f32[1,256,128]{2,1,0:T(8,128)S(1)}, f32[1,256,128]{2,1,0:T(8,128)S(1)}, u32[]{:S(2)}, u32[]{:S(2)}) collective-permute-start(f32[1,256,128]{2,1,0:T(8,128)S(1)} %get-tuple-element.42.field_ref.refs_0_), channel_id=1, source_target_pairs={{0,16},{1,2},{2,1},{3,4},{4,3},{5,6},{6,5},{7,8},{8,7},{9,10},{10,... | collective-permute-start | bytes 393224 | tf_op jit(solution)/shard_map/ppermute | solution.py:355
  9.2 1.0 %collective-permute-start.17 = (f32[1,256,128]{2,1,0:T(8,128)S(1)}, f32[1,256,128]{2,1,0:T(8,128)S(1)}, u32[]{:S(2)}, u32[]{:S(2)}) collective-permute-start(f32[1,256,128]{2,1,0:T(8,128)S(1)} %get-tuple-element.42.field_ref.refs_0_), channel_id=1, source_target_pairs={{0,1},{1,0},{2,3},{3,2},{4,5},{5,4},{6,7},{7,6},{8,9},{9,8},{10,11... | collective-permute-start | bytes 393224 | tf_op jit(solution)/shard_map/ppermute | solution.py:356
  10.1 1.5 %collective-permute-start.10 = (f32[1,256,128]{2,1,0:T(8,128)S(1)}, f32[1,256,128]{2,1,0:T(8,128)S(1)}, u32[]{:S(2)}, u32[]{:S(2)}) collective-permute-start(f32[1,256,128]{2,1,0:T(8,128)S(1)} %get-tuple-element.41.field_ref.refs_3_.refs_4_), channel_id=1, source_target_pairs={{0,16},{1,2},{2,1},{3,4},{4,3},{5,6},{6,5},{7,8},{8,7},{9,10},{10,... | collective-permute-start | bytes 393224 | tf_op jit(solution)/shard_map/ppermute | solution.py:355
  11.6 0.0 collective-permute-done.far_ref
  11.6 0.0 collective-permute-start.11
  11.6 0.0 collective-permute-done.1.near_ref
  11.6 0.2 shard_map.96
  11.9 1.3 %collective-permute-start.4 = (f32[1,256,128]{2,1,0:T(8,128)S(1)}, f32[1,256,128]{2,1,0:T(8,128)S(1)}, u32[]{:S(2)}, u32[]{:S(2)}) collective-permute-start(f32[1,256,128]{2,1,0:T(8,128)S(1)} %get-tuple-element.39.field_ref.refs_6_.refs_8_), channel_id=1, source_target_pairs={{0,16},{1,2},{2,1},{3,4},{4,3},{5,6},{6,5},{7,8},{8,7},{9,10},{10,... | collective-permute-start | bytes 393224 | tf_op jit(solution)/shard_map/ppermute | solution.py:355
  13.2 0.0 collective-permute-done.16.far_ref
  13.2 1.7 %collective-permute-start.5 = (f32[1,256,128]{2,1,0:T(8,128)S(1)}, f32[1,256,128]{2,1,0:T(8,128)S(1)}, u32[]{:S(2)}, u32[]{:S(2)}) collective-permute-start(f32[1,256,128]{2,1,0:T(8,128)S(1)} %get-tuple-element.39.field_ref.refs_6_.refs_8_), channel_id=1, source_target_pairs={{0,1},{1,0},{2,3},{3,2},{4,5},{5,4},{6,7},{7,6},{8,9},{9,8},{10,11... | collective-permute-start | bytes 393224 | tf_op jit(solution)/shard_map/ppermute | solution.py:356
  14.9 0.0 collective-permute-done.17.near_ref
  14.9 0.3 shard_map.101.field_ref.refs_1_
  15.1 1.6 %collective-permute-start.18 = (f32[1,256,128]{2,1,0:T(8,128)S(1)}, f32[1,256,128]{2,1,0:T(8,128)S(1)}, u32[]{:S(2)}, u32[]{:S(2)}) collective-permute-start(f32[1,256,128]{2,1,0:T(8,128)S(1)} %shard_map.101.field_ref.refs_1_), channel_id=1, source_target_pairs={{0,16},{1,2},{2,1},{3,4},{4,3},{5,6},{6,5},{7,8},{8,7},{9,10},{10,... | collective-permute-start | bytes 393224 | tf_op jit(solution)/shard_map/ppermute | solution.py:355
  16.7 0.0 collective-permute-done.10.far_ref
  16.7 1.0 %collective-permute-start.19 = (f32[1,256,128]{2,1,0:T(8,128)S(1)}, f32[1,256,128]{2,1,0:T(8,128)S(1)}, u32[]{:S(2)}, u32[]{:S(2)}) collective-permute-start(f32[1,256,128]{2,1,0:T(8,128)S(1)} %shard_map.101.field_ref.refs_1_), channel_id=1, source_target_pairs={{0,1},{1,0},{2,3},{3,2},{4,5},{5,4},{6,7},{7,6},{8,9},{9,8},{10,11... | collective-permute-start | bytes 393224 | tf_op jit(solution)/shard_map/ppermute | solution.py:356
  17.7 0.3 shard_map.99.field_ref.refs_4_.refs_5_
  17.9 1.6 %collective-permute-start.12 = (f32[1,256,128]{2,1,0:T(8,128)S(1)}, f32[1,256,128]{2,1,0:T(8,128)S(1)}, u32[]{:S(2)}, u32[]{:S(2)}) collective-permute-start(f32[1,256,128]{2,1,0:T(8,128)S(1)} %shard_map.99.field_ref.refs_4_.refs_5_), channel_id=1, source_target_pairs={{0,16},{1,2},{2,1},{3,4},{4,3},{5,6},{6,5},{7,8},{8,7},{9,10},{10,... | collective-permute-start | bytes 393224 | tf_op jit(solution)/shard_map/ppermute | solution.py:355
  19.5 1.5 %collective-permute-start.13 = (f32[1,256,128]{2,1,0:T(8,128)S(1)}, f32[1,256,128]{2,1,0:T(8,128)S(1)}, u32[]{:S(2)}, u32[]{:S(2)}) collective-permute-start(f32[1,256,128]{2,1,0:T(8,128)S(1)} %shard_map.99.field_ref.refs_4_.refs_5_), channel_id=1, source_target_pairs={{0,1},{1,0},{2,3},{3,2},{4,5},{5,4},{6,7},{7,6},{8,9},{9,8},{10,11... | collective-permute-start | bytes 393224 | tf_op jit(solution)/shard_map/ppermute | solution.py:356
  21.0 0.0 collective-permute-done.5.near_ref
  21.0 0.3 shard_map.97.field_ref.refs_7_.refs_9_
  21.3 1.6 %collective-permute-start.6 = (f32[1,256,128]{2,1,0:T(8,128)S(1)}, f32[1,256,128]{2,1,0:T(8,128)S(1)}, u32[]{:S(2)}, u32[]{:S(2)}) collective-permute-start(f32[1,256,128]{2,1,0:T(8,128)S(1)} %shard_map.97.field_ref.refs_7_.refs_9_), channel_id=1, source_target_pairs={{0,16},{1,2},{2,1},{3,4},{4,3},{5,6},{6,5},{7,8},{8,7},{9,10},{10,... | collective-permute-start | bytes 393224 | tf_op jit(solution)/shard_map/ppermute | solution.py:355
  22.8 0.0 collective-permute-done.18.far_ref
  22.9 0.3 shard_map.102.refs_2_.field_ref
  23.1 1.0 %collective-permute-start.20 = (f32[1,256,128]{2,1,0:T(8,128)S(1)}, f32[1,256,128]{2,1,0:T(8,128)S(1)}, u32[]{:S(2)}, u32[]{:S(2)}) collective-permute-start(f32[1,256,128]{2,1,0:T(8,128)S(1)} %shard_map.102.refs_2_.field_ref), channel_id=1, source_target_pairs={{0,16},{1,2},{2,1},{3,4},{4,3},{5,6},{6,5},{7,8},{8,7},{9,10},{10,... | collective-permute-start | bytes 393224 | tf_op jit(solution)/shard_map/ppermute | solution.py:355
  24.2 1.9 %collective-permute-start.21 = (f32[1,256,128]{2,1,0:T(8,128)S(1)}, f32[1,256,128]{2,1,0:T(8,128)S(1)}, u32[]{:S(2)}, u32[]{:S(2)}) collective-permute-start(f32[1,256,128]{2,1,0:T(8,128)S(1)} %shard_map.102.refs_2_.field_ref), channel_id=1, source_target_pairs={{0,1},{1,0},{2,3},{3,2},{4,5},{5,4},{6,7},{7,6},{8,9},{9,8},{10,11... | collective-permute-start | bytes 393224 | tf_op jit(solution)/shard_map/ppermute | solution.py:356
  26.1 0.3 shard_map.100.refs_5_.field_ref.refs_6_
  26.4 1.6 %collective-permute-start.14 = (f32[1,256,128]{2,1,0:T(8,128)S(1)}, f32[1,256,128]{2,1,0:T(8,128)S(1)}, u32[]{:S(2)}, u32[]{:S(2)}) collective-permute-start(f32[1,256,128]{2,1,0:T(8,128)S(1)} %shard_map.100.refs_5_.field_ref.refs_6_), channel_id=1, source_target_pairs={{0,16},{1,2},{2,1},{3,4},{4,3},{5,6},{6,5},{7,8},{8,7},{9,10},{10,... | collective-permute-start | bytes 393224 | tf_op jit(solution)/shard_map/ppermute | solution.py:355
  27.9 0.0 collective-permute-done.6.far_ref
  27.9 1.0 %collective-permute-start.15 = (f32[1,256,128]{2,1,0:T(8,128)S(1)}, f32[1,256,128]{2,1,0:T(8,128)S(1)}, u32[]{:S(2)}, u32[]{:S(2)}) collective-permute-start(f32[1,256,128]{2,1,0:T(8,128)S(1)} %shard_map.100.refs_5_.field_ref.refs_6_), channel_id=1, source_target_pairs={{0,1},{1,0},{2,3},{3,2},{4,5},{5,4},{6,7},{7,6},{8,9},{9,8},{10,11... | collective-permute-start | bytes 393224 | tf_op jit(solution)/shard_map/ppermute | solution.py:356
  28.9 0.0 collective-permute-done.7.near_ref
  28.9 0.3 shard_map.98.refs_8_.field_ref.refs_10_
  29.2 1.6 %collective-permute-start.8 = (f32[1,256,128]{2,1,0:T(8,128)S(1)}, f32[1,256,128]{2,1,0:T(8,128)S(1)}, u32[]{:S(2)}, u32[]{:S(2)}) collective-permute-start(f32[1,256,128]{2,1,0:T(8,128)S(1)} %shard_map.98.refs_8_.field_ref.refs_10_), channel_id=1, source_target_pairs={{0,16},{1,2},{2,1},{3,4},{4,3},{5,6},{6,5},{7,8},{8,7},{9,10},{10,... | collective-permute-start | bytes 393224 | tf_op jit(solution)/shard_map/ppermute | solution.py:355
  30.7 1.0 %collective-permute-start.9 = (f32[1,256,128]{2,1,0:T(8,128)S(1)}, f32[1,256,128]{2,1,0:T(8,128)S(1)}, u32[]{:S(2)}, u32[]{:S(2)}) collective-permute-start(f32[1,256,128]{2,1,0:T(8,128)S(1)} %shard_map.98.refs_8_.field_ref.refs_10_), channel_id=1, source_target_pairs={{0,1},{1,0},{2,3},{3,2},{4,5},{5,4},{6,7},{7,6},{8,9},{9,8},{10,11... | collective-permute-start | bytes 393224 | tf_op jit(solution)/shard_map/ppermute | solution.py:356
  31.7 2.1 %shard_map.103 = (f32[8,128]{1,0:T(8,128)S(1)}, f32[7,3,256,128]{3,2,1,0:T(8,128)S(1)}, f32[7,3,256,128]{3,2,1,0:T(8,128)S(1)}) custom-call(f32[256,128]{1,0:T(8,128)S(1)} %get-tuple-element.43.diagonal_ref, f32[1,256,128]{2,1,0:T(8,128)S(1)} %get-tuple-element.42.field_ref.refs_0_, f32[1,256,128]{2,1,0:T(8,128)S(1)} %shard_map.101.field_ref.refs_1_, ...), custom_call_target="tpu_custom_call" | custom-call | tf_op jit(solution)/shard_map/pallas_call | solution.py:327
  33.8 0.5 shard_map.104
  34.3 0.0 collective-permute-done.14.far_ref
  34.3 0.5 shard_map.105
  34.8 0.5 shard_map.106
  35.3 1.1 %collective-permute-start.22 = (f32[1,128]{1,0:T(1,128)S(1)}, f32[1,128]{1,0:T(1,128)S(1)}, u32[]{:S(2)}, u32[]{:S(2)}) collective-permute-start(f32[1,128]{1,0:T(1,128)S(1)} %get-tuple-element.49), channel_id=1, source_target_pairs={{0,1},{1,0},{2,3},{3,2},{4,5},{5,4},{6,7},{7,6},{8,9},{9,8},{10,11... | collective-permute-start | bytes 1544 | tf_op jit(solution)/shard_map/ppermute | solution.py:405
  36.4 0.8 %collective-permute-done.22 = f32[1,128]{1,0:T(1,128)S(1)} collective-permute-done((f32[1,128]{1,0:T(1,128)S(1)}, f32[1,128]{1,0:T(1,128)S(1)}, u32[]{:S(2)}, u32[]{:S(2)}) %collective-permute-start.22) | collective-permute-done | bytes 544 | tf_op jit(solution)/shard_map/ppermute | solution.py:405
  37.2 15.6 %all_to_all.5.moments_ref = f32[16,1,128]{2,1,0:T(1,128)S(1)} all-to-all(f32[16,1,128]{2,1,0:T(1,128)S(1)} %broadcast_in_dim.7), channel_id=1, replica_groups=mesh['diamond'=2,'chip'=8,'core'=2] {'diamond','chip'}, dimensions={0} | all-to-all | bytes 16384 | tf_op jit(solution)/shard_map/all_to_all | solution.py:406
  52.9 1.3 %shard_map.107 = (f32[3,256,128]{2,1,0:T(8,128)}, f32[3,256,128]{2,1,0:T(8,128)}, f32[256,128]{1,0:T(8,128)}) custom-call(f32[16,1,128]{2,1,0:T(1,128)S(1)} %all_to_all.5.moments_ref, f32[256,128]{1,0:T(8,128)S(1)} %get-tuple-element.43.diagonal_ref, f32[256,128]{1,0:T(8,128)S(1)} %get-tuple-element.50.next_ref, ...), custom_call_target="tpu_custom_call" | custom-call | tf_op jit(solution)/shard_map/pallas_call | solution.py:327
  (15 shorter events, 0.0 us)
Async XLA Ops:
  0.6 6.5 %collective-permute-start.2 = (f32[1,256,128]{2,1,0:T(8,128)}, f32[1,256,128]{2,1,0:T(8,128)S(1)}, u32[]{:S(2)}, u32[]{:S(2)}) collective-permute-start(f32[1,256,128]{2,1,0:T(8,128)} %bitcast.22), channel_id=1, source_target_pairs={{0,16},{1,2},{2,1},{3,4},{4,3},{5,6},{6,5},{7,8},{8,7},{9,10},{10,... | collective-permute-start | bytes 393224 | tf_op jit(solution)/shard_map/ppermute | solution.py:355
  3.6 3.5 %collective-permute-start.3 = (f32[1,256,128]{2,1,0:T(8,128)}, f32[1,256,128]{2,1,0:T(8,128)S(1)}, u32[]{:S(2)}, u32[]{:S(2)}) collective-permute-start(f32[1,256,128]{2,1,0:T(8,128)} %bitcast.23), channel_id=1, source_target_pairs={{0,1},{1,0},{2,3},{3,2},{4,5},{5,4},{6,7},{7,6},{8,9},{9,8},{10,11... | collective-permute-start | bytes 393224 | tf_op jit(solution)/shard_map/ppermute | solution.py:356
  5.4 6.2 %collective-permute-start = (f32[1,256,128]{2,1,0:T(8,128)S(1)}, f32[1,256,128]{2,1,0:T(8,128)S(1)}, u32[]{:S(2)}, u32[]{:S(2)}) collective-permute-start(f32[1,256,128]{2,1,0:T(8,128)S(1)} %bitcast.16), channel_id=1, source_target_pairs={{0,16},{1,2},{2,1},{3,4},{4,3},{5,6},{6,5},{7,8},{8,7},{9,10},{10,... | collective-permute-start | bytes 393224 | tf_op jit(solution)/shard_map/ppermute | solution.py:355
  7.0 4.6 %collective-permute-start.1 = (f32[1,256,128]{2,1,0:T(8,128)S(1)}, f32[1,256,128]{2,1,0:T(8,128)S(1)}, u32[]{:S(2)}, u32[]{:S(2)}) collective-permute-start(f32[1,256,128]{2,1,0:T(8,128)S(1)} %bitcast.17), channel_id=1, source_target_pairs={{0,1},{1,0},{2,3},{3,2},{4,5},{5,4},{6,7},{7,6},{8,9},{9,8},{10,11... | collective-permute-start | bytes 393224 | tf_op jit(solution)/shard_map/ppermute | solution.py:356
  7.4 5.8 %collective-permute-start.16 = (f32[1,256,128]{2,1,0:T(8,128)S(1)}, f32[1,256,128]{2,1,0:T(8,128)S(1)}, u32[]{:S(2)}, u32[]{:S(2)}) collective-permute-start(f32[1,256,128]{2,1,0:T(8,128)S(1)} %get-tuple-element.42.field_ref.refs_0_), channel_id=1, source_target_pairs={{0,16},{1,2},{2,1},{3,4},{4,3},{5,6},{6,5},{7,8},{8,7},{9,10},{10,... | collective-permute-start | bytes 393224 | tf_op jit(solution)/shard_map/ppermute | solution.py:355
  9.2 5.7 %collective-permute-start.17 = (f32[1,256,128]{2,1,0:T(8,128)S(1)}, f32[1,256,128]{2,1,0:T(8,128)S(1)}, u32[]{:S(2)}, u32[]{:S(2)}) collective-permute-start(f32[1,256,128]{2,1,0:T(8,128)S(1)} %get-tuple-element.42.field_ref.refs_0_), channel_id=1, source_target_pairs={{0,1},{1,0},{2,3},{3,2},{4,5},{5,4},{6,7},{7,6},{8,9},{9,8},{10,11... | collective-permute-start | bytes 393224 | tf_op jit(solution)/shard_map/ppermute | solution.py:356
  10.1 6.5 %collective-permute-start.10 = (f32[1,256,128]{2,1,0:T(8,128)S(1)}, f32[1,256,128]{2,1,0:T(8,128)S(1)}, u32[]{:S(2)}, u32[]{:S(2)}) collective-permute-start(f32[1,256,128]{2,1,0:T(8,128)S(1)} %get-tuple-element.41.field_ref.refs_3_.refs_4_), channel_id=1, source_target_pairs={{0,16},{1,2},{2,1},{3,4},{4,3},{5,6},{6,5},{7,8},{8,7},{9,10},{10,... | collective-permute-start | bytes 393224 | tf_op jit(solution)/shard_map/ppermute | solution.py:355
  11.6 6.1 %collective-permute-start.11 = (f32[1,256,128]{2,1,0:T(8,128)S(1)}, f32[1,256,128]{2,1,0:T(8,128)S(1)}, u32[]{:S(2)}, u32[]{:S(2)}) collective-permute-start(f32[1,256,128]{2,1,0:T(8,128)S(1)} %get-tuple-element.41.field_ref.refs_3_.refs_4_), channel_id=1, source_target_pairs={{0,1},{1,0},{2,3},{3,2},{4,5},{5,4},{6,7},{7,6},{8,9},{9,8},{10,11... | collective-permute-start | bytes 393224 | tf_op jit(solution)/shard_map/ppermute | solution.py:356
  11.9 7.6 %collective-permute-start.4 = (f32[1,256,128]{2,1,0:T(8,128)S(1)}, f32[1,256,128]{2,1,0:T(8,128)S(1)}, u32[]{:S(2)}, u32[]{:S(2)}) collective-permute-start(f32[1,256,128]{2,1,0:T(8,128)S(1)} %get-tuple-element.39.field_ref.refs_6_.refs_8_), channel_id=1, source_target_pairs={{0,16},{1,2},{2,1},{3,4},{4,3},{5,6},{6,5},{7,8},{8,7},{9,10},{10,... | collective-permute-start | bytes 393224 | tf_op jit(solution)/shard_map/ppermute | solution.py:355
  13.2 7.9 %collective-permute-start.5 = (f32[1,256,128]{2,1,0:T(8,128)S(1)}, f32[1,256,128]{2,1,0:T(8,128)S(1)}, u32[]{:S(2)}, u32[]{:S(2)}) collective-permute-start(f32[1,256,128]{2,1,0:T(8,128)S(1)} %get-tuple-element.39.field_ref.refs_6_.refs_8_), channel_id=1, source_target_pairs={{0,1},{1,0},{2,3},{3,2},{4,5},{5,4},{6,7},{7,6},{8,9},{9,8},{10,11... | collective-permute-start | bytes 393224 | tf_op jit(solution)/shard_map/ppermute | solution.py:356
  15.1 7.7 %collective-permute-start.18 = (f32[1,256,128]{2,1,0:T(8,128)S(1)}, f32[1,256,128]{2,1,0:T(8,128)S(1)}, u32[]{:S(2)}, u32[]{:S(2)}) collective-permute-start(f32[1,256,128]{2,1,0:T(8,128)S(1)} %shard_map.101.field_ref.refs_1_), channel_id=1, source_target_pairs={{0,16},{1,2},{2,1},{3,4},{4,3},{5,6},{6,5},{7,8},{8,7},{9,10},{10,... | collective-permute-start | bytes 393224 | tf_op jit(solution)/shard_map/ppermute | solution.py:355
  16.7 6.2 %collective-permute-start.19 = (f32[1,256,128]{2,1,0:T(8,128)S(1)}, f32[1,256,128]{2,1,0:T(8,128)S(1)}, u32[]{:S(2)}, u32[]{:S(2)}) collective-permute-start(f32[1,256,128]{2,1,0:T(8,128)S(1)} %shard_map.101.field_ref.refs_1_), channel_id=1, source_target_pairs={{0,1},{1,0},{2,3},{3,2},{4,5},{5,4},{6,7},{7,6},{8,9},{9,8},{10,11... | collective-permute-start | bytes 393224 | tf_op jit(solution)/shard_map/ppermute | solution.py:356
  17.9 6.2 %collective-permute-start.12 = (f32[1,256,128]{2,1,0:T(8,128)S(1)}, f32[1,256,128]{2,1,0:T(8,128)S(1)}, u32[]{:S(2)}, u32[]{:S(2)}) collective-permute-start(f32[1,256,128]{2,1,0:T(8,128)S(1)} %shard_map.99.field_ref.refs_4_.refs_5_), channel_id=1, source_target_pairs={{0,16},{1,2},{2,1},{3,4},{4,3},{5,6},{6,5},{7,8},{8,7},{9,10},{10,... | collective-permute-start | bytes 393224 | tf_op jit(solution)/shard_map/ppermute | solution.py:355
  19.5 6.6 %collective-permute-start.13 = (f32[1,256,128]{2,1,0:T(8,128)S(1)}, f32[1,256,128]{2,1,0:T(8,128)S(1)}, u32[]{:S(2)}, u32[]{:S(2)}) collective-permute-start(f32[1,256,128]{2,1,0:T(8,128)S(1)} %shard_map.99.field_ref.refs_4_.refs_5_), channel_id=1, source_target_pairs={{0,1},{1,0},{2,3},{3,2},{4,5},{5,4},{6,7},{7,6},{8,9},{9,8},{10,11... | collective-permute-start | bytes 393224 | tf_op jit(solution)/shard_map/ppermute | solution.py:356
  21.3 6.6 %collective-permute-start.6 = (f32[1,256,128]{2,1,0:T(8,128)S(1)}, f32[1,256,128]{2,1,0:T(8,128)S(1)}, u32[]{:S(2)}, u32[]{:S(2)}) collective-permute-start(f32[1,256,128]{2,1,0:T(8,128)S(1)} %shard_map.97.field_ref.refs_7_.refs_9_), channel_id=1, source_target_pairs={{0,16},{1,2},{2,1},{3,4},{4,3},{5,6},{6,5},{7,8},{8,7},{9,10},{10,... | collective-permute-start | bytes 393224 | tf_op jit(solution)/shard_map/ppermute | solution.py:355
  22.9 6.1 %collective-permute-start.7 = (f32[1,256,128]{2,1,0:T(8,128)S(1)}, f32[1,256,128]{2,1,0:T(8,128)S(1)}, u32[]{:S(2)}, u32[]{:S(2)}) collective-permute-start(f32[1,256,128]{2,1,0:T(8,128)S(1)} %shard_map.97.field_ref.refs_7_.refs_9_), channel_id=1, source_target_pairs={{0,1},{1,0},{2,3},{3,2},{4,5},{5,4},{6,7},{7,6},{8,9},{9,8},{10,11... | collective-permute-start | bytes 393224 | tf_op jit(solution)/shard_map/ppermute | solution.py:356
  23.1 7.6 %collective-permute-start.20 = (f32[1,256,128]{2,1,0:T(8,128)S(1)}, f32[1,256,128]{2,1,0:T(8,128)S(1)}, u32[]{:S(2)}, u32[]{:S(2)}) collective-permute-start(f32[1,256,128]{2,1,0:T(8,128)S(1)} %shard_map.102.refs_2_.field_ref), channel_id=1, source_target_pairs={{0,16},{1,2},{2,1},{3,4},{4,3},{5,6},{6,5},{7,8},{8,7},{9,10},{10,... | collective-permute-start | bytes 393224 | tf_op jit(solution)/shard_map/ppermute | solution.py:355
  24.2 9.6 %collective-permute-start.21 = (f32[1,256,128]{2,1,0:T(8,128)S(1)}, f32[1,256,128]{2,1,0:T(8,128)S(1)}, u32[]{:S(2)}, u32[]{:S(2)}) collective-permute-start(f32[1,256,128]{2,1,0:T(8,128)S(1)} %shard_map.102.refs_2_.field_ref), channel_id=1, source_target_pairs={{0,1},{1,0},{2,3},{3,2},{4,5},{5,4},{6,7},{7,6},{8,9},{9,8},{10,11... | collective-permute-start | bytes 393224 | tf_op jit(solution)/shard_map/ppermute | solution.py:356
  26.4 7.9 %collective-permute-start.14 = (f32[1,256,128]{2,1,0:T(8,128)S(1)}, f32[1,256,128]{2,1,0:T(8,128)S(1)}, u32[]{:S(2)}, u32[]{:S(2)}) collective-permute-start(f32[1,256,128]{2,1,0:T(8,128)S(1)} %shard_map.100.refs_5_.field_ref.refs_6_), channel_id=1, source_target_pairs={{0,16},{1,2},{2,1},{3,4},{4,3},{5,6},{6,5},{7,8},{8,7},{9,10},{10,... | collective-permute-start | bytes 393224 | tf_op jit(solution)/shard_map/ppermute | solution.py:355
  27.9 6.4 %collective-permute-start.15 = (f32[1,256,128]{2,1,0:T(8,128)S(1)}, f32[1,256,128]{2,1,0:T(8,128)S(1)}, u32[]{:S(2)}, u32[]{:S(2)}) collective-permute-start(f32[1,256,128]{2,1,0:T(8,128)S(1)} %shard_map.100.refs_5_.field_ref.refs_6_), channel_id=1, source_target_pairs={{0,1},{1,0},{2,3},{3,2},{4,5},{5,4},{6,7},{7,6},{8,9},{9,8},{10,11... | collective-permute-start | bytes 393224 | tf_op jit(solution)/shard_map/ppermute | solution.py:356
  29.2 5.6 %collective-permute-start.8 = (f32[1,256,128]{2,1,0:T(8,128)S(1)}, f32[1,256,128]{2,1,0:T(8,128)S(1)}, u32[]{:S(2)}, u32[]{:S(2)}) collective-permute-start(f32[1,256,128]{2,1,0:T(8,128)S(1)} %shard_map.98.refs_8_.field_ref.refs_10_), channel_id=1, source_target_pairs={{0,16},{1,2},{2,1},{3,4},{4,3},{5,6},{6,5},{7,8},{8,7},{9,10},{10,... | collective-permute-start | bytes 393224 | tf_op jit(solution)/shard_map/ppermute | solution.py:355
  30.7 4.0 %collective-permute-start.9 = (f32[1,256,128]{2,1,0:T(8,128)S(1)}, f32[1,256,128]{2,1,0:T(8,128)S(1)}, u32[]{:S(2)}, u32[]{:S(2)}) collective-permute-start(f32[1,256,128]{2,1,0:T(8,128)S(1)} %shard_map.98.refs_8_.field_ref.refs_10_), channel_id=1, source_target_pairs={{0,1},{1,0},{2,3},{3,2},{4,5},{5,4},{6,7},{7,6},{8,9},{9,8},{10,11... | collective-permute-start | bytes 393224 | tf_op jit(solution)/shard_map/ppermute | solution.py:356
  35.3 2.0 %collective-permute-start.22 = (f32[1,128]{1,0:T(1,128)S(1)}, f32[1,128]{1,0:T(1,128)S(1)}, u32[]{:S(2)}, u32[]{:S(2)}) collective-permute-start(f32[1,128]{1,0:T(1,128)S(1)} %get-tuple-element.49), channel_id=1, source_target_pairs={{0,1},{1,0},{2,3},{3,2},{4,5},{5,4},{6,7},{7,6},{8,9},{9,8},{10,11... | collective-permute-start | bytes 1544 | tf_op jit(solution)/shard_map/ppermute | solution.py:405

commit v5 on v3

--- a/solution.py
+++ b/solution.py
@@ -273,8 +273,10 @@
     return answer, residual
 
 
-def finish_kernel(moments_ref, diagonal_ref, *refs):
-    *refs, solution_hbm, residual_hbm, solution_ref, residual_ref, sems = refs
+def finish_kernel(moments_ref, diagonal_ref, next_ref, *refs):
+    *refs, solution_hbm, residual_hbm, next_hbm, solution_ref, residual_ref, sems, next_sem = refs
+    copies = [pltpu.make_async_copy(next_ref, next_hbm, next_sem)]
+    copies[0].start()
     streams = [refs[4 * i : 4 * i + 4] for i in range(len(SPLITS))]
     rows = [moments_ref[device] for device in range(moments_ref.shape[0])]
     while len(rows) > 1:
@@ -298,7 +300,6 @@
     total, layers = diagonal_ref.shape
     chosen = [jnp.broadcast_to(c, (CHUNK, layers)) for c in chosen]
     center, answer, residual = chosen[0], chosen[1:4], chosen[4:8]
-    copies = []
     for (low, high), stream in zip(SPLITS, streams):
         for at in range(high - low):
             for start in range(0, total, CHUNK):
@@ -400,9 +401,9 @@
         streams[i].append(field)
     moments = lax.all_to_all(moments, NAMES, 0, 0)
     fields = [field for stream in streams for field in stream]
-    answer, residual = call(
-        finish_kernel, [triple, triple], moments, diagonal, *fields,
-        scratch=[triple, triple, pltpu.SemaphoreType.DMA((2, 3))], out_place=pltpu.HBM,
+    answer, residual, adjoint_next = call(
+        finish_kernel, [triple, triple, flat], moments, diagonal, adjoint_next, *fields,
+        scratch=[triple, triple, pltpu.SemaphoreType.DMA((2, 3)), pltpu.SemaphoreType.DMA], out_place=pltpu.HBM,
     )
     whole = (3, 1, 1, rows, layers)
     return answer.reshape(whole), residual.reshape(whole), adjoint_next.reshape(adjoint_temp.shape)

time: 50.5 us -> 51.9 us (1.028)
  blocking collectives: 13.9 us -> 15.3 us
  starting transfers between devices: 26.6 us -> 27.3 us
  Pallas kernels: 9.04 us -> 8.39 us
    all_to_all x1, blocking collectives: 13.9 us -> 15.3 us  [body(): moments = lax.all_to_all(moments, NAMES, 0, 0)]
    ppermute x11, starting transfers between devices: 8.28 us -> 9.38 us  [exchange(): near = lax.ppermute(value, NAMES, beside)]
    pallas_call x14, Pallas kernels: 9.04 us -> 8.39 us  [call(): pl.pallas_call(kernel, out_shape=outs, in_specs=[pl.BlockSpec(memory_spac...]
  transfers between devices with their start and end apart: 22 -> 22, of which waited for: 0 -> 0; matrix products, arithmetic and copies ran while one was open for 0% -> 0% of each run, Pallas kernels for 15% -> 13%
where the time goes in v5:
time: 51.9 us; the launch traced here: 51.8 us
  starting transfers between devices  27.3 us (53%)
  blocking collectives  15.3 us (29%)
  Pallas kernels  8.39 us (16%)
  between operations  0.73 us (1%)
    ppermute x11, starting transfers between devices, exchange(): far = lax.ppermute(value, NAMES, across)  17.9 us
    all_to_all x1, blocking collectives, body(): moments = lax.all_to_all(moments, NAMES, 0, 0)  15.3 us
    ppermute x11, starting transfers between devices, exchange(): near = lax.ppermute(value, NAMES, beside)  9.38 us
    pallas_call x14, Pallas kernels, call(): pl.pallas_call(kernel, out_shape=outs, in_specs=[pl.BlockSpec(memory_spac...  8.39 us
  transfers between devices with their start and end apart: 22, of which 0 were waited for; matrix products, arithmetic and copies ran while one was open for 0% of the time, Pallas kernels for 13%

profile of v5, /device:TPU:0, one launch (start us, length us, event | category | flops | bytes accessed | tf_op | source)
XLA Modules:
  0.0 51.8 jit_solution(12976920034670147583)
XLA Ops:
  0.6 3.0 %collective-permute-start.2 = (f32[1,256,128]{2,1,0:T(8,128)}, f32[1,256,128]{2,1,0:T(8,128)S(1)}, u32[]{:S(2)}, u32[]{:S(2)}) collective-permute-start(f32[1,256,128]{2,1,0:T(8,128)} %bitcast.20), channel_id=1, source_target_pairs={{0,16},{1,2},{2,1},{3,4},{4,3},{5,6},{6,5},{7,8},{8,7},{9,10},{10,... | collective-permute-start | bytes 393224 | tf_op jit(solution)/shard_map/ppermute | solution.py:352
  3.6 0.1 collective-permute-start.3
  3.8 1.7 %shard_map.94 = (f32[256,128]{1,0:T(8,128)S(1)}, f32[4,256,128]{2,1,0:T(8,128)S(1)}, f32[256,128]{1,0:T(8,128)S(1)}, f32[3,256,128]{2,1,0:T(8,128)S(1)}, f32[256...) custom-call(f32[256,128]{1,0:T(8,128)} %bitcast.18, ...), custom_call_target="tpu_custom_call" | custom-call | tf_op jit(solution)/shard_map/pallas_call | solution.py:324
  5.4 1.6 %collective-permute-start = (f32[1,256,128]{2,1,0:T(8,128)S(1)}, f32[1,256,128]{2,1,0:T(8,128)S(1)}, u32[]{:S(2)}, u32[]{:S(2)}) collective-permute-start(f32[1,256,128]{2,1,0:T(8,128)S(1)} %bitcast.14), channel_id=1, source_target_pairs={{0,16},{1,2},{2,1},{3,4},{4,3},{5,6},{6,5},{7,8},{8,7},{9,10},{10,... | collective-permute-start | bytes 393224 | tf_op jit(solution)/shard_map/ppermute | solution.py:352
  7.0 0.1 collective-permute-start.1
  7.1 0.0 collective-permute-done.2.far_ref
  7.1 0.0 collective-permute-done.3.near_ref
  7.1 0.3 shard_map.95
  7.4 1.7 %collective-permute-start.16 = (f32[1,256,128]{2,1,0:T(8,128)S(1)}, f32[1,256,128]{2,1,0:T(8,128)S(1)}, u32[]{:S(2)}, u32[]{:S(2)}) collective-permute-start(f32[1,256,128]{2,1,0:T(8,128)S(1)} %get-tuple-element.42.field_ref.refs_0_), channel_id=1, source_target_pairs={{0,16},{1,2},{2,1},{3,4},{4,3},{5,6},{6,5},{7,8},{8,7},{9,10},{10,... | collective-permute-start | bytes 393224 | tf_op jit(solution)/shard_map/ppermute | solution.py:352
  9.2 1.0 %collective-permute-start.17 = (f32[1,256,128]{2,1,0:T(8,128)S(1)}, f32[1,256,128]{2,1,0:T(8,128)S(1)}, u32[]{:S(2)}, u32[]{:S(2)}) collective-permute-start(f32[1,256,128]{2,1,0:T(8,128)S(1)} %get-tuple-element.42.field_ref.refs_0_), channel_id=1, source_target_pairs={{0,1},{1,0},{2,3},{3,2},{4,5},{5,4},{6,7},{7,6},{8,9},{9,8},{10,11... | collective-permute-start | bytes 393224 | tf_op jit(solution)/shard_map/ppermute | solution.py:353
  10.1 1.5 %collective-permute-start.10 = (f32[1,256,128]{2,1,0:T(8,128)S(1)}, f32[1,256,128]{2,1,0:T(8,128)S(1)}, u32[]{:S(2)}, u32[]{:S(2)}) collective-permute-start(f32[1,256,128]{2,1,0:T(8,128)S(1)} %get-tuple-element.41.field_ref.refs_3_.refs_4_), channel_id=1, source_target_pairs={{0,16},{1,2},{2,1},{3,4},{4,3},{5,6},{6,5},{7,8},{8,7},{9,10},{10,... | collective-permute-start | bytes 393224 | tf_op jit(solution)/shard_map/ppermute | solution.py:352
  11.6 0.0 collective-permute-done.far_ref
  11.6 0.0 collective-permute-start.11
  11.6 0.0 collective-permute-done.1.near_ref
  11.6 0.2 shard_map.96
  11.9 1.3 %collective-permute-start.4 = (f32[1,256,128]{2,1,0:T(8,128)S(1)}, f32[1,256,128]{2,1,0:T(8,128)S(1)}, u32[]{:S(2)}, u32[]{:S(2)}) collective-permute-start(f32[1,256,128]{2,1,0:T(8,128)S(1)} %get-tuple-element.39.field_ref.refs_6_.refs_8_), channel_id=1, source_target_pairs={{0,16},{1,2},{2,1},{3,4},{4,3},{5,6},{6,5},{7,8},{8,7},{9,10},{10,... | collective-permute-start | bytes 393224 | tf_op jit(solution)/shard_map/ppermute | solution.py:352
  13.2 0.0 collective-permute-done.16.far_ref
  13.2 1.7 %collective-permute-start.5 = (f32[1,256,128]{2,1,0:T(8,128)S(1)}, f32[1,256,128]{2,1,0:T(8,128)S(1)}, u32[]{:S(2)}, u32[]{:S(2)}) collective-permute-start(f32[1,256,128]{2,1,0:T(8,128)S(1)} %get-tuple-element.39.field_ref.refs_6_.refs_8_), channel_id=1, source_target_pairs={{0,1},{1,0},{2,3},{3,2},{4,5},{5,4},{6,7},{7,6},{8,9},{9,8},{10,11... | collective-permute-start | bytes 393224 | tf_op jit(solution)/shard_map/ppermute | solution.py:353
  14.9 0.3 shard_map.101.field_ref.refs_1_
  15.1 1.6 %collective-permute-start.18 = (f32[1,256,128]{2,1,0:T(8,128)S(1)}, f32[1,256,128]{2,1,0:T(8,128)S(1)}, u32[]{:S(2)}, u32[]{:S(2)}) collective-permute-start(f32[1,256,128]{2,1,0:T(8,128)S(1)} %shard_map.101.field_ref.refs_1_), channel_id=1, source_target_pairs={{0,16},{1,2},{2,1},{3,4},{4,3},{5,6},{6,5},{7,8},{8,7},{9,10},{10,... | collective-permute-start | bytes 393224 | tf_op jit(solution)/shard_map/ppermute | solution.py:352
  16.7 1.0 %collective-permute-start.19 = (f32[1,256,128]{2,1,0:T(8,128)S(1)}, f32[1,256,128]{2,1,0:T(8,128)S(1)}, u32[]{:S(2)}, u32[]{:S(2)}) collective-permute-start(f32[1,256,128]{2,1,0:T(8,128)S(1)} %shard_map.101.field_ref.refs_1_), channel_id=1, source_target_pairs={{0,1},{1,0},{2,3},{3,2},{4,5},{5,4},{6,7},{7,6},{8,9},{9,8},{10,11... | collective-permute-start | bytes 393224 | tf_op jit(solution)/shard_map/ppermute | solution.py:353
  17.7 0.0 collective-permute-done.11.near_ref
  17.7 0.3 shard_map.99.field_ref.refs_4_.refs_5_
  17.9 1.6 %collective-permute-start.12 = (f32[1,256,128]{2,1,0:T(8,128)S(1)}, f32[1,256,128]{2,1,0:T(8,128)S(1)}, u32[]{:S(2)}, u32[]{:S(2)}) collective-permute-start(f32[1,256,128]{2,1,0:T(8,128)S(1)} %shard_map.99.field_ref.refs_4_.refs_5_), channel_id=1, source_target_pairs={{0,16},{1,2},{2,1},{3,4},{4,3},{5,6},{6,5},{7,8},{8,7},{9,10},{10,... | collective-permute-start | bytes 393224 | tf_op jit(solution)/shard_map/ppermute | solution.py:352
  19.5 0.0 collective-permute-done.4.far_ref
  19.5 1.5 %collective-permute-start.13 = (f32[1,256,128]{2,1,0:T(8,128)S(1)}, f32[1,256,128]{2,1,0:T(8,128)S(1)}, u32[]{:S(2)}, u32[]{:S(2)}) collective-permute-start(f32[1,256,128]{2,1,0:T(8,128)S(1)} %shard_map.99.field_ref.refs_4_.refs_5_), channel_id=1, source_target_pairs={{0,1},{1,0},{2,3},{3,2},{4,5},{5,4},{6,7},{7,6},{8,9},{9,8},{10,11... | collective-permute-start | bytes 393224 | tf_op jit(solution)/shard_map/ppermute | solution.py:353
  21.0 0.0 collective-permute-done.5.near_ref
  21.0 0.3 shard_map.97.field_ref.refs_7_.refs_9_
  21.3 1.6 %collective-permute-start.6 = (f32[1,256,128]{2,1,0:T(8,128)S(1)}, f32[1,256,128]{2,1,0:T(8,128)S(1)}, u32[]{:S(2)}, u32[]{:S(2)}) collective-permute-start(f32[1,256,128]{2,1,0:T(8,128)S(1)} %shard_map.97.field_ref.refs_7_.refs_9_), channel_id=1, source_target_pairs={{0,16},{1,2},{2,1},{3,4},{4,3},{5,6},{6,5},{7,8},{8,7},{9,10},{10,... | collective-permute-start | bytes 393224 | tf_op jit(solution)/shard_map/ppermute | solution.py:352
  22.9 0.0 collective-permute-done.18.far_ref
  22.9 0.3 shard_map.102.refs_2_.field_ref
  23.1 1.0 %collective-permute-start.20 = (f32[1,256,128]{2,1,0:T(8,128)S(1)}, f32[1,256,128]{2,1,0:T(8,128)S(1)}, u32[]{:S(2)}, u32[]{:S(2)}) collective-permute-start(f32[1,256,128]{2,1,0:T(8,128)S(1)} %shard_map.102.refs_2_.field_ref), channel_id=1, source_target_pairs={{0,16},{1,2},{2,1},{3,4},{4,3},{5,6},{6,5},{7,8},{8,7},{9,10},{10,... | collective-permute-start | bytes 393224 | tf_op jit(solution)/shard_map/ppermute | solution.py:352
  24.2 0.0 collective-permute-done.12.far_ref
  24.2 1.9 %collective-permute-start.21 = (f32[1,256,128]{2,1,0:T(8,128)S(1)}, f32[1,256,128]{2,1,0:T(8,128)S(1)}, u32[]{:S(2)}, u32[]{:S(2)}) collective-permute-start(f32[1,256,128]{2,1,0:T(8,128)S(1)} %shard_map.102.refs_2_.field_ref), channel_id=1, source_target_pairs={{0,1},{1,0},{2,3},{3,2},{4,5},{5,4},{6,7},{7,6},{8,9},{9,8},{10,11... | collective-permute-start | bytes 393224 | tf_op jit(solution)/shard_map/ppermute | solution.py:353
  26.1 0.0 collective-permute-done.13.near_ref
  26.1 0.3 shard_map.100.refs_5_.field_ref.refs_6_
  26.4 1.6 %collective-permute-start.14 = (f32[1,256,128]{2,1,0:T(8,128)S(1)}, f32[1,256,128]{2,1,0:T(8,128)S(1)}, u32[]{:S(2)}, u32[]{:S(2)}) collective-permute-start(f32[1,256,128]{2,1,0:T(8,128)S(1)} %shard_map.100.refs_5_.field_ref.refs_6_), channel_id=1, source_target_pairs={{0,16},{1,2},{2,1},{3,4},{4,3},{5,6},{6,5},{7,8},{8,7},{9,10},{10,... | collective-permute-start | bytes 393224 | tf_op jit(solution)/shard_map/ppermute | solution.py:352
  27.9 1.0 %collective-permute-start.15 = (f32[1,256,128]{2,1,0:T(8,128)S(1)}, f32[1,256,128]{2,1,0:T(8,128)S(1)}, u32[]{:S(2)}, u32[]{:S(2)}) collective-permute-start(f32[1,256,128]{2,1,0:T(8,128)S(1)} %shard_map.100.refs_5_.field_ref.refs_6_), channel_id=1, source_target_pairs={{0,1},{1,0},{2,3},{3,2},{4,5},{5,4},{6,7},{7,6},{8,9},{9,8},{10,11... | collective-permute-start | bytes 393224 | tf_op jit(solution)/shard_map/ppermute | solution.py:353
  28.9 0.0 collective-permute-done.7.near_ref
  28.9 0.3 shard_map.98.refs_8_.field_ref.refs_10_
  29.2 1.6 %collective-permute-start.8 = (f32[1,256,128]{2,1,0:T(8,128)S(1)}, f32[1,256,128]{2,1,0:T(8,128)S(1)}, u32[]{:S(2)}, u32[]{:S(2)}) collective-permute-start(f32[1,256,128]{2,1,0:T(8,128)S(1)} %shard_map.98.refs_8_.field_ref.refs_10_), channel_id=1, source_target_pairs={{0,16},{1,2},{2,1},{3,4},{4,3},{5,6},{6,5},{7,8},{8,7},{9,10},{10,... | collective-permute-start | bytes 393224 | tf_op jit(solution)/shard_map/ppermute | solution.py:352
  30.7 1.0 %collective-permute-start.9 = (f32[1,256,128]{2,1,0:T(8,128)S(1)}, f32[1,256,128]{2,1,0:T(8,128)S(1)}, u32[]{:S(2)}, u32[]{:S(2)}) collective-permute-start(f32[1,256,128]{2,1,0:T(8,128)S(1)} %shard_map.98.refs_8_.field_ref.refs_10_), channel_id=1, source_target_pairs={{0,1},{1,0},{2,3},{3,2},{4,5},{5,4},{6,7},{7,6},{8,9},{9,8},{10,11... | collective-permute-start | bytes 393224 | tf_op jit(solution)/shard_map/ppermute | solution.py:353
  31.7 2.0 %shard_map.103 = (f32[8,128]{1,0:T(8,128)S(1)}, f32[7,3,256,128]{3,2,1,0:T(8,128)S(1)}, f32[7,3,256,128]{3,2,1,0:T(8,128)S(1)}) custom-call(f32[256,128]{1,0:T(8,128)S(1)} %get-tuple-element.43.diagonal_ref, f32[1,256,128]{2,1,0:T(8,128)S(1)} %get-tuple-element.42.field_ref.refs_0_, f32[1,256,128]{2,1,0:T(8,128)S(1)} %shard_map.101.field_ref.refs_1_, ...), custom_call_target="tpu_custom_call" | custom-call | tf_op jit(solution)/shard_map/pallas_call | solution.py:324
  33.8 0.5 shard_map.104
  34.2 0.5 shard_map.105
  34.7 0.5 shard_map.106
  35.2 15.3 %all_to_all.5.moments_ref = f32[32,1,128]{2,1,0:T(1,128)S(1)} all-to-all(f32[32,1,128]{2,1,0:T(1,128)S(1)} %get-tuple-element.49), channel_id=1, replica_groups=mesh['diamond'=2,'tile'=16] {'diamond','tile'}, dimensions={0} | all-to-all | bytes 32768 | tf_op jit(solution)/shard_map/all_to_all | solution.py:402
  50.5 1.3 %shard_map.107 = (f32[3,256,128]{2,1,0:T(8,128)}, f32[3,256,128]{2,1,0:T(8,128)}, f32[256,128]{1,0:T(8,128)}) custom-call(f32[32,1,128]{2,1,0:T(1,128)S(1)} %all_to_all.5.moments_ref, f32[256,128]{1,0:T(8,128)S(1)} %get-tuple-element.43.diagonal_ref, f32[256,128]{1,0:T(8,128)S(1)} %get-tuple-element.50.next_ref, ...), custom_call_target="tpu_custom_call" | custom-call | tf_op jit(solution)/shard_map/pallas_call | solution.py:324
  (11 shorter events, 0.0 us)
Async XLA Ops:
  0.6 6.5 %collective-permute-start.2 = (f32[1,256,128]{2,1,0:T(8,128)}, f32[1,256,128]{2,1,0:T(8,128)S(1)}, u32[]{:S(2)}, u32[]{:S(2)}) collective-permute-start(f32[1,256,128]{2,1,0:T(8,128)} %bitcast.20), channel_id=1, source_target_pairs={{0,16},{1,2},{2,1},{3,4},{4,3},{5,6},{6,5},{7,8},{8,7},{9,10},{10,... | collective-permute-start | bytes 393224 | tf_op jit(solution)/shard_map/ppermute | solution.py:352
  3.6 3.5 %collective-permute-start.3 = (f32[1,256,128]{2,1,0:T(8,128)}, f32[1,256,128]{2,1,0:T(8,128)S(1)}, u32[]{:S(2)}, u32[]{:S(2)}) collective-permute-start(f32[1,256,128]{2,1,0:T(8,128)} %bitcast.21), channel_id=1, source_target_pairs={{0,1},{1,0},{2,3},{3,2},{4,5},{5,4},{6,7},{7,6},{8,9},{9,8},{10,11... | collective-permute-start | bytes 393224 | tf_op jit(solution)/shard_map/ppermute | solution.py:353
  5.4 6.2 %collective-permute-start = (f32[1,256,128]{2,1,0:T(8,128)S(1)}, f32[1,256,128]{2,1,0:T(8,128)S(1)}, u32[]{:S(2)}, u32[]{:S(2)}) collective-permute-start(f32[1,256,128]{2,1,0:T(8,128)S(1)} %bitcast.14), channel_id=1, source_target_pairs={{0,16},{1,2},{2,1},{3,4},{4,3},{5,6},{6,5},{7,8},{8,7},{9,10},{10,... | collective-permute-start | bytes 393224 | tf_op jit(solution)/shard_map/ppermute | solution.py:352
  7.0 4.6 %collective-permute-start.1 = (f32[1,256,128]{2,1,0:T(8,128)S(1)}, f32[1,256,128]{2,1,0:T(8,128)S(1)}, u32[]{:S(2)}, u32[]{:S(2)}) collective-permute-start(f32[1,256,128]{2,1,0:T(8,128)S(1)} %bitcast.15), channel_id=1, source_target_pairs={{0,1},{1,0},{2,3},{3,2},{4,5},{5,4},{6,7},{7,6},{8,9},{9,8},{10,11... | collective-permute-start | bytes 393224 | tf_op jit(solution)/shard_map/ppermute | solution.py:353
  7.4 5.8 %collective-permute-start.16 = (f32[1,256,128]{2,1,0:T(8,128)S(1)}, f32[1,256,128]{2,1,0:T(8,128)S(1)}, u32[]{:S(2)}, u32[]{:S(2)}) collective-permute-start(f32[1,256,128]{2,1,0:T(8,128)S(1)} %get-tuple-element.42.field_ref.refs_0_), channel_id=1, source_target_pairs={{0,16},{1,2},{2,1},{3,4},{4,3},{5,6},{6,5},{7,8},{8,7},{9,10},{10,... | collective-permute-start | bytes 393224 | tf_op jit(solution)/shard_map/ppermute | solution.py:352
  9.2 5.7 %collective-permute-start.17 = (f32[1,256,128]{2,1,0:T(8,128)S(1)}, f32[1,256,128]{2,1,0:T(8,128)S(1)}, u32[]{:S(2)}, u32[]{:S(2)}) collective-permute-start(f32[1,256,128]{2,1,0:T(8,128)S(1)} %get-tuple-element.42.field_ref.refs_0_), channel_id=1, source_target_pairs={{0,1},{1,0},{2,3},{3,2},{4,5},{5,4},{6,7},{7,6},{8,9},{9,8},{10,11... | collective-permute-start | bytes 393224 | tf_op jit(solution)/shard_map/ppermute | solution.py:353
  10.1 6.5 %collective-permute-start.10 = (f32[1,256,128]{2,1,0:T(8,128)S(1)}, f32[1,256,128]{2,1,0:T(8,128)S(1)}, u32[]{:S(2)}, u32[]{:S(2)}) collective-permute-start(f32[1,256,128]{2,1,0:T(8,128)S(1)} %get-tuple-element.41.field_ref.refs_3_.refs_4_), channel_id=1, source_target_pairs={{0,16},{1,2},{2,1},{3,4},{4,3},{5,6},{6,5},{7,8},{8,7},{9,10},{10,... | collective-permute-start | bytes 393224 | tf_op jit(solution)/shard_map/ppermute | solution.py:352
  11.6 6.0 %collective-permute-start.11 = (f32[1,256,128]{2,1,0:T(8,128)S(1)}, f32[1,256,128]{2,1,0:T(8,128)S(1)}, u32[]{:S(2)}, u32[]{:S(2)}) collective-permute-start(f32[1,256,128]{2,1,0:T(8,128)S(1)} %get-tuple-element.41.field_ref.refs_3_.refs_4_), channel_id=1, source_target_pairs={{0,1},{1,0},{2,3},{3,2},{4,5},{5,4},{6,7},{7,6},{8,9},{9,8},{10,11... | collective-permute-start | bytes 393224 | tf_op jit(solution)/shard_map/ppermute | solution.py:353
  11.9 7.6 %collective-permute-start.4 = (f32[1,256,128]{2,1,0:T(8,128)S(1)}, f32[1,256,128]{2,1,0:T(8,128)S(1)}, u32[]{:S(2)}, u32[]{:S(2)}) collective-permute-start(f32[1,256,128]{2,1,0:T(8,128)S(1)} %get-tuple-element.39.field_ref.refs_6_.refs_8_), channel_id=1, source_target_pairs={{0,16},{1,2},{2,1},{3,4},{4,3},{5,6},{6,5},{7,8},{8,7},{9,10},{10,... | collective-permute-start | bytes 393224 | tf_op jit(solution)/shard_map/ppermute | solution.py:352
  13.2 7.9 %collective-permute-start.5 = (f32[1,256,128]{2,1,0:T(8,128)S(1)}, f32[1,256,128]{2,1,0:T(8,128)S(1)}, u32[]{:S(2)}, u32[]{:S(2)}) collective-permute-start(f32[1,256,128]{2,1,0:T(8,128)S(1)} %get-tuple-element.39.field_ref.refs_6_.refs_8_), channel_id=1, source_target_pairs={{0,1},{1,0},{2,3},{3,2},{4,5},{5,4},{6,7},{7,6},{8,9},{9,8},{10,11... | collective-permute-start | bytes 393224 | tf_op jit(solution)/shard_map/ppermute | solution.py:353
  15.1 7.7 %collective-permute-start.18 = (f32[1,256,128]{2,1,0:T(8,128)S(1)}, f32[1,256,128]{2,1,0:T(8,128)S(1)}, u32[]{:S(2)}, u32[]{:S(2)}) collective-permute-start(f32[1,256,128]{2,1,0:T(8,128)S(1)} %shard_map.101.field_ref.refs_1_), channel_id=1, source_target_pairs={{0,16},{1,2},{2,1},{3,4},{4,3},{5,6},{6,5},{7,8},{8,7},{9,10},{10,... | collective-permute-start | bytes 393224 | tf_op jit(solution)/shard_map/ppermute | solution.py:352
  16.7 6.2 %collective-permute-start.19 = (f32[1,256,128]{2,1,0:T(8,128)S(1)}, f32[1,256,128]{2,1,0:T(8,128)S(1)}, u32[]{:S(2)}, u32[]{:S(2)}) collective-permute-start(f32[1,256,128]{2,1,0:T(8,128)S(1)} %shard_map.101.field_ref.refs_1_), channel_id=1, source_target_pairs={{0,1},{1,0},{2,3},{3,2},{4,5},{5,4},{6,7},{7,6},{8,9},{9,8},{10,11... | collective-permute-start | bytes 393224 | tf_op jit(solution)/shard_map/ppermute | solution.py:353
  17.9 6.2 %collective-permute-start.12 = (f32[1,256,128]{2,1,0:T(8,128)S(1)}, f32[1,256,128]{2,1,0:T(8,128)S(1)}, u32[]{:S(2)}, u32[]{:S(2)}) collective-permute-start(f32[1,256,128]{2,1,0:T(8,128)S(1)} %shard_map.99.field_ref.refs_4_.refs_5_), channel_id=1, source_target_pairs={{0,16},{1,2},{2,1},{3,4},{4,3},{5,6},{6,5},{7,8},{8,7},{9,10},{10,... | collective-permute-start | bytes 393224 | tf_op jit(solution)/shard_map/ppermute | solution.py:352
  19.5 6.6 %collective-permute-start.13 = (f32[1,256,128]{2,1,0:T(8,128)S(1)}, f32[1,256,128]{2,1,0:T(8,128)S(1)}, u32[]{:S(2)}, u32[]{:S(2)}) collective-permute-start(f32[1,256,128]{2,1,0:T(8,128)S(1)} %shard_map.99.field_ref.refs_4_.refs_5_), channel_id=1, source_target_pairs={{0,1},{1,0},{2,3},{3,2},{4,5},{5,4},{6,7},{7,6},{8,9},{9,8},{10,11... | collective-permute-start | bytes 393224 | tf_op jit(solution)/shard_map/ppermute | solution.py:353
  21.3 6.6 %collective-permute-start.6 = (f32[1,256,128]{2,1,0:T(8,128)S(1)}, f32[1,256,128]{2,1,0:T(8,128)S(1)}, u32[]{:S(2)}, u32[]{:S(2)}) collective-permute-start(f32[1,256,128]{2,1,0:T(8,128)S(1)} %shard_map.97.field_ref.refs_7_.refs_9_), channel_id=1, source_target_pairs={{0,16},{1,2},{2,1},{3,4},{4,3},{5,6},{6,5},{7,8},{8,7},{9,10},{10,... | collective-permute-start | bytes 393224 | tf_op jit(solution)/shard_map/ppermute | solution.py:352
  22.9 6.1 %collective-permute-start.7 = (f32[1,256,128]{2,1,0:T(8,128)S(1)}, f32[1,256,128]{2,1,0:T(8,128)S(1)}, u32[]{:S(2)}, u32[]{:S(2)}) collective-permute-start(f32[1,256,128]{2,1,0:T(8,128)S(1)} %shard_map.97.field_ref.refs_7_.refs_9_), channel_id=1, source_target_pairs={{0,1},{1,0},{2,3},{3,2},{4,5},{5,4},{6,7},{7,6},{8,9},{9,8},{10,11... | collective-permute-start | bytes 393224 | tf_op jit(solution)/shard_map/ppermute | solution.py:353
  23.1 7.6 %collective-permute-start.20 = (f32[1,256,128]{2,1,0:T(8,128)S(1)}, f32[1,256,128]{2,1,0:T(8,128)S(1)}, u32[]{:S(2)}, u32[]{:S(2)}) collective-permute-start(f32[1,256,128]{2,1,0:T(8,128)S(1)} %shard_map.102.refs_2_.field_ref), channel_id=1, source_target_pairs={{0,16},{1,2},{2,1},{3,4},{4,3},{5,6},{6,5},{7,8},{8,7},{9,10},{10,... | collective-permute-start | bytes 393224 | tf_op jit(solution)/shard_map/ppermute | solution.py:352
  24.2 9.6 %collective-permute-start.21 = (f32[1,256,128]{2,1,0:T(8,128)S(1)}, f32[1,256,128]{2,1,0:T(8,128)S(1)}, u32[]{:S(2)}, u32[]{:S(2)}) collective-permute-start(f32[1,256,128]{2,1,0:T(8,128)S(1)} %shard_map.102.refs_2_.field_ref), channel_id=1, source_target_pairs={{0,1},{1,0},{2,3},{3,2},{4,5},{5,4},{6,7},{7,6},{8,9},{9,8},{10,11... | collective-permute-start | bytes 393224 | tf_op jit(solution)/shard_map/ppermute | solution.py:353
  26.4 7.9 %collective-permute-start.14 = (f32[1,256,128]{2,1,0:T(8,128)S(1)}, f32[1,256,128]{2,1,0:T(8,128)S(1)}, u32[]{:S(2)}, u32[]{:S(2)}) collective-permute-start(f32[1,256,128]{2,1,0:T(8,128)S(1)} %shard_map.100.refs_5_.field_ref.refs_6_), channel_id=1, source_target_pairs={{0,16},{1,2},{2,1},{3,4},{4,3},{5,6},{6,5},{7,8},{8,7},{9,10},{10,... | collective-permute-start | bytes 393224 | tf_op jit(solution)/shard_map/ppermute | solution.py:352
  27.9 6.3 %collective-permute-start.15 = (f32[1,256,128]{2,1,0:T(8,128)S(1)}, f32[1,256,128]{2,1,0:T(8,128)S(1)}, u32[]{:S(2)}, u32[]{:S(2)}) collective-permute-start(f32[1,256,128]{2,1,0:T(8,128)S(1)} %shard_map.100.refs_5_.field_ref.refs_6_), channel_id=1, source_target_pairs={{0,1},{1,0},{2,3},{3,2},{4,5},{5,4},{6,7},{7,6},{8,9},{9,8},{10,11... | collective-permute-start | bytes 393224 | tf_op jit(solution)/shard_map/ppermute | solution.py:353
  29.2 5.5 %collective-permute-start.8 = (f32[1,256,128]{2,1,0:T(8,128)S(1)}, f32[1,256,128]{2,1,0:T(8,128)S(1)}, u32[]{:S(2)}, u32[]{:S(2)}) collective-permute-start(f32[1,256,128]{2,1,0:T(8,128)S(1)} %shard_map.98.refs_8_.field_ref.refs_10_), channel_id=1, source_target_pairs={{0,16},{1,2},{2,1},{3,4},{4,3},{5,6},{6,5},{7,8},{8,7},{9,10},{10,... | collective-permute-start | bytes 393224 | tf_op jit(solution)/shard_map/ppermute | solution.py:352
  30.7 4.0 %collective-permute-start.9 = (f32[1,256,128]{2,1,0:T(8,128)S(1)}, f32[1,256,128]{2,1,0:T(8,128)S(1)}, u32[]{:S(2)}, u32[]{:S(2)}) collective-permute-start(f32[1,256,128]{2,1,0:T(8,128)S(1)} %shard_map.98.refs_8_.field_ref.refs_10_), channel_id=1, source_target_pairs={{0,1},{1,0},{2,3},{3,2},{4,5},{5,4},{6,7},{7,6},{8,9},{9,8},{10,11... | collective-permute-start | bytes 393224 | tf_op jit(solution)/shard_map/ppermute | solution.py:353

commit v6 on v5

--- a/solution.py
+++ b/solution.py
@@ -144,7 +144,7 @@
     return sum(w * v for w, v in zip(weights, around))
 
 
-def apply_kernel(far_ref, near_ref, field_ref, weights_ref, matrix_ref, out_ref, moved_ref):
+def apply_kernel(far_ref, near_ref, field_ref, weights_ref, matrix_ref, after_ref, out_ref, moved_ref):
     unfold(matrix_ref, far_ref, moved_ref)
     for start in range(0, field_ref.shape[1], CHUNK):
         here = slice(start, start + CHUNK)
@@ -384,7 +384,8 @@
     for step in range(ITERS - 1):
         for i, shape in enumerate(shapes):
             near, far = swapped[i]
-            (field,) = call(apply_kernel, [shape], far, near, streams[i][-1], weights, matrix, scratch=[shape])
+            after = swapped[0][0] if step + 2 == ITERS and i + 1 == len(shapes) else near
+            (field,) = call(apply_kernel, [shape], far, near, streams[i][-1], weights, matrix, after, scratch=[shape])
             swapped[i] = exchange(field)
             streams[i].append(field)
     many = (len(CENTERS), *triple)

time: 51.9 us -> 52 us (level)
  starting transfers between devices: 27.3 us -> 26.3 us
  waiting for transfers between devices: 0.06 us -> 0.63 us
    ppermute x11, waiting for transfers between devices: 0.03 us -> 0.6 us  [exchange(): far = lax.ppermute(value, NAMES, across)]
    all_to_all x1, blocking collectives: 15.3 us -> 15.8 us  [body(): moments = lax.all_to_all(moments, NAMES, 0, 0)]
  transfers between devices with their start and end apart: 22 -> 22, of which waited for: 0 -> 2; matrix products, arithmetic and copies ran while one was open for 0% -> 0% of each run, Pallas kernels for 13% -> 13%
where the time goes in v6:
time: 52 us; the launch traced here: 51.9 us
  starting transfers between devices  26.3 us (51%)
  blocking collectives  15.8 us (30%)
  Pallas kernels  8.4 us (16%)
  between operations  0.73 us (1%)
  waiting for transfers between devices  0.63 us (1%)
    ppermute x11, starting transfers between devices, exchange(): far = lax.ppermute(value, NAMES, across)  17.4 us
    all_to_all x1, blocking collectives, body(): moments = lax.all_to_all(moments, NAMES, 0, 0)  15.8 us
    ppermute x11, starting transfers between devices, exchange(): near = lax.ppermute(value, NAMES, beside)  8.88 us
    pallas_call x14, Pallas kernels, call(): pl.pallas_call(kernel, out_shape=outs, in_specs=[pl.BlockSpec(memory_spac...  8.4 us
  transfers between devices with their start and end apart: 22, of which 2 were waited for; matrix products, arithmetic and copies ran while one was open for 0% of the time, Pallas kernels for 13%

profile of v6, /device:TPU:0, one launch (start us, length us, event | category | flops | bytes accessed | tf_op | source)
XLA Modules:
  0.0 51.9 jit_solution(13395757377669557108)
XLA Ops:
  0.6 3.0 %collective-permute-start.2 = (f32[1,256,128]{2,1,0:T(8,128)}, f32[1,256,128]{2,1,0:T(8,128)S(1)}, u32[]{:S(2)}, u32[]{:S(2)}) collective-permute-start(f32[1,256,128]{2,1,0:T(8,128)} %bitcast.20), channel_id=1, source_target_pairs={{0,16},{1,2},{2,1},{3,4},{4,3},{5,6},{6,5},{7,8},{8,7},{9,10},{10,... | collective-permute-start | bytes 393224 | tf_op jit(solution)/shard_map/ppermute | solution.py:352
  3.6 0.1 collective-permute-start.3
  3.8 1.7 %shard_map.94 = (f32[256,128]{1,0:T(8,128)S(1)}, f32[4,256,128]{2,1,0:T(8,128)S(1)}, f32[256,128]{1,0:T(8,128)S(1)}, f32[3,256,128]{2,1,0:T(8,128)S(1)}, f32[256...) custom-call(f32[256,128]{1,0:T(8,128)} %bitcast.18, ...), custom_call_target="tpu_custom_call" | custom-call | tf_op jit(solution)/shard_map/pallas_call | solution.py:324
  5.4 1.6 %collective-permute-start = (f32[1,256,128]{2,1,0:T(8,128)S(1)}, f32[1,256,128]{2,1,0:T(8,128)S(1)}, u32[]{:S(2)}, u32[]{:S(2)}) collective-permute-start(f32[1,256,128]{2,1,0:T(8,128)S(1)} %bitcast.14), channel_id=1, source_target_pairs={{0,16},{1,2},{2,1},{3,4},{4,3},{5,6},{6,5},{7,8},{8,7},{9,10},{10,... | collective-permute-start | bytes 393224 | tf_op jit(solution)/shard_map/ppermute | solution.py:352
  7.0 0.1 collective-permute-start.1
  7.1 0.0 collective-permute-done.2.far_ref
  7.1 0.0 collective-permute-done.3.near_ref
  7.1 0.3 shard_map.95
  7.4 1.7 %collective-permute-start.8 = (f32[1,256,128]{2,1,0:T(8,128)S(1)}, f32[1,256,128]{2,1,0:T(8,128)S(1)}, u32[]{:S(2)}, u32[]{:S(2)}) collective-permute-start(f32[1,256,128]{2,1,0:T(8,128)S(1)} %get-tuple-element.41.field_ref.refs_0_), channel_id=1, source_target_pairs={{0,16},{1,2},{2,1},{3,4},{4,3},{5,6},{6,5},{7,8},{8,7},{9,10},{10,... | collective-permute-start | bytes 393224 | tf_op jit(solution)/shard_map/ppermute | solution.py:352
  9.2 1.0 %collective-permute-start.9 = (f32[1,256,128]{2,1,0:T(8,128)S(1)}, f32[1,256,128]{2,1,0:T(8,128)S(1)}, u32[]{:S(2)}, u32[]{:S(2)}) collective-permute-start(f32[1,256,128]{2,1,0:T(8,128)S(1)} %get-tuple-element.41.field_ref.refs_0_), channel_id=1, source_target_pairs={{0,1},{1,0},{2,3},{3,2},{4,5},{5,4},{6,7},{7,6},{8,9},{9,8},{10,11... | collective-permute-start | bytes 393224 | tf_op jit(solution)/shard_map/ppermute | solution.py:353
  10.1 1.5 %collective-permute-start.15 = (f32[1,256,128]{2,1,0:T(8,128)S(1)}, f32[1,256,128]{2,1,0:T(8,128)S(1)}, u32[]{:S(2)}, u32[]{:S(2)}) collective-permute-start(f32[1,256,128]{2,1,0:T(8,128)S(1)} %get-tuple-element.42.field_ref.refs_3_.refs_4_), channel_id=1, source_target_pairs={{0,16},{1,2},{2,1},{3,4},{4,3},{5,6},{6,5},{7,8},{8,7},{9,10},{10,... | collective-permute-start | bytes 393224 | tf_op jit(solution)/shard_map/ppermute | solution.py:352
  11.6 0.0 collective-permute-done.far_ref
  11.6 0.0 collective-permute-start.16
  11.6 0.0 collective-permute-done.1.near_ref
  11.6 0.2 shard_map.96
  11.9 1.3 %collective-permute-start.4 = (f32[1,256,128]{2,1,0:T(8,128)S(1)}, f32[1,256,128]{2,1,0:T(8,128)S(1)}, u32[]{:S(2)}, u32[]{:S(2)}) collective-permute-start(f32[1,256,128]{2,1,0:T(8,128)S(1)} %get-tuple-element.39.field_ref.refs_6_.refs_8_), channel_id=1, source_target_pairs={{0,16},{1,2},{2,1},{3,4},{4,3},{5,6},{6,5},{7,8},{8,7},{9,10},{10,... | collective-permute-start | bytes 393224 | tf_op jit(solution)/shard_map/ppermute | solution.py:352
  13.2 0.0 collective-permute-done.8.far_ref
  13.2 1.7 %collective-permute-start.5 = (f32[1,256,128]{2,1,0:T(8,128)S(1)}, f32[1,256,128]{2,1,0:T(8,128)S(1)}, u32[]{:S(2)}, u32[]{:S(2)}) collective-permute-start(f32[1,256,128]{2,1,0:T(8,128)S(1)} %get-tuple-element.39.field_ref.refs_6_.refs_8_), channel_id=1, source_target_pairs={{0,1},{1,0},{2,3},{3,2},{4,5},{5,4},{6,7},{7,6},{8,9},{9,8},{10,11... | collective-permute-start | bytes 393224 | tf_op jit(solution)/shard_map/ppermute | solution.py:353
  14.9 0.3 shard_map.98.field_ref.refs_1_
  15.1 1.6 %collective-permute-start.10 = (f32[1,256,128]{2,1,0:T(8,128)S(1)}, f32[1,256,128]{2,1,0:T(8,128)S(1)}, u32[]{:S(2)}, u32[]{:S(2)}) collective-permute-start(f32[1,256,128]{2,1,0:T(8,128)S(1)} %shard_map.98.field_ref.refs_1_), channel_id=1, source_target_pairs={{0,16},{1,2},{2,1},{3,4},{4,3},{5,6},{6,5},{7,8},{8,7},{9,10},{10,... | collective-permute-start | bytes 393224 | tf_op jit(solution)/shard_map/ppermute | solution.py:352
  16.7 1.0 %collective-permute-start.11 = (f32[1,256,128]{2,1,0:T(8,128)S(1)}, f32[1,256,128]{2,1,0:T(8,128)S(1)}, u32[]{:S(2)}, u32[]{:S(2)}) collective-permute-start(f32[1,256,128]{2,1,0:T(8,128)S(1)} %shard_map.98.field_ref.refs_1_), channel_id=1, source_target_pairs={{0,1},{1,0},{2,3},{3,2},{4,5},{5,4},{6,7},{7,6},{8,9},{9,8},{10,11... | collective-permute-start | bytes 393224 | tf_op jit(solution)/shard_map/ppermute | solution.py:353
  17.7 0.0 collective-permute-done.16.near_ref.after_ref
  17.7 0.3 shard_map.101.field_ref.refs_4_.refs_5_
  17.9 1.6 %collective-permute-start.17 = (f32[1,256,128]{2,1,0:T(8,128)S(1)}, f32[1,256,128]{2,1,0:T(8,128)S(1)}, u32[]{:S(2)}, u32[]{:S(2)}) collective-permute-start(f32[1,256,128]{2,1,0:T(8,128)S(1)} %shard_map.101.field_ref.refs_4_.refs_5_), channel_id=1, source_target_pairs={{0,16},{1,2},{2,1},{3,4},{4,3},{5,6},{6,5},{7,8},{8,7},{9,10},{10,... | collective-permute-start | bytes 393224 | tf_op jit(solution)/shard_map/ppermute | solution.py:352
  19.5 0.0 collective-permute-done.4.far_ref
  19.5 1.5 %collective-permute-start.18 = (f32[1,256,128]{2,1,0:T(8,128)S(1)}, f32[1,256,128]{2,1,0:T(8,128)S(1)}, u32[]{:S(2)}, u32[]{:S(2)}) collective-permute-start(f32[1,256,128]{2,1,0:T(8,128)S(1)} %shard_map.101.field_ref.refs_4_.refs_5_), channel_id=1, source_target_pairs={{0,1},{1,0},{2,3},{3,2},{4,5},{5,4},{6,7},{7,6},{8,9},{9,8},{10,11... | collective-permute-start | bytes 393224 | tf_op jit(solution)/shard_map/ppermute | solution.py:353
  21.0 0.0 collective-permute-done.5.near_ref.after_ref
  21.0 0.3 shard_map.97.field_ref.refs_7_.refs_9_
  21.3 1.6 %collective-permute-start.6 = (f32[1,256,128]{2,1,0:T(8,128)S(1)}, f32[1,256,128]{2,1,0:T(8,128)S(1)}, u32[]{:S(2)}, u32[]{:S(2)}) collective-permute-start(f32[1,256,128]{2,1,0:T(8,128)S(1)} %shard_map.97.field_ref.refs_7_.refs_9_), channel_id=1, source_target_pairs={{0,16},{1,2},{2,1},{3,4},{4,3},{5,6},{6,5},{7,8},{8,7},{9,10},{10,... | collective-permute-start | bytes 393224 | tf_op jit(solution)/shard_map/ppermute | solution.py:352
  22.9 0.0 collective-permute-done.10.far_ref
  22.9 0.3 shard_map.99.refs_2_.field_ref
  23.1 0.6 %collective-permute-start.12 = (f32[1,256,128]{2,1,0:T(8,128)S(1)}, f32[1,256,128]{2,1,0:T(8,128)S(1)}, u32[]{:S(2)}, u32[]{:S(2)}) collective-permute-start(f32[1,256,128]{2,1,0:T(8,128)S(1)} %shard_map.99.refs_2_.field_ref), channel_id=1, source_target_pairs={{0,1},{1,0},{2,3},{3,2},{4,5},{5,4},{6,7},{7,6},{8,9},{9,8},{10,11... | collective-permute-start | bytes 393224 | tf_op jit(solution)/shard_map/ppermute | solution.py:353
  23.7 0.8 %collective-permute-start.21 = (f32[1,256,128]{2,1,0:T(8,128)S(1)}, f32[1,256,128]{2,1,0:T(8,128)S(1)}, u32[]{:S(2)}, u32[]{:S(2)}) collective-permute-start(f32[1,256,128]{2,1,0:T(8,128)S(1)} %shard_map.99.refs_2_.field_ref), channel_id=1, source_target_pairs={{0,16},{1,2},{2,1},{3,4},{4,3},{5,6},{6,5},{7,8},{8,7},{9,10},{10,... | collective-permute-start | bytes 393224 | tf_op jit(solution)/shard_map/ppermute | solution.py:352
  24.5 0.0 collective-permute-done.18.near_ref.after_ref
  24.5 0.3 shard_map.102.refs_5_.field_ref.refs_6_
  24.7 1.3 %collective-permute-start.19 = (f32[1,256,128]{2,1,0:T(8,128)S(1)}, f32[1,256,128]{2,1,0:T(8,128)S(1)}, u32[]{:S(2)}, u32[]{:S(2)}) collective-permute-start(f32[1,256,128]{2,1,0:T(8,128)S(1)} %shard_map.102.refs_5_.field_ref.refs_6_), channel_id=1, source_target_pairs={{0,16},{1,2},{2,1},{3,4},{4,3},{5,6},{6,5},{7,8},{8,7},{9,10},{10,... | collective-permute-start | bytes 393224 | tf_op jit(solution)/shard_map/ppermute | solution.py:352
  26.1 0.3 collective-permute-done.6.far_ref
  26.3 2.7 %collective-permute-start.20 = (f32[1,256,128]{2,1,0:T(8,128)S(1)}, f32[1,256,128]{2,1,0:T(8,128)S(1)}, u32[]{:S(2)}, u32[]{:S(2)}) collective-permute-start(f32[1,256,128]{2,1,0:T(8,128)S(1)} %shard_map.102.refs_5_.field_ref.refs_6_), channel_id=1, source_target_pairs={{0,1},{1,0},{2,3},{3,2},{4,5},{5,4},{6,7},{7,6},{8,9},{9,8},{10,11... | collective-permute-start | bytes 393224 | tf_op jit(solution)/shard_map/ppermute | solution.py:353
  29.0 0.3 shard_map.100.refs_8_.field_ref.refs_10_
  29.3 1.6 %collective-permute-start.13 = (f32[1,256,128]{2,1,0:T(8,128)S(1)}, f32[1,256,128]{2,1,0:T(8,128)S(1)}, u32[]{:S(2)}, u32[]{:S(2)}) collective-permute-start(f32[1,256,128]{2,1,0:T(8,128)S(1)} %shard_map.100.refs_8_.field_ref.refs_10_), channel_id=1, source_target_pairs={{0,16},{1,2},{2,1},{3,4},{4,3},{5,6},{6,5},{7,8},{8,7},{9,10},{10,... | collective-permute-start | bytes 393224 | tf_op jit(solution)/shard_map/ppermute | solution.py:352
  30.8 0.2 collective-permute-start.14
  31.0 2.0 %shard_map.103 = (f32[8,128]{1,0:T(8,128)S(1)}, f32[7,3,256,128]{3,2,1,0:T(8,128)S(1)}, f32[7,3,256,128]{3,2,1,0:T(8,128)S(1)}) custom-call(f32[256,128]{1,0:T(8,128)S(1)} %get-tuple-element.43.diagonal_ref, f32[1,256,128]{2,1,0:T(8,128)S(1)} %get-tuple-element.41.field_ref.refs_0_, f32[1,256,128]{2,1,0:T(8,128)S(1)} %shard_map.98.field_ref.refs_1_, ...), custom_call_target="tpu_custom_call" | custom-call | tf_op jit(solution)/shard_map/pallas_call | solution.py:324
  33.0 0.5 shard_map.104
  33.5 0.5 shard_map.105
  34.0 0.3 collective-permute-done.13.far_ref
  34.3 0.5 shard_map.106
  34.8 15.8 %all_to_all.5.moments_ref = f32[32,1,128]{2,1,0:T(1,128)S(1)} all-to-all(f32[32,1,128]{2,1,0:T(1,128)S(1)} %get-tuple-element.49), channel_id=1, replica_groups=mesh['diamond'=2,'tile'=16] {'diamond','tile'}, dimensions={0} | all-to-all | bytes 32768 | tf_op jit(solution)/shard_map/all_to_all | solution.py:403
  50.6 1.3 %shard_map.107 = (f32[3,256,128]{2,1,0:T(8,128)}, f32[3,256,128]{2,1,0:T(8,128)}, f32[256,128]{1,0:T(8,128)}) custom-call(f32[32,1,128]{2,1,0:T(1,128)S(1)} %all_to_all.5.moments_ref, f32[256,128]{1,0:T(8,128)S(1)} %get-tuple-element.43.diagonal_ref, f32[256,128]{1,0:T(8,128)S(1)} %get-tuple-element.50.next_ref, ...), custom_call_target="tpu_custom_call" | custom-call | tf_op jit(solution)/shard_map/pallas_call | solution.py:324
  (11 shorter events, 0.0 us)
Async XLA Ops:
  0.6 6.5 %collective-permute-start.2 = (f32[1,256,128]{2,1,0:T(8,128)}, f32[1,256,128]{2,1,0:T(8,128)S(1)}, u32[]{:S(2)}, u32[]{:S(2)}) collective-permute-start(f32[1,256,128]{2,1,0:T(8,128)} %bitcast.20), channel_id=1, source_target_pairs={{0,16},{1,2},{2,1},{3,4},{4,3},{5,6},{6,5},{7,8},{8,7},{9,10},{10,... | collective-permute-start | bytes 393224 | tf_op jit(solution)/shard_map/ppermute | solution.py:352
  3.6 3.5 %collective-permute-start.3 = (f32[1,256,128]{2,1,0:T(8,128)}, f32[1,256,128]{2,1,0:T(8,128)S(1)}, u32[]{:S(2)}, u32[]{:S(2)}) collective-permute-start(f32[1,256,128]{2,1,0:T(8,128)} %bitcast.21), channel_id=1, source_target_pairs={{0,1},{1,0},{2,3},{3,2},{4,5},{5,4},{6,7},{7,6},{8,9},{9,8},{10,11... | collective-permute-start | bytes 393224 | tf_op jit(solution)/shard_map/ppermute | solution.py:353
  5.4 6.2 %collective-permute-start = (f32[1,256,128]{2,1,0:T(8,128)S(1)}, f32[1,256,128]{2,1,0:T(8,128)S(1)}, u32[]{:S(2)}, u32[]{:S(2)}) collective-permute-start(f32[1,256,128]{2,1,0:T(8,128)S(1)} %bitcast.14), channel_id=1, source_target_pairs={{0,16},{1,2},{2,1},{3,4},{4,3},{5,6},{6,5},{7,8},{8,7},{9,10},{10,... | collective-permute-start | bytes 393224 | tf_op jit(solution)/shard_map/ppermute | solution.py:352
  7.0 4.6 %collective-permute-start.1 = (f32[1,256,128]{2,1,0:T(8,128)S(1)}, f32[1,256,128]{2,1,0:T(8,128)S(1)}, u32[]{:S(2)}, u32[]{:S(2)}) collective-permute-start(f32[1,256,128]{2,1,0:T(8,128)S(1)} %bitcast.15), channel_id=1, source_target_pairs={{0,1},{1,0},{2,3},{3,2},{4,5},{5,4},{6,7},{7,6},{8,9},{9,8},{10,11... | collective-permute-start | bytes 393224 | tf_op jit(solution)/shard_map/ppermute | solution.py:353
  7.4 5.8 %collective-permute-start.8 = (f32[1,256,128]{2,1,0:T(8,128)S(1)}, f32[1,256,128]{2,1,0:T(8,128)S(1)}, u32[]{:S(2)}, u32[]{:S(2)}) collective-permute-start(f32[1,256,128]{2,1,0:T(8,128)S(1)} %get-tuple-element.41.field_ref.refs_0_), channel_id=1, source_target_pairs={{0,16},{1,2},{2,1},{3,4},{4,3},{5,6},{6,5},{7,8},{8,7},{9,10},{10,... | collective-permute-start | bytes 393224 | tf_op jit(solution)/shard_map/ppermute | solution.py:352
  9.2 5.7 %collective-permute-start.9 = (f32[1,256,128]{2,1,0:T(8,128)S(1)}, f32[1,256,128]{2,1,0:T(8,128)S(1)}, u32[]{:S(2)}, u32[]{:S(2)}) collective-permute-start(f32[1,256,128]{2,1,0:T(8,128)S(1)} %get-tuple-element.41.field_ref.refs_0_), channel_id=1, source_target_pairs={{0,1},{1,0},{2,3},{3,2},{4,5},{5,4},{6,7},{7,6},{8,9},{9,8},{10,11... | collective-permute-start | bytes 393224 | tf_op jit(solution)/shard_map/ppermute | solution.py:353
  10.1 6.5 %collective-permute-start.15 = (f32[1,256,128]{2,1,0:T(8,128)S(1)}, f32[1,256,128]{2,1,0:T(8,128)S(1)}, u32[]{:S(2)}, u32[]{:S(2)}) collective-permute-start(f32[1,256,128]{2,1,0:T(8,128)S(1)} %get-tuple-element.42.field_ref.refs_3_.refs_4_), channel_id=1, source_target_pairs={{0,16},{1,2},{2,1},{3,4},{4,3},{5,6},{6,5},{7,8},{8,7},{9,10},{10,... | collective-permute-start | bytes 393224 | tf_op jit(solution)/shard_map/ppermute | solution.py:352
  11.6 6.0 %collective-permute-start.16 = (f32[1,256,128]{2,1,0:T(8,128)S(1)}, f32[1,256,128]{2,1,0:T(8,128)S(1)}, u32[]{:S(2)}, u32[]{:S(2)}) collective-permute-start(f32[1,256,128]{2,1,0:T(8,128)S(1)} %get-tuple-element.42.field_ref.refs_3_.refs_4_), channel_id=1, source_target_pairs={{0,1},{1,0},{2,3},{3,2},{4,5},{5,4},{6,7},{7,6},{8,9},{9,8},{10,11... | collective-permute-start | bytes 393224 | tf_op jit(solution)/shard_map/ppermute | solution.py:353
  11.9 7.6 %collective-permute-start.4 = (f32[1,256,128]{2,1,0:T(8,128)S(1)}, f32[1,256,128]{2,1,0:T(8,128)S(1)}, u32[]{:S(2)}, u32[]{:S(2)}) collective-permute-start(f32[1,256,128]{2,1,0:T(8,128)S(1)} %get-tuple-element.39.field_ref.refs_6_.refs_8_), channel_id=1, source_target_pairs={{0,16},{1,2},{2,1},{3,4},{4,3},{5,6},{6,5},{7,8},{8,7},{9,10},{10,... | collective-permute-start | bytes 393224 | tf_op jit(solution)/shard_map/ppermute | solution.py:352
  13.2 7.9 %collective-permute-start.5 = (f32[1,256,128]{2,1,0:T(8,128)S(1)}, f32[1,256,128]{2,1,0:T(8,128)S(1)}, u32[]{:S(2)}, u32[]{:S(2)}) collective-permute-start(f32[1,256,128]{2,1,0:T(8,128)S(1)} %get-tuple-element.39.field_ref.refs_6_.refs_8_), channel_id=1, source_target_pairs={{0,1},{1,0},{2,3},{3,2},{4,5},{5,4},{6,7},{7,6},{8,9},{9,8},{10,11... | collective-permute-start | bytes 393224 | tf_op jit(solution)/shard_map/ppermute | solution.py:353
  15.1 7.7 %collective-permute-start.10 = (f32[1,256,128]{2,1,0:T(8,128)S(1)}, f32[1,256,128]{2,1,0:T(8,128)S(1)}, u32[]{:S(2)}, u32[]{:S(2)}) collective-permute-start(f32[1,256,128]{2,1,0:T(8,128)S(1)} %shard_map.98.field_ref.refs_1_), channel_id=1, source_target_pairs={{0,16},{1,2},{2,1},{3,4},{4,3},{5,6},{6,5},{7,8},{8,7},{9,10},{10,... | collective-permute-start | bytes 393224 | tf_op jit(solution)/shard_map/ppermute | solution.py:352
  16.7 6.2 %collective-permute-start.11 = (f32[1,256,128]{2,1,0:T(8,128)S(1)}, f32[1,256,128]{2,1,0:T(8,128)S(1)}, u32[]{:S(2)}, u32[]{:S(2)}) collective-permute-start(f32[1,256,128]{2,1,0:T(8,128)S(1)} %shard_map.98.field_ref.refs_1_), channel_id=1, source_target_pairs={{0,1},{1,0},{2,3},{3,2},{4,5},{5,4},{6,7},{7,6},{8,9},{9,8},{10,11... | collective-permute-start | bytes 393224 | tf_op jit(solution)/shard_map/ppermute | solution.py:353
  17.9 5.8 %collective-permute-start.17 = (f32[1,256,128]{2,1,0:T(8,128)S(1)}, f32[1,256,128]{2,1,0:T(8,128)S(1)}, u32[]{:S(2)}, u32[]{:S(2)}) collective-permute-start(f32[1,256,128]{2,1,0:T(8,128)S(1)} %shard_map.101.field_ref.refs_4_.refs_5_), channel_id=1, source_target_pairs={{0,16},{1,2},{2,1},{3,4},{4,3},{5,6},{6,5},{7,8},{8,7},{9,10},{10,... | collective-permute-start | bytes 393224 | tf_op jit(solution)/shard_map/ppermute | solution.py:352
  19.5 5.0 %collective-permute-start.18 = (f32[1,256,128]{2,1,0:T(8,128)S(1)}, f32[1,256,128]{2,1,0:T(8,128)S(1)}, u32[]{:S(2)}, u32[]{:S(2)}) collective-permute-start(f32[1,256,128]{2,1,0:T(8,128)S(1)} %shard_map.101.field_ref.refs_4_.refs_5_), channel_id=1, source_target_pairs={{0,1},{1,0},{2,3},{3,2},{4,5},{5,4},{6,7},{7,6},{8,9},{9,8},{10,11... | collective-permute-start | bytes 393224 | tf_op jit(solution)/shard_map/ppermute | solution.py:353
  21.3 5.0 %collective-permute-start.6 = (f32[1,256,128]{2,1,0:T(8,128)S(1)}, f32[1,256,128]{2,1,0:T(8,128)S(1)}, u32[]{:S(2)}, u32[]{:S(2)}) collective-permute-start(f32[1,256,128]{2,1,0:T(8,128)S(1)} %shard_map.97.field_ref.refs_7_.refs_9_), channel_id=1, source_target_pairs={{0,16},{1,2},{2,1},{3,4},{4,3},{5,6},{6,5},{7,8},{8,7},{9,10},{10,... | collective-permute-start | bytes 393224 | tf_op jit(solution)/shard_map/ppermute | solution.py:352
  22.9 6.1 %collective-permute-start.7 = (f32[1,256,128]{2,1,0:T(8,128)S(1)}, f32[1,256,128]{2,1,0:T(8,128)S(1)}, u32[]{:S(2)}, u32[]{:S(2)}) collective-permute-start(f32[1,256,128]{2,1,0:T(8,128)S(1)} %shard_map.97.field_ref.refs_7_.refs_9_), channel_id=1, source_target_pairs={{0,1},{1,0},{2,3},{3,2},{4,5},{5,4},{6,7},{7,6},{8,9},{9,8},{10,11... | collective-permute-start | bytes 393224 | tf_op jit(solution)/shard_map/ppermute | solution.py:353
  23.1 5.9 %collective-permute-start.12 = (f32[1,256,128]{2,1,0:T(8,128)S(1)}, f32[1,256,128]{2,1,0:T(8,128)S(1)}, u32[]{:S(2)}, u32[]{:S(2)}) collective-permute-start(f32[1,256,128]{2,1,0:T(8,128)S(1)} %shard_map.99.refs_2_.field_ref), channel_id=1, source_target_pairs={{0,1},{1,0},{2,3},{3,2},{4,5},{5,4},{6,7},{7,6},{8,9},{9,8},{10,11... | collective-permute-start | bytes 393224 | tf_op jit(solution)/shard_map/ppermute | solution.py:353
  23.7 9.3 %collective-permute-start.21 = (f32[1,256,128]{2,1,0:T(8,128)S(1)}, f32[1,256,128]{2,1,0:T(8,128)S(1)}, u32[]{:S(2)}, u32[]{:S(2)}) collective-permute-start(f32[1,256,128]{2,1,0:T(8,128)S(1)} %shard_map.99.refs_2_.field_ref), channel_id=1, source_target_pairs={{0,16},{1,2},{2,1},{3,4},{4,3},{5,6},{6,5},{7,8},{8,7},{9,10},{10,... | collective-permute-start | bytes 393224 | tf_op jit(solution)/shard_map/ppermute | solution.py:352
  24.7 8.8 %collective-permute-start.19 = (f32[1,256,128]{2,1,0:T(8,128)S(1)}, f32[1,256,128]{2,1,0:T(8,128)S(1)}, u32[]{:S(2)}, u32[]{:S(2)}) collective-permute-start(f32[1,256,128]{2,1,0:T(8,128)S(1)} %shard_map.102.refs_5_.field_ref.refs_6_), channel_id=1, source_target_pairs={{0,16},{1,2},{2,1},{3,4},{4,3},{5,6},{6,5},{7,8},{8,7},{9,10},{10,... | collective-permute-start | bytes 393224 | tf_op jit(solution)/shard_map/ppermute | solution.py:352
  26.3 7.2 %collective-permute-start.20 = (f32[1,256,128]{2,1,0:T(8,128)S(1)}, f32[1,256,128]{2,1,0:T(8,128)S(1)}, u32[]{:S(2)}, u32[]{:S(2)}) collective-permute-start(f32[1,256,128]{2,1,0:T(8,128)S(1)} %shard_map.102.refs_5_.field_ref.refs_6_), channel_id=1, source_target_pairs={{0,1},{1,0},{2,3},{3,2},{4,5},{5,4},{6,7},{7,6},{8,9},{9,8},{10,11... | collective-permute-start | bytes 393224 | tf_op jit(solution)/shard_map/ppermute | solution.py:353
  29.3 5.0 %collective-permute-start.13 = (f32[1,256,128]{2,1,0:T(8,128)S(1)}, f32[1,256,128]{2,1,0:T(8,128)S(1)}, u32[]{:S(2)}, u32[]{:S(2)}) collective-permute-start(f32[1,256,128]{2,1,0:T(8,128)S(1)} %shard_map.100.refs_8_.field_ref.refs_10_), channel_id=1, source_target_pairs={{0,16},{1,2},{2,1},{3,4},{4,3},{5,6},{6,5},{7,8},{8,7},{9,10},{10,... | collective-permute-start | bytes 393224 | tf_op jit(solution)/shard_map/ppermute | solution.py:352
  30.8 3.5 %collective-permute-start.14 = (f32[1,256,128]{2,1,0:T(8,128)S(1)}, f32[1,256,128]{2,1,0:T(8,128)S(1)}, u32[]{:S(2)}, u32[]{:S(2)}) collective-permute-start(f32[1,256,128]{2,1,0:T(8,128)S(1)} %shard_map.100.refs_8_.field_ref.refs_10_), channel_id=1, source_target_pairs={{0,1},{1,0},{2,3},{3,2},{4,5},{5,4},{6,7},{7,6},{8,9},{9,8},{10,11... | collective-permute-start | bytes 393224 | tf_op jit(solution)/shard_map/ppermute | solution.py:353

commit v7 on v5

--- a/solution.py
+++ b/solution.py
@@ -1,5 +1,3 @@
-import functools
-
 import jax
 import jax.numpy as jnp
 from jax import lax
@@ -31,6 +29,14 @@
     return pltpu.roll(block, count - 1, 1), pltpu.roll(block, 1, 1)
 
 
+def sides(load, start, total):
+    mid, after, before = rows_around(load, start, total)
+    place = start + lax.broadcasted_iota(jnp.int32, mid.shape, 0)
+    layer = lax.broadcasted_iota(jnp.int32, mid.shape, 1)
+    inside = [place < total - 1, place > 0, layer < mid.shape[1] - 1, layer > 0]
+    return mid, [after, before, *layers_around(mid)], inside
+
+
 def split3(value):
     top = value.astype(jnp.bfloat16)
     rest = value - top.astype(jnp.float32)
@@ -39,15 +45,17 @@
     return [top, middle, bottom]
 
 
-def fold_matrix(edge_ref, pole_ref):
+def fold_matrix(edge_ref, pole_ref, kind):
     group, tile = lax.axis_index("diamond"), lax.axis_index("tile")
-    final = lax.axis_size("tile") - 1
+    last = lax.axis_size("tile") - 1
     count = edge_ref.shape[1]
     rows = lax.broadcasted_iota(jnp.int32, (count, count), 0)
     same = lax.broadcasted_iota(jnp.int32, (1, count), 1)
-    edge = jnp.where(group == 0, edge_ref[1:2], edge_ref[0:1])
-    pole = jnp.where(group == 0, pole_ref[1:2], pole_ref[0:1])
-    line = jnp.where(tile == 0, pole, jnp.where(tile == final, edge, same))
+    side = 1 - group if kind == 1 else group
+    skip = 2 if kind == 2 else 0
+    edge = jnp.where(side == 0, edge_ref[1:2], edge_ref[0:1])
+    pole = jnp.where(side == 0, pole_ref[1:2], pole_ref[0:1])
+    line = jnp.where(tile == skip, pole, jnp.where(tile == last - skip, edge, same))
     return (rows == line).astype(jnp.bfloat16)
 
 
@@ -63,7 +71,7 @@
 
 def local_kernel(
     temp_hbm, misfit_hbm, visc_hbm, velocity_hbm, forcing_hbm, edge_hbm, pole_hbm,
-    half_ref, side_ref, base_ref, right_ref, part_ref, speed_ref, matrix_ref, temp_ref,
+    half_ref, side_ref, base_ref, right_ref, part_ref, speed_ref, matrix_ref, back_ref, ahead_ref, temp_ref,
     misfit_ref, visc_ref, velocity_ref, edge_ref, pole_ref, sems,
 ):
     sources = [visc_hbm, temp_hbm, edge_hbm, pole_hbm, velocity_hbm, misfit_hbm, forcing_hbm]
@@ -76,20 +84,16 @@
     total, layers = temp_ref.shape
     for copy in copies:
         copy.wait()
-    matrix_ref[...] = fold_matrix(edge_ref, pole_ref)
+    for kind, ref in enumerate((matrix_ref, back_ref, ahead_ref)):
+        ref[...] = fold_matrix(edge_ref, pole_ref, kind)
     for start in range(0, total, CHUNK):
         here = slice(start, start + CHUNK)
-        visc, visc_after, visc_before = rows_around(lambda a, b: visc_ref[a:b], start, total)
-        temp, temp_after, temp_before = rows_around(lambda a, b: temp_ref[a:b], start, total)
-        place = start + lax.broadcasted_iota(jnp.int32, (CHUNK, layers), 0)
-        layer = lax.broadcasted_iota(jnp.int32, (CHUNK, layers), 1)
-        inside = [place < total - 1, place > 0, layer < layers - 1, layer > 0]
-        visc_near = [visc_after, visc_before, *layers_around(visc)]
-        temp_near = [temp_after, temp_before, *layers_around(temp)]
+        visc, visc_near, inside = sides(lambda a, b: visc_ref[a:b], start, total)
+        temp, temp_near, _ = sides(lambda a, b: temp_ref[a:b], start, total)
         zero = jnp.zeros_like(visc)
         weights = [jnp.where(m, 0.5 * (visc + v), zero) for m, v in zip(inside, visc_near)]
         temps = [jnp.where(m, t, zero) for m, t in zip(inside, temp_near)]
-        half_ref[here] = 0.5 * visc
+        half_ref[0, here] = 0.5 * visc
         for k in range(4):
             side_ref[k, here] = weights[k]
         base_ref[here] = MASS_TERM + sum(weights)
@@ -102,30 +106,27 @@
 
 
 def weigh_kernel(
-    far_ref, near_ref, half_ref, side_ref, base_ref, right_ref, matrix_ref,
-    weights_ref, diagonal_ref, inverse_ref, *refs,
-):
-    *first_refs, moved_ref = refs
+    far_ref, near_ref, half_ref, side_ref, base_ref, matrix_ref,
+    weights_ref, diagonal_ref, inverse_ref, moved_ref,
+):
     unfold(matrix_ref, far_ref, moved_ref)
-    for start in range(0, half_ref.shape[0], CHUNK):
-        here = slice(start, start + CHUNK)
-        visc = half_ref[here]
+    for start in range(0, half_ref.shape[1], CHUNK):
+        here = slice(start, start + CHUNK)
+        visc = half_ref[0, here]
         weights = [visc + 0.5 * near_ref[0, here], visc + 0.5 * moved_ref[0, here]]
         diagonal = base_ref[here] + weights[0] + weights[1]
         diagonal_ref[here] = diagonal
         inverse = 1.0 / diagonal
         inverse_ref[here] = inverse
-        for (low, high), first_ref in zip(SPLITS, first_refs):
-            for at in range(low, high):
-                first_ref[at - low, here] = right_ref[at, here] * inverse
         weights += [side_ref[k, here] for k in range(4)]
         for k in range(6):
             weights_ref[k, here] = weights[k] * inverse
 
 
 def step_kernel(
-    far_ref, near_ref, right_ref, part_ref, speed_ref, inverse_ref, matrix_ref, next_ref, first_ref, moved_ref
-):
+    far_ref, near_ref, right_ref, part_ref, speed_ref, inverse_ref, matrix_ref, next_ref, *refs
+):
+    *first_refs, moved_ref = refs
     unfold(matrix_ref, far_ref, moved_ref)
     for start in range(0, part_ref.shape[0], CHUNK):
         here = slice(start, start + CHUNK)
@@ -134,7 +135,10 @@
             DIFFUSION * (near + far) + speed_ref[here] * (near - far)
         )
         next_ref[here] = adjoint_next
-        first_ref[0, here] = (right_ref[2, here] + BUOYANCY * adjoint_next) * inverse_ref[here]
+        inverse = inverse_ref[here]
+        first_refs[0][0, here] = right_ref[0, here] * inverse
+        first_refs[1][0, here] = right_ref[1, here] * inverse
+        first_refs[2][0, here] = (right_ref[2, here] + BUOYANCY * adjoint_next) * inverse
 
 
 def average(start, at, field_ref, near_ref, moved_ref, weights):
@@ -144,13 +148,54 @@
     return sum(w * v for w, v in zip(weights, around))
 
 
-def apply_kernel(far_ref, near_ref, field_ref, weights_ref, matrix_ref, out_ref, moved_ref):
-    unfold(matrix_ref, far_ref, moved_ref)
+def apply_rows(field_ref, near_ref, moved_ref, weights_ref, out_ref):
     for start in range(0, field_ref.shape[1], CHUNK):
         here = slice(start, start + CHUNK)
         weights = [weights_ref[k, here] for k in range(6)]
         for at in range(field_ref.shape[0]):
             out_ref[at, here] = average(start, at, field_ref, near_ref, moved_ref, weights)
+
+
+def deep_weigh_kernel(
+    second_ref, third_ref, first_ref, half_ref, back_ref, ahead_ref, after_ref, first_weights_ref, second_weights_ref, *moved_refs
+):
+    unfold(back_ref, half_ref, moved_refs[0])
+    unfold(ahead_ref, third_ref, moved_refs[1])
+    total = half_ref.shape[1]
+    for start in range(0, total, CHUNK):
+        here = slice(start, start + CHUNK)
+        between = 0.5 * (first_ref[0, here] + second_ref[0, here])
+        beyond = (moved_refs[0][0, here], 0.5 * moved_refs[1][0, here])
+        outs = (first_weights_ref, second_weights_ref)
+        for row_ref, other, out_ref in zip((first_ref, second_ref), beyond, outs):
+            visc, near, inside = sides(lambda a, b: row_ref[0, a:b], start, total)
+            weights = [between, 0.5 * visc + other]
+            weights += [jnp.where(m, 0.5 * (visc + v), jnp.zeros_like(visc)) for m, v in zip(inside, near)]
+            inverse = 1.0 / (MASS_TERM + sum(weights))
+            for k in range(6):
+                out_ref[k, here] = weights[k] * inverse
+
+
+def deep_first_kernel(
+    first_ref, second_ref, third_ref, near_ref, field_ref, weights_ref, first_weights_ref, second_weights_ref,
+    matrix_ref, back_ref, ahead_ref, after_ref, out_ref, out_first_ref, out_second_ref, moved_ref,
+):
+    unfold(matrix_ref, first_ref, moved_ref)
+    apply_rows(field_ref, near_ref, moved_ref, weights_ref, out_ref)
+    unfold(back_ref, field_ref, moved_ref)
+    apply_rows(first_ref, second_ref, moved_ref, first_weights_ref, out_first_ref)
+    unfold(ahead_ref, third_ref, moved_ref)
+    apply_rows(second_ref, first_ref, moved_ref, second_weights_ref, out_second_ref)
+
+
+def deep_second_kernel(
+    first_ref, second_ref, near_ref, field_ref, weights_ref, first_weights_ref, matrix_ref, back_ref, after_ref,
+    out_ref, out_first_ref, moved_ref,
+):
+    unfold(matrix_ref, first_ref, moved_ref)
+    apply_rows(field_ref, near_ref, moved_ref, weights_ref, out_ref)
+    unfold(back_ref, field_ref, moved_ref)
+    apply_rows(first_ref, second_ref, moved_ref, first_weights_ref, out_first_ref)
 
 
 def fold8(value):
@@ -170,31 +215,28 @@
     return jnp.where(moment_lanes(k), column, 0.0)
 
 
-def early_kernel(diagonal_ref, *refs):
-    moments_ref, left_ref, shift_ref = refs[-3:]
+def early_kernel(diagonal_ref, y0_ref, y1_ref, y2_ref, moments_ref, left_ref, shift_ref):
     total, layers = diagonal_ref.shape
     sums = [[jnp.zeros((8, layers), jnp.float32) for _ in CENTERS] for _ in range(5)]
-    for i, (low, high) in enumerate(SPLITS):
-        y0_ref, y1_ref, y2_ref = refs[3 * i : 3 * i + 3]
-        for start in range(0, total, CHUNK):
-            here = slice(start, start + CHUNK)
-            diagonal = diagonal_ref[here]
-            for at in range(high - low):
-                y0, y1, y2 = y0_ref[at, here], y1_ref[at, here], y2_ref[at, here]
-                d0 = diagonal * y0
-                m0 = fold8(d0 * y0)
-                for j, center in enumerate(CENTERS):
-                    q1 = y1 - center * y0
-                    t2 = y2 - center * y1
-                    q2 = t2 - center * q1
-                    d1, d2 = diagonal * q1, diagonal * q2
-                    left_ref[j, low + at, here] = d2
-                    shift_ref[j, low + at, here] = center * (y2 + t2 + q2)
-                    sums[0][j] += m0
-                    sums[1][j] += fold8(d0 * q1)
-                    sums[2][j] += fold8(d1 * q1)
-                    sums[3][j] += fold8(d1 * q2)
-                    sums[4][j] += fold8(d2 * q2)
+    for start in range(0, total, CHUNK):
+        here = slice(start, start + CHUNK)
+        diagonal = diagonal_ref[here]
+        for at in range(y0_ref.shape[0]):
+            y0, y1, y2 = y0_ref[at, here], y1_ref[at, here], y2_ref[at, here]
+            d0 = diagonal * y0
+            m0 = fold8(d0 * y0)
+            for j, center in enumerate(CENTERS):
+                q1 = y1 - center * y0
+                t2 = y2 - center * y1
+                q2 = t2 - center * q1
+                d1, d2 = diagonal * q1, diagonal * q2
+                left_ref[j, at, here] = d2
+                shift_ref[j, at, here] = center * (y2 + t2 + q2)
+                sums[0][j] += m0
+                sums[1][j] += fold8(d0 * q1)
+                sums[2][j] += fold8(d1 * q1)
+                sums[3][j] += fold8(d1 * q2)
+                sums[4][j] += fold8(d2 * q2)
     moments_ref[...] = sum(place_moment(k, sums[k]) for k in range(5))
 
 
@@ -207,7 +249,7 @@
 
 
 def last_kernel(
-    low, far_ref, near_ref, field_ref, weights_ref, matrix_ref, earlier_ref, left_ref, shift_ref,
+    far_ref, near_ref, field_ref, weights_ref, matrix_ref, earlier_ref, left_ref, shift_ref,
     out_ref, moments_ref, moved_ref,
 ):
     unfold(matrix_ref, far_ref, moved_ref)
@@ -220,7 +262,7 @@
             y3 = average(start, at, field_ref, near_ref, moved_ref, weights)
             out_ref[at, here] = y3
             for j in range(len(CENTERS)):
-                sums[j] += fold8(left_ref[j, low + at, here] * (y3 - shift_ref[j, low + at, here]))
+                sums[j] += fold8(left_ref[j, at, here] * (y3 - shift_ref[j, at, here]))
     message = earlier_ref[...] + place_moment(5, sums)
     if len(moments_ref.shape) == 2:
         moments_ref[...] = message
@@ -347,62 +389,96 @@
 NAMES = ("diamond", "tile")
 
 
+def neighbour(value):
+    beside, _ = ring_pairs(lax.axis_size("diamond"), lax.axis_size("tile"))
+    return lax.ppermute(value, NAMES, beside)
+
+
+def far_row(value, distance):
+    tiles = lax.axis_size("tile")
+    size = lax.axis_size("diamond") * tiles
+    device = [i if i < tiles else tiles + size - 1 - i for i in range(size)]
+    pairs = []
+    for place in range(size):
+        source = (place - distance if place % 2 == 0 else place + distance) % size
+        pairs.append((device[source], device[place]))
+    return lax.ppermute(value, NAMES, sorted(pairs))
+
+
 def exchange(value):
-    beside, across = ring_pairs(lax.axis_size("diamond"), lax.axis_size("tile"))
-    far = lax.ppermute(value, NAMES, across)
-    near = lax.ppermute(value, NAMES, beside)
-    return near, far
+    return neighbour(value), far_row(value, 1)
 
 
 def body(adjoint_temp, misfit, viscosity, velocity, forcing, edge_table, pole_table):
     rows, layers = adjoint_temp.shape[2:]
     devices = lax.axis_size("diamond") * lax.axis_size("tile")
-    flat, triple = (rows, layers), (3, rows, layers)
+    flat, triple, single, double = (rows, layers), (3, rows, layers), (1, rows, layers), (2, rows, layers)
     temp, source, visc = (v.reshape(flat) for v in (adjoint_temp, misfit, viscosity))
     visc_near, visc_far = exchange(visc[None])
+    visc_second, visc_third = far_row(visc[None], 2), far_row(visc[None], 3)
     table = pltpu.VMEM(edge_table.shape, edge_table.dtype)
-    half, side, base, right, part, speed, matrix, sent = call(
-        local_kernel,
-        [flat, (4, *flat), flat, triple, flat, flat, jax.ShapeDtypeStruct((rows, rows), jnp.bfloat16), flat],
+    square = jax.ShapeDtypeStruct((rows, rows), jnp.bfloat16)
+    half, side, base, right, part, speed, matrix, back, ahead, sent = call(
+        local_kernel, [single, (4, *flat), flat, triple, flat, flat, square, square, square, flat],
         temp, source, visc, velocity.reshape(triple), forcing.reshape(triple), edge_table, pole_table,
         scratch=[flat, flat, triple, table, table, pltpu.SemaphoreType.DMA((7,))],
         place=pltpu.HBM,
     )
     temp_near, temp_far = exchange(sent[None])
-    shapes = [(high - low, rows, layers) for low, high in SPLITS]
-    weights, diagonal, inverse, *first = call(
-        weigh_kernel, [(6, *flat), flat, flat, *shapes[:-1]],
-        visc_far, visc_near, half, side, base, right, matrix, scratch=[(1, *flat)],
-    )
-    adjoint_next, *rest = call(
-        step_kernel, [flat, shapes[-1]],
-        temp_far, temp_near, right, part, speed, inverse, matrix, scratch=[(1, *flat)],
-    )
-    first += rest
-    streams = [[field] for field in first]
-    swapped = [exchange(field) for field in first]
-    for step in range(ITERS - 1):
-        for i, shape in enumerate(shapes):
-            near, far = swapped[i]
-            (field,) = call(apply_kernel, [shape], far, near, streams[i][-1], weights, matrix, scratch=[shape])
-            swapped[i] = exchange(field)
-            streams[i].append(field)
-    many = (len(CENTERS), *triple)
-    moments, left, shift = call(
-        early_kernel, [(8, 128), many, many], diagonal, *[field for stream in streams for field in stream]
-    )
-    for i, shape in enumerate(shapes):
-        near, far = swapped[i]
-        sums = (8, 128) if i + 1 < len(shapes) else (devices, 1, 128)
+    weights, diagonal, inverse = call(
+        weigh_kernel, [(6, *flat), flat, flat],
+        visc_far, visc_near, half, side, base, matrix, scratch=[single],
+    )
+    adjoint_next, *first = call(
+        step_kernel, [flat, single, single, single],
+        temp_far, temp_near, right, part, speed, inverse, matrix, scratch=[single],
+    )
+    halos = [[far_row(y, 1), far_row(y, 2), far_row(y, 3), neighbour(y)] for y in first]
+    deep = call(
+        deep_weigh_kernel, [(6, *flat)] * 2,
+        visc_second, visc_third, visc_far, half, back, ahead, first[0], scratch=[single, single],
+    )
+    streams = [[y] for y in first]
+    many = (len(CENTERS), *single)
+
+    def one(i, after):
+        y1, first_row, second_row = call(
+            deep_first_kernel, [single] * 3,
+            *halos[i], first[i], weights, *deep, matrix, back, ahead, after, scratch=[single],
+        )
+        streams[i].append(y1)
+        return first_row, second_row, neighbour(y1)
+
+    def two(i, rows_near, after):
+        y2, first_row = call(
+            deep_second_kernel, [single] * 2,
+            *rows_near, streams[i][1], weights, deep[0], matrix, back, after, scratch=[single],
+        )
+        streams[i].append(y2)
+        return first_row, neighbour(y2)
+
+    def early(i):
+        return call(early_kernel, [(8, 128), many, many], diagonal, *streams[i])
+
+    a = one(0, weights)
+    b = one(1, streams[0][1])
+    a = two(0, a, streams[1][1])
+    early_a = early(0)
+    c = one(2, early_a[0])
+    b = two(1, b, streams[2][1])
+    c = two(2, c, streams[1][2])
+    early_b, early_c = early(1), early(2)
+    moments = early_a[0] + early_b[0] + early_c[0]
+    for i, (swapped, prepared) in enumerate(((a, early_a), (b, early_b), (c, early_c))):
         field, moments = call(
-            functools.partial(last_kernel, SPLITS[i][0]), [shape, sums],
-            far, near, streams[i][-1], weights, matrix, moments, left, shift, scratch=[shape],
+            last_kernel, [single, (devices, 1, 128) if i == 2 else (8, 128)],
+            *swapped, streams[i][2], weights, matrix, moments, *prepared[1:], scratch=[single],
         )
         streams[i].append(field)
     moments = lax.all_to_all(moments, NAMES, 0, 0)
-    fields = [field for stream in streams for field in stream]
     answer, residual, adjoint_next = call(
-        finish_kernel, [triple, triple, flat], moments, diagonal, adjoint_next, *fields,
+        finish_kernel, [triple, triple, flat],
+        moments, diagonal, adjoint_next, *[field for stream in streams for field in stream],
         scratch=[triple, triple, pltpu.SemaphoreType.DMA((2, 3)), pltpu.SemaphoreType.DMA], out_place=pltpu.HBM,
     )
     whole = (3, 1, 1, rows, layers)

time: 51.9 us -> 57 us (1.098)
  waiting for transfers between devices: 0.06 us -> 3.87 us
  blocking collectives: 15.3 us -> 12.4 us
  starting transfers between devices: 27.3 us -> 30 us
  Pallas kernels: 8.39 us -> 9.75 us
    ppermute x22 -> x24, waiting for transfers between devices: 0.06 us -> 3.87 us  [the longest x13 3.71 us: far_row(): return lax.ppermute(value, NAMES, sorted(pairs))]
    all_to_all x1, blocking collectives: 15.3 us -> 12.4 us  [body(): moments = lax.all_to_all(moments, NAMES, 0, 0)]
    ppermute x22 -> x24, starting transfers between devices: 27.3 us -> 30 us  [the longest x13 26.7 us: far_row(): return lax.ppermute(value, NAMES, sorted(pairs))]
    pallas_call x14 -> x17, Pallas kernels: 8.39 us -> 9.75 us  [call(): pl.pallas_call(kernel, out_shape=outs, in_specs=[pl.BlockSpec(memory_spac...]
  transfers between devices with their start and end apart: 22 -> 24, of which waited for: 0 -> 4; matrix products, arithmetic and copies ran while one was open for 0% -> 0% of each run, Pallas kernels for 13% -> 14%
where the time goes in v7:
time: 57 us; the launch traced here: 56.8 us
  starting transfers between devices  30 us (53%)
  blocking collectives  12.4 us (22%)
  Pallas kernels  9.75 us (17%)
  waiting for transfers between devices  3.87 us (7%)
  between operations  0.78 us (1%)
    ppermute x13, starting transfers between devices, far_row(): return lax.ppermute(value, NAMES, sorted(pairs))  26.7 us
    all_to_all x1, blocking collectives, body(): moments = lax.all_to_all(moments, NAMES, 0, 0)  12.4 us
    pallas_call x17, Pallas kernels, call(): pl.pallas_call(kernel, out_shape=outs, in_specs=[pl.BlockSpec(memory_spac...  9.75 us
    ppermute x13, waiting for transfers between devices, far_row(): return lax.ppermute(value, NAMES, sorted(pairs))  3.71 us
    ppermute x11, starting transfers between devices, neighbour(): return lax.ppermute(value, NAMES, beside)  3.26 us
  transfers between devices with their start and end apart: 24, of which 4 were waited for; matrix products, arithmetic and copies ran while one was open for 0% of the time, Pallas kernels for 14%

profile of v7, /device:TPU:0, one launch (start us, length us, event | category | flops | bytes accessed | tf_op | source)
XLA Modules:
  0.0 56.8 jit_solution(1965943039658787763)
XLA Ops:
  0.6 3.0 %collective-permute-start.2 = (f32[1,256,128]{2,1,0:T(8,128)}, f32[1,256,128]{2,1,0:T(8,128)S(1)}, u32[]{:S(2)}, u32[]{:S(2)}) collective-permute-start(f32[1,256,128]{2,1,0:T(8,128)} %bitcast.20), channel_id=1, source_target_pairs={{0,16},{1,2},{2,1},{3,4},{4,3},{5,6},{6,5},{7,8},{8,7},{9,10},{10,... | collective-permute-start | bytes 393224 | tf_op jit(solution)/shard_map/ppermute | solution.py:405
  3.6 0.1 collective-permute-start.3
  3.8 1.8 %shard_map.94 = (f32[1,256,128]{2,1,0:T(8,128)S(1)}, f32[4,256,128]{2,1,0:T(8,128)S(1)}, f32[256,128]{1,0:T(8,128)S(1)}, f32[3,256,128]{2,1,0:T(8,128)S(1)}, f32...) custom-call(f32[256,128]{1,0:T(8,128)} %bitcast.18, ...), custom_call_target="tpu_custom_call" | custom-call | tf_op jit(solution)/shard_map/pallas_call | solution.py:366
  5.6 1.6 %collective-permute-start = (f32[1,256,128]{2,1,0:T(8,128)S(1)}, f32[1,256,128]{2,1,0:T(8,128)S(1)}, u32[]{:S(2)}, u32[]{:S(2)}) collective-permute-start(f32[1,256,128]{2,1,0:T(8,128)S(1)} %bitcast.14), channel_id=1, source_target_pairs={{0,16},{1,2},{2,1},{3,4},{4,3},{5,6},{6,5},{7,8},{8,7},{9,10},{10,... | collective-permute-start | bytes 393224 | tf_op jit(solution)/shard_map/ppermute | solution.py:405
  7.1 0.1 collective-permute-start.1
  7.3 1.5 %collective-permute-start.8 = (f32[1,256,128]{2,1,0:T(8,128)S(1)}, f32[1,256,128]{2,1,0:T(8,128)S(1)}, u32[]{:S(2)}, u32[]{:S(2)}) collective-permute-start(f32[1,256,128]{2,1,0:T(8,128)S(1)} %bitcast.23), channel_id=1, source_target_pairs={{0,2},{1,16},{2,4},{3,1},{4,6},{5,3},{6,8},{7,5},{8,10},{9,7},{10,... | collective-permute-start | bytes 393224 | tf_op jit(solution)/shard_map/ppermute | solution.py:405
  8.8 0.0 collective-permute-done.2.far_ref.first_ref
  8.8 2.4 %collective-permute-start.9 = (f32[1,256,128]{2,1,0:T(8,128)S(1)}, f32[1,256,128]{2,1,0:T(8,128)S(1)}, u32[]{:S(2)}, u32[]{:S(2)}) collective-permute-start(f32[1,256,128]{2,1,0:T(8,128)S(1)} %bitcast.24), channel_id=1, source_target_pairs={{0,18},{1,4},{2,16},{3,6},{4,1},{5,8},{6,3},{7,10},{8,5},{9,12},{1... | collective-permute-start | bytes 393224 | tf_op jit(solution)/shard_map/ppermute | solution.py:405
  11.2 0.0 collective-permute-done.3.near_ref
  11.2 0.3 shard_map.95
  11.5 0.0 collective-permute-done.far_ref
  11.5 0.0 collective-permute-done.1.near_ref
  11.5 0.2 shard_map.96
  11.8 1.0 %collective-permute-start.10 = (f32[1,256,128]{2,1,0:T(8,128)S(1)}, f32[1,256,128]{2,1,0:T(8,128)S(1)}, u32[]{:S(2)}, u32[]{:S(2)}) collective-permute-start(f32[1,256,128]{2,1,0:T(8,128)S(1)} %get-tuple-element.68.after_ref.field_ref.y0_ref.refs_0_), channel_id=1, source_target_pairs={{0,16},{1,2},{2,1},{3,4},{4,3},{5,6},{6,5},{7,8},{8,7},{9,10},{10,... | collective-permute-start | bytes 393224 | tf_op jit(solution)/shard_map/ppermute | solution.py:405
  12.7 2.0 %collective-permute-start.11 = (f32[1,256,128]{2,1,0:T(8,128)S(1)}, f32[1,256,128]{2,1,0:T(8,128)S(1)}, u32[]{:S(2)}, u32[]{:S(2)}) collective-permute-start(f32[1,256,128]{2,1,0:T(8,128)S(1)} %get-tuple-element.68.after_ref.field_ref.y0_ref.refs_0_), channel_id=1, source_target_pairs={{0,2},{1,16},{2,4},{3,1},{4,6},{5,3},{6,8},{7,5},{8,10},{9,7},{10,... | collective-permute-start | bytes 393224 | tf_op jit(solution)/shard_map/ppermute | solution.py:405
  14.8 1.9 %collective-permute-start.12 = (f32[1,256,128]{2,1,0:T(8,128)S(1)}, f32[1,256,128]{2,1,0:T(8,128)S(1)}, u32[]{:S(2)}, u32[]{:S(2)}) collective-permute-start(f32[1,256,128]{2,1,0:T(8,128)S(1)} %get-tuple-element.68.after_ref.field_ref.y0_ref.refs_0_), channel_id=1, source_target_pairs={{0,18},{1,4},{2,16},{3,6},{4,1},{5,8},{6,3},{7,10},{8,5},{9,12},{1... | collective-permute-start | bytes 393224 | tf_op jit(solution)/shard_map/ppermute | solution.py:405
  16.7 0.6 %collective-permute-start.13 = (f32[1,256,128]{2,1,0:T(8,128)S(1)}, f32[1,256,128]{2,1,0:T(8,128)S(1)}, u32[]{:S(2)}, u32[]{:S(2)}) collective-permute-start(f32[1,256,128]{2,1,0:T(8,128)S(1)} %get-tuple-element.68.after_ref.field_ref.y0_ref.refs_0_), channel_id=1, source_target_pairs={{0,1},{1,0},{2,3},{3,2},{4,5},{5,4},{6,7},{7,6},{8,9},{9,8},{10,11... | collective-permute-start | bytes 393224 | tf_op jit(solution)/shard_map/ppermute | solution.py:394
  17.3 1.5 %collective-permute-start.15 = (f32[1,256,128]{2,1,0:T(8,128)S(1)}, f32[1,256,128]{2,1,0:T(8,128)S(1)}, u32[]{:S(2)}, u32[]{:S(2)}) collective-permute-start(f32[1,256,128]{2,1,0:T(8,128)S(1)} %get-tuple-element.75.field_ref.y0_ref.refs_4_), channel_id=1, source_target_pairs={{0,16},{1,2},{2,1},{3,4},{4,3},{5,6},{6,5},{7,8},{8,7},{9,10},{10,... | collective-permute-start | bytes 393224 | tf_op jit(solution)/shard_map/ppermute | solution.py:405
  18.8 6.9 %collective-permute-start.16 = (f32[1,256,128]{2,1,0:T(8,128)S(1)}, f32[1,256,128]{2,1,0:T(8,128)S(1)}, u32[]{:S(2)}, u32[]{:S(2)}) collective-permute-start(f32[1,256,128]{2,1,0:T(8,128)S(1)} %get-tuple-element.75.field_ref.y0_ref.refs_4_), channel_id=1, source_target_pairs={{0,2},{1,16},{2,4},{3,1},{4,6},{5,3},{6,8},{7,5},{8,10},{9,7},{10,... | collective-permute-start | bytes 393224 | tf_op jit(solution)/shard_map/ppermute | solution.py:405
  25.7 1.0 %collective-permute-start.17 = (f32[1,256,128]{2,1,0:T(8,128)S(1)}, f32[1,256,128]{2,1,0:T(8,128)S(1)}, u32[]{:S(2)}, u32[]{:S(2)}) collective-permute-start(f32[1,256,128]{2,1,0:T(8,128)S(1)} %get-tuple-element.75.field_ref.y0_ref.refs_4_), channel_id=1, source_target_pairs={{0,18},{1,4},{2,16},{3,6},{4,1},{5,8},{6,3},{7,10},{8,5},{9,12},{1... | collective-permute-start | bytes 393224 | tf_op jit(solution)/shard_map/ppermute | solution.py:405
  26.7 0.5 shard_map.97
  27.2 0.5 shard_map.98
  27.7 0.6 collective-permute-start.14
  28.2 0.5 collective-permute-start.4
  28.8 0.8 %collective-permute-done.16.second_ref = f32[1,256,128]{2,1,0:T(8,128)S(1)} collective-permute-done((f32[1,256,128]{2,1,0:T(8,128)S(1)}, f32[1,256,128]{2,1,0:T(8,128)S(1)}, u32[]{:S(2)}, u32[]{:S(2)}) %collective-permute-start.16) | collective-permute-done | bytes 131104 | tf_op jit(solution)/shard_map/ppermute | solution.py:405
  29.6 2.4 %collective-permute-start.5 = (f32[1,256,128]{2,1,0:T(8,128)S(1)}, f32[1,256,128]{2,1,0:T(8,128)S(1)}, u32[]{:S(2)}, u32[]{:S(2)}) collective-permute-start(f32[1,256,128]{2,1,0:T(8,128)S(1)} %get-tuple-element.64.field_ref.y0_ref.refs_8_), channel_id=1, source_target_pairs={{0,2},{1,16},{2,4},{3,1},{4,6},{5,3},{6,8},{7,5},{8,10},{9,7},{10,... | collective-permute-start | bytes 393224 | tf_op jit(solution)/shard_map/ppermute | solution.py:405
  32.1 0.9 %collective-permute-start.6 = (f32[1,256,128]{2,1,0:T(8,128)S(1)}, f32[1,256,128]{2,1,0:T(8,128)S(1)}, u32[]{:S(2)}, u32[]{:S(2)}) collective-permute-start(f32[1,256,128]{2,1,0:T(8,128)S(1)} %get-tuple-element.64.field_ref.y0_ref.refs_8_), channel_id=1, source_target_pairs={{0,18},{1,4},{2,16},{3,6},{4,1},{5,8},{6,3},{7,10},{8,5},{9,12},{1... | collective-permute-start | bytes 393224 | tf_op jit(solution)/shard_map/ppermute | solution.py:405
  33.0 0.5 shard_map.99
  33.5 0.6 collective-permute-start.20
  34.0 0.3 shard_map.100
  34.4 0.7 %shard_map.101 = (f32[8,128]{1,0:T(8,128)S(1)}, f32[7,1,256,128]{3,2,1,0:T(8,128)S(1)}, f32[7,1,256,128]{3,2,1,0:T(8,128)S(1)}) custom-call(f32[256,128]{1,0:T(8,128)S(1)} %get-tuple-element.71.diagonal_ref, f32[1,256,128]{2,1,0:T(8,128)S(1)} %get-tuple-element.68.after_ref.field_ref.y0_ref.refs_0_, ...), custom_call_target="tpu_custom_call" | custom-call | tf_op jit(solution)/shard_map/pallas_call | solution.py:366
  35.1 2.6 %collective-permute-done.5.second_ref = f32[1,256,128]{2,1,0:T(8,128)S(1)} collective-permute-done((f32[1,256,128]{2,1,0:T(8,128)S(1)}, f32[1,256,128]{2,1,0:T(8,128)S(1)}, u32[]{:S(2)}, u32[]{:S(2)}) %collective-permute-start.5) | collective-permute-done | bytes 131104 | tf_op jit(solution)/shard_map/ppermute | solution.py:405
  37.7 0.2 collective-permute-done.6.third_ref
  37.9 0.5 shard_map.102
  38.4 0.1 collective-permute-start.19
  38.5 0.5 collective-permute-start.23
  39.0 0.3 shard_map.103
  39.3 0.7 %shard_map.105 = (f32[8,128]{1,0:T(8,128)S(1)}, f32[7,1,256,128]{3,2,1,0:T(8,128)S(1)}, f32[7,1,256,128]{3,2,1,0:T(8,128)S(1)}) custom-call(f32[256,128]{1,0:T(8,128)S(1)} %get-tuple-element.71.diagonal_ref, f32[1,256,128]{2,1,0:T(8,128)S(1)} %get-tuple-element.75.field_ref.y0_ref.refs_4_, ...), custom_call_target="tpu_custom_call" | custom-call | tf_op jit(solution)/shard_map/pallas_call | solution.py:366
  40.0 0.1 collective-permute-start.22
  40.2 0.3 shard_map.104
  40.5 0.7 %shard_map.106 = (f32[8,128]{1,0:T(8,128)S(1)}, f32[7,1,256,128]{3,2,1,0:T(8,128)S(1)}, f32[7,1,256,128]{3,2,1,0:T(8,128)S(1)}) custom-call(f32[256,128]{1,0:T(8,128)S(1)} %get-tuple-element.71.diagonal_ref, f32[1,256,128]{2,1,0:T(8,128)S(1)} %get-tuple-element.64.field_ref.y0_ref.refs_8_, ...), custom_call_target="tpu_custom_call" | custom-call | tf_op jit(solution)/shard_map/pallas_call | solution.py:366
  41.2 0.5 collective-permute-start.21
  41.7 0.4 shard_map.107
  42.2 0.4 shard_map.108
  42.6 0.1 collective-permute-done.21.near_ref
  42.7 0.4 shard_map.109
  43.2 12.4 %all_to_all.5.moments_ref = f32[32,1,128]{2,1,0:T(1,128)S(1)} all-to-all(f32[32,1,128]{2,1,0:T(1,128)S(1)} %get-tuple-element.99), channel_id=1, replica_groups=mesh['diamond'=2,'tile'=16] {'diamond','tile'}, dimensions={0} | all-to-all | bytes 32768 | tf_op jit(solution)/shard_map/all_to_all | solution.py:478
  55.6 1.3 %shard_map.110 = (f32[3,256,128]{2,1,0:T(8,128)}, f32[3,256,128]{2,1,0:T(8,128)}, f32[256,128]{1,0:T(8,128)}) custom-call(f32[32,1,128]{2,1,0:T(1,128)S(1)} %all_to_all.5.moments_ref, f32[256,128]{1,0:T(8,128)S(1)} %get-tuple-element.71.diagonal_ref, f32[256,128]{1,0:T(8,128)S(1)} %get-tuple-element.100.next_ref, ...), custom_call_target="tpu_custom_call" | custom-call | tf_op jit(solution)/shard_map/pallas_call | solution.py:366
  (21 shorter events, 0.1 us)
Async XLA Ops:
  0.6 8.2 %collective-permute-start.2 = (f32[1,256,128]{2,1,0:T(8,128)}, f32[1,256,128]{2,1,0:T(8,128)S(1)}, u32[]{:S(2)}, u32[]{:S(2)}) collective-permute-start(f32[1,256,128]{2,1,0:T(8,128)} %bitcast.20), channel_id=1, source_target_pairs={{0,16},{1,2},{2,1},{3,4},{4,3},{5,6},{6,5},{7,8},{8,7},{9,10},{10,... | collective-permute-start | bytes 393224 | tf_op jit(solution)/shard_map/ppermute | solution.py:405
  3.6 7.6 %collective-permute-start.3 = (f32[1,256,128]{2,1,0:T(8,128)}, f32[1,256,128]{2,1,0:T(8,128)S(1)}, u32[]{:S(2)}, u32[]{:S(2)}) collective-permute-start(f32[1,256,128]{2,1,0:T(8,128)} %bitcast.21), channel_id=1, source_target_pairs={{0,1},{1,0},{2,3},{3,2},{4,5},{5,4},{6,7},{7,6},{8,9},{9,8},{10,11... | collective-permute-start | bytes 393224 | tf_op jit(solution)/shard_map/ppermute | solution.py:394
  3.8 3.5 %copy-start = (f32[1,1,256,128]{3,2,1,0:T(8,128)S(1)}, f32[1,1,256,128]{3,2,1,0:T(8,128)}, u32[]{:S(2)}) copy-start(f32[1,1,256,128]{3,2,1,0:T(8,128)} %param.9) | copy-start | bytes 393220
  5.6 5.9 %collective-permute-start = (f32[1,256,128]{2,1,0:T(8,128)S(1)}, f32[1,256,128]{2,1,0:T(8,128)S(1)}, u32[]{:S(2)}, u32[]{:S(2)}) collective-permute-start(f32[1,256,128]{2,1,0:T(8,128)S(1)} %bitcast.14), channel_id=1, source_target_pairs={{0,16},{1,2},{2,1},{3,4},{4,3},{5,6},{6,5},{7,8},{8,7},{9,10},{10,... | collective-permute-start | bytes 393224 | tf_op jit(solution)/shard_map/ppermute | solution.py:405
  7.1 4.4 %collective-permute-start.1 = (f32[1,256,128]{2,1,0:T(8,128)S(1)}, f32[1,256,128]{2,1,0:T(8,128)S(1)}, u32[]{:S(2)}, u32[]{:S(2)}) collective-permute-start(f32[1,256,128]{2,1,0:T(8,128)S(1)} %bitcast.15), channel_id=1, source_target_pairs={{0,1},{1,0},{2,3},{3,2},{4,5},{5,4},{6,7},{7,6},{8,9},{9,8},{10,11... | collective-permute-start | bytes 393224 | tf_op jit(solution)/shard_map/ppermute | solution.py:394
  7.3 9.4 %collective-permute-start.8 = (f32[1,256,128]{2,1,0:T(8,128)S(1)}, f32[1,256,128]{2,1,0:T(8,128)S(1)}, u32[]{:S(2)}, u32[]{:S(2)}) collective-permute-start(f32[1,256,128]{2,1,0:T(8,128)S(1)} %bitcast.23), channel_id=1, source_target_pairs={{0,2},{1,16},{2,4},{3,1},{4,6},{5,3},{6,8},{7,5},{8,10},{9,7},{10,... | collective-permute-start | bytes 393224 | tf_op jit(solution)/shard_map/ppermute | solution.py:405
  8.8 8.5 %collective-permute-start.9 = (f32[1,256,128]{2,1,0:T(8,128)S(1)}, f32[1,256,128]{2,1,0:T(8,128)S(1)}, u32[]{:S(2)}, u32[]{:S(2)}) collective-permute-start(f32[1,256,128]{2,1,0:T(8,128)S(1)} %bitcast.24), channel_id=1, source_target_pairs={{0,18},{1,4},{2,16},{3,6},{4,1},{5,8},{6,3},{7,10},{8,5},{9,12},{1... | collective-permute-start | bytes 393224 | tf_op jit(solution)/shard_map/ppermute | solution.py:405
  11.8 7.1 %collective-permute-start.10 = (f32[1,256,128]{2,1,0:T(8,128)S(1)}, f32[1,256,128]{2,1,0:T(8,128)S(1)}, u32[]{:S(2)}, u32[]{:S(2)}) collective-permute-start(f32[1,256,128]{2,1,0:T(8,128)S(1)} %get-tuple-element.68.after_ref.field_ref.y0_ref.refs_0_), channel_id=1, source_target_pairs={{0,16},{1,2},{2,1},{3,4},{4,3},{5,6},{6,5},{7,8},{8,7},{9,10},{10,... | collective-permute-start | bytes 393224 | tf_op jit(solution)/shard_map/ppermute | solution.py:405
  12.7 12.9 %collective-permute-start.11 = (f32[1,256,128]{2,1,0:T(8,128)S(1)}, f32[1,256,128]{2,1,0:T(8,128)S(1)}, u32[]{:S(2)}, u32[]{:S(2)}) collective-permute-start(f32[1,256,128]{2,1,0:T(8,128)S(1)} %get-tuple-element.68.after_ref.field_ref.y0_ref.refs_0_), channel_id=1, source_target_pairs={{0,2},{1,16},{2,4},{3,1},{4,6},{5,3},{6,8},{7,5},{8,10},{9,7},{10,... | collective-permute-start | bytes 393224 | tf_op jit(solution)/shard_map/ppermute | solution.py:405
  14.8 11.9 %collective-permute-start.12 = (f32[1,256,128]{2,1,0:T(8,128)S(1)}, f32[1,256,128]{2,1,0:T(8,128)S(1)}, u32[]{:S(2)}, u32[]{:S(2)}) collective-permute-start(f32[1,256,128]{2,1,0:T(8,128)S(1)} %get-tuple-element.68.after_ref.field_ref.y0_ref.refs_0_), channel_id=1, source_target_pairs={{0,18},{1,4},{2,16},{3,6},{4,1},{5,8},{6,3},{7,10},{8,5},{9,12},{1... | collective-permute-start | bytes 393224 | tf_op jit(solution)/shard_map/ppermute | solution.py:405
  16.7 10.5 %collective-permute-start.13 = (f32[1,256,128]{2,1,0:T(8,128)S(1)}, f32[1,256,128]{2,1,0:T(8,128)S(1)}, u32[]{:S(2)}, u32[]{:S(2)}) collective-permute-start(f32[1,256,128]{2,1,0:T(8,128)S(1)} %get-tuple-element.68.after_ref.field_ref.y0_ref.refs_0_), channel_id=1, source_target_pairs={{0,1},{1,0},{2,3},{3,2},{4,5},{5,4},{6,7},{7,6},{8,9},{9,8},{10,11... | collective-permute-start | bytes 393224 | tf_op jit(solution)/shard_map/ppermute | solution.py:394
  17.3 10.9 %collective-permute-start.15 = (f32[1,256,128]{2,1,0:T(8,128)S(1)}, f32[1,256,128]{2,1,0:T(8,128)S(1)}, u32[]{:S(2)}, u32[]{:S(2)}) collective-permute-start(f32[1,256,128]{2,1,0:T(8,128)S(1)} %get-tuple-element.75.field_ref.y0_ref.refs_4_), channel_id=1, source_target_pairs={{0,16},{1,2},{2,1},{3,4},{4,3},{5,6},{6,5},{7,8},{8,7},{9,10},{10,... | collective-permute-start | bytes 393224 | tf_op jit(solution)/shard_map/ppermute | solution.py:405
  18.8 10.8 %collective-permute-start.16 = (f32[1,256,128]{2,1,0:T(8,128)S(1)}, f32[1,256,128]{2,1,0:T(8,128)S(1)}, u32[]{:S(2)}, u32[]{:S(2)}) collective-permute-start(f32[1,256,128]{2,1,0:T(8,128)S(1)} %get-tuple-element.75.field_ref.y0_ref.refs_4_), channel_id=1, source_target_pairs={{0,2},{1,16},{2,4},{3,1},{4,6},{5,3},{6,8},{7,5},{8,10},{9,7},{10,... | collective-permute-start | bytes 393224 | tf_op jit(solution)/shard_map/ppermute | solution.py:405
  25.7 6.4 %collective-permute-start.17 = (f32[1,256,128]{2,1,0:T(8,128)S(1)}, f32[1,256,128]{2,1,0:T(8,128)S(1)}, u32[]{:S(2)}, u32[]{:S(2)}) collective-permute-start(f32[1,256,128]{2,1,0:T(8,128)S(1)} %get-tuple-element.75.field_ref.y0_ref.refs_4_), channel_id=1, source_target_pairs={{0,18},{1,4},{2,16},{3,6},{4,1},{5,8},{6,3},{7,10},{8,5},{9,12},{1... | collective-permute-start | bytes 393224 | tf_op jit(solution)/shard_map/ppermute | solution.py:405
  26.7 6.3 %collective-permute-start.18 = (f32[1,256,128]{2,1,0:T(8,128)S(1)}, f32[1,256,128]{2,1,0:T(8,128)S(1)}, u32[]{:S(2)}, u32[]{:S(2)}) collective-permute-start(f32[1,256,128]{2,1,0:T(8,128)S(1)} %get-tuple-element.75.field_ref.y0_ref.refs_4_), channel_id=1, source_target_pairs={{0,1},{1,0},{2,3},{3,2},{4,5},{5,4},{6,7},{7,6},{8,9},{9,8},{10,11... | collective-permute-start | bytes 393224 | tf_op jit(solution)/shard_map/ppermute | solution.py:394
  27.7 5.8 %collective-permute-start.14 = (f32[1,256,128]{2,1,0:T(8,128)S(1)}, f32[1,256,128]{2,1,0:T(8,128)S(1)}, u32[]{:S(2)}, u32[]{:S(2)}) collective-permute-start(f32[1,256,128]{2,1,0:T(8,128)S(1)} %get-tuple-element.72.after_ref.field_ref.y1_ref.refs_1_), channel_id=1, source_target_pairs={{0,1},{1,0},{2,3},{3,2},{4,5},{5,4},{6,7},{7,6},{8,9},{9,8},{10,11... | collective-permute-start | bytes 393224 | tf_op jit(solution)/shard_map/ppermute | solution.py:394
  28.2 6.8 %collective-permute-start.4 = (f32[1,256,128]{2,1,0:T(8,128)S(1)}, f32[1,256,128]{2,1,0:T(8,128)S(1)}, u32[]{:S(2)}, u32[]{:S(2)}) collective-permute-start(f32[1,256,128]{2,1,0:T(8,128)S(1)} %get-tuple-element.64.field_ref.y0_ref.refs_8_), channel_id=1, source_target_pairs={{0,16},{1,2},{2,1},{3,4},{4,3},{5,6},{6,5},{7,8},{8,7},{9,10},{10,... | collective-permute-start | bytes 393224 | tf_op jit(solution)/shard_map/ppermute | solution.py:405
  29.6 8.1 %collective-permute-start.5 = (f32[1,256,128]{2,1,0:T(8,128)S(1)}, f32[1,256,128]{2,1,0:T(8,128)S(1)}, u32[]{:S(2)}, u32[]{:S(2)}) collective-permute-start(f32[1,256,128]{2,1,0:T(8,128)S(1)} %get-tuple-element.64.field_ref.y0_ref.refs_8_), channel_id=1, source_target_pairs={{0,2},{1,16},{2,4},{3,1},{4,6},{5,3},{6,8},{7,5},{8,10},{9,7},{10,... | collective-permute-start | bytes 393224 | tf_op jit(solution)/shard_map/ppermute | solution.py:405
  32.1 5.9 %collective-permute-start.6 = (f32[1,256,128]{2,1,0:T(8,128)S(1)}, f32[1,256,128]{2,1,0:T(8,128)S(1)}, u32[]{:S(2)}, u32[]{:S(2)}) collective-permute-start(f32[1,256,128]{2,1,0:T(8,128)S(1)} %get-tuple-element.64.field_ref.y0_ref.refs_8_), channel_id=1, source_target_pairs={{0,18},{1,4},{2,16},{3,6},{4,1},{5,8},{6,3},{7,10},{8,5},{9,12},{1... | collective-permute-start | bytes 393224 | tf_op jit(solution)/shard_map/ppermute | solution.py:405
  33.0 4.9 %collective-permute-start.7 = (f32[1,256,128]{2,1,0:T(8,128)S(1)}, f32[1,256,128]{2,1,0:T(8,128)S(1)}, u32[]{:S(2)}, u32[]{:S(2)}) collective-permute-start(f32[1,256,128]{2,1,0:T(8,128)S(1)} %get-tuple-element.64.field_ref.y0_ref.refs_8_), channel_id=1, source_target_pairs={{0,1},{1,0},{2,3},{3,2},{4,5},{5,4},{6,7},{7,6},{8,9},{9,8},{10,11... | collective-permute-start | bytes 393224 | tf_op jit(solution)/shard_map/ppermute | solution.py:394
  33.5 5.5 %collective-permute-start.20 = (f32[1,256,128]{2,1,0:T(8,128)S(1)}, f32[1,256,128]{2,1,0:T(8,128)S(1)}, u32[]{:S(2)}, u32[]{:S(2)}) collective-permute-start(f32[1,256,128]{2,1,0:T(8,128)S(1)} %get-tuple-element.76.after_ref.field_ref.y1_ref.refs_5_), channel_id=1, source_target_pairs={{0,1},{1,0},{2,3},{3,2},{4,5},{5,4},{6,7},{7,6},{8,9},{9,8},{10,11... | collective-permute-start | bytes 393224 | tf_op jit(solution)/shard_map/ppermute | solution.py:394
  38.4 1.8 %collective-permute-start.19 = (f32[1,256,128]{2,1,0:T(8,128)S(1)}, f32[1,256,128]{2,1,0:T(8,128)S(1)}, u32[]{:S(2)}, u32[]{:S(2)}) collective-permute-start(f32[1,256,128]{2,1,0:T(8,128)S(1)} %get-tuple-element.81.after_ref.field_ref.y1_ref.refs_9_), channel_id=1, source_target_pairs={{0,1},{1,0},{2,3},{3,2},{4,5},{5,4},{6,7},{7,6},{8,9},{9,8},{10,11... | collective-permute-start | bytes 393224 | tf_op jit(solution)/shard_map/ppermute | solution.py:394
  38.5 3.2 %collective-permute-start.23 = (f32[1,256,128]{2,1,0:T(8,128)S(1)}, f32[1,256,128]{2,1,0:T(8,128)S(1)}, u32[]{:S(2)}, u32[]{:S(2)}) collective-permute-start(f32[1,256,128]{2,1,0:T(8,128)S(1)} %get-tuple-element.77.y2_ref.field_ref.refs_2_), channel_id=1, source_target_pairs={{0,1},{1,0},{2,3},{3,2},{4,5},{5,4},{6,7},{7,6},{8,9},{9,8},{10,11... | collective-permute-start | bytes 393224 | tf_op jit(solution)/shard_map/ppermute | solution.py:394
  40.0 2.1 %collective-permute-start.22 = (f32[1,256,128]{2,1,0:T(8,128)S(1)}, f32[1,256,128]{2,1,0:T(8,128)S(1)}, u32[]{:S(2)}, u32[]{:S(2)}) collective-permute-start(f32[1,256,128]{2,1,0:T(8,128)S(1)} %get-tuple-element.84.after_ref.y2_ref.field_ref.refs_6_), channel_id=1, source_target_pairs={{0,1},{1,0},{2,3},{3,2},{4,5},{5,4},{6,7},{7,6},{8,9},{9,8},{10,11... | collective-permute-start | bytes 393224 | tf_op jit(solution)/shard_map/ppermute | solution.py:394
  41.2 1.5 %collective-permute-start.21 = (f32[1,256,128]{2,1,0:T(8,128)S(1)}, f32[1,256,128]{2,1,0:T(8,128)S(1)}, u32[]{:S(2)}, u32[]{:S(2)}) collective-permute-start(f32[1,256,128]{2,1,0:T(8,128)S(1)} %get-tuple-element.86.y2_ref.field_ref.refs_10_), channel_id=1, source_target_pairs={{0,1},{1,0},{2,3},{3,2},{4,5},{5,4},{6,7},{7,6},{8,9},{9,8},{10,11... | collective-permute-start | bytes 393224 | tf_op jit(solution)/shard_map/ppermute | solution.py:394

commit v8 on v3

--- a/solution.py
+++ b/solution.py
@@ -12,7 +12,7 @@
 DIFFUSION = 1.0
 MASS_TERM = 0.5
 BUOYANCY = 1.0
-CENTERS = (0.0, 0.45, -0.45, 0.75, -0.75, 0.95, -0.95)
+CENTERS = (1.0, 0.55, 1.45, 0.25, 1.75, 0.05, 1.95)
 CHUNK = 32
 SPLITS = ((0, 1), (1, 2), (2, 3))
 
@@ -141,7 +141,7 @@
     here = slice(start, start + CHUNK)
     mid, after, before = rows_around(lambda a, b: field_ref[at, a:b], start, field_ref.shape[1])
     around = [near_ref[at, here], moved_ref[at, here], after, before, *layers_around(mid)]
-    return sum(w * v for w, v in zip(weights, around))
+    return mid - sum(w * v for w, v in zip(weights, around))
 
 
 def apply_kernel(far_ref, near_ref, field_ref, weights_ref, matrix_ref, out_ref, moved_ref):
@@ -253,9 +253,9 @@
 
 def recurrence(moments, centers):
     def operator(poly):
-        result = [(1.0 - centers) * a for a in poly] + [jnp.zeros_like(centers)]
+        result = [centers * a for a in poly] + [jnp.zeros_like(centers)]
         for i, a in enumerate(poly):
-            result[i + 1] = result[i + 1] - a
+            result[i + 1] = result[i + 1] + a
         return result
 
     one = jnp.ones_like(centers)

time: 50.5 us -> 50.5 us (level)
  no operation moved by 1% of the time
where the time goes in v8:
time: 50.5 us; the launch traced here: 50.3 us
  starting transfers between devices  26.6 us (53%)
  blocking collectives  13.9 us (28%)
  Pallas kernels  9.04 us (18%)
  between operations  0.72 us (1%)
    ppermute x11, starting transfers between devices, exchange(): far = lax.ppermute(value, NAMES, across)  18.3 us
    all_to_all x1, blocking collectives, body(): moments = lax.all_to_all(moments, NAMES, 0, 0)  13.9 us
    pallas_call x14, Pallas kernels, call(): pl.pallas_call(kernel, out_shape=outs, in_specs=[pl.BlockSpec(memory_spac...  9.04 us
    ppermute x11, starting transfers between devices, exchange(): near = lax.ppermute(value, NAMES, beside)  8.25 us
  transfers between devices with their start and end apart: 22, of which 0 were waited for; matrix products, arithmetic and copies ran while one was open for 0% of the time, Pallas kernels for 15%

profile of v8, /device:TPU:0, one launch (start us, length us, event | category | flops | bytes accessed | tf_op | source)
XLA Modules:
  0.0 50.3 jit_solution(6942977613873646380)
XLA Ops:
  0.6 3.0 %collective-permute-start.2 = (f32[1,256,128]{2,1,0:T(8,128)}, f32[1,256,128]{2,1,0:T(8,128)S(1)}, u32[]{:S(2)}, u32[]{:S(2)}) collective-permute-start(f32[1,256,128]{2,1,0:T(8,128)} %bitcast.20), channel_id=1, source_target_pairs={{0,16},{1,2},{2,1},{3,4},{4,3},{5,6},{6,5},{7,8},{8,7},{9,10},{10,... | collective-permute-start | bytes 393224 | tf_op jit(solution)/shard_map/ppermute | solution.py:351
  3.6 0.1 collective-permute-start.3
  3.8 1.7 %shard_map.94 = (f32[256,128]{1,0:T(8,128)S(1)}, f32[4,256,128]{2,1,0:T(8,128)S(1)}, f32[256,128]{1,0:T(8,128)S(1)}, f32[3,256,128]{2,1,0:T(8,128)S(1)}, f32[256...) custom-call(f32[256,128]{1,0:T(8,128)} %bitcast.18, ...), custom_call_target="tpu_custom_call" | custom-call | tf_op jit(solution)/shard_map/pallas_call | solution.py:323
  5.4 1.6 %collective-permute-start = (f32[1,256,128]{2,1,0:T(8,128)S(1)}, f32[1,256,128]{2,1,0:T(8,128)S(1)}, u32[]{:S(2)}, u32[]{:S(2)}) collective-permute-start(f32[1,256,128]{2,1,0:T(8,128)S(1)} %bitcast.14), channel_id=1, source_target_pairs={{0,16},{1,2},{2,1},{3,4},{4,3},{5,6},{6,5},{7,8},{8,7},{9,10},{10,... | collective-permute-start | bytes 393224 | tf_op jit(solution)/shard_map/ppermute | solution.py:351
  7.0 0.1 collective-permute-start.1
  7.1 0.0 collective-permute-done.2.far_ref
  7.1 0.0 collective-permute-done.3.near_ref
  7.1 0.3 shard_map.95
  7.4 1.7 %collective-permute-start.16 = (f32[1,256,128]{2,1,0:T(8,128)S(1)}, f32[1,256,128]{2,1,0:T(8,128)S(1)}, u32[]{:S(2)}, u32[]{:S(2)}) collective-permute-start(f32[1,256,128]{2,1,0:T(8,128)S(1)} %get-tuple-element.41.field_ref.refs_0_), channel_id=1, source_target_pairs={{0,16},{1,2},{2,1},{3,4},{4,3},{5,6},{6,5},{7,8},{8,7},{9,10},{10,... | collective-permute-start | bytes 393224 | tf_op jit(solution)/shard_map/ppermute | solution.py:351
  9.2 1.0 %collective-permute-start.17 = (f32[1,256,128]{2,1,0:T(8,128)S(1)}, f32[1,256,128]{2,1,0:T(8,128)S(1)}, u32[]{:S(2)}, u32[]{:S(2)}) collective-permute-start(f32[1,256,128]{2,1,0:T(8,128)S(1)} %get-tuple-element.41.field_ref.refs_0_), channel_id=1, source_target_pairs={{0,1},{1,0},{2,3},{3,2},{4,5},{5,4},{6,7},{7,6},{8,9},{9,8},{10,11... | collective-permute-start | bytes 393224 | tf_op jit(solution)/shard_map/ppermute | solution.py:352
  10.1 1.5 %collective-permute-start.10 = (f32[1,256,128]{2,1,0:T(8,128)S(1)}, f32[1,256,128]{2,1,0:T(8,128)S(1)}, u32[]{:S(2)}, u32[]{:S(2)}) collective-permute-start(f32[1,256,128]{2,1,0:T(8,128)S(1)} %get-tuple-element.40.field_ref.refs_3_.refs_4_), channel_id=1, source_target_pairs={{0,16},{1,2},{2,1},{3,4},{4,3},{5,6},{6,5},{7,8},{8,7},{9,10},{10,... | collective-permute-start | bytes 393224 | tf_op jit(solution)/shard_map/ppermute | solution.py:351
  11.6 0.0 collective-permute-done.far_ref
  11.6 0.0 collective-permute-start.11
  11.6 0.0 collective-permute-done.1.near_ref
  11.6 0.9 %shard_map.96 = (f32[256,128]{1,0:T(8,128)}, f32[1,256,128]{2,1,0:T(8,128)S(1)}) custom-call(f32[1,256,128]{2,1,0:T(8,128)S(1)} %collective-permute-done.far_ref, f32[1,256,128]{2,1,0:T(8,128)S(1)} %collective-permute-done.1.near_ref, f32[3,256,128]{2,1,0:T(8,128)S(1)} %get-tuple-element.30.right_ref, f32[256,128]{1,0:T(8,128)S(1)} %get-tuple-element.31.part_ref, ...), custom_call_target="tpu_custom_call" | custom-call | tf_op jit(solution)/shard_map/pallas_call | solution.py:323
  12.5 1.2 %collective-permute-start.4 = (f32[1,256,128]{2,1,0:T(8,128)S(1)}, f32[1,256,128]{2,1,0:T(8,128)S(1)}, u32[]{:S(2)}, u32[]{:S(2)}) collective-permute-start(f32[1,256,128]{2,1,0:T(8,128)S(1)} %get-tuple-element.38.field_ref.refs_6_.refs_8_), channel_id=1, source_target_pairs={{0,16},{1,2},{2,1},{3,4},{4,3},{5,6},{6,5},{7,8},{8,7},{9,10},{10,... | collective-permute-start | bytes 393224 | tf_op jit(solution)/shard_map/ppermute | solution.py:351
  13.8 0.0 collective-permute-done.16.far_ref
  13.8 1.1 %collective-permute-start.5 = (f32[1,256,128]{2,1,0:T(8,128)S(1)}, f32[1,256,128]{2,1,0:T(8,128)S(1)}, u32[]{:S(2)}, u32[]{:S(2)}) collective-permute-start(f32[1,256,128]{2,1,0:T(8,128)S(1)} %get-tuple-element.38.field_ref.refs_6_.refs_8_), channel_id=1, source_target_pairs={{0,1},{1,0},{2,3},{3,2},{4,5},{5,4},{6,7},{7,6},{8,9},{9,8},{10,11... | collective-permute-start | bytes 393224 | tf_op jit(solution)/shard_map/ppermute | solution.py:352
  14.9 0.3 shard_map.101.field_ref.refs_1_
  15.1 1.6 %collective-permute-start.18 = (f32[1,256,128]{2,1,0:T(8,128)S(1)}, f32[1,256,128]{2,1,0:T(8,128)S(1)}, u32[]{:S(2)}, u32[]{:S(2)}) collective-permute-start(f32[1,256,128]{2,1,0:T(8,128)S(1)} %shard_map.101.field_ref.refs_1_), channel_id=1, source_target_pairs={{0,16},{1,2},{2,1},{3,4},{4,3},{5,6},{6,5},{7,8},{8,7},{9,10},{10,... | collective-permute-start | bytes 393224 | tf_op jit(solution)/shard_map/ppermute | solution.py:351
  16.7 1.0 %collective-permute-start.19 = (f32[1,256,128]{2,1,0:T(8,128)S(1)}, f32[1,256,128]{2,1,0:T(8,128)S(1)}, u32[]{:S(2)}, u32[]{:S(2)}) collective-permute-start(f32[1,256,128]{2,1,0:T(8,128)S(1)} %shard_map.101.field_ref.refs_1_), channel_id=1, source_target_pairs={{0,1},{1,0},{2,3},{3,2},{4,5},{5,4},{6,7},{7,6},{8,9},{9,8},{10,11... | collective-permute-start | bytes 393224 | tf_op jit(solution)/shard_map/ppermute | solution.py:352
  17.7 0.0 collective-permute-done.11.near_ref
  17.7 0.3 shard_map.99.field_ref.refs_4_.refs_5_
  18.0 1.6 %collective-permute-start.12 = (f32[1,256,128]{2,1,0:T(8,128)S(1)}, f32[1,256,128]{2,1,0:T(8,128)S(1)}, u32[]{:S(2)}, u32[]{:S(2)}) collective-permute-start(f32[1,256,128]{2,1,0:T(8,128)S(1)} %shard_map.99.field_ref.refs_4_.refs_5_), channel_id=1, source_target_pairs={{0,16},{1,2},{2,1},{3,4},{4,3},{5,6},{6,5},{7,8},{8,7},{9,10},{10,... | collective-permute-start | bytes 393224 | tf_op jit(solution)/shard_map/ppermute | solution.py:351
  19.5 1.0 %collective-permute-start.13 = (f32[1,256,128]{2,1,0:T(8,128)S(1)}, f32[1,256,128]{2,1,0:T(8,128)S(1)}, u32[]{:S(2)}, u32[]{:S(2)}) collective-permute-start(f32[1,256,128]{2,1,0:T(8,128)S(1)} %shard_map.99.field_ref.refs_4_.refs_5_), channel_id=1, source_target_pairs={{0,1},{1,0},{2,3},{3,2},{4,5},{5,4},{6,7},{7,6},{8,9},{9,8},{10,11... | collective-permute-start | bytes 393224 | tf_op jit(solution)/shard_map/ppermute | solution.py:352
  20.5 0.3 shard_map.97.field_ref.refs_7_.refs_9_
  20.8 1.6 %collective-permute-start.6 = (f32[1,256,128]{2,1,0:T(8,128)S(1)}, f32[1,256,128]{2,1,0:T(8,128)S(1)}, u32[]{:S(2)}, u32[]{:S(2)}) collective-permute-start(f32[1,256,128]{2,1,0:T(8,128)S(1)} %shard_map.97.field_ref.refs_7_.refs_9_), channel_id=1, source_target_pairs={{0,16},{1,2},{2,1},{3,4},{4,3},{5,6},{6,5},{7,8},{8,7},{9,10},{10,... | collective-permute-start | bytes 393224 | tf_op jit(solution)/shard_map/ppermute | solution.py:351
  22.3 0.0 collective-permute-start.7
  22.4 0.3 shard_map.102.refs_2_.field_ref
  22.6 1.6 %collective-permute-start.20 = (f32[1,256,128]{2,1,0:T(8,128)S(1)}, f32[1,256,128]{2,1,0:T(8,128)S(1)}, u32[]{:S(2)}, u32[]{:S(2)}) collective-permute-start(f32[1,256,128]{2,1,0:T(8,128)S(1)} %shard_map.102.refs_2_.field_ref), channel_id=1, source_target_pairs={{0,16},{1,2},{2,1},{3,4},{4,3},{5,6},{6,5},{7,8},{8,7},{9,10},{10,... | collective-permute-start | bytes 393224 | tf_op jit(solution)/shard_map/ppermute | solution.py:351
  24.2 1.9 %collective-permute-start.21 = (f32[1,256,128]{2,1,0:T(8,128)S(1)}, f32[1,256,128]{2,1,0:T(8,128)S(1)}, u32[]{:S(2)}, u32[]{:S(2)}) collective-permute-start(f32[1,256,128]{2,1,0:T(8,128)S(1)} %shard_map.102.refs_2_.field_ref), channel_id=1, source_target_pairs={{0,1},{1,0},{2,3},{3,2},{4,5},{5,4},{6,7},{7,6},{8,9},{9,8},{10,11... | collective-permute-start | bytes 393224 | tf_op jit(solution)/shard_map/ppermute | solution.py:352
  26.1 0.0 collective-permute-done.13.near_ref
  26.1 0.3 shard_map.100.refs_5_.field_ref.refs_6_
  26.4 1.6 %collective-permute-start.14 = (f32[1,256,128]{2,1,0:T(8,128)S(1)}, f32[1,256,128]{2,1,0:T(8,128)S(1)}, u32[]{:S(2)}, u32[]{:S(2)}) collective-permute-start(f32[1,256,128]{2,1,0:T(8,128)S(1)} %shard_map.100.refs_5_.field_ref.refs_6_), channel_id=1, source_target_pairs={{0,16},{1,2},{2,1},{3,4},{4,3},{5,6},{6,5},{7,8},{8,7},{9,10},{10,... | collective-permute-start | bytes 393224 | tf_op jit(solution)/shard_map/ppermute | solution.py:351
  27.9 0.0 collective-permute-done.6.far_ref
  27.9 1.0 %collective-permute-start.15 = (f32[1,256,128]{2,1,0:T(8,128)S(1)}, f32[1,256,128]{2,1,0:T(8,128)S(1)}, u32[]{:S(2)}, u32[]{:S(2)}) collective-permute-start(f32[1,256,128]{2,1,0:T(8,128)S(1)} %shard_map.100.refs_5_.field_ref.refs_6_), channel_id=1, source_target_pairs={{0,1},{1,0},{2,3},{3,2},{4,5},{5,4},{6,7},{7,6},{8,9},{9,8},{10,11... | collective-permute-start | bytes 393224 | tf_op jit(solution)/shard_map/ppermute | solution.py:352
  28.9 0.3 shard_map.98.refs_8_.field_ref.refs_10_
  29.2 1.6 %collective-permute-start.8 = (f32[1,256,128]{2,1,0:T(8,128)S(1)}, f32[1,256,128]{2,1,0:T(8,128)S(1)}, u32[]{:S(2)}, u32[]{:S(2)}) collective-permute-start(f32[1,256,128]{2,1,0:T(8,128)S(1)} %shard_map.98.refs_8_.field_ref.refs_10_), channel_id=1, source_target_pairs={{0,16},{1,2},{2,1},{3,4},{4,3},{5,6},{6,5},{7,8},{8,7},{9,10},{10,... | collective-permute-start | bytes 393224 | tf_op jit(solution)/shard_map/ppermute | solution.py:351
  30.7 1.0 %collective-permute-start.9 = (f32[1,256,128]{2,1,0:T(8,128)S(1)}, f32[1,256,128]{2,1,0:T(8,128)S(1)}, u32[]{:S(2)}, u32[]{:S(2)}) collective-permute-start(f32[1,256,128]{2,1,0:T(8,128)S(1)} %shard_map.98.refs_8_.field_ref.refs_10_), channel_id=1, source_target_pairs={{0,1},{1,0},{2,3},{3,2},{4,5},{5,4},{6,7},{7,6},{8,9},{9,8},{10,11... | collective-permute-start | bytes 393224 | tf_op jit(solution)/shard_map/ppermute | solution.py:352
  31.7 2.0 %shard_map.103 = (f32[8,128]{1,0:T(8,128)S(1)}, f32[7,3,256,128]{3,2,1,0:T(8,128)S(1)}, f32[7,3,256,128]{3,2,1,0:T(8,128)S(1)}) custom-call(f32[256,128]{1,0:T(8,128)S(1)} %get-tuple-element.42.diagonal_ref, f32[1,256,128]{2,1,0:T(8,128)S(1)} %get-tuple-element.41.field_ref.refs_0_, f32[1,256,128]{2,1,0:T(8,128)S(1)} %shard_map.101.field_ref.refs_1_, ...), custom_call_target="tpu_custom_call" | custom-call | tf_op jit(solution)/shard_map/pallas_call | solution.py:323
  33.8 0.5 shard_map.104
  34.2 0.0 collective-permute-done.14.far_ref
  34.2 0.0 collective-permute-done.15.near_ref
  34.2 0.5 shard_map.105
  34.7 0.0 collective-permute-done.8.far_ref
  34.7 0.5 shard_map.106
  35.2 13.9 %all_to_all.5.moments_ref = f32[32,1,128]{2,1,0:T(1,128)S(1)} all-to-all(f32[32,1,128]{2,1,0:T(1,128)S(1)} %get-tuple-element.48), channel_id=1, replica_groups=mesh['diamond'=2,'tile'=16] {'diamond','tile'}, dimensions={0} | all-to-all | bytes 32768 | tf_op jit(solution)/shard_map/all_to_all | solution.py:401
  49.0 1.2 %shard_map.107 = (f32[3,256,128]{2,1,0:T(8,128)}, f32[3,256,128]{2,1,0:T(8,128)}) custom-call(f32[32,1,128]{2,1,0:T(1,128)S(1)} %all_to_all.5.moments_ref, f32[256,128]{1,0:T(8,128)S(1)} %get-tuple-element.42.diagonal_ref, f32[1,256,128]{2,1,0:T(8,128)S(1)} %get-tuple-element.41.field_ref.refs_0_, f32[1,256,128]{2,1,0:T(8,128)S(1)} %shard_map.101.field_ref.refs_1_, ...), custom_call_target="tpu_custom_call" | custom-call | tf_op jit(solution)/shard_map/pallas_call | solution.py:323
  (11 shorter events, 0.0 us)
Async XLA Ops:
  0.6 6.5 %collective-permute-start.2 = (f32[1,256,128]{2,1,0:T(8,128)}, f32[1,256,128]{2,1,0:T(8,128)S(1)}, u32[]{:S(2)}, u32[]{:S(2)}) collective-permute-start(f32[1,256,128]{2,1,0:T(8,128)} %bitcast.20), channel_id=1, source_target_pairs={{0,16},{1,2},{2,1},{3,4},{4,3},{5,6},{6,5},{7,8},{8,7},{9,10},{10,... | collective-permute-start | bytes 393224 | tf_op jit(solution)/shard_map/ppermute | solution.py:351
  3.6 3.5 %collective-permute-start.3 = (f32[1,256,128]{2,1,0:T(8,128)}, f32[1,256,128]{2,1,0:T(8,128)S(1)}, u32[]{:S(2)}, u32[]{:S(2)}) collective-permute-start(f32[1,256,128]{2,1,0:T(8,128)} %bitcast.21), channel_id=1, source_target_pairs={{0,1},{1,0},{2,3},{3,2},{4,5},{5,4},{6,7},{7,6},{8,9},{9,8},{10,11... | collective-permute-start | bytes 393224 | tf_op jit(solution)/shard_map/ppermute | solution.py:352
  5.4 6.2 %collective-permute-start = (f32[1,256,128]{2,1,0:T(8,128)S(1)}, f32[1,256,128]{2,1,0:T(8,128)S(1)}, u32[]{:S(2)}, u32[]{:S(2)}) collective-permute-start(f32[1,256,128]{2,1,0:T(8,128)S(1)} %bitcast.14), channel_id=1, source_target_pairs={{0,16},{1,2},{2,1},{3,4},{4,3},{5,6},{6,5},{7,8},{8,7},{9,10},{10,... | collective-permute-start | bytes 393224 | tf_op jit(solution)/shard_map/ppermute | solution.py:351
  7.0 4.6 %collective-permute-start.1 = (f32[1,256,128]{2,1,0:T(8,128)S(1)}, f32[1,256,128]{2,1,0:T(8,128)S(1)}, u32[]{:S(2)}, u32[]{:S(2)}) collective-permute-start(f32[1,256,128]{2,1,0:T(8,128)S(1)} %bitcast.15), channel_id=1, source_target_pairs={{0,1},{1,0},{2,3},{3,2},{4,5},{5,4},{6,7},{7,6},{8,9},{9,8},{10,11... | collective-permute-start | bytes 393224 | tf_op jit(solution)/shard_map/ppermute | solution.py:352
  7.4 6.3 %collective-permute-start.16 = (f32[1,256,128]{2,1,0:T(8,128)S(1)}, f32[1,256,128]{2,1,0:T(8,128)S(1)}, u32[]{:S(2)}, u32[]{:S(2)}) collective-permute-start(f32[1,256,128]{2,1,0:T(8,128)S(1)} %get-tuple-element.41.field_ref.refs_0_), channel_id=1, source_target_pairs={{0,16},{1,2},{2,1},{3,4},{4,3},{5,6},{6,5},{7,8},{8,7},{9,10},{10,... | collective-permute-start | bytes 393224 | tf_op jit(solution)/shard_map/ppermute | solution.py:351
  9.2 5.7 %collective-permute-start.17 = (f32[1,256,128]{2,1,0:T(8,128)S(1)}, f32[1,256,128]{2,1,0:T(8,128)S(1)}, u32[]{:S(2)}, u32[]{:S(2)}) collective-permute-start(f32[1,256,128]{2,1,0:T(8,128)S(1)} %get-tuple-element.41.field_ref.refs_0_), channel_id=1, source_target_pairs={{0,1},{1,0},{2,3},{3,2},{4,5},{5,4},{6,7},{7,6},{8,9},{9,8},{10,11... | collective-permute-start | bytes 393224 | tf_op jit(solution)/shard_map/ppermute | solution.py:352
  10.1 6.5 %collective-permute-start.10 = (f32[1,256,128]{2,1,0:T(8,128)S(1)}, f32[1,256,128]{2,1,0:T(8,128)S(1)}, u32[]{:S(2)}, u32[]{:S(2)}) collective-permute-start(f32[1,256,128]{2,1,0:T(8,128)S(1)} %get-tuple-element.40.field_ref.refs_3_.refs_4_), channel_id=1, source_target_pairs={{0,16},{1,2},{2,1},{3,4},{4,3},{5,6},{6,5},{7,8},{8,7},{9,10},{10,... | collective-permute-start | bytes 393224 | tf_op jit(solution)/shard_map/ppermute | solution.py:351
  11.6 6.1 %collective-permute-start.11 = (f32[1,256,128]{2,1,0:T(8,128)S(1)}, f32[1,256,128]{2,1,0:T(8,128)S(1)}, u32[]{:S(2)}, u32[]{:S(2)}) collective-permute-start(f32[1,256,128]{2,1,0:T(8,128)S(1)} %get-tuple-element.40.field_ref.refs_3_.refs_4_), channel_id=1, source_target_pairs={{0,1},{1,0},{2,3},{3,2},{4,5},{5,4},{6,7},{7,6},{8,9},{9,8},{10,11... | collective-permute-start | bytes 393224 | tf_op jit(solution)/shard_map/ppermute | solution.py:352
  12.5 7.0 %collective-permute-start.4 = (f32[1,256,128]{2,1,0:T(8,128)S(1)}, f32[1,256,128]{2,1,0:T(8,128)S(1)}, u32[]{:S(2)}, u32[]{:S(2)}) collective-permute-start(f32[1,256,128]{2,1,0:T(8,128)S(1)} %get-tuple-element.38.field_ref.refs_6_.refs_8_), channel_id=1, source_target_pairs={{0,16},{1,2},{2,1},{3,4},{4,3},{5,6},{6,5},{7,8},{8,7},{9,10},{10,... | collective-permute-start | bytes 393224 | tf_op jit(solution)/shard_map/ppermute | solution.py:351
  13.8 6.7 %collective-permute-start.5 = (f32[1,256,128]{2,1,0:T(8,128)S(1)}, f32[1,256,128]{2,1,0:T(8,128)S(1)}, u32[]{:S(2)}, u32[]{:S(2)}) collective-permute-start(f32[1,256,128]{2,1,0:T(8,128)S(1)} %get-tuple-element.38.field_ref.refs_6_.refs_8_), channel_id=1, source_target_pairs={{0,1},{1,0},{2,3},{3,2},{4,5},{5,4},{6,7},{7,6},{8,9},{9,8},{10,11... | collective-permute-start | bytes 393224 | tf_op jit(solution)/shard_map/ppermute | solution.py:352
  15.1 7.2 %collective-permute-start.18 = (f32[1,256,128]{2,1,0:T(8,128)S(1)}, f32[1,256,128]{2,1,0:T(8,128)S(1)}, u32[]{:S(2)}, u32[]{:S(2)}) collective-permute-start(f32[1,256,128]{2,1,0:T(8,128)S(1)} %shard_map.101.field_ref.refs_1_), channel_id=1, source_target_pairs={{0,16},{1,2},{2,1},{3,4},{4,3},{5,6},{6,5},{7,8},{8,7},{9,10},{10,... | collective-permute-start | bytes 393224 | tf_op jit(solution)/shard_map/ppermute | solution.py:351
  16.7 5.7 %collective-permute-start.19 = (f32[1,256,128]{2,1,0:T(8,128)S(1)}, f32[1,256,128]{2,1,0:T(8,128)S(1)}, u32[]{:S(2)}, u32[]{:S(2)}) collective-permute-start(f32[1,256,128]{2,1,0:T(8,128)S(1)} %shard_map.101.field_ref.refs_1_), channel_id=1, source_target_pairs={{0,1},{1,0},{2,3},{3,2},{4,5},{5,4},{6,7},{7,6},{8,9},{9,8},{10,11... | collective-permute-start | bytes 393224 | tf_op jit(solution)/shard_map/ppermute | solution.py:352
  18.0 6.2 %collective-permute-start.12 = (f32[1,256,128]{2,1,0:T(8,128)S(1)}, f32[1,256,128]{2,1,0:T(8,128)S(1)}, u32[]{:S(2)}, u32[]{:S(2)}) collective-permute-start(f32[1,256,128]{2,1,0:T(8,128)S(1)} %shard_map.99.field_ref.refs_4_.refs_5_), channel_id=1, source_target_pairs={{0,16},{1,2},{2,1},{3,4},{4,3},{5,6},{6,5},{7,8},{8,7},{9,10},{10,... | collective-permute-start | bytes 393224 | tf_op jit(solution)/shard_map/ppermute | solution.py:351
  19.5 6.6 %collective-permute-start.13 = (f32[1,256,128]{2,1,0:T(8,128)S(1)}, f32[1,256,128]{2,1,0:T(8,128)S(1)}, u32[]{:S(2)}, u32[]{:S(2)}) collective-permute-start(f32[1,256,128]{2,1,0:T(8,128)S(1)} %shard_map.99.field_ref.refs_4_.refs_5_), channel_id=1, source_target_pairs={{0,1},{1,0},{2,3},{3,2},{4,5},{5,4},{6,7},{7,6},{8,9},{9,8},{10,11... | collective-permute-start | bytes 393224 | tf_op jit(solution)/shard_map/ppermute | solution.py:352
  20.8 7.2 %collective-permute-start.6 = (f32[1,256,128]{2,1,0:T(8,128)S(1)}, f32[1,256,128]{2,1,0:T(8,128)S(1)}, u32[]{:S(2)}, u32[]{:S(2)}) collective-permute-start(f32[1,256,128]{2,1,0:T(8,128)S(1)} %shard_map.97.field_ref.refs_7_.refs_9_), channel_id=1, source_target_pairs={{0,16},{1,2},{2,1},{3,4},{4,3},{5,6},{6,5},{7,8},{8,7},{9,10},{10,... | collective-permute-start | bytes 393224 | tf_op jit(solution)/shard_map/ppermute | solution.py:351
  22.3 6.6 %collective-permute-start.7 = (f32[1,256,128]{2,1,0:T(8,128)S(1)}, f32[1,256,128]{2,1,0:T(8,128)S(1)}, u32[]{:S(2)}, u32[]{:S(2)}) collective-permute-start(f32[1,256,128]{2,1,0:T(8,128)S(1)} %shard_map.97.field_ref.refs_7_.refs_9_), channel_id=1, source_target_pairs={{0,1},{1,0},{2,3},{3,2},{4,5},{5,4},{6,7},{7,6},{8,9},{9,8},{10,11... | collective-permute-start | bytes 393224 | tf_op jit(solution)/shard_map/ppermute | solution.py:352
  22.6 8.1 %collective-permute-start.20 = (f32[1,256,128]{2,1,0:T(8,128)S(1)}, f32[1,256,128]{2,1,0:T(8,128)S(1)}, u32[]{:S(2)}, u32[]{:S(2)}) collective-permute-start(f32[1,256,128]{2,1,0:T(8,128)S(1)} %shard_map.102.refs_2_.field_ref), channel_id=1, source_target_pairs={{0,16},{1,2},{2,1},{3,4},{4,3},{5,6},{6,5},{7,8},{8,7},{9,10},{10,... | collective-permute-start | bytes 393224 | tf_op jit(solution)/shard_map/ppermute | solution.py:351
  24.2 9.6 %collective-permute-start.21 = (f32[1,256,128]{2,1,0:T(8,128)S(1)}, f32[1,256,128]{2,1,0:T(8,128)S(1)}, u32[]{:S(2)}, u32[]{:S(2)}) collective-permute-start(f32[1,256,128]{2,1,0:T(8,128)S(1)} %shard_map.102.refs_2_.field_ref), channel_id=1, source_target_pairs={{0,1},{1,0},{2,3},{3,2},{4,5},{5,4},{6,7},{7,6},{8,9},{9,8},{10,11... | collective-permute-start | bytes 393224 | tf_op jit(solution)/shard_map/ppermute | solution.py:352
  26.4 7.9 %collective-permute-start.14 = (f32[1,256,128]{2,1,0:T(8,128)S(1)}, f32[1,256,128]{2,1,0:T(8,128)S(1)}, u32[]{:S(2)}, u32[]{:S(2)}) collective-permute-start(f32[1,256,128]{2,1,0:T(8,128)S(1)} %shard_map.100.refs_5_.field_ref.refs_6_), channel_id=1, source_target_pairs={{0,16},{1,2},{2,1},{3,4},{4,3},{5,6},{6,5},{7,8},{8,7},{9,10},{10,... | collective-permute-start | bytes 393224 | tf_op jit(solution)/shard_map/ppermute | solution.py:351
  27.9 6.3 %collective-permute-start.15 = (f32[1,256,128]{2,1,0:T(8,128)S(1)}, f32[1,256,128]{2,1,0:T(8,128)S(1)}, u32[]{:S(2)}, u32[]{:S(2)}) collective-permute-start(f32[1,256,128]{2,1,0:T(8,128)S(1)} %shard_map.100.refs_5_.field_ref.refs_6_), channel_id=1, source_target_pairs={{0,1},{1,0},{2,3},{3,2},{4,5},{5,4},{6,7},{7,6},{8,9},{9,8},{10,11... | collective-permute-start | bytes 393224 | tf_op jit(solution)/shard_map/ppermute | solution.py:352
  29.2 5.5 %collective-permute-start.8 = (f32[1,256,128]{2,1,0:T(8,128)S(1)}, f32[1,256,128]{2,1,0:T(8,128)S(1)}, u32[]{:S(2)}, u32[]{:S(2)}) collective-permute-start(f32[1,256,128]{2,1,0:T(8,128)S(1)} %shard_map.98.refs_8_.field_ref.refs_10_), channel_id=1, source_target_pairs={{0,16},{1,2},{2,1},{3,4},{4,3},{5,6},{6,5},{7,8},{8,7},{9,10},{10,... | collective-permute-start | bytes 393224 | tf_op jit(solution)/shard_map/ppermute | solution.py:351
  30.7 3.9 %collective-permute-start.9 = (f32[1,256,128]{2,1,0:T(8,128)S(1)}, f32[1,256,128]{2,1,0:T(8,128)S(1)}, u32[]{:S(2)}, u32[]{:S(2)}) collective-permute-start(f32[1,256,128]{2,1,0:T(8,128)S(1)} %shard_map.98.refs_8_.field_ref.refs_10_), channel_id=1, source_target_pairs={{0,1},{1,0},{2,3},{3,2},{4,5},{5,4},{6,7},{7,6},{8,9},{9,8},{10,11... | collective-permute-start | bytes 393224 | tf_op jit(solution)/shard_map/ppermute | solution.py:352

commit v9 on v8

--- a/solution.py
+++ b/solution.py
@@ -12,7 +12,7 @@
 DIFFUSION = 1.0
 MASS_TERM = 0.5
 BUOYANCY = 1.0
-CENTERS = (1.0, 0.55, 1.45, 0.25, 1.75, 0.05, 1.95)
+CENTERS = (0.8, 0.4, 1.3, 0.05, 1.8)
 CHUNK = 32
 SPLITS = ((0, 1), (1, 2), (2, 3))
 
@@ -198,14 +198,6 @@
     moments_ref[...] = sum(place_moment(k, sums[k]) for k in range(5))
 
 
-def powers(center, y0, y1, y2, y3):
-    q1 = y1 - center * y0
-    t2 = y2 - center * y1
-    q2 = t2 - center * q1
-    q3 = (y3 - center * y2 - center * t2) - center * q2
-    return q1, q2, q3
-
-
 def last_kernel(
     low, far_ref, near_ref, field_ref, weights_ref, matrix_ref, earlier_ref, left_ref, shift_ref,
     out_ref, moments_ref, moved_ref,
@@ -265,12 +257,12 @@
         image = operator(direction)
         step_size = product_now / inner(direction, image, moments)
         answer = axpy(step_size, direction, answer)
-        residual = axpy(-step_size, image, residual)
         if step + 1 < ITERS:
+            residual = axpy(-step_size, image, residual)
             product_next = inner(residual, residual, moments)
             direction = axpy(product_next / product_now, direction, residual)
             product_now = product_next
-    return answer, residual
+    return answer
 
 
 def finish_kernel(moments_ref, diagonal_ref, *refs):
@@ -285,8 +277,8 @@
     centers = jnp.zeros((8, 1), jnp.float32)
     for j, center in enumerate(CENTERS):
         centers = jnp.where(place == j, center, centers)
-    answer, residual = recurrence(moments, centers)
-    packed = [centers, *answer, *residual]
+    a0, a1, a2 = recurrence(moments, centers)
+    packed = [a0 - centers * (a1 - centers * a2), a1 - (2.0 * centers) * a2, a2]
     mean = centers[0:1] + moments[1][0:1] / moments[0][0:1]
     best = jnp.abs(mean - centers[0:1])
     chosen = [p[0:1] for p in packed]
@@ -296,19 +288,15 @@
         best = jnp.where(better, away, best)
         chosen = [jnp.where(better, p[j : j + 1], c) for p, c in zip(packed, chosen)]
     total, layers = diagonal_ref.shape
-    chosen = [jnp.broadcast_to(c, (CHUNK, layers)) for c in chosen]
-    center, answer, residual = chosen[0], chosen[1:4], chosen[4:8]
+    a0, a1, a2 = [jnp.broadcast_to(c, (CHUNK, layers)) for c in chosen]
     copies = []
     for (low, high), stream in zip(SPLITS, streams):
         for at in range(high - low):
             for start in range(0, total, CHUNK):
                 here = slice(start, start + CHUNK)
-                values = [ref[at, here] for ref in stream]
-                q1, q2, q3 = powers(center, *values)
-                solution_ref[low + at, here] = answer[0] * values[0] + answer[1] * q1 + answer[2] * q2
-                residual_ref[low + at, here] = diagonal_ref[here] * (
-                    residual[0] * values[0] + residual[1] * q1 + residual[2] * q2 + residual[3] * q3
-                )
+                y0, y1, y2, y3 = [ref[at, here] for ref in stream]
+                solution_ref[low + at, here] = a0 * y0 + a1 * y1 + a2 * y2
+                residual_ref[low + at, here] = diagonal_ref[here] * (y0 - (a0 * y1 + a1 * y2 + a2 * y3))
             for k, (source, target) in enumerate(((solution_ref, solution_hbm), (residual_ref, residual_hbm))):
                 copies.append(pltpu.make_async_copy(source.at[low + at], target.at[low + at], sems.at[k, low + at]))
                 copies[-1].start()

time: 50.5 us -> 50.4 us (level)
  Pallas kernels: 9.04 us -> 8.41 us
    pallas_call x14, Pallas kernels: 9.04 us -> 8.41 us  [call(): pl.pallas_call(kernel, out_shape=outs, in_specs=[pl.BlockSpec(memory_spac...]
  transfers between devices with their start and end apart: 22 -> 22, of which waited for: 0 -> 1; matrix products, arithmetic and copies ran while one was open for 0% -> 0% of each run, Pallas kernels for 15% -> 14%
where the time goes in v9:
time: 50.4 us; the launch traced here: 50.2 us
  starting transfers between devices  26.6 us (53%)
  blocking collectives  14.3 us (28%)
  Pallas kernels  8.41 us (17%)
  between operations  0.72 us (1%)
    ppermute x11, starting transfers between devices, exchange(): far = lax.ppermute(value, NAMES, across)  18.3 us
    all_to_all x1, blocking collectives, body(): moments = lax.all_to_all(moments, NAMES, 0, 0)  14.3 us
    pallas_call x14, Pallas kernels, call(): pl.pallas_call(kernel, out_shape=outs, in_specs=[pl.BlockSpec(memory_spac...  8.41 us
    ppermute x11, starting transfers between devices, exchange(): near = lax.ppermute(value, NAMES, beside)  8.25 us
  transfers between devices with their start and end apart: 22, of which 1 were waited for; matrix products, arithmetic and copies ran while one was open for 0% of the time, Pallas kernels for 14%

profile of v9, /device:TPU:0, one launch (start us, length us, event | category | flops | bytes accessed | tf_op | source)
XLA Modules:
  0.0 50.2 jit_solution(4130525758320441506)
XLA Ops:
  0.6 3.0 %collective-permute-start.2 = (f32[1,256,128]{2,1,0:T(8,128)}, f32[1,256,128]{2,1,0:T(8,128)S(1)}, u32[]{:S(2)}, u32[]{:S(2)}) collective-permute-start(f32[1,256,128]{2,1,0:T(8,128)} %bitcast.20), channel_id=1, source_target_pairs={{0,16},{1,2},{2,1},{3,4},{4,3},{5,6},{6,5},{7,8},{8,7},{9,10},{10,... | collective-permute-start | bytes 393224 | tf_op jit(solution)/shard_map/ppermute | solution.py:339
  3.6 0.1 collective-permute-start.3
  3.8 1.7 %shard_map.94 = (f32[256,128]{1,0:T(8,128)S(1)}, f32[4,256,128]{2,1,0:T(8,128)S(1)}, f32[256,128]{1,0:T(8,128)S(1)}, f32[3,256,128]{2,1,0:T(8,128)S(1)}, f32[256...) custom-call(f32[256,128]{1,0:T(8,128)} %bitcast.18, ...), custom_call_target="tpu_custom_call" | custom-call | tf_op jit(solution)/shard_map/pallas_call | solution.py:311
  5.4 1.6 %collective-permute-start = (f32[1,256,128]{2,1,0:T(8,128)S(1)}, f32[1,256,128]{2,1,0:T(8,128)S(1)}, u32[]{:S(2)}, u32[]{:S(2)}) collective-permute-start(f32[1,256,128]{2,1,0:T(8,128)S(1)} %bitcast.14), channel_id=1, source_target_pairs={{0,16},{1,2},{2,1},{3,4},{4,3},{5,6},{6,5},{7,8},{8,7},{9,10},{10,... | collective-permute-start | bytes 393224 | tf_op jit(solution)/shard_map/ppermute | solution.py:339
  7.0 0.1 collective-permute-start.1
  7.1 0.0 collective-permute-done.2.far_ref
  7.1 0.0 collective-permute-done.3.near_ref
  7.1 0.3 shard_map.95
  7.4 1.7 %collective-permute-start.16 = (f32[1,256,128]{2,1,0:T(8,128)S(1)}, f32[1,256,128]{2,1,0:T(8,128)S(1)}, u32[]{:S(2)}, u32[]{:S(2)}) collective-permute-start(f32[1,256,128]{2,1,0:T(8,128)S(1)} %get-tuple-element.41.field_ref.refs_0_), channel_id=1, source_target_pairs={{0,16},{1,2},{2,1},{3,4},{4,3},{5,6},{6,5},{7,8},{8,7},{9,10},{10,... | collective-permute-start | bytes 393224 | tf_op jit(solution)/shard_map/ppermute | solution.py:339
  9.2 1.0 %collective-permute-start.17 = (f32[1,256,128]{2,1,0:T(8,128)S(1)}, f32[1,256,128]{2,1,0:T(8,128)S(1)}, u32[]{:S(2)}, u32[]{:S(2)}) collective-permute-start(f32[1,256,128]{2,1,0:T(8,128)S(1)} %get-tuple-element.41.field_ref.refs_0_), channel_id=1, source_target_pairs={{0,1},{1,0},{2,3},{3,2},{4,5},{5,4},{6,7},{7,6},{8,9},{9,8},{10,11... | collective-permute-start | bytes 393224 | tf_op jit(solution)/shard_map/ppermute | solution.py:340
  10.1 1.5 %collective-permute-start.10 = (f32[1,256,128]{2,1,0:T(8,128)S(1)}, f32[1,256,128]{2,1,0:T(8,128)S(1)}, u32[]{:S(2)}, u32[]{:S(2)}) collective-permute-start(f32[1,256,128]{2,1,0:T(8,128)S(1)} %get-tuple-element.40.field_ref.refs_3_.refs_4_), channel_id=1, source_target_pairs={{0,16},{1,2},{2,1},{3,4},{4,3},{5,6},{6,5},{7,8},{8,7},{9,10},{10,... | collective-permute-start | bytes 393224 | tf_op jit(solution)/shard_map/ppermute | solution.py:339
  11.6 0.0 collective-permute-done.far_ref
  11.6 0.0 collective-permute-start.11
  11.6 0.0 collective-permute-done.1.near_ref
  11.6 0.9 %shard_map.96 = (f32[256,128]{1,0:T(8,128)}, f32[1,256,128]{2,1,0:T(8,128)S(1)}) custom-call(f32[1,256,128]{2,1,0:T(8,128)S(1)} %collective-permute-done.far_ref, f32[1,256,128]{2,1,0:T(8,128)S(1)} %collective-permute-done.1.near_ref, f32[3,256,128]{2,1,0:T(8,128)S(1)} %get-tuple-element.30.right_ref, f32[256,128]{1,0:T(8,128)S(1)} %get-tuple-element.31.part_ref, ...), custom_call_target="tpu_custom_call" | custom-call | tf_op jit(solution)/shard_map/pallas_call | solution.py:311
  12.5 1.2 %collective-permute-start.4 = (f32[1,256,128]{2,1,0:T(8,128)S(1)}, f32[1,256,128]{2,1,0:T(8,128)S(1)}, u32[]{:S(2)}, u32[]{:S(2)}) collective-permute-start(f32[1,256,128]{2,1,0:T(8,128)S(1)} %get-tuple-element.38.field_ref.refs_6_.refs_8_), channel_id=1, source_target_pairs={{0,16},{1,2},{2,1},{3,4},{4,3},{5,6},{6,5},{7,8},{8,7},{9,10},{10,... | collective-permute-start | bytes 393224 | tf_op jit(solution)/shard_map/ppermute | solution.py:339
  13.8 0.0 collective-permute-done.16.far_ref
  13.8 1.1 %collective-permute-start.5 = (f32[1,256,128]{2,1,0:T(8,128)S(1)}, f32[1,256,128]{2,1,0:T(8,128)S(1)}, u32[]{:S(2)}, u32[]{:S(2)}) collective-permute-start(f32[1,256,128]{2,1,0:T(8,128)S(1)} %get-tuple-element.38.field_ref.refs_6_.refs_8_), channel_id=1, source_target_pairs={{0,1},{1,0},{2,3},{3,2},{4,5},{5,4},{6,7},{7,6},{8,9},{9,8},{10,11... | collective-permute-start | bytes 393224 | tf_op jit(solution)/shard_map/ppermute | solution.py:340
  14.9 0.0 collective-permute-done.17.near_ref
  14.9 0.3 shard_map.101.field_ref.refs_1_
  15.1 1.6 %collective-permute-start.18 = (f32[1,256,128]{2,1,0:T(8,128)S(1)}, f32[1,256,128]{2,1,0:T(8,128)S(1)}, u32[]{:S(2)}, u32[]{:S(2)}) collective-permute-start(f32[1,256,128]{2,1,0:T(8,128)S(1)} %shard_map.101.field_ref.refs_1_), channel_id=1, source_target_pairs={{0,16},{1,2},{2,1},{3,4},{4,3},{5,6},{6,5},{7,8},{8,7},{9,10},{10,... | collective-permute-start | bytes 393224 | tf_op jit(solution)/shard_map/ppermute | solution.py:339
  16.7 0.0 collective-permute-done.10.far_ref
  16.7 1.0 %collective-permute-start.19 = (f32[1,256,128]{2,1,0:T(8,128)S(1)}, f32[1,256,128]{2,1,0:T(8,128)S(1)}, u32[]{:S(2)}, u32[]{:S(2)}) collective-permute-start(f32[1,256,128]{2,1,0:T(8,128)S(1)} %shard_map.101.field_ref.refs_1_), channel_id=1, source_target_pairs={{0,1},{1,0},{2,3},{3,2},{4,5},{5,4},{6,7},{7,6},{8,9},{9,8},{10,11... | collective-permute-start | bytes 393224 | tf_op jit(solution)/shard_map/ppermute | solution.py:340
  17.7 0.0 collective-permute-done.11.near_ref
  17.7 0.3 shard_map.99.field_ref.refs_4_.refs_5_
  18.0 1.6 %collective-permute-start.12 = (f32[1,256,128]{2,1,0:T(8,128)S(1)}, f32[1,256,128]{2,1,0:T(8,128)S(1)}, u32[]{:S(2)}, u32[]{:S(2)}) collective-permute-start(f32[1,256,128]{2,1,0:T(8,128)S(1)} %shard_map.99.field_ref.refs_4_.refs_5_), channel_id=1, source_target_pairs={{0,16},{1,2},{2,1},{3,4},{4,3},{5,6},{6,5},{7,8},{8,7},{9,10},{10,... | collective-permute-start | bytes 393224 | tf_op jit(solution)/shard_map/ppermute | solution.py:339
  19.5 1.0 %collective-permute-start.13 = (f32[1,256,128]{2,1,0:T(8,128)S(1)}, f32[1,256,128]{2,1,0:T(8,128)S(1)}, u32[]{:S(2)}, u32[]{:S(2)}) collective-permute-start(f32[1,256,128]{2,1,0:T(8,128)S(1)} %shard_map.99.field_ref.refs_4_.refs_5_), channel_id=1, source_target_pairs={{0,1},{1,0},{2,3},{3,2},{4,5},{5,4},{6,7},{7,6},{8,9},{9,8},{10,11... | collective-permute-start | bytes 393224 | tf_op jit(solution)/shard_map/ppermute | solution.py:340
  20.5 0.3 shard_map.97.field_ref.refs_7_.refs_9_
  20.8 1.6 %collective-permute-start.6 = (f32[1,256,128]{2,1,0:T(8,128)S(1)}, f32[1,256,128]{2,1,0:T(8,128)S(1)}, u32[]{:S(2)}, u32[]{:S(2)}) collective-permute-start(f32[1,256,128]{2,1,0:T(8,128)S(1)} %shard_map.97.field_ref.refs_7_.refs_9_), channel_id=1, source_target_pairs={{0,16},{1,2},{2,1},{3,4},{4,3},{5,6},{6,5},{7,8},{8,7},{9,10},{10,... | collective-permute-start | bytes 393224 | tf_op jit(solution)/shard_map/ppermute | solution.py:339
  22.3 0.0 collective-permute-start.7
  22.4 0.3 shard_map.102.refs_2_.field_ref
  22.6 1.6 %collective-permute-start.20 = (f32[1,256,128]{2,1,0:T(8,128)S(1)}, f32[1,256,128]{2,1,0:T(8,128)S(1)}, u32[]{:S(2)}, u32[]{:S(2)}) collective-permute-start(f32[1,256,128]{2,1,0:T(8,128)S(1)} %shard_map.102.refs_2_.field_ref), channel_id=1, source_target_pairs={{0,16},{1,2},{2,1},{3,4},{4,3},{5,6},{6,5},{7,8},{8,7},{9,10},{10,... | collective-permute-start | bytes 393224 | tf_op jit(solution)/shard_map/ppermute | solution.py:339
  24.2 1.9 %collective-permute-start.21 = (f32[1,256,128]{2,1,0:T(8,128)S(1)}, f32[1,256,128]{2,1,0:T(8,128)S(1)}, u32[]{:S(2)}, u32[]{:S(2)}) collective-permute-start(f32[1,256,128]{2,1,0:T(8,128)S(1)} %shard_map.102.refs_2_.field_ref), channel_id=1, source_target_pairs={{0,1},{1,0},{2,3},{3,2},{4,5},{5,4},{6,7},{7,6},{8,9},{9,8},{10,11... | collective-permute-start | bytes 393224 | tf_op jit(solution)/shard_map/ppermute | solution.py:340
  26.1 0.0 collective-permute-done.13.near_ref
  26.1 0.3 shard_map.100.refs_5_.field_ref.refs_6_
  26.4 1.6 %collective-permute-start.14 = (f32[1,256,128]{2,1,0:T(8,128)S(1)}, f32[1,256,128]{2,1,0:T(8,128)S(1)}, u32[]{:S(2)}, u32[]{:S(2)}) collective-permute-start(f32[1,256,128]{2,1,0:T(8,128)S(1)} %shard_map.100.refs_5_.field_ref.refs_6_), channel_id=1, source_target_pairs={{0,16},{1,2},{2,1},{3,4},{4,3},{5,6},{6,5},{7,8},{8,7},{9,10},{10,... | collective-permute-start | bytes 393224 | tf_op jit(solution)/shard_map/ppermute | solution.py:339
  27.9 0.0 collective-permute-done.6.far_ref
  27.9 1.0 %collective-permute-start.15 = (f32[1,256,128]{2,1,0:T(8,128)S(1)}, f32[1,256,128]{2,1,0:T(8,128)S(1)}, u32[]{:S(2)}, u32[]{:S(2)}) collective-permute-start(f32[1,256,128]{2,1,0:T(8,128)S(1)} %shard_map.100.refs_5_.field_ref.refs_6_), channel_id=1, source_target_pairs={{0,1},{1,0},{2,3},{3,2},{4,5},{5,4},{6,7},{7,6},{8,9},{9,8},{10,11... | collective-permute-start | bytes 393224 | tf_op jit(solution)/shard_map/ppermute | solution.py:340
  28.9 0.3 shard_map.98.refs_8_.field_ref.refs_10_
  29.2 1.6 %collective-permute-start.8 = (f32[1,256,128]{2,1,0:T(8,128)S(1)}, f32[1,256,128]{2,1,0:T(8,128)S(1)}, u32[]{:S(2)}, u32[]{:S(2)}) collective-permute-start(f32[1,256,128]{2,1,0:T(8,128)S(1)} %shard_map.98.refs_8_.field_ref.refs_10_), channel_id=1, source_target_pairs={{0,16},{1,2},{2,1},{3,4},{4,3},{5,6},{6,5},{7,8},{8,7},{9,10},{10,... | collective-permute-start | bytes 393224 | tf_op jit(solution)/shard_map/ppermute | solution.py:339
  30.7 1.0 %collective-permute-start.9 = (f32[1,256,128]{2,1,0:T(8,128)S(1)}, f32[1,256,128]{2,1,0:T(8,128)S(1)}, u32[]{:S(2)}, u32[]{:S(2)}) collective-permute-start(f32[1,256,128]{2,1,0:T(8,128)S(1)} %shard_map.98.refs_8_.field_ref.refs_10_), channel_id=1, source_target_pairs={{0,1},{1,0},{2,3},{3,2},{4,5},{5,4},{6,7},{7,6},{8,9},{9,8},{10,11... | collective-permute-start | bytes 393224 | tf_op jit(solution)/shard_map/ppermute | solution.py:340
  31.7 1.5 %shard_map.103 = (f32[8,128]{1,0:T(8,128)S(1)}, f32[5,3,256,128]{3,2,1,0:T(8,128)S(1)}, f32[5,3,256,128]{3,2,1,0:T(8,128)S(1)}) custom-call(f32[256,128]{1,0:T(8,128)S(1)} %get-tuple-element.42.diagonal_ref, f32[1,256,128]{2,1,0:T(8,128)S(1)} %get-tuple-element.41.field_ref.refs_0_, f32[1,256,128]{2,1,0:T(8,128)S(1)} %shard_map.101.field_ref.refs_1_, ...), custom_call_target="tpu_custom_call" | custom-call | tf_op jit(solution)/shard_map/pallas_call | solution.py:311
  33.2 0.4 shard_map.104
  33.7 0.4 shard_map.105
  34.1 0.1 collective-permute-done.8.far_ref
  34.2 0.5 shard_map.106
  34.7 14.3 %all_to_all.5.moments_ref = f32[32,1,128]{2,1,0:T(1,128)S(1)} all-to-all(f32[32,1,128]{2,1,0:T(1,128)S(1)} %get-tuple-element.48), channel_id=1, replica_groups=mesh['diamond'=2,'tile'=16] {'diamond','tile'}, dimensions={0} | all-to-all | bytes 32768 | tf_op jit(solution)/shard_map/all_to_all | solution.py:389
  49.0 1.2 %shard_map.107 = (f32[3,256,128]{2,1,0:T(8,128)}, f32[3,256,128]{2,1,0:T(8,128)}) custom-call(f32[32,1,128]{2,1,0:T(1,128)S(1)} %all_to_all.5.moments_ref, f32[256,128]{1,0:T(8,128)S(1)} %get-tuple-element.42.diagonal_ref, f32[1,256,128]{2,1,0:T(8,128)S(1)} %get-tuple-element.41.field_ref.refs_0_, f32[1,256,128]{2,1,0:T(8,128)S(1)} %shard_map.101.field_ref.refs_1_, ...), custom_call_target="tpu_custom_call" | custom-call | tf_op jit(solution)/shard_map/pallas_call | solution.py:311
  (11 shorter events, 0.0 us)
Async XLA Ops:
  0.6 6.5 %collective-permute-start.2 = (f32[1,256,128]{2,1,0:T(8,128)}, f32[1,256,128]{2,1,0:T(8,128)S(1)}, u32[]{:S(2)}, u32[]{:S(2)}) collective-permute-start(f32[1,256,128]{2,1,0:T(8,128)} %bitcast.20), channel_id=1, source_target_pairs={{0,16},{1,2},{2,1},{3,4},{4,3},{5,6},{6,5},{7,8},{8,7},{9,10},{10,... | collective-permute-start | bytes 393224 | tf_op jit(solution)/shard_map/ppermute | solution.py:339
  3.6 3.5 %collective-permute-start.3 = (f32[1,256,128]{2,1,0:T(8,128)}, f32[1,256,128]{2,1,0:T(8,128)S(1)}, u32[]{:S(2)}, u32[]{:S(2)}) collective-permute-start(f32[1,256,128]{2,1,0:T(8,128)} %bitcast.21), channel_id=1, source_target_pairs={{0,1},{1,0},{2,3},{3,2},{4,5},{5,4},{6,7},{7,6},{8,9},{9,8},{10,11... | collective-permute-start | bytes 393224 | tf_op jit(solution)/shard_map/ppermute | solution.py:340
  5.4 6.2 %collective-permute-start = (f32[1,256,128]{2,1,0:T(8,128)S(1)}, f32[1,256,128]{2,1,0:T(8,128)S(1)}, u32[]{:S(2)}, u32[]{:S(2)}) collective-permute-start(f32[1,256,128]{2,1,0:T(8,128)S(1)} %bitcast.14), channel_id=1, source_target_pairs={{0,16},{1,2},{2,1},{3,4},{4,3},{5,6},{6,5},{7,8},{8,7},{9,10},{10,... | collective-permute-start | bytes 393224 | tf_op jit(solution)/shard_map/ppermute | solution.py:339
  7.0 4.6 %collective-permute-start.1 = (f32[1,256,128]{2,1,0:T(8,128)S(1)}, f32[1,256,128]{2,1,0:T(8,128)S(1)}, u32[]{:S(2)}, u32[]{:S(2)}) collective-permute-start(f32[1,256,128]{2,1,0:T(8,128)S(1)} %bitcast.15), channel_id=1, source_target_pairs={{0,1},{1,0},{2,3},{3,2},{4,5},{5,4},{6,7},{7,6},{8,9},{9,8},{10,11... | collective-permute-start | bytes 393224 | tf_op jit(solution)/shard_map/ppermute | solution.py:340
  7.4 6.3 %collective-permute-start.16 = (f32[1,256,128]{2,1,0:T(8,128)S(1)}, f32[1,256,128]{2,1,0:T(8,128)S(1)}, u32[]{:S(2)}, u32[]{:S(2)}) collective-permute-start(f32[1,256,128]{2,1,0:T(8,128)S(1)} %get-tuple-element.41.field_ref.refs_0_), channel_id=1, source_target_pairs={{0,16},{1,2},{2,1},{3,4},{4,3},{5,6},{6,5},{7,8},{8,7},{9,10},{10,... | collective-permute-start | bytes 393224 | tf_op jit(solution)/shard_map/ppermute | solution.py:339
  9.2 5.7 %collective-permute-start.17 = (f32[1,256,128]{2,1,0:T(8,128)S(1)}, f32[1,256,128]{2,1,0:T(8,128)S(1)}, u32[]{:S(2)}, u32[]{:S(2)}) collective-permute-start(f32[1,256,128]{2,1,0:T(8,128)S(1)} %get-tuple-element.41.field_ref.refs_0_), channel_id=1, source_target_pairs={{0,1},{1,0},{2,3},{3,2},{4,5},{5,4},{6,7},{7,6},{8,9},{9,8},{10,11... | collective-permute-start | bytes 393224 | tf_op jit(solution)/shard_map/ppermute | solution.py:340
  10.1 6.5 %collective-permute-start.10 = (f32[1,256,128]{2,1,0:T(8,128)S(1)}, f32[1,256,128]{2,1,0:T(8,128)S(1)}, u32[]{:S(2)}, u32[]{:S(2)}) collective-permute-start(f32[1,256,128]{2,1,0:T(8,128)S(1)} %get-tuple-element.40.field_ref.refs_3_.refs_4_), channel_id=1, source_target_pairs={{0,16},{1,2},{2,1},{3,4},{4,3},{5,6},{6,5},{7,8},{8,7},{9,10},{10,... | collective-permute-start | bytes 393224 | tf_op jit(solution)/shard_map/ppermute | solution.py:339
  11.6 6.1 %collective-permute-start.11 = (f32[1,256,128]{2,1,0:T(8,128)S(1)}, f32[1,256,128]{2,1,0:T(8,128)S(1)}, u32[]{:S(2)}, u32[]{:S(2)}) collective-permute-start(f32[1,256,128]{2,1,0:T(8,128)S(1)} %get-tuple-element.40.field_ref.refs_3_.refs_4_), channel_id=1, source_target_pairs={{0,1},{1,0},{2,3},{3,2},{4,5},{5,4},{6,7},{7,6},{8,9},{9,8},{10,11... | collective-permute-start | bytes 393224 | tf_op jit(solution)/shard_map/ppermute | solution.py:340
  12.5 7.0 %collective-permute-start.4 = (f32[1,256,128]{2,1,0:T(8,128)S(1)}, f32[1,256,128]{2,1,0:T(8,128)S(1)}, u32[]{:S(2)}, u32[]{:S(2)}) collective-permute-start(f32[1,256,128]{2,1,0:T(8,128)S(1)} %get-tuple-element.38.field_ref.refs_6_.refs_8_), channel_id=1, source_target_pairs={{0,16},{1,2},{2,1},{3,4},{4,3},{5,6},{6,5},{7,8},{8,7},{9,10},{10,... | collective-permute-start | bytes 393224 | tf_op jit(solution)/shard_map/ppermute | solution.py:339
  13.8 6.7 %collective-permute-start.5 = (f32[1,256,128]{2,1,0:T(8,128)S(1)}, f32[1,256,128]{2,1,0:T(8,128)S(1)}, u32[]{:S(2)}, u32[]{:S(2)}) collective-permute-start(f32[1,256,128]{2,1,0:T(8,128)S(1)} %get-tuple-element.38.field_ref.refs_6_.refs_8_), channel_id=1, source_target_pairs={{0,1},{1,0},{2,3},{3,2},{4,5},{5,4},{6,7},{7,6},{8,9},{9,8},{10,11... | collective-permute-start | bytes 393224 | tf_op jit(solution)/shard_map/ppermute | solution.py:340
  15.1 7.2 %collective-permute-start.18 = (f32[1,256,128]{2,1,0:T(8,128)S(1)}, f32[1,256,128]{2,1,0:T(8,128)S(1)}, u32[]{:S(2)}, u32[]{:S(2)}) collective-permute-start(f32[1,256,128]{2,1,0:T(8,128)S(1)} %shard_map.101.field_ref.refs_1_), channel_id=1, source_target_pairs={{0,16},{1,2},{2,1},{3,4},{4,3},{5,6},{6,5},{7,8},{8,7},{9,10},{10,... | collective-permute-start | bytes 393224 | tf_op jit(solution)/shard_map/ppermute | solution.py:339
  16.7 5.7 %collective-permute-start.19 = (f32[1,256,128]{2,1,0:T(8,128)S(1)}, f32[1,256,128]{2,1,0:T(8,128)S(1)}, u32[]{:S(2)}, u32[]{:S(2)}) collective-permute-start(f32[1,256,128]{2,1,0:T(8,128)S(1)} %shard_map.101.field_ref.refs_1_), channel_id=1, source_target_pairs={{0,1},{1,0},{2,3},{3,2},{4,5},{5,4},{6,7},{7,6},{8,9},{9,8},{10,11... | collective-permute-start | bytes 393224 | tf_op jit(solution)/shard_map/ppermute | solution.py:340
  18.0 6.2 %collective-permute-start.12 = (f32[1,256,128]{2,1,0:T(8,128)S(1)}, f32[1,256,128]{2,1,0:T(8,128)S(1)}, u32[]{:S(2)}, u32[]{:S(2)}) collective-permute-start(f32[1,256,128]{2,1,0:T(8,128)S(1)} %shard_map.99.field_ref.refs_4_.refs_5_), channel_id=1, source_target_pairs={{0,16},{1,2},{2,1},{3,4},{4,3},{5,6},{6,5},{7,8},{8,7},{9,10},{10,... | collective-permute-start | bytes 393224 | tf_op jit(solution)/shard_map/ppermute | solution.py:339
  19.5 6.6 %collective-permute-start.13 = (f32[1,256,128]{2,1,0:T(8,128)S(1)}, f32[1,256,128]{2,1,0:T(8,128)S(1)}, u32[]{:S(2)}, u32[]{:S(2)}) collective-permute-start(f32[1,256,128]{2,1,0:T(8,128)S(1)} %shard_map.99.field_ref.refs_4_.refs_5_), channel_id=1, source_target_pairs={{0,1},{1,0},{2,3},{3,2},{4,5},{5,4},{6,7},{7,6},{8,9},{9,8},{10,11... | collective-permute-start | bytes 393224 | tf_op jit(solution)/shard_map/ppermute | solution.py:340
  20.8 7.2 %collective-permute-start.6 = (f32[1,256,128]{2,1,0:T(8,128)S(1)}, f32[1,256,128]{2,1,0:T(8,128)S(1)}, u32[]{:S(2)}, u32[]{:S(2)}) collective-permute-start(f32[1,256,128]{2,1,0:T(8,128)S(1)} %shard_map.97.field_ref.refs_7_.refs_9_), channel_id=1, source_target_pairs={{0,16},{1,2},{2,1},{3,4},{4,3},{5,6},{6,5},{7,8},{8,7},{9,10},{10,... | collective-permute-start | bytes 393224 | tf_op jit(solution)/shard_map/ppermute | solution.py:339
  22.3 6.6 %collective-permute-start.7 = (f32[1,256,128]{2,1,0:T(8,128)S(1)}, f32[1,256,128]{2,1,0:T(8,128)S(1)}, u32[]{:S(2)}, u32[]{:S(2)}) collective-permute-start(f32[1,256,128]{2,1,0:T(8,128)S(1)} %shard_map.97.field_ref.refs_7_.refs_9_), channel_id=1, source_target_pairs={{0,1},{1,0},{2,3},{3,2},{4,5},{5,4},{6,7},{7,6},{8,9},{9,8},{10,11... | collective-permute-start | bytes 393224 | tf_op jit(solution)/shard_map/ppermute | solution.py:340
  22.6 8.1 %collective-permute-start.20 = (f32[1,256,128]{2,1,0:T(8,128)S(1)}, f32[1,256,128]{2,1,0:T(8,128)S(1)}, u32[]{:S(2)}, u32[]{:S(2)}) collective-permute-start(f32[1,256,128]{2,1,0:T(8,128)S(1)} %shard_map.102.refs_2_.field_ref), channel_id=1, source_target_pairs={{0,16},{1,2},{2,1},{3,4},{4,3},{5,6},{6,5},{7,8},{8,7},{9,10},{10,... | collective-permute-start | bytes 393224 | tf_op jit(solution)/shard_map/ppermute | solution.py:339
  24.2 9.0 %collective-permute-start.21 = (f32[1,256,128]{2,1,0:T(8,128)S(1)}, f32[1,256,128]{2,1,0:T(8,128)S(1)}, u32[]{:S(2)}, u32[]{:S(2)}) collective-permute-start(f32[1,256,128]{2,1,0:T(8,128)S(1)} %shard_map.102.refs_2_.field_ref), channel_id=1, source_target_pairs={{0,1},{1,0},{2,3},{3,2},{4,5},{5,4},{6,7},{7,6},{8,9},{9,8},{10,11... | collective-permute-start | bytes 393224 | tf_op jit(solution)/shard_map/ppermute | solution.py:340
  26.4 7.3 %collective-permute-start.14 = (f32[1,256,128]{2,1,0:T(8,128)S(1)}, f32[1,256,128]{2,1,0:T(8,128)S(1)}, u32[]{:S(2)}, u32[]{:S(2)}) collective-permute-start(f32[1,256,128]{2,1,0:T(8,128)S(1)} %shard_map.100.refs_5_.field_ref.refs_6_), channel_id=1, source_target_pairs={{0,16},{1,2},{2,1},{3,4},{4,3},{5,6},{6,5},{7,8},{8,7},{9,10},{10,... | collective-permute-start | bytes 393224 | tf_op jit(solution)/shard_map/ppermute | solution.py:339
  27.9 5.8 %collective-permute-start.15 = (f32[1,256,128]{2,1,0:T(8,128)S(1)}, f32[1,256,128]{2,1,0:T(8,128)S(1)}, u32[]{:S(2)}, u32[]{:S(2)}) collective-permute-start(f32[1,256,128]{2,1,0:T(8,128)S(1)} %shard_map.100.refs_5_.field_ref.refs_6_), channel_id=1, source_target_pairs={{0,1},{1,0},{2,3},{3,2},{4,5},{5,4},{6,7},{7,6},{8,9},{9,8},{10,11... | collective-permute-start | bytes 393224 | tf_op jit(solution)/shard_map/ppermute | solution.py:340
  29.2 5.0 %collective-permute-start.8 = (f32[1,256,128]{2,1,0:T(8,128)S(1)}, f32[1,256,128]{2,1,0:T(8,128)S(1)}, u32[]{:S(2)}, u32[]{:S(2)}) collective-permute-start(f32[1,256,128]{2,1,0:T(8,128)S(1)} %shard_map.98.refs_8_.field_ref.refs_10_), channel_id=1, source_target_pairs={{0,16},{1,2},{2,1},{3,4},{4,3},{5,6},{6,5},{7,8},{8,7},{9,10},{10,... | collective-permute-start | bytes 393224 | tf_op jit(solution)/shard_map/ppermute | solution.py:339
  30.7 3.5 %collective-permute-start.9 = (f32[1,256,128]{2,1,0:T(8,128)S(1)}, f32[1,256,128]{2,1,0:T(8,128)S(1)}, u32[]{:S(2)}, u32[]{:S(2)}) collective-permute-start(f32[1,256,128]{2,1,0:T(8,128)S(1)} %shard_map.98.refs_8_.field_ref.refs_10_), channel_id=1, source_target_pairs={{0,1},{1,0},{2,3},{3,2},{4,5},{5,4},{6,7},{7,6},{8,9},{9,8},{10,11... | collective-permute-start | bytes 393224 | tf_op jit(solution)/shard_map/ppermute | solution.py:340

commit v10 on v9

--- a/solution.py
+++ b/solution.py
@@ -124,7 +124,7 @@
 
 
 def step_kernel(
-    far_ref, near_ref, right_ref, part_ref, speed_ref, inverse_ref, matrix_ref, next_ref, first_ref, moved_ref
+    near_ref, far_ref, right_ref, part_ref, speed_ref, inverse_ref, matrix_ref, next_ref, first_ref, moved_ref
 ):
     unfold(matrix_ref, far_ref, moved_ref)
     for start in range(0, part_ref.shape[0], CHUNK):
@@ -363,7 +363,7 @@
     )
     adjoint_next, *rest = call(
         step_kernel, [flat, shapes[-1]],
-        temp_far, temp_near, right, part, speed, inverse, matrix, scratch=[(1, *flat)],
+        temp_near, temp_far, right, part, speed, inverse, matrix, scratch=[(1, *flat)],
     )
     first += rest
     streams = [[field] for field in first]

time: 50.4 us -> 51.7 us (1.026)
  blocking collectives: 14.3 us -> 15.6 us
    all_to_all x1, blocking collectives: 14.3 us -> 15.6 us  [body(): moments = lax.all_to_all(moments, NAMES, 0, 0)]
  transfers between devices with their start and end apart: 22 -> 22, of which waited for: 1 -> 1; matrix products, arithmetic and copies ran while one was open for 0% -> 0% of each run, Pallas kernels for 14% -> 13%
where the time goes in v10:
time: 51.7 us; the launch traced here: 51.5 us
  starting transfers between devices  26.6 us (51%)
  blocking collectives  15.6 us (30%)
  Pallas kernels  8.41 us (16%)
  between operations  0.72 us (1%)
    ppermute x11, starting transfers between devices, exchange(): far = lax.ppermute(value, NAMES, across)  18.1 us
    all_to_all x1, blocking collectives, body(): moments = lax.all_to_all(moments, NAMES, 0, 0)  15.6 us
    ppermute x11, starting transfers between devices, exchange(): near = lax.ppermute(value, NAMES, beside)  8.54 us
    pallas_call x14, Pallas kernels, call(): pl.pallas_call(kernel, out_shape=outs, in_specs=[pl.BlockSpec(memory_spac...  8.41 us
  transfers between devices with their start and end apart: 22, of which 1 were waited for; matrix products, arithmetic and copies ran while one was open for 0% of the time, Pallas kernels for 13%

profile of v10, /device:TPU:0, one launch (start us, length us, event | category | flops | bytes accessed | tf_op | source)
XLA Modules:
  0.0 51.5 jit_solution(5811659555650545101)
XLA Ops:
  0.6 3.0 %collective-permute-start.2 = (f32[1,256,128]{2,1,0:T(8,128)}, f32[1,256,128]{2,1,0:T(8,128)S(1)}, u32[]{:S(2)}, u32[]{:S(2)}) collective-permute-start(f32[1,256,128]{2,1,0:T(8,128)} %bitcast.20), channel_id=1, source_target_pairs={{0,16},{1,2},{2,1},{3,4},{4,3},{5,6},{6,5},{7,8},{8,7},{9,10},{10,... | collective-permute-start | bytes 393224 | tf_op jit(solution)/shard_map/ppermute | solution.py:339
  3.6 0.1 collective-permute-start.3
  3.8 1.7 %shard_map.94 = (f32[256,128]{1,0:T(8,128)S(1)}, f32[4,256,128]{2,1,0:T(8,128)S(1)}, f32[256,128]{1,0:T(8,128)S(1)}, f32[3,256,128]{2,1,0:T(8,128)S(1)}, f32[256...) custom-call(f32[256,128]{1,0:T(8,128)} %bitcast.18, ...), custom_call_target="tpu_custom_call" | custom-call | tf_op jit(solution)/shard_map/pallas_call | solution.py:311
  5.4 0.4 collective-permute-start
  5.9 1.2 %collective-permute-start.1 = (f32[1,256,128]{2,1,0:T(8,128)S(1)}, f32[1,256,128]{2,1,0:T(8,128)S(1)}, u32[]{:S(2)}, u32[]{:S(2)}) collective-permute-start(f32[1,256,128]{2,1,0:T(8,128)S(1)} %bitcast.15), channel_id=1, source_target_pairs={{0,16},{1,2},{2,1},{3,4},{4,3},{5,6},{6,5},{7,8},{8,7},{9,10},{10,... | collective-permute-start | bytes 393224 | tf_op jit(solution)/shard_map/ppermute | solution.py:339
  7.1 0.0 collective-permute-done.2.far_ref
  7.1 0.0 collective-permute-done.3.near_ref
  7.1 0.3 shard_map.95
  7.4 1.8 %collective-permute-start.16 = (f32[1,256,128]{2,1,0:T(8,128)S(1)}, f32[1,256,128]{2,1,0:T(8,128)S(1)}, u32[]{:S(2)}, u32[]{:S(2)}) collective-permute-start(f32[1,256,128]{2,1,0:T(8,128)S(1)} %get-tuple-element.41.field_ref.refs_0_), channel_id=1, source_target_pairs={{0,16},{1,2},{2,1},{3,4},{4,3},{5,6},{6,5},{7,8},{8,7},{9,10},{10,... | collective-permute-start | bytes 393224 | tf_op jit(solution)/shard_map/ppermute | solution.py:339
  9.2 1.0 %collective-permute-start.17 = (f32[1,256,128]{2,1,0:T(8,128)S(1)}, f32[1,256,128]{2,1,0:T(8,128)S(1)}, u32[]{:S(2)}, u32[]{:S(2)}) collective-permute-start(f32[1,256,128]{2,1,0:T(8,128)S(1)} %get-tuple-element.41.field_ref.refs_0_), channel_id=1, source_target_pairs={{0,1},{1,0},{2,3},{3,2},{4,5},{5,4},{6,7},{7,6},{8,9},{9,8},{10,11... | collective-permute-start | bytes 393224 | tf_op jit(solution)/shard_map/ppermute | solution.py:340
  10.1 1.5 %collective-permute-start.10 = (f32[1,256,128]{2,1,0:T(8,128)S(1)}, f32[1,256,128]{2,1,0:T(8,128)S(1)}, u32[]{:S(2)}, u32[]{:S(2)}) collective-permute-start(f32[1,256,128]{2,1,0:T(8,128)S(1)} %get-tuple-element.40.field_ref.refs_3_.refs_4_), channel_id=1, source_target_pairs={{0,16},{1,2},{2,1},{3,4},{4,3},{5,6},{6,5},{7,8},{8,7},{9,10},{10,... | collective-permute-start | bytes 393224 | tf_op jit(solution)/shard_map/ppermute | solution.py:339
  11.6 0.0 collective-permute-done.near_ref
  11.6 0.0 collective-permute-start.11
  11.6 0.0 collective-permute-done.1.far_ref
  11.6 0.9 %shard_map.96 = (f32[256,128]{1,0:T(8,128)}, f32[1,256,128]{2,1,0:T(8,128)S(1)}) custom-call(f32[1,256,128]{2,1,0:T(8,128)S(1)} %collective-permute-done.near_ref, f32[1,256,128]{2,1,0:T(8,128)S(1)} %collective-permute-done.1.far_ref, f32[3,256,128]{2,1,0:T(8,128)S(1)} %get-tuple-element.30.right_ref, f32[256,128]{1,0:T(8,128)S(1)} %get-tuple-element.31.part_ref, ...), custom_call_target="tpu_custom_call" | custom-call | tf_op jit(solution)/shard_map/pallas_call | solution.py:311
  12.5 1.2 %collective-permute-start.4 = (f32[1,256,128]{2,1,0:T(8,128)S(1)}, f32[1,256,128]{2,1,0:T(8,128)S(1)}, u32[]{:S(2)}, u32[]{:S(2)}) collective-permute-start(f32[1,256,128]{2,1,0:T(8,128)S(1)} %get-tuple-element.38.field_ref.refs_6_.refs_8_), channel_id=1, source_target_pairs={{0,16},{1,2},{2,1},{3,4},{4,3},{5,6},{6,5},{7,8},{8,7},{9,10},{10,... | collective-permute-start | bytes 393224 | tf_op jit(solution)/shard_map/ppermute | solution.py:339
  13.8 0.0 collective-permute-done.16.far_ref
  13.8 1.1 %collective-permute-start.5 = (f32[1,256,128]{2,1,0:T(8,128)S(1)}, f32[1,256,128]{2,1,0:T(8,128)S(1)}, u32[]{:S(2)}, u32[]{:S(2)}) collective-permute-start(f32[1,256,128]{2,1,0:T(8,128)S(1)} %get-tuple-element.38.field_ref.refs_6_.refs_8_), channel_id=1, source_target_pairs={{0,1},{1,0},{2,3},{3,2},{4,5},{5,4},{6,7},{7,6},{8,9},{9,8},{10,11... | collective-permute-start | bytes 393224 | tf_op jit(solution)/shard_map/ppermute | solution.py:340
  14.9 0.3 shard_map.101.field_ref.refs_1_
  15.1 1.6 %collective-permute-start.18 = (f32[1,256,128]{2,1,0:T(8,128)S(1)}, f32[1,256,128]{2,1,0:T(8,128)S(1)}, u32[]{:S(2)}, u32[]{:S(2)}) collective-permute-start(f32[1,256,128]{2,1,0:T(8,128)S(1)} %shard_map.101.field_ref.refs_1_), channel_id=1, source_target_pairs={{0,16},{1,2},{2,1},{3,4},{4,3},{5,6},{6,5},{7,8},{8,7},{9,10},{10,... | collective-permute-start | bytes 393224 | tf_op jit(solution)/shard_map/ppermute | solution.py:339
  16.7 1.0 %collective-permute-start.19 = (f32[1,256,128]{2,1,0:T(8,128)S(1)}, f32[1,256,128]{2,1,0:T(8,128)S(1)}, u32[]{:S(2)}, u32[]{:S(2)}) collective-permute-start(f32[1,256,128]{2,1,0:T(8,128)S(1)} %shard_map.101.field_ref.refs_1_), channel_id=1, source_target_pairs={{0,1},{1,0},{2,3},{3,2},{4,5},{5,4},{6,7},{7,6},{8,9},{9,8},{10,11... | collective-permute-start | bytes 393224 | tf_op jit(solution)/shard_map/ppermute | solution.py:340
  17.7 0.0 collective-permute-done.11.near_ref
  17.7 0.3 shard_map.99.field_ref.refs_4_.refs_5_
  18.0 1.6 %collective-permute-start.12 = (f32[1,256,128]{2,1,0:T(8,128)S(1)}, f32[1,256,128]{2,1,0:T(8,128)S(1)}, u32[]{:S(2)}, u32[]{:S(2)}) collective-permute-start(f32[1,256,128]{2,1,0:T(8,128)S(1)} %shard_map.99.field_ref.refs_4_.refs_5_), channel_id=1, source_target_pairs={{0,16},{1,2},{2,1},{3,4},{4,3},{5,6},{6,5},{7,8},{8,7},{9,10},{10,... | collective-permute-start | bytes 393224 | tf_op jit(solution)/shard_map/ppermute | solution.py:339
  19.5 1.0 %collective-permute-start.13 = (f32[1,256,128]{2,1,0:T(8,128)S(1)}, f32[1,256,128]{2,1,0:T(8,128)S(1)}, u32[]{:S(2)}, u32[]{:S(2)}) collective-permute-start(f32[1,256,128]{2,1,0:T(8,128)S(1)} %shard_map.99.field_ref.refs_4_.refs_5_), channel_id=1, source_target_pairs={{0,1},{1,0},{2,3},{3,2},{4,5},{5,4},{6,7},{7,6},{8,9},{9,8},{10,11... | collective-permute-start | bytes 393224 | tf_op jit(solution)/shard_map/ppermute | solution.py:340
  20.5 0.3 shard_map.97.field_ref.refs_7_.refs_9_
  20.8 1.6 %collective-permute-start.6 = (f32[1,256,128]{2,1,0:T(8,128)S(1)}, f32[1,256,128]{2,1,0:T(8,128)S(1)}, u32[]{:S(2)}, u32[]{:S(2)}) collective-permute-start(f32[1,256,128]{2,1,0:T(8,128)S(1)} %shard_map.97.field_ref.refs_7_.refs_9_), channel_id=1, source_target_pairs={{0,16},{1,2},{2,1},{3,4},{4,3},{5,6},{6,5},{7,8},{8,7},{9,10},{10,... | collective-permute-start | bytes 393224 | tf_op jit(solution)/shard_map/ppermute | solution.py:339
  22.3 0.5 collective-permute-start.7
  22.8 0.0 collective-permute-done.19.near_ref
  22.8 0.3 shard_map.102.refs_2_.field_ref
  23.1 1.6 %collective-permute-start.20 = (f32[1,256,128]{2,1,0:T(8,128)S(1)}, f32[1,256,128]{2,1,0:T(8,128)S(1)}, u32[]{:S(2)}, u32[]{:S(2)}) collective-permute-start(f32[1,256,128]{2,1,0:T(8,128)S(1)} %shard_map.102.refs_2_.field_ref), channel_id=1, source_target_pairs={{0,16},{1,2},{2,1},{3,4},{4,3},{5,6},{6,5},{7,8},{8,7},{9,10},{10,... | collective-permute-start | bytes 393224 | tf_op jit(solution)/shard_map/ppermute | solution.py:339
  24.6 0.0 collective-permute-done.12.far_ref
  24.6 1.5 %collective-permute-start.21 = (f32[1,256,128]{2,1,0:T(8,128)S(1)}, f32[1,256,128]{2,1,0:T(8,128)S(1)}, u32[]{:S(2)}, u32[]{:S(2)}) collective-permute-start(f32[1,256,128]{2,1,0:T(8,128)S(1)} %shard_map.102.refs_2_.field_ref), channel_id=1, source_target_pairs={{0,1},{1,0},{2,3},{3,2},{4,5},{5,4},{6,7},{7,6},{8,9},{9,8},{10,11... | collective-permute-start | bytes 393224 | tf_op jit(solution)/shard_map/ppermute | solution.py:340
  26.1 0.0 collective-permute-done.13.near_ref
  26.1 0.3 shard_map.100.refs_5_.field_ref.refs_6_
  26.4 1.6 %collective-permute-start.14 = (f32[1,256,128]{2,1,0:T(8,128)S(1)}, f32[1,256,128]{2,1,0:T(8,128)S(1)}, u32[]{:S(2)}, u32[]{:S(2)}) collective-permute-start(f32[1,256,128]{2,1,0:T(8,128)S(1)} %shard_map.100.refs_5_.field_ref.refs_6_), channel_id=1, source_target_pairs={{0,16},{1,2},{2,1},{3,4},{4,3},{5,6},{6,5},{7,8},{8,7},{9,10},{10,... | collective-permute-start | bytes 393224 | tf_op jit(solution)/shard_map/ppermute | solution.py:339
  27.9 0.0 collective-permute-done.6.far_ref
  27.9 1.0 %collective-permute-start.15 = (f32[1,256,128]{2,1,0:T(8,128)S(1)}, f32[1,256,128]{2,1,0:T(8,128)S(1)}, u32[]{:S(2)}, u32[]{:S(2)}) collective-permute-start(f32[1,256,128]{2,1,0:T(8,128)S(1)} %shard_map.100.refs_5_.field_ref.refs_6_), channel_id=1, source_target_pairs={{0,1},{1,0},{2,3},{3,2},{4,5},{5,4},{6,7},{7,6},{8,9},{9,8},{10,11... | collective-permute-start | bytes 393224 | tf_op jit(solution)/shard_map/ppermute | solution.py:340
  28.9 0.3 shard_map.98.refs_8_.field_ref.refs_10_
  29.2 1.6 %collective-permute-start.8 = (f32[1,256,128]{2,1,0:T(8,128)S(1)}, f32[1,256,128]{2,1,0:T(8,128)S(1)}, u32[]{:S(2)}, u32[]{:S(2)}) collective-permute-start(f32[1,256,128]{2,1,0:T(8,128)S(1)} %shard_map.98.refs_8_.field_ref.refs_10_), channel_id=1, source_target_pairs={{0,16},{1,2},{2,1},{3,4},{4,3},{5,6},{6,5},{7,8},{8,7},{9,10},{10,... | collective-permute-start | bytes 393224 | tf_op jit(solution)/shard_map/ppermute | solution.py:339
  30.7 1.0 %collective-permute-start.9 = (f32[1,256,128]{2,1,0:T(8,128)S(1)}, f32[1,256,128]{2,1,0:T(8,128)S(1)}, u32[]{:S(2)}, u32[]{:S(2)}) collective-permute-start(f32[1,256,128]{2,1,0:T(8,128)S(1)} %shard_map.98.refs_8_.field_ref.refs_10_), channel_id=1, source_target_pairs={{0,1},{1,0},{2,3},{3,2},{4,5},{5,4},{6,7},{7,6},{8,9},{9,8},{10,11... | collective-permute-start | bytes 393224 | tf_op jit(solution)/shard_map/ppermute | solution.py:340
  31.7 1.5 %shard_map.103 = (f32[8,128]{1,0:T(8,128)S(1)}, f32[5,3,256,128]{3,2,1,0:T(8,128)S(1)}, f32[5,3,256,128]{3,2,1,0:T(8,128)S(1)}) custom-call(f32[256,128]{1,0:T(8,128)S(1)} %get-tuple-element.42.diagonal_ref, f32[1,256,128]{2,1,0:T(8,128)S(1)} %get-tuple-element.41.field_ref.refs_0_, f32[1,256,128]{2,1,0:T(8,128)S(1)} %shard_map.101.field_ref.refs_1_, ...), custom_call_target="tpu_custom_call" | custom-call | tf_op jit(solution)/shard_map/pallas_call | solution.py:311
  33.2 0.4 shard_map.104
  33.7 0.4 shard_map.105
  34.1 0.1 collective-permute-done.8.far_ref
  34.2 0.5 shard_map.106
  34.7 15.6 %all_to_all.5.moments_ref = f32[32,1,128]{2,1,0:T(1,128)S(1)} all-to-all(f32[32,1,128]{2,1,0:T(1,128)S(1)} %get-tuple-element.48), channel_id=1, replica_groups=mesh['diamond'=2,'tile'=16] {'diamond','tile'}, dimensions={0} | all-to-all | bytes 32768 | tf_op jit(solution)/shard_map/all_to_all | solution.py:389
  50.3 1.2 %shard_map.107 = (f32[3,256,128]{2,1,0:T(8,128)}, f32[3,256,128]{2,1,0:T(8,128)}) custom-call(f32[32,1,128]{2,1,0:T(1,128)S(1)} %all_to_all.5.moments_ref, f32[256,128]{1,0:T(8,128)S(1)} %get-tuple-element.42.diagonal_ref, f32[1,256,128]{2,1,0:T(8,128)S(1)} %get-tuple-element.41.field_ref.refs_0_, f32[1,256,128]{2,1,0:T(8,128)S(1)} %shard_map.101.field_ref.refs_1_, ...), custom_call_target="tpu_custom_call" | custom-call | tf_op jit(solution)/shard_map/pallas_call | solution.py:311
  (11 shorter events, 0.0 us)
Async XLA Ops:
  0.6 6.4 %collective-permute-start.2 = (f32[1,256,128]{2,1,0:T(8,128)}, f32[1,256,128]{2,1,0:T(8,128)S(1)}, u32[]{:S(2)}, u32[]{:S(2)}) collective-permute-start(f32[1,256,128]{2,1,0:T(8,128)} %bitcast.20), channel_id=1, source_target_pairs={{0,16},{1,2},{2,1},{3,4},{4,3},{5,6},{6,5},{7,8},{8,7},{9,10},{10,... | collective-permute-start | bytes 393224 | tf_op jit(solution)/shard_map/ppermute | solution.py:339
  3.6 3.4 %collective-permute-start.3 = (f32[1,256,128]{2,1,0:T(8,128)}, f32[1,256,128]{2,1,0:T(8,128)S(1)}, u32[]{:S(2)}, u32[]{:S(2)}) collective-permute-start(f32[1,256,128]{2,1,0:T(8,128)} %bitcast.21), channel_id=1, source_target_pairs={{0,1},{1,0},{2,3},{3,2},{4,5},{5,4},{6,7},{7,6},{8,9},{9,8},{10,11... | collective-permute-start | bytes 393224 | tf_op jit(solution)/shard_map/ppermute | solution.py:340
  5.4 6.2 %collective-permute-start = (f32[1,256,128]{2,1,0:T(8,128)S(1)}, f32[1,256,128]{2,1,0:T(8,128)S(1)}, u32[]{:S(2)}, u32[]{:S(2)}) collective-permute-start(f32[1,256,128]{2,1,0:T(8,128)S(1)} %bitcast.14), channel_id=1, source_target_pairs={{0,1},{1,0},{2,3},{3,2},{4,5},{5,4},{6,7},{7,6},{8,9},{9,8},{10,11... | collective-permute-start | bytes 393224 | tf_op jit(solution)/shard_map/ppermute | solution.py:340
  5.9 5.8 %collective-permute-start.1 = (f32[1,256,128]{2,1,0:T(8,128)S(1)}, f32[1,256,128]{2,1,0:T(8,128)S(1)}, u32[]{:S(2)}, u32[]{:S(2)}) collective-permute-start(f32[1,256,128]{2,1,0:T(8,128)S(1)} %bitcast.15), channel_id=1, source_target_pairs={{0,16},{1,2},{2,1},{3,4},{4,3},{5,6},{6,5},{7,8},{8,7},{9,10},{10,... | collective-permute-start | bytes 393224 | tf_op jit(solution)/shard_map/ppermute | solution.py:339
  7.4 6.4 %collective-permute-start.16 = (f32[1,256,128]{2,1,0:T(8,128)S(1)}, f32[1,256,128]{2,1,0:T(8,128)S(1)}, u32[]{:S(2)}, u32[]{:S(2)}) collective-permute-start(f32[1,256,128]{2,1,0:T(8,128)S(1)} %get-tuple-element.41.field_ref.refs_0_), channel_id=1, source_target_pairs={{0,16},{1,2},{2,1},{3,4},{4,3},{5,6},{6,5},{7,8},{8,7},{9,10},{10,... | collective-permute-start | bytes 393224 | tf_op jit(solution)/shard_map/ppermute | solution.py:339
  9.2 5.7 %collective-permute-start.17 = (f32[1,256,128]{2,1,0:T(8,128)S(1)}, f32[1,256,128]{2,1,0:T(8,128)S(1)}, u32[]{:S(2)}, u32[]{:S(2)}) collective-permute-start(f32[1,256,128]{2,1,0:T(8,128)S(1)} %get-tuple-element.41.field_ref.refs_0_), channel_id=1, source_target_pairs={{0,1},{1,0},{2,3},{3,2},{4,5},{5,4},{6,7},{7,6},{8,9},{9,8},{10,11... | collective-permute-start | bytes 393224 | tf_op jit(solution)/shard_map/ppermute | solution.py:340
  10.1 6.5 %collective-permute-start.10 = (f32[1,256,128]{2,1,0:T(8,128)S(1)}, f32[1,256,128]{2,1,0:T(8,128)S(1)}, u32[]{:S(2)}, u32[]{:S(2)}) collective-permute-start(f32[1,256,128]{2,1,0:T(8,128)S(1)} %get-tuple-element.40.field_ref.refs_3_.refs_4_), channel_id=1, source_target_pairs={{0,16},{1,2},{2,1},{3,4},{4,3},{5,6},{6,5},{7,8},{8,7},{9,10},{10,... | collective-permute-start | bytes 393224 | tf_op jit(solution)/shard_map/ppermute | solution.py:339
  11.6 6.1 %collective-permute-start.11 = (f32[1,256,128]{2,1,0:T(8,128)S(1)}, f32[1,256,128]{2,1,0:T(8,128)S(1)}, u32[]{:S(2)}, u32[]{:S(2)}) collective-permute-start(f32[1,256,128]{2,1,0:T(8,128)S(1)} %get-tuple-element.40.field_ref.refs_3_.refs_4_), channel_id=1, source_target_pairs={{0,1},{1,0},{2,3},{3,2},{4,5},{5,4},{6,7},{7,6},{8,9},{9,8},{10,11... | collective-permute-start | bytes 393224 | tf_op jit(solution)/shard_map/ppermute | solution.py:340
  12.5 7.0 %collective-permute-start.4 = (f32[1,256,128]{2,1,0:T(8,128)S(1)}, f32[1,256,128]{2,1,0:T(8,128)S(1)}, u32[]{:S(2)}, u32[]{:S(2)}) collective-permute-start(f32[1,256,128]{2,1,0:T(8,128)S(1)} %get-tuple-element.38.field_ref.refs_6_.refs_8_), channel_id=1, source_target_pairs={{0,16},{1,2},{2,1},{3,4},{4,3},{5,6},{6,5},{7,8},{8,7},{9,10},{10,... | collective-permute-start | bytes 393224 | tf_op jit(solution)/shard_map/ppermute | solution.py:339
  13.8 6.7 %collective-permute-start.5 = (f32[1,256,128]{2,1,0:T(8,128)S(1)}, f32[1,256,128]{2,1,0:T(8,128)S(1)}, u32[]{:S(2)}, u32[]{:S(2)}) collective-permute-start(f32[1,256,128]{2,1,0:T(8,128)S(1)} %get-tuple-element.38.field_ref.refs_6_.refs_8_), channel_id=1, source_target_pairs={{0,1},{1,0},{2,3},{3,2},{4,5},{5,4},{6,7},{7,6},{8,9},{9,8},{10,11... | collective-permute-start | bytes 393224 | tf_op jit(solution)/shard_map/ppermute | solution.py:340
  15.1 7.2 %collective-permute-start.18 = (f32[1,256,128]{2,1,0:T(8,128)S(1)}, f32[1,256,128]{2,1,0:T(8,128)S(1)}, u32[]{:S(2)}, u32[]{:S(2)}) collective-permute-start(f32[1,256,128]{2,1,0:T(8,128)S(1)} %shard_map.101.field_ref.refs_1_), channel_id=1, source_target_pairs={{0,16},{1,2},{2,1},{3,4},{4,3},{5,6},{6,5},{7,8},{8,7},{9,10},{10,... | collective-permute-start | bytes 393224 | tf_op jit(solution)/shard_map/ppermute | solution.py:339
  16.7 6.1 %collective-permute-start.19 = (f32[1,256,128]{2,1,0:T(8,128)S(1)}, f32[1,256,128]{2,1,0:T(8,128)S(1)}, u32[]{:S(2)}, u32[]{:S(2)}) collective-permute-start(f32[1,256,128]{2,1,0:T(8,128)S(1)} %shard_map.101.field_ref.refs_1_), channel_id=1, source_target_pairs={{0,1},{1,0},{2,3},{3,2},{4,5},{5,4},{6,7},{7,6},{8,9},{9,8},{10,11... | collective-permute-start | bytes 393224 | tf_op jit(solution)/shard_map/ppermute | solution.py:340
  18.0 6.7 %collective-permute-start.12 = (f32[1,256,128]{2,1,0:T(8,128)S(1)}, f32[1,256,128]{2,1,0:T(8,128)S(1)}, u32[]{:S(2)}, u32[]{:S(2)}) collective-permute-start(f32[1,256,128]{2,1,0:T(8,128)S(1)} %shard_map.99.field_ref.refs_4_.refs_5_), channel_id=1, source_target_pairs={{0,16},{1,2},{2,1},{3,4},{4,3},{5,6},{6,5},{7,8},{8,7},{9,10},{10,... | collective-permute-start | bytes 393224 | tf_op jit(solution)/shard_map/ppermute | solution.py:339
  19.5 6.6 %collective-permute-start.13 = (f32[1,256,128]{2,1,0:T(8,128)S(1)}, f32[1,256,128]{2,1,0:T(8,128)S(1)}, u32[]{:S(2)}, u32[]{:S(2)}) collective-permute-start(f32[1,256,128]{2,1,0:T(8,128)S(1)} %shard_map.99.field_ref.refs_4_.refs_5_), channel_id=1, source_target_pairs={{0,1},{1,0},{2,3},{3,2},{4,5},{5,4},{6,7},{7,6},{8,9},{9,8},{10,11... | collective-permute-start | bytes 393224 | tf_op jit(solution)/shard_map/ppermute | solution.py:340
  20.8 7.2 %collective-permute-start.6 = (f32[1,256,128]{2,1,0:T(8,128)S(1)}, f32[1,256,128]{2,1,0:T(8,128)S(1)}, u32[]{:S(2)}, u32[]{:S(2)}) collective-permute-start(f32[1,256,128]{2,1,0:T(8,128)S(1)} %shard_map.97.field_ref.refs_7_.refs_9_), channel_id=1, source_target_pairs={{0,16},{1,2},{2,1},{3,4},{4,3},{5,6},{6,5},{7,8},{8,7},{9,10},{10,... | collective-permute-start | bytes 393224 | tf_op jit(solution)/shard_map/ppermute | solution.py:339
  22.3 6.6 %collective-permute-start.7 = (f32[1,256,128]{2,1,0:T(8,128)S(1)}, f32[1,256,128]{2,1,0:T(8,128)S(1)}, u32[]{:S(2)}, u32[]{:S(2)}) collective-permute-start(f32[1,256,128]{2,1,0:T(8,128)S(1)} %shard_map.97.field_ref.refs_7_.refs_9_), channel_id=1, source_target_pairs={{0,1},{1,0},{2,3},{3,2},{4,5},{5,4},{6,7},{7,6},{8,9},{9,8},{10,11... | collective-permute-start | bytes 393224 | tf_op jit(solution)/shard_map/ppermute | solution.py:340
  23.1 7.7 %collective-permute-start.20 = (f32[1,256,128]{2,1,0:T(8,128)S(1)}, f32[1,256,128]{2,1,0:T(8,128)S(1)}, u32[]{:S(2)}, u32[]{:S(2)}) collective-permute-start(f32[1,256,128]{2,1,0:T(8,128)S(1)} %shard_map.102.refs_2_.field_ref), channel_id=1, source_target_pairs={{0,16},{1,2},{2,1},{3,4},{4,3},{5,6},{6,5},{7,8},{8,7},{9,10},{10,... | collective-permute-start | bytes 393224 | tf_op jit(solution)/shard_map/ppermute | solution.py:339
  24.6 8.6 %collective-permute-start.21 = (f32[1,256,128]{2,1,0:T(8,128)S(1)}, f32[1,256,128]{2,1,0:T(8,128)S(1)}, u32[]{:S(2)}, u32[]{:S(2)}) collective-permute-start(f32[1,256,128]{2,1,0:T(8,128)S(1)} %shard_map.102.refs_2_.field_ref), channel_id=1, source_target_pairs={{0,1},{1,0},{2,3},{3,2},{4,5},{5,4},{6,7},{7,6},{8,9},{9,8},{10,11... | collective-permute-start | bytes 393224 | tf_op jit(solution)/shard_map/ppermute | solution.py:340
  26.4 7.3 %collective-permute-start.14 = (f32[1,256,128]{2,1,0:T(8,128)S(1)}, f32[1,256,128]{2,1,0:T(8,128)S(1)}, u32[]{:S(2)}, u32[]{:S(2)}) collective-permute-start(f32[1,256,128]{2,1,0:T(8,128)S(1)} %shard_map.100.refs_5_.field_ref.refs_6_), channel_id=1, source_target_pairs={{0,16},{1,2},{2,1},{3,4},{4,3},{5,6},{6,5},{7,8},{8,7},{9,10},{10,... | collective-permute-start | bytes 393224 | tf_op jit(solution)/shard_map/ppermute | solution.py:339
  27.9 5.8 %collective-permute-start.15 = (f32[1,256,128]{2,1,0:T(8,128)S(1)}, f32[1,256,128]{2,1,0:T(8,128)S(1)}, u32[]{:S(2)}, u32[]{:S(2)}) collective-permute-start(f32[1,256,128]{2,1,0:T(8,128)S(1)} %shard_map.100.refs_5_.field_ref.refs_6_), channel_id=1, source_target_pairs={{0,1},{1,0},{2,3},{3,2},{4,5},{5,4},{6,7},{7,6},{8,9},{9,8},{10,11... | collective-permute-start | bytes 393224 | tf_op jit(solution)/shard_map/ppermute | solution.py:340
  29.2 5.0 %collective-permute-start.8 = (f32[1,256,128]{2,1,0:T(8,128)S(1)}, f32[1,256,128]{2,1,0:T(8,128)S(1)}, u32[]{:S(2)}, u32[]{:S(2)}) collective-permute-start(f32[1,256,128]{2,1,0:T(8,128)S(1)} %shard_map.98.refs_8_.field_ref.refs_10_), channel_id=1, source_target_pairs={{0,16},{1,2},{2,1},{3,4},{4,3},{5,6},{6,5},{7,8},{8,7},{9,10},{10,... | collective-permute-start | bytes 393224 | tf_op jit(solution)/shard_map/ppermute | solution.py:339
  30.7 3.5 %collective-permute-start.9 = (f32[1,256,128]{2,1,0:T(8,128)S(1)}, f32[1,256,128]{2,1,0:T(8,128)S(1)}, u32[]{:S(2)}, u32[]{:S(2)}) collective-permute-start(f32[1,256,128]{2,1,0:T(8,128)S(1)} %shard_map.98.refs_8_.field_ref.refs_10_), channel_id=1, source_target_pairs={{0,1},{1,0},{2,3},{3,2},{4,5},{5,4},{6,7},{7,6},{8,9},{9,8},{10,11... | collective-permute-start | bytes 393224 | tf_op jit(solution)/shard_map/ppermute | solution.py:340

commit v11 on v10

--- a/solution.py
+++ b/solution.py
@@ -144,7 +144,7 @@
     return mid - sum(w * v for w, v in zip(weights, around))
 
 
-def apply_kernel(far_ref, near_ref, field_ref, weights_ref, matrix_ref, out_ref, moved_ref):
+def apply_kernel(near_ref, far_ref, field_ref, weights_ref, matrix_ref, out_ref, moved_ref):
     unfold(matrix_ref, far_ref, moved_ref)
     for start in range(0, field_ref.shape[1], CHUNK):
         here = slice(start, start + CHUNK)
@@ -220,6 +220,10 @@
         row = jnp.sum(message, axis=0, keepdims=True)
         for device in range(moments_ref.shape[0]):
             moments_ref[device] = row
+
+
+def last_near_kernel(low, near_ref, far_ref, *refs):
+    last_kernel(low, far_ref, near_ref, *refs)
 
 
 def inner(left, right, moments, shift=0):
@@ -371,7 +375,7 @@
     for step in range(ITERS - 1):
         for i, shape in enumerate(shapes):
             near, far = swapped[i]
-            (field,) = call(apply_kernel, [shape], far, near, streams[i][-1], weights, matrix, scratch=[shape])
+            (field,) = call(apply_kernel, [shape], near, far, streams[i][-1], weights, matrix, scratch=[shape])
             swapped[i] = exchange(field)
             streams[i].append(field)
     many = (len(CENTERS), *triple)
@@ -381,9 +385,10 @@
     for i, shape in enumerate(shapes):
         near, far = swapped[i]
         sums = (8, 128) if i + 1 < len(shapes) else (devices, 1, 128)
+        kernel, halo = (last_near_kernel, [near, far]) if i == 0 else (last_kernel, [far, near])
         field, moments = call(
-            functools.partial(last_kernel, SPLITS[i][0]), [shape, sums],
-            far, near, streams[i][-1], weights, matrix, moments, left, shift, scratch=[shape],
+            functools.partial(kernel, SPLITS[i][0]), [shape, sums],
+            *halo, streams[i][-1], weights, matrix, moments, left, shift, scratch=[shape],
         )
         streams[i].append(field)
     moments = lax.all_to_all(moments, NAMES, 0, 0)

time: 51.7 us -> 50.5 us (0.977)
  blocking collectives: 15.6 us -> 14.4 us
    ppermute x11, starting transfers between devices: 8.54 us -> 9.96 us  [exchange(): near = lax.ppermute(value, NAMES, beside)]
    ppermute x11, starting transfers between devices: 18.1 us -> 16.8 us  [exchange(): far = lax.ppermute(value, NAMES, across)]
    all_to_all x1, blocking collectives: 15.6 us -> 14.4 us  [body(): moments = lax.all_to_all(moments, NAMES, 0, 0)]
  transfers between devices with their start and end apart: 22 -> 22, of which waited for: 1 -> 0; matrix products, arithmetic and copies ran while one was open for 0% -> 0% of each run, Pallas kernels for 13% -> 13%
where the time goes in v11:
time: 50.5 us; the launch traced here: 50.3 us
  starting transfers between devices  26.7 us (53%)
  blocking collectives  14.4 us (29%)
  Pallas kernels  8.42 us (17%)
  between operations  0.72 us (1%)
    ppermute x11, starting transfers between devices, exchange(): far = lax.ppermute(value, NAMES, across)  16.8 us
    all_to_all x1, blocking collectives, body(): moments = lax.all_to_all(moments, NAMES, 0, 0)  14.4 us
    ppermute x11, starting transfers between devices, exchange(): near = lax.ppermute(value, NAMES, beside)  9.96 us
    pallas_call x14, Pallas kernels, call(): pl.pallas_call(kernel, out_shape=outs, in_specs=[pl.BlockSpec(memory_spac...  8.42 us
  transfers between devices with their start and end apart: 22, of which 0 were waited for; matrix products, arithmetic and copies ran while one was open for 0% of the time, Pallas kernels for 13%

profile of v11, /device:TPU:0, one launch (start us, length us, event | category | flops | bytes accessed | tf_op | source)
XLA Modules:
  0.0 50.3 jit_solution(9452504120040161505)
XLA Ops:
  0.6 3.0 %collective-permute-start.2 = (f32[1,256,128]{2,1,0:T(8,128)}, f32[1,256,128]{2,1,0:T(8,128)S(1)}, u32[]{:S(2)}, u32[]{:S(2)}) collective-permute-start(f32[1,256,128]{2,1,0:T(8,128)} %bitcast.20), channel_id=1, source_target_pairs={{0,16},{1,2},{2,1},{3,4},{4,3},{5,6},{6,5},{7,8},{8,7},{9,10},{10,... | collective-permute-start | bytes 393224 | tf_op jit(solution)/shard_map/ppermute | solution.py:343
  3.6 0.1 collective-permute-start.3
  3.8 1.7 %shard_map.94 = (f32[256,128]{1,0:T(8,128)S(1)}, f32[4,256,128]{2,1,0:T(8,128)S(1)}, f32[256,128]{1,0:T(8,128)S(1)}, f32[3,256,128]{2,1,0:T(8,128)S(1)}, f32[256...) custom-call(f32[256,128]{1,0:T(8,128)} %bitcast.18, ...), custom_call_target="tpu_custom_call" | custom-call | tf_op jit(solution)/shard_map/pallas_call | solution.py:315
  5.4 0.4 collective-permute-start
  5.9 1.2 %collective-permute-start.1 = (f32[1,256,128]{2,1,0:T(8,128)S(1)}, f32[1,256,128]{2,1,0:T(8,128)S(1)}, u32[]{:S(2)}, u32[]{:S(2)}) collective-permute-start(f32[1,256,128]{2,1,0:T(8,128)S(1)} %bitcast.15), channel_id=1, source_target_pairs={{0,16},{1,2},{2,1},{3,4},{4,3},{5,6},{6,5},{7,8},{8,7},{9,10},{10,... | collective-permute-start | bytes 393224 | tf_op jit(solution)/shard_map/ppermute | solution.py:343
  7.1 0.0 collective-permute-done.2.far_ref
  7.1 0.0 collective-permute-done.3.near_ref
  7.1 0.3 shard_map.95
  7.4 0.4 collective-permute-start.16
  7.8 1.5 %collective-permute-start.17 = (f32[1,256,128]{2,1,0:T(8,128)S(1)}, f32[1,256,128]{2,1,0:T(8,128)S(1)}, u32[]{:S(2)}, u32[]{:S(2)}) collective-permute-start(f32[1,256,128]{2,1,0:T(8,128)S(1)} %get-tuple-element.41.field_ref.refs_0_), channel_id=1, source_target_pairs={{0,16},{1,2},{2,1},{3,4},{4,3},{5,6},{6,5},{7,8},{8,7},{9,10},{10,... | collective-permute-start | bytes 393224 | tf_op jit(solution)/shard_map/ppermute | solution.py:343
  9.3 0.9 %collective-permute-start.10 = (f32[1,256,128]{2,1,0:T(8,128)S(1)}, f32[1,256,128]{2,1,0:T(8,128)S(1)}, u32[]{:S(2)}, u32[]{:S(2)}) collective-permute-start(f32[1,256,128]{2,1,0:T(8,128)S(1)} %get-tuple-element.40.field_ref.refs_3_.refs_4_), channel_id=1, source_target_pairs={{0,1},{1,0},{2,3},{3,2},{4,5},{5,4},{6,7},{7,6},{8,9},{9,8},{10,11... | collective-permute-start | bytes 393224 | tf_op jit(solution)/shard_map/ppermute | solution.py:344
  10.2 0.0 collective-permute-done.near_ref
  10.2 1.5 %collective-permute-start.11 = (f32[1,256,128]{2,1,0:T(8,128)S(1)}, f32[1,256,128]{2,1,0:T(8,128)S(1)}, u32[]{:S(2)}, u32[]{:S(2)}) collective-permute-start(f32[1,256,128]{2,1,0:T(8,128)S(1)} %get-tuple-element.40.field_ref.refs_3_.refs_4_), channel_id=1, source_target_pairs={{0,16},{1,2},{2,1},{3,4},{4,3},{5,6},{6,5},{7,8},{8,7},{9,10},{10,... | collective-permute-start | bytes 393224 | tf_op jit(solution)/shard_map/ppermute | solution.py:343
  11.7 0.0 collective-permute-done.1.far_ref
  11.7 0.9 %shard_map.96 = (f32[256,128]{1,0:T(8,128)}, f32[1,256,128]{2,1,0:T(8,128)S(1)}) custom-call(f32[1,256,128]{2,1,0:T(8,128)S(1)} %collective-permute-done.near_ref, f32[1,256,128]{2,1,0:T(8,128)S(1)} %collective-permute-done.1.far_ref, f32[3,256,128]{2,1,0:T(8,128)S(1)} %get-tuple-element.30.right_ref, f32[256,128]{1,0:T(8,128)S(1)} %get-tuple-element.31.part_ref, ...), custom_call_target="tpu_custom_call" | custom-call | tf_op jit(solution)/shard_map/pallas_call | solution.py:315
  12.6 0.0 collective-permute-start.4
  12.6 0.0 collective-permute-done.16.near_ref
  12.6 1.4 %collective-permute-start.5 = (f32[1,256,128]{2,1,0:T(8,128)S(1)}, f32[1,256,128]{2,1,0:T(8,128)S(1)}, u32[]{:S(2)}, u32[]{:S(2)}) collective-permute-start(f32[1,256,128]{2,1,0:T(8,128)S(1)} %get-tuple-element.38.field_ref.refs_6_.refs_8_), channel_id=1, source_target_pairs={{0,16},{1,2},{2,1},{3,4},{4,3},{5,6},{6,5},{7,8},{8,7},{9,10},{10,... | collective-permute-start | bytes 393224 | tf_op jit(solution)/shard_map/ppermute | solution.py:343
  14.1 0.0 collective-permute-done.17.far_ref
  14.1 0.3 shard_map.101.field_ref.refs_1_
  14.3 0.4 collective-permute-start.18
  14.7 0.0 collective-permute-done.10.near_ref
  14.7 1.5 %collective-permute-start.19 = (f32[1,256,128]{2,1,0:T(8,128)S(1)}, f32[1,256,128]{2,1,0:T(8,128)S(1)}, u32[]{:S(2)}, u32[]{:S(2)}) collective-permute-start(f32[1,256,128]{2,1,0:T(8,128)S(1)} %shard_map.101.field_ref.refs_1_), channel_id=1, source_target_pairs={{0,16},{1,2},{2,1},{3,4},{4,3},{5,6},{6,5},{7,8},{8,7},{9,10},{10,... | collective-permute-start | bytes 393224 | tf_op jit(solution)/shard_map/ppermute | solution.py:343
  16.2 0.3 shard_map.99.field_ref.refs_4_.refs_5_
  16.5 1.6 %collective-permute-start.12 = (f32[1,256,128]{2,1,0:T(8,128)S(1)}, f32[1,256,128]{2,1,0:T(8,128)S(1)}, u32[]{:S(2)}, u32[]{:S(2)}) collective-permute-start(f32[1,256,128]{2,1,0:T(8,128)S(1)} %shard_map.99.field_ref.refs_4_.refs_5_), channel_id=1, source_target_pairs={{0,1},{1,0},{2,3},{3,2},{4,5},{5,4},{6,7},{7,6},{8,9},{9,8},{10,11... | collective-permute-start | bytes 393224 | tf_op jit(solution)/shard_map/ppermute | solution.py:344
  18.1 0.0 collective-permute-done.4.near_ref
  18.1 1.5 %collective-permute-start.13 = (f32[1,256,128]{2,1,0:T(8,128)S(1)}, f32[1,256,128]{2,1,0:T(8,128)S(1)}, u32[]{:S(2)}, u32[]{:S(2)}) collective-permute-start(f32[1,256,128]{2,1,0:T(8,128)S(1)} %shard_map.99.field_ref.refs_4_.refs_5_), channel_id=1, source_target_pairs={{0,16},{1,2},{2,1},{3,4},{4,3},{5,6},{6,5},{7,8},{8,7},{9,10},{10,... | collective-permute-start | bytes 393224 | tf_op jit(solution)/shard_map/ppermute | solution.py:343
  19.6 0.3 shard_map.97.field_ref.refs_7_.refs_9_
  19.9 1.1 %collective-permute-start.6 = (f32[1,256,128]{2,1,0:T(8,128)S(1)}, f32[1,256,128]{2,1,0:T(8,128)S(1)}, u32[]{:S(2)}, u32[]{:S(2)}) collective-permute-start(f32[1,256,128]{2,1,0:T(8,128)S(1)} %shard_map.97.field_ref.refs_7_.refs_9_), channel_id=1, source_target_pairs={{0,1},{1,0},{2,3},{3,2},{4,5},{5,4},{6,7},{7,6},{8,9},{9,8},{10,11... | collective-permute-start | bytes 393224 | tf_op jit(solution)/shard_map/ppermute | solution.py:344
  21.0 1.5 %collective-permute-start.7 = (f32[1,256,128]{2,1,0:T(8,128)S(1)}, f32[1,256,128]{2,1,0:T(8,128)S(1)}, u32[]{:S(2)}, u32[]{:S(2)}) collective-permute-start(f32[1,256,128]{2,1,0:T(8,128)S(1)} %shard_map.97.field_ref.refs_7_.refs_9_), channel_id=1, source_target_pairs={{0,16},{1,2},{2,1},{3,4},{4,3},{5,6},{6,5},{7,8},{8,7},{9,10},{10,... | collective-permute-start | bytes 393224 | tf_op jit(solution)/shard_map/ppermute | solution.py:343
  22.5 0.3 shard_map.102.refs_2_.refs_0_
  22.8 1.0 %collective-permute-start.20 = (f32[1,256,128]{2,1,0:T(8,128)S(1)}, f32[1,256,128]{2,1,0:T(8,128)S(1)}, u32[]{:S(2)}, u32[]{:S(2)}) collective-permute-start(f32[1,256,128]{2,1,0:T(8,128)S(1)} %shard_map.102.refs_2_.refs_0_), channel_id=1, source_target_pairs={{0,1},{1,0},{2,3},{3,2},{4,5},{5,4},{6,7},{7,6},{8,9},{9,8},{10,11... | collective-permute-start | bytes 393224 | tf_op jit(solution)/shard_map/ppermute | solution.py:344
  23.8 1.5 %collective-permute-start.21 = (f32[1,256,128]{2,1,0:T(8,128)S(1)}, f32[1,256,128]{2,1,0:T(8,128)S(1)}, u32[]{:S(2)}, u32[]{:S(2)}) collective-permute-start(f32[1,256,128]{2,1,0:T(8,128)S(1)} %shard_map.102.refs_2_.refs_0_), channel_id=1, source_target_pairs={{0,16},{1,2},{2,1},{3,4},{4,3},{5,6},{6,5},{7,8},{8,7},{9,10},{10,... | collective-permute-start | bytes 393224 | tf_op jit(solution)/shard_map/ppermute | solution.py:343
  25.3 0.3 shard_map.100.refs_5_.field_ref.refs_6_
  25.6 0.6 %collective-permute-start.14 = (f32[1,256,128]{2,1,0:T(8,128)S(1)}, f32[1,256,128]{2,1,0:T(8,128)S(1)}, u32[]{:S(2)}, u32[]{:S(2)}) collective-permute-start(f32[1,256,128]{2,1,0:T(8,128)S(1)} %shard_map.100.refs_5_.field_ref.refs_6_), channel_id=1, source_target_pairs={{0,16},{1,2},{2,1},{3,4},{4,3},{5,6},{6,5},{7,8},{8,7},{9,10},{10,... | collective-permute-start | bytes 393224 | tf_op jit(solution)/shard_map/ppermute | solution.py:343
  26.2 1.4 %collective-permute-start.15 = (f32[1,256,128]{2,1,0:T(8,128)S(1)}, f32[1,256,128]{2,1,0:T(8,128)S(1)}, u32[]{:S(2)}, u32[]{:S(2)}) collective-permute-start(f32[1,256,128]{2,1,0:T(8,128)S(1)} %shard_map.100.refs_5_.field_ref.refs_6_), channel_id=1, source_target_pairs={{0,1},{1,0},{2,3},{3,2},{4,5},{5,4},{6,7},{7,6},{8,9},{9,8},{10,11... | collective-permute-start | bytes 393224 | tf_op jit(solution)/shard_map/ppermute | solution.py:344
  27.6 0.0 collective-permute-done.7.far_ref
  27.6 0.3 shard_map.98.refs_8_.field_ref.refs_10_
  27.9 1.6 %collective-permute-start.8 = (f32[1,256,128]{2,1,0:T(8,128)S(1)}, f32[1,256,128]{2,1,0:T(8,128)S(1)}, u32[]{:S(2)}, u32[]{:S(2)}) collective-permute-start(f32[1,256,128]{2,1,0:T(8,128)S(1)} %shard_map.98.refs_8_.field_ref.refs_10_), channel_id=1, source_target_pairs={{0,16},{1,2},{2,1},{3,4},{4,3},{5,6},{6,5},{7,8},{8,7},{9,10},{10,... | collective-permute-start | bytes 393224 | tf_op jit(solution)/shard_map/ppermute | solution.py:343
  29.5 0.0 collective-permute-done.20.near_ref
  29.5 2.4 %collective-permute-start.9 = (f32[1,256,128]{2,1,0:T(8,128)S(1)}, f32[1,256,128]{2,1,0:T(8,128)S(1)}, u32[]{:S(2)}, u32[]{:S(2)}) collective-permute-start(f32[1,256,128]{2,1,0:T(8,128)S(1)} %shard_map.98.refs_8_.field_ref.refs_10_), channel_id=1, source_target_pairs={{0,1},{1,0},{2,3},{3,2},{4,5},{5,4},{6,7},{7,6},{8,9},{9,8},{10,11... | collective-permute-start | bytes 393224 | tf_op jit(solution)/shard_map/ppermute | solution.py:344
  31.8 1.5 %shard_map.103 = (f32[8,128]{1,0:T(8,128)S(1)}, f32[5,3,256,128]{3,2,1,0:T(8,128)S(1)}, f32[5,3,256,128]{3,2,1,0:T(8,128)S(1)}) custom-call(f32[256,128]{1,0:T(8,128)S(1)} %get-tuple-element.42.diagonal_ref, f32[1,256,128]{2,1,0:T(8,128)S(1)} %get-tuple-element.41.field_ref.refs_0_, f32[1,256,128]{2,1,0:T(8,128)S(1)} %shard_map.101.field_ref.refs_1_, ...), custom_call_target="tpu_custom_call" | custom-call | tf_op jit(solution)/shard_map/pallas_call | solution.py:315
  33.3 0.0 collective-permute-done.21.far_ref
  33.4 0.4 shard_map.104
  33.8 0.4 shard_map.105
  34.3 0.5 shard_map.106
  34.7 14.4 %all_to_all.5.moments_ref = f32[32,1,128]{2,1,0:T(1,128)S(1)} all-to-all(f32[32,1,128]{2,1,0:T(1,128)S(1)} %get-tuple-element.48), channel_id=1, replica_groups=mesh['diamond'=2,'tile'=16] {'diamond','tile'}, dimensions={0} | all-to-all | bytes 32768 | tf_op jit(solution)/shard_map/all_to_all | solution.py:394
  49.2 1.2 %shard_map.107 = (f32[3,256,128]{2,1,0:T(8,128)}, f32[3,256,128]{2,1,0:T(8,128)}) custom-call(f32[32,1,128]{2,1,0:T(1,128)S(1)} %all_to_all.5.moments_ref, f32[256,128]{1,0:T(8,128)S(1)} %get-tuple-element.42.diagonal_ref, f32[1,256,128]{2,1,0:T(8,128)S(1)} %get-tuple-element.41.field_ref.refs_0_, f32[1,256,128]{2,1,0:T(8,128)S(1)} %shard_map.101.field_ref.refs_1_, ...), custom_call_target="tpu_custom_call" | custom-call | tf_op jit(solution)/shard_map/pallas_call | solution.py:315
  (11 shorter events, 0.0 us)
Async XLA Ops:
  0.6 6.4 %collective-permute-start.2 = (f32[1,256,128]{2,1,0:T(8,128)}, f32[1,256,128]{2,1,0:T(8,128)S(1)}, u32[]{:S(2)}, u32[]{:S(2)}) collective-permute-start(f32[1,256,128]{2,1,0:T(8,128)} %bitcast.20), channel_id=1, source_target_pairs={{0,16},{1,2},{2,1},{3,4},{4,3},{5,6},{6,5},{7,8},{8,7},{9,10},{10,... | collective-permute-start | bytes 393224 | tf_op jit(solution)/shard_map/ppermute | solution.py:343
  3.6 3.4 %collective-permute-start.3 = (f32[1,256,128]{2,1,0:T(8,128)}, f32[1,256,128]{2,1,0:T(8,128)S(1)}, u32[]{:S(2)}, u32[]{:S(2)}) collective-permute-start(f32[1,256,128]{2,1,0:T(8,128)} %bitcast.21), channel_id=1, source_target_pairs={{0,1},{1,0},{2,3},{3,2},{4,5},{5,4},{6,7},{7,6},{8,9},{9,8},{10,11... | collective-permute-start | bytes 393224 | tf_op jit(solution)/shard_map/ppermute | solution.py:344
  5.4 4.8 %collective-permute-start = (f32[1,256,128]{2,1,0:T(8,128)S(1)}, f32[1,256,128]{2,1,0:T(8,128)S(1)}, u32[]{:S(2)}, u32[]{:S(2)}) collective-permute-start(f32[1,256,128]{2,1,0:T(8,128)S(1)} %bitcast.14), channel_id=1, source_target_pairs={{0,1},{1,0},{2,3},{3,2},{4,5},{5,4},{6,7},{7,6},{8,9},{9,8},{10,11... | collective-permute-start | bytes 393224 | tf_op jit(solution)/shard_map/ppermute | solution.py:344
  5.9 5.8 %collective-permute-start.1 = (f32[1,256,128]{2,1,0:T(8,128)S(1)}, f32[1,256,128]{2,1,0:T(8,128)S(1)}, u32[]{:S(2)}, u32[]{:S(2)}) collective-permute-start(f32[1,256,128]{2,1,0:T(8,128)S(1)} %bitcast.15), channel_id=1, source_target_pairs={{0,16},{1,2},{2,1},{3,4},{4,3},{5,6},{6,5},{7,8},{8,7},{9,10},{10,... | collective-permute-start | bytes 393224 | tf_op jit(solution)/shard_map/ppermute | solution.py:343
  7.4 5.3 %collective-permute-start.16 = (f32[1,256,128]{2,1,0:T(8,128)S(1)}, f32[1,256,128]{2,1,0:T(8,128)S(1)}, u32[]{:S(2)}, u32[]{:S(2)}) collective-permute-start(f32[1,256,128]{2,1,0:T(8,128)S(1)} %get-tuple-element.41.field_ref.refs_0_), channel_id=1, source_target_pairs={{0,1},{1,0},{2,3},{3,2},{4,5},{5,4},{6,7},{7,6},{8,9},{9,8},{10,11... | collective-permute-start | bytes 393224 | tf_op jit(solution)/shard_map/ppermute | solution.py:344
  7.8 6.3 %collective-permute-start.17 = (f32[1,256,128]{2,1,0:T(8,128)S(1)}, f32[1,256,128]{2,1,0:T(8,128)S(1)}, u32[]{:S(2)}, u32[]{:S(2)}) collective-permute-start(f32[1,256,128]{2,1,0:T(8,128)S(1)} %get-tuple-element.41.field_ref.refs_0_), channel_id=1, source_target_pairs={{0,16},{1,2},{2,1},{3,4},{4,3},{5,6},{6,5},{7,8},{8,7},{9,10},{10,... | collective-permute-start | bytes 393224 | tf_op jit(solution)/shard_map/ppermute | solution.py:343
  9.3 5.4 %collective-permute-start.10 = (f32[1,256,128]{2,1,0:T(8,128)S(1)}, f32[1,256,128]{2,1,0:T(8,128)S(1)}, u32[]{:S(2)}, u32[]{:S(2)}) collective-permute-start(f32[1,256,128]{2,1,0:T(8,128)S(1)} %get-tuple-element.40.field_ref.refs_3_.refs_4_), channel_id=1, source_target_pairs={{0,1},{1,0},{2,3},{3,2},{4,5},{5,4},{6,7},{7,6},{8,9},{9,8},{10,11... | collective-permute-start | bytes 393224 | tf_op jit(solution)/shard_map/ppermute | solution.py:344
  10.2 6.0 %collective-permute-start.11 = (f32[1,256,128]{2,1,0:T(8,128)S(1)}, f32[1,256,128]{2,1,0:T(8,128)S(1)}, u32[]{:S(2)}, u32[]{:S(2)}) collective-permute-start(f32[1,256,128]{2,1,0:T(8,128)S(1)} %get-tuple-element.40.field_ref.refs_3_.refs_4_), channel_id=1, source_target_pairs={{0,16},{1,2},{2,1},{3,4},{4,3},{5,6},{6,5},{7,8},{8,7},{9,10},{10,... | collective-permute-start | bytes 393224 | tf_op jit(solution)/shard_map/ppermute | solution.py:343
  12.6 5.5 %collective-permute-start.4 = (f32[1,256,128]{2,1,0:T(8,128)S(1)}, f32[1,256,128]{2,1,0:T(8,128)S(1)}, u32[]{:S(2)}, u32[]{:S(2)}) collective-permute-start(f32[1,256,128]{2,1,0:T(8,128)S(1)} %get-tuple-element.38.field_ref.refs_6_.refs_8_), channel_id=1, source_target_pairs={{0,1},{1,0},{2,3},{3,2},{4,5},{5,4},{6,7},{7,6},{8,9},{9,8},{10,11... | collective-permute-start | bytes 393224 | tf_op jit(solution)/shard_map/ppermute | solution.py:344
  12.6 7.0 %collective-permute-start.5 = (f32[1,256,128]{2,1,0:T(8,128)S(1)}, f32[1,256,128]{2,1,0:T(8,128)S(1)}, u32[]{:S(2)}, u32[]{:S(2)}) collective-permute-start(f32[1,256,128]{2,1,0:T(8,128)S(1)} %get-tuple-element.38.field_ref.refs_6_.refs_8_), channel_id=1, source_target_pairs={{0,16},{1,2},{2,1},{3,4},{4,3},{5,6},{6,5},{7,8},{8,7},{9,10},{10,... | collective-permute-start | bytes 393224 | tf_op jit(solution)/shard_map/ppermute | solution.py:343
  14.3 6.7 %collective-permute-start.18 = (f32[1,256,128]{2,1,0:T(8,128)S(1)}, f32[1,256,128]{2,1,0:T(8,128)S(1)}, u32[]{:S(2)}, u32[]{:S(2)}) collective-permute-start(f32[1,256,128]{2,1,0:T(8,128)S(1)} %shard_map.101.field_ref.refs_1_), channel_id=1, source_target_pairs={{0,1},{1,0},{2,3},{3,2},{4,5},{5,4},{6,7},{7,6},{8,9},{9,8},{10,11... | collective-permute-start | bytes 393224 | tf_op jit(solution)/shard_map/ppermute | solution.py:344
  14.7 7.8 %collective-permute-start.19 = (f32[1,256,128]{2,1,0:T(8,128)S(1)}, f32[1,256,128]{2,1,0:T(8,128)S(1)}, u32[]{:S(2)}, u32[]{:S(2)}) collective-permute-start(f32[1,256,128]{2,1,0:T(8,128)S(1)} %shard_map.101.field_ref.refs_1_), channel_id=1, source_target_pairs={{0,16},{1,2},{2,1},{3,4},{4,3},{5,6},{6,5},{7,8},{8,7},{9,10},{10,... | collective-permute-start | bytes 393224 | tf_op jit(solution)/shard_map/ppermute | solution.py:343
  16.5 7.4 %collective-permute-start.12 = (f32[1,256,128]{2,1,0:T(8,128)S(1)}, f32[1,256,128]{2,1,0:T(8,128)S(1)}, u32[]{:S(2)}, u32[]{:S(2)}) collective-permute-start(f32[1,256,128]{2,1,0:T(8,128)S(1)} %shard_map.99.field_ref.refs_4_.refs_5_), channel_id=1, source_target_pairs={{0,1},{1,0},{2,3},{3,2},{4,5},{5,4},{6,7},{7,6},{8,9},{9,8},{10,11... | collective-permute-start | bytes 393224 | tf_op jit(solution)/shard_map/ppermute | solution.py:344
  18.1 7.2 %collective-permute-start.13 = (f32[1,256,128]{2,1,0:T(8,128)S(1)}, f32[1,256,128]{2,1,0:T(8,128)S(1)}, u32[]{:S(2)}, u32[]{:S(2)}) collective-permute-start(f32[1,256,128]{2,1,0:T(8,128)S(1)} %shard_map.99.field_ref.refs_4_.refs_5_), channel_id=1, source_target_pairs={{0,16},{1,2},{2,1},{3,4},{4,3},{5,6},{6,5},{7,8},{8,7},{9,10},{10,... | collective-permute-start | bytes 393224 | tf_op jit(solution)/shard_map/ppermute | solution.py:343
  19.9 6.3 %collective-permute-start.6 = (f32[1,256,128]{2,1,0:T(8,128)S(1)}, f32[1,256,128]{2,1,0:T(8,128)S(1)}, u32[]{:S(2)}, u32[]{:S(2)}) collective-permute-start(f32[1,256,128]{2,1,0:T(8,128)S(1)} %shard_map.97.field_ref.refs_7_.refs_9_), channel_id=1, source_target_pairs={{0,1},{1,0},{2,3},{3,2},{4,5},{5,4},{6,7},{7,6},{8,9},{9,8},{10,11... | collective-permute-start | bytes 393224 | tf_op jit(solution)/shard_map/ppermute | solution.py:344
  21.0 6.6 %collective-permute-start.7 = (f32[1,256,128]{2,1,0:T(8,128)S(1)}, f32[1,256,128]{2,1,0:T(8,128)S(1)}, u32[]{:S(2)}, u32[]{:S(2)}) collective-permute-start(f32[1,256,128]{2,1,0:T(8,128)S(1)} %shard_map.97.field_ref.refs_7_.refs_9_), channel_id=1, source_target_pairs={{0,16},{1,2},{2,1},{3,4},{4,3},{5,6},{6,5},{7,8},{8,7},{9,10},{10,... | collective-permute-start | bytes 393224 | tf_op jit(solution)/shard_map/ppermute | solution.py:343
  22.8 6.7 %collective-permute-start.20 = (f32[1,256,128]{2,1,0:T(8,128)S(1)}, f32[1,256,128]{2,1,0:T(8,128)S(1)}, u32[]{:S(2)}, u32[]{:S(2)}) collective-permute-start(f32[1,256,128]{2,1,0:T(8,128)S(1)} %shard_map.102.refs_2_.refs_0_), channel_id=1, source_target_pairs={{0,1},{1,0},{2,3},{3,2},{4,5},{5,4},{6,7},{7,6},{8,9},{9,8},{10,11... | collective-permute-start | bytes 393224 | tf_op jit(solution)/shard_map/ppermute | solution.py:344
  23.8 9.5 %collective-permute-start.21 = (f32[1,256,128]{2,1,0:T(8,128)S(1)}, f32[1,256,128]{2,1,0:T(8,128)S(1)}, u32[]{:S(2)}, u32[]{:S(2)}) collective-permute-start(f32[1,256,128]{2,1,0:T(8,128)S(1)} %shard_map.102.refs_2_.refs_0_), channel_id=1, source_target_pairs={{0,16},{1,2},{2,1},{3,4},{4,3},{5,6},{6,5},{7,8},{8,7},{9,10},{10,... | collective-permute-start | bytes 393224 | tf_op jit(solution)/shard_map/ppermute | solution.py:343
  25.6 8.2 %collective-permute-start.14 = (f32[1,256,128]{2,1,0:T(8,128)S(1)}, f32[1,256,128]{2,1,0:T(8,128)S(1)}, u32[]{:S(2)}, u32[]{:S(2)}) collective-permute-start(f32[1,256,128]{2,1,0:T(8,128)S(1)} %shard_map.100.refs_5_.field_ref.refs_6_), channel_id=1, source_target_pairs={{0,16},{1,2},{2,1},{3,4},{4,3},{5,6},{6,5},{7,8},{8,7},{9,10},{10,... | collective-permute-start | bytes 393224 | tf_op jit(solution)/shard_map/ppermute | solution.py:343
  26.2 7.6 %collective-permute-start.15 = (f32[1,256,128]{2,1,0:T(8,128)S(1)}, f32[1,256,128]{2,1,0:T(8,128)S(1)}, u32[]{:S(2)}, u32[]{:S(2)}) collective-permute-start(f32[1,256,128]{2,1,0:T(8,128)S(1)} %shard_map.100.refs_5_.field_ref.refs_6_), channel_id=1, source_target_pairs={{0,1},{1,0},{2,3},{3,2},{4,5},{5,4},{6,7},{7,6},{8,9},{9,8},{10,11... | collective-permute-start | bytes 393224 | tf_op jit(solution)/shard_map/ppermute | solution.py:344
  27.9 6.4 %collective-permute-start.8 = (f32[1,256,128]{2,1,0:T(8,128)S(1)}, f32[1,256,128]{2,1,0:T(8,128)S(1)}, u32[]{:S(2)}, u32[]{:S(2)}) collective-permute-start(f32[1,256,128]{2,1,0:T(8,128)S(1)} %shard_map.98.refs_8_.field_ref.refs_10_), channel_id=1, source_target_pairs={{0,16},{1,2},{2,1},{3,4},{4,3},{5,6},{6,5},{7,8},{8,7},{9,10},{10,... | collective-permute-start | bytes 393224 | tf_op jit(solution)/shard_map/ppermute | solution.py:343
  29.5 4.8 %collective-permute-start.9 = (f32[1,256,128]{2,1,0:T(8,128)S(1)}, f32[1,256,128]{2,1,0:T(8,128)S(1)}, u32[]{:S(2)}, u32[]{:S(2)}) collective-permute-start(f32[1,256,128]{2,1,0:T(8,128)S(1)} %shard_map.98.refs_8_.field_ref.refs_10_), channel_id=1, source_target_pairs={{0,1},{1,0},{2,3},{3,2},{4,5},{5,4},{6,7},{7,6},{8,9},{9,8},{10,11... | collective-permute-start | bytes 393224 | tf_op jit(solution)/shard_map/ppermute | solution.py:344

commit v12 on v11

--- a/solution.py
+++ b/solution.py
@@ -269,8 +269,10 @@
     return answer
 
 
-def finish_kernel(moments_ref, diagonal_ref, *refs):
-    *refs, solution_hbm, residual_hbm, solution_ref, residual_ref, sems = refs
+def finish_kernel(moments_ref, diagonal_ref, next_ref, *refs):
+    *refs, solution_hbm, residual_hbm, next_hbm, solution_ref, residual_ref, sems, next_sem = refs
+    copies = [pltpu.make_async_copy(next_ref, next_hbm, next_sem)]
+    copies[0].start()
     streams = [refs[4 * i : 4 * i + 4] for i in range(len(SPLITS))]
     rows = [moments_ref[device] for device in range(moments_ref.shape[0])]
     while len(rows) > 1:
@@ -293,7 +295,6 @@
         chosen = [jnp.where(better, p[j : j + 1], c) for p, c in zip(packed, chosen)]
     total, layers = diagonal_ref.shape
     a0, a1, a2 = [jnp.broadcast_to(c, (CHUNK, layers)) for c in chosen]
-    copies = []
     for (low, high), stream in zip(SPLITS, streams):
         for at in range(high - low):
             for start in range(0, total, CHUNK):
@@ -393,9 +394,9 @@
         streams[i].append(field)
     moments = lax.all_to_all(moments, NAMES, 0, 0)
     fields = [field for stream in streams for field in stream]
-    answer, residual = call(
-        finish_kernel, [triple, triple], moments, diagonal, *fields,
-        scratch=[triple, triple, pltpu.SemaphoreType.DMA((2, 3))], out_place=pltpu.HBM,
+    answer, residual, adjoint_next = call(
+        finish_kernel, [triple, triple, flat], moments, diagonal, adjoint_next, *fields,
+        scratch=[triple, triple, pltpu.SemaphoreType.DMA((2, 3)), pltpu.SemaphoreType.DMA], out_place=pltpu.HBM,
     )
     whole = (3, 1, 1, rows, layers)
     return answer.reshape(whole), residual.reshape(whole), adjoint_next.reshape(adjoint_temp.shape)

time: 50.5 us -> 51.1 us (1.012)
  waiting for transfers between devices: 0.06 us -> 1.12 us
  Pallas kernels: 8.42 us -> 7.75 us
    ppermute x11, waiting for transfers between devices: 0.03 us -> 1.09 us  [exchange(): far = lax.ppermute(value, NAMES, across)]
    pallas_call x14, Pallas kernels: 8.42 us -> 7.75 us  [call(): pl.pallas_call(kernel, out_shape=outs, in_specs=[pl.BlockSpec(memory_spac...]
  transfers between devices with their start and end apart: 22 -> 22, of which waited for: 0 -> 1; matrix products, arithmetic and copies ran while one was open for 0% -> 0% of each run, Pallas kernels for 13% -> 12%
where the time goes in v12:
time: 51.1 us; the launch traced here: 50.9 us
  starting transfers between devices  26.4 us (52%)
  blocking collectives  14.9 us (29%)
  Pallas kernels  7.75 us (15%)
  waiting for transfers between devices  1.12 us (2%)
  between operations  0.75 us (1%)
    ppermute x11, starting transfers between devices, exchange(): far = lax.ppermute(value, NAMES, across)  16.8 us
    all_to_all x1, blocking collectives, body(): moments = lax.all_to_all(moments, NAMES, 0, 0)  14.9 us
    ppermute x11, starting transfers between devices, exchange(): near = lax.ppermute(value, NAMES, beside)  9.58 us
    pallas_call x14, Pallas kernels, call(): pl.pallas_call(kernel, out_shape=outs, in_specs=[pl.BlockSpec(memory_spac...  7.75 us
    ppermute x11, waiting for transfers between devices, exchange(): far = lax.ppermute(value, NAMES, across)  1.09 us
  transfers between devices with their start and end apart: 22, of which 1 were waited for; matrix products, arithmetic and copies ran while one was open for 0% of the time, Pallas kernels for 12%

profile of v12, /device:TPU:0, one launch (start us, length us, event | category | flops | bytes accessed | tf_op | source)
XLA Modules:
  0.0 50.9 jit_solution(5150130182631078029)
XLA Ops:
  0.6 3.0 %collective-permute-start.2 = (f32[1,256,128]{2,1,0:T(8,128)}, f32[1,256,128]{2,1,0:T(8,128)S(1)}, u32[]{:S(2)}, u32[]{:S(2)}) collective-permute-start(f32[1,256,128]{2,1,0:T(8,128)} %bitcast.20), channel_id=1, source_target_pairs={{0,16},{1,2},{2,1},{3,4},{4,3},{5,6},{6,5},{7,8},{8,7},{9,10},{10,... | collective-permute-start | bytes 393224 | tf_op jit(solution)/shard_map/ppermute | solution.py:344
  3.6 0.1 collective-permute-start.3
  3.8 1.7 %shard_map.94 = (f32[256,128]{1,0:T(8,128)S(1)}, f32[4,256,128]{2,1,0:T(8,128)S(1)}, f32[256,128]{1,0:T(8,128)S(1)}, f32[3,256,128]{2,1,0:T(8,128)S(1)}, f32[256...) custom-call(f32[256,128]{1,0:T(8,128)} %bitcast.18, ...), custom_call_target="tpu_custom_call" | custom-call | tf_op jit(solution)/shard_map/pallas_call | solution.py:316
  5.4 0.4 collective-permute-start
  5.9 1.2 %collective-permute-start.1 = (f32[1,256,128]{2,1,0:T(8,128)S(1)}, f32[1,256,128]{2,1,0:T(8,128)S(1)}, u32[]{:S(2)}, u32[]{:S(2)}) collective-permute-start(f32[1,256,128]{2,1,0:T(8,128)S(1)} %bitcast.15), channel_id=1, source_target_pairs={{0,16},{1,2},{2,1},{3,4},{4,3},{5,6},{6,5},{7,8},{8,7},{9,10},{10,... | collective-permute-start | bytes 393224 | tf_op jit(solution)/shard_map/ppermute | solution.py:344
  7.1 0.0 collective-permute-done.2.far_ref
  7.1 0.3 shard_map.95
  7.4 0.4 collective-permute-start.16
  7.8 1.5 %collective-permute-start.17 = (f32[1,256,128]{2,1,0:T(8,128)S(1)}, f32[1,256,128]{2,1,0:T(8,128)S(1)}, u32[]{:S(2)}, u32[]{:S(2)}) collective-permute-start(f32[1,256,128]{2,1,0:T(8,128)S(1)} %get-tuple-element.42.field_ref.refs_0_), channel_id=1, source_target_pairs={{0,16},{1,2},{2,1},{3,4},{4,3},{5,6},{6,5},{7,8},{8,7},{9,10},{10,... | collective-permute-start | bytes 393224 | tf_op jit(solution)/shard_map/ppermute | solution.py:344
  9.3 0.9 %collective-permute-start.10 = (f32[1,256,128]{2,1,0:T(8,128)S(1)}, f32[1,256,128]{2,1,0:T(8,128)S(1)}, u32[]{:S(2)}, u32[]{:S(2)}) collective-permute-start(f32[1,256,128]{2,1,0:T(8,128)S(1)} %get-tuple-element.41.field_ref.refs_3_.refs_4_), channel_id=1, source_target_pairs={{0,1},{1,0},{2,3},{3,2},{4,5},{5,4},{6,7},{7,6},{8,9},{9,8},{10,11... | collective-permute-start | bytes 393224 | tf_op jit(solution)/shard_map/ppermute | solution.py:345
  10.2 1.5 %collective-permute-start.11 = (f32[1,256,128]{2,1,0:T(8,128)S(1)}, f32[1,256,128]{2,1,0:T(8,128)S(1)}, u32[]{:S(2)}, u32[]{:S(2)}) collective-permute-start(f32[1,256,128]{2,1,0:T(8,128)S(1)} %get-tuple-element.41.field_ref.refs_3_.refs_4_), channel_id=1, source_target_pairs={{0,16},{1,2},{2,1},{3,4},{4,3},{5,6},{6,5},{7,8},{8,7},{9,10},{10,... | collective-permute-start | bytes 393224 | tf_op jit(solution)/shard_map/ppermute | solution.py:344
  11.7 0.0 collective-permute-done.1.far_ref
  11.7 0.2 shard_map.96
  12.0 0.1 collective-permute-start.4
  12.0 0.0 collective-permute-done.16.near_ref
  12.0 1.4 %collective-permute-start.5 = (f32[1,256,128]{2,1,0:T(8,128)S(1)}, f32[1,256,128]{2,1,0:T(8,128)S(1)}, u32[]{:S(2)}, u32[]{:S(2)}) collective-permute-start(f32[1,256,128]{2,1,0:T(8,128)S(1)} %get-tuple-element.39.field_ref.refs_6_.refs_8_), channel_id=1, source_target_pairs={{0,16},{1,2},{2,1},{3,4},{4,3},{5,6},{6,5},{7,8},{8,7},{9,10},{10,... | collective-permute-start | bytes 393224 | tf_op jit(solution)/shard_map/ppermute | solution.py:344
  13.5 0.0 collective-permute-done.17.far_ref
  13.5 0.3 shard_map.101.field_ref.refs_1_
  13.7 0.4 collective-permute-start.18
  14.1 1.5 %collective-permute-start.19 = (f32[1,256,128]{2,1,0:T(8,128)S(1)}, f32[1,256,128]{2,1,0:T(8,128)S(1)}, u32[]{:S(2)}, u32[]{:S(2)}) collective-permute-start(f32[1,256,128]{2,1,0:T(8,128)S(1)} %shard_map.101.field_ref.refs_1_), channel_id=1, source_target_pairs={{0,16},{1,2},{2,1},{3,4},{4,3},{5,6},{6,5},{7,8},{8,7},{9,10},{10,... | collective-permute-start | bytes 393224 | tf_op jit(solution)/shard_map/ppermute | solution.py:344
  15.6 0.0 collective-permute-done.11.far_ref
  15.6 0.3 shard_map.99.field_ref.refs_4_.refs_5_
  15.9 2.2 %collective-permute-start.12 = (f32[1,256,128]{2,1,0:T(8,128)S(1)}, f32[1,256,128]{2,1,0:T(8,128)S(1)}, u32[]{:S(2)}, u32[]{:S(2)}) collective-permute-start(f32[1,256,128]{2,1,0:T(8,128)S(1)} %shard_map.99.field_ref.refs_4_.refs_5_), channel_id=1, source_target_pairs={{0,1},{1,0},{2,3},{3,2},{4,5},{5,4},{6,7},{7,6},{8,9},{9,8},{10,11... | collective-permute-start | bytes 393224 | tf_op jit(solution)/shard_map/ppermute | solution.py:345
  18.1 0.0 collective-permute-done.4.near_ref
  18.1 1.5 %collective-permute-start.13 = (f32[1,256,128]{2,1,0:T(8,128)S(1)}, f32[1,256,128]{2,1,0:T(8,128)S(1)}, u32[]{:S(2)}, u32[]{:S(2)}) collective-permute-start(f32[1,256,128]{2,1,0:T(8,128)S(1)} %shard_map.99.field_ref.refs_4_.refs_5_), channel_id=1, source_target_pairs={{0,16},{1,2},{2,1},{3,4},{4,3},{5,6},{6,5},{7,8},{8,7},{9,10},{10,... | collective-permute-start | bytes 393224 | tf_op jit(solution)/shard_map/ppermute | solution.py:344
  19.6 0.3 shard_map.97.field_ref.refs_7_.refs_9_
  19.9 2.0 %collective-permute-start.6 = (f32[1,256,128]{2,1,0:T(8,128)S(1)}, f32[1,256,128]{2,1,0:T(8,128)S(1)}, u32[]{:S(2)}, u32[]{:S(2)}) collective-permute-start(f32[1,256,128]{2,1,0:T(8,128)S(1)} %shard_map.97.field_ref.refs_7_.refs_9_), channel_id=1, source_target_pairs={{0,1},{1,0},{2,3},{3,2},{4,5},{5,4},{6,7},{7,6},{8,9},{9,8},{10,11... | collective-permute-start | bytes 393224 | tf_op jit(solution)/shard_map/ppermute | solution.py:345
  21.9 1.5 %collective-permute-start.7 = (f32[1,256,128]{2,1,0:T(8,128)S(1)}, f32[1,256,128]{2,1,0:T(8,128)S(1)}, u32[]{:S(2)}, u32[]{:S(2)}) collective-permute-start(f32[1,256,128]{2,1,0:T(8,128)S(1)} %shard_map.97.field_ref.refs_7_.refs_9_), channel_id=1, source_target_pairs={{0,16},{1,2},{2,1},{3,4},{4,3},{5,6},{6,5},{7,8},{8,7},{9,10},{10,... | collective-permute-start | bytes 393224 | tf_op jit(solution)/shard_map/ppermute | solution.py:344
  23.4 0.0 collective-permute-done.19.far_ref
  23.4 0.3 shard_map.102.refs_2_.refs_0_
  23.6 0.1 collective-permute-start.20
  23.7 0.0 collective-permute-done.12.near_ref
  23.7 0.9 %collective-permute-start.21 = (f32[1,256,128]{2,1,0:T(8,128)S(1)}, f32[1,256,128]{2,1,0:T(8,128)S(1)}, u32[]{:S(2)}, u32[]{:S(2)}) collective-permute-start(f32[1,256,128]{2,1,0:T(8,128)S(1)} %shard_map.102.refs_2_.refs_0_), channel_id=1, source_target_pairs={{0,16},{1,2},{2,1},{3,4},{4,3},{5,6},{6,5},{7,8},{8,7},{9,10},{10,... | collective-permute-start | bytes 393224 | tf_op jit(solution)/shard_map/ppermute | solution.py:344
  24.6 0.0 collective-permute-done.13.far_ref
  24.6 0.3 shard_map.100.refs_5_.field_ref.refs_6_
  24.9 1.3 %collective-permute-start.14 = (f32[1,256,128]{2,1,0:T(8,128)S(1)}, f32[1,256,128]{2,1,0:T(8,128)S(1)}, u32[]{:S(2)}, u32[]{:S(2)}) collective-permute-start(f32[1,256,128]{2,1,0:T(8,128)S(1)} %shard_map.100.refs_5_.field_ref.refs_6_), channel_id=1, source_target_pairs={{0,16},{1,2},{2,1},{3,4},{4,3},{5,6},{6,5},{7,8},{8,7},{9,10},{10,... | collective-permute-start | bytes 393224 | tf_op jit(solution)/shard_map/ppermute | solution.py:344
  26.1 0.0 collective-permute-done.6.near_ref
  26.1 2.9 %collective-permute-start.15 = (f32[1,256,128]{2,1,0:T(8,128)S(1)}, f32[1,256,128]{2,1,0:T(8,128)S(1)}, u32[]{:S(2)}, u32[]{:S(2)}) collective-permute-start(f32[1,256,128]{2,1,0:T(8,128)S(1)} %shard_map.100.refs_5_.field_ref.refs_6_), channel_id=1, source_target_pairs={{0,1},{1,0},{2,3},{3,2},{4,5},{5,4},{6,7},{7,6},{8,9},{9,8},{10,11... | collective-permute-start | bytes 393224 | tf_op jit(solution)/shard_map/ppermute | solution.py:345
  29.1 0.3 shard_map.98.refs_8_.field_ref.refs_10_
  29.3 1.6 %collective-permute-start.8 = (f32[1,256,128]{2,1,0:T(8,128)S(1)}, f32[1,256,128]{2,1,0:T(8,128)S(1)}, u32[]{:S(2)}, u32[]{:S(2)}) collective-permute-start(f32[1,256,128]{2,1,0:T(8,128)S(1)} %shard_map.98.refs_8_.field_ref.refs_10_), channel_id=1, source_target_pairs={{0,16},{1,2},{2,1},{3,4},{4,3},{5,6},{6,5},{7,8},{8,7},{9,10},{10,... | collective-permute-start | bytes 393224 | tf_op jit(solution)/shard_map/ppermute | solution.py:344
  30.9 0.0 collective-permute-done.20.near_ref
  30.9 1.5 %shard_map.103 = (f32[8,128]{1,0:T(8,128)S(1)}, f32[5,3,256,128]{3,2,1,0:T(8,128)S(1)}, f32[5,3,256,128]{3,2,1,0:T(8,128)S(1)}) custom-call(f32[256,128]{1,0:T(8,128)S(1)} %get-tuple-element.43.diagonal_ref, f32[1,256,128]{2,1,0:T(8,128)S(1)} %get-tuple-element.42.field_ref.refs_0_, f32[1,256,128]{2,1,0:T(8,128)S(1)} %shard_map.101.field_ref.refs_1_, ...), custom_call_target="tpu_custom_call" | custom-call | tf_op jit(solution)/shard_map/pallas_call | solution.py:316
  32.4 0.4 shard_map.104
  32.9 0.4 shard_map.105
  33.3 1.1 %collective-permute-done.8.far_ref = f32[1,256,128]{2,1,0:T(8,128)S(1)} collective-permute-done((f32[1,256,128]{2,1,0:T(8,128)S(1)}, f32[1,256,128]{2,1,0:T(8,128)S(1)}, u32[]{:S(2)}, u32[]{:S(2)}) %collective-permute-start.8) | collective-permute-done | bytes 131104 | tf_op jit(solution)/shard_map/ppermute | solution.py:344
  34.4 0.5 shard_map.106
  34.8 14.9 %all_to_all.5.moments_ref = f32[32,1,128]{2,1,0:T(1,128)S(1)} all-to-all(f32[32,1,128]{2,1,0:T(1,128)S(1)} %get-tuple-element.49), channel_id=1, replica_groups=mesh['diamond'=2,'tile'=16] {'diamond','tile'}, dimensions={0} | all-to-all | bytes 32768 | tf_op jit(solution)/shard_map/all_to_all | solution.py:395
  49.8 1.2 %shard_map.107 = (f32[3,256,128]{2,1,0:T(8,128)}, f32[3,256,128]{2,1,0:T(8,128)}, f32[256,128]{1,0:T(8,128)}) custom-call(f32[32,1,128]{2,1,0:T(1,128)S(1)} %all_to_all.5.moments_ref, f32[256,128]{1,0:T(8,128)S(1)} %get-tuple-element.43.diagonal_ref, f32[256,128]{1,0:T(8,128)S(1)} %get-tuple-element.50.next_ref, ...), custom_call_target="tpu_custom_call" | custom-call | tf_op jit(solution)/shard_map/pallas_call | solution.py:316
  (11 shorter events, 0.0 us)
Async XLA Ops:
  0.6 6.4 %collective-permute-start.2 = (f32[1,256,128]{2,1,0:T(8,128)}, f32[1,256,128]{2,1,0:T(8,128)S(1)}, u32[]{:S(2)}, u32[]{:S(2)}) collective-permute-start(f32[1,256,128]{2,1,0:T(8,128)} %bitcast.20), channel_id=1, source_target_pairs={{0,16},{1,2},{2,1},{3,4},{4,3},{5,6},{6,5},{7,8},{8,7},{9,10},{10,... | collective-permute-start | bytes 393224 | tf_op jit(solution)/shard_map/ppermute | solution.py:344
  3.6 3.4 %collective-permute-start.3 = (f32[1,256,128]{2,1,0:T(8,128)}, f32[1,256,128]{2,1,0:T(8,128)S(1)}, u32[]{:S(2)}, u32[]{:S(2)}) collective-permute-start(f32[1,256,128]{2,1,0:T(8,128)} %bitcast.21), channel_id=1, source_target_pairs={{0,1},{1,0},{2,3},{3,2},{4,5},{5,4},{6,7},{7,6},{8,9},{9,8},{10,11... | collective-permute-start | bytes 393224 | tf_op jit(solution)/shard_map/ppermute | solution.py:345
  5.4 4.8 %collective-permute-start = (f32[1,256,128]{2,1,0:T(8,128)S(1)}, f32[1,256,128]{2,1,0:T(8,128)S(1)}, u32[]{:S(2)}, u32[]{:S(2)}) collective-permute-start(f32[1,256,128]{2,1,0:T(8,128)S(1)} %bitcast.14), channel_id=1, source_target_pairs={{0,1},{1,0},{2,3},{3,2},{4,5},{5,4},{6,7},{7,6},{8,9},{9,8},{10,11... | collective-permute-start | bytes 393224 | tf_op jit(solution)/shard_map/ppermute | solution.py:345
  5.9 5.8 %collective-permute-start.1 = (f32[1,256,128]{2,1,0:T(8,128)S(1)}, f32[1,256,128]{2,1,0:T(8,128)S(1)}, u32[]{:S(2)}, u32[]{:S(2)}) collective-permute-start(f32[1,256,128]{2,1,0:T(8,128)S(1)} %bitcast.15), channel_id=1, source_target_pairs={{0,16},{1,2},{2,1},{3,4},{4,3},{5,6},{6,5},{7,8},{8,7},{9,10},{10,... | collective-permute-start | bytes 393224 | tf_op jit(solution)/shard_map/ppermute | solution.py:344
  7.4 4.7 %collective-permute-start.16 = (f32[1,256,128]{2,1,0:T(8,128)S(1)}, f32[1,256,128]{2,1,0:T(8,128)S(1)}, u32[]{:S(2)}, u32[]{:S(2)}) collective-permute-start(f32[1,256,128]{2,1,0:T(8,128)S(1)} %get-tuple-element.42.field_ref.refs_0_), channel_id=1, source_target_pairs={{0,1},{1,0},{2,3},{3,2},{4,5},{5,4},{6,7},{7,6},{8,9},{9,8},{10,11... | collective-permute-start | bytes 393224 | tf_op jit(solution)/shard_map/ppermute | solution.py:345
  7.8 5.7 %collective-permute-start.17 = (f32[1,256,128]{2,1,0:T(8,128)S(1)}, f32[1,256,128]{2,1,0:T(8,128)S(1)}, u32[]{:S(2)}, u32[]{:S(2)}) collective-permute-start(f32[1,256,128]{2,1,0:T(8,128)S(1)} %get-tuple-element.42.field_ref.refs_0_), channel_id=1, source_target_pairs={{0,16},{1,2},{2,1},{3,4},{4,3},{5,6},{6,5},{7,8},{8,7},{9,10},{10,... | collective-permute-start | bytes 393224 | tf_op jit(solution)/shard_map/ppermute | solution.py:344
  9.3 4.9 %collective-permute-start.10 = (f32[1,256,128]{2,1,0:T(8,128)S(1)}, f32[1,256,128]{2,1,0:T(8,128)S(1)}, u32[]{:S(2)}, u32[]{:S(2)}) collective-permute-start(f32[1,256,128]{2,1,0:T(8,128)S(1)} %get-tuple-element.41.field_ref.refs_3_.refs_4_), channel_id=1, source_target_pairs={{0,1},{1,0},{2,3},{3,2},{4,5},{5,4},{6,7},{7,6},{8,9},{9,8},{10,11... | collective-permute-start | bytes 393224 | tf_op jit(solution)/shard_map/ppermute | solution.py:345
  10.2 5.4 %collective-permute-start.11 = (f32[1,256,128]{2,1,0:T(8,128)S(1)}, f32[1,256,128]{2,1,0:T(8,128)S(1)}, u32[]{:S(2)}, u32[]{:S(2)}) collective-permute-start(f32[1,256,128]{2,1,0:T(8,128)S(1)} %get-tuple-element.41.field_ref.refs_3_.refs_4_), channel_id=1, source_target_pairs={{0,16},{1,2},{2,1},{3,4},{4,3},{5,6},{6,5},{7,8},{8,7},{9,10},{10,... | collective-permute-start | bytes 393224 | tf_op jit(solution)/shard_map/ppermute | solution.py:344
  12.0 6.2 %collective-permute-start.4 = (f32[1,256,128]{2,1,0:T(8,128)S(1)}, f32[1,256,128]{2,1,0:T(8,128)S(1)}, u32[]{:S(2)}, u32[]{:S(2)}) collective-permute-start(f32[1,256,128]{2,1,0:T(8,128)S(1)} %get-tuple-element.39.field_ref.refs_6_.refs_8_), channel_id=1, source_target_pairs={{0,1},{1,0},{2,3},{3,2},{4,5},{5,4},{6,7},{7,6},{8,9},{9,8},{10,11... | collective-permute-start | bytes 393224 | tf_op jit(solution)/shard_map/ppermute | solution.py:345
  12.0 7.6 %collective-permute-start.5 = (f32[1,256,128]{2,1,0:T(8,128)S(1)}, f32[1,256,128]{2,1,0:T(8,128)S(1)}, u32[]{:S(2)}, u32[]{:S(2)}) collective-permute-start(f32[1,256,128]{2,1,0:T(8,128)S(1)} %get-tuple-element.39.field_ref.refs_6_.refs_8_), channel_id=1, source_target_pairs={{0,16},{1,2},{2,1},{3,4},{4,3},{5,6},{6,5},{7,8},{8,7},{9,10},{10,... | collective-permute-start | bytes 393224 | tf_op jit(solution)/shard_map/ppermute | solution.py:344
  13.7 8.1 %collective-permute-start.18 = (f32[1,256,128]{2,1,0:T(8,128)S(1)}, f32[1,256,128]{2,1,0:T(8,128)S(1)}, u32[]{:S(2)}, u32[]{:S(2)}) collective-permute-start(f32[1,256,128]{2,1,0:T(8,128)S(1)} %shard_map.101.field_ref.refs_1_), channel_id=1, source_target_pairs={{0,1},{1,0},{2,3},{3,2},{4,5},{5,4},{6,7},{7,6},{8,9},{9,8},{10,11... | collective-permute-start | bytes 393224 | tf_op jit(solution)/shard_map/ppermute | solution.py:345
  14.1 9.2 %collective-permute-start.19 = (f32[1,256,128]{2,1,0:T(8,128)S(1)}, f32[1,256,128]{2,1,0:T(8,128)S(1)}, u32[]{:S(2)}, u32[]{:S(2)}) collective-permute-start(f32[1,256,128]{2,1,0:T(8,128)S(1)} %shard_map.101.field_ref.refs_1_), channel_id=1, source_target_pairs={{0,16},{1,2},{2,1},{3,4},{4,3},{5,6},{6,5},{7,8},{8,7},{9,10},{10,... | collective-permute-start | bytes 393224 | tf_op jit(solution)/shard_map/ppermute | solution.py:344
  15.9 7.8 %collective-permute-start.12 = (f32[1,256,128]{2,1,0:T(8,128)S(1)}, f32[1,256,128]{2,1,0:T(8,128)S(1)}, u32[]{:S(2)}, u32[]{:S(2)}) collective-permute-start(f32[1,256,128]{2,1,0:T(8,128)S(1)} %shard_map.99.field_ref.refs_4_.refs_5_), channel_id=1, source_target_pairs={{0,1},{1,0},{2,3},{3,2},{4,5},{5,4},{6,7},{7,6},{8,9},{9,8},{10,11... | collective-permute-start | bytes 393224 | tf_op jit(solution)/shard_map/ppermute | solution.py:345
  18.1 6.5 %collective-permute-start.13 = (f32[1,256,128]{2,1,0:T(8,128)S(1)}, f32[1,256,128]{2,1,0:T(8,128)S(1)}, u32[]{:S(2)}, u32[]{:S(2)}) collective-permute-start(f32[1,256,128]{2,1,0:T(8,128)S(1)} %shard_map.99.field_ref.refs_4_.refs_5_), channel_id=1, source_target_pairs={{0,16},{1,2},{2,1},{3,4},{4,3},{5,6},{6,5},{7,8},{8,7},{9,10},{10,... | collective-permute-start | bytes 393224 | tf_op jit(solution)/shard_map/ppermute | solution.py:344
  19.9 6.2 %collective-permute-start.6 = (f32[1,256,128]{2,1,0:T(8,128)S(1)}, f32[1,256,128]{2,1,0:T(8,128)S(1)}, u32[]{:S(2)}, u32[]{:S(2)}) collective-permute-start(f32[1,256,128]{2,1,0:T(8,128)S(1)} %shard_map.97.field_ref.refs_7_.refs_9_), channel_id=1, source_target_pairs={{0,1},{1,0},{2,3},{3,2},{4,5},{5,4},{6,7},{7,6},{8,9},{9,8},{10,11... | collective-permute-start | bytes 393224 | tf_op jit(solution)/shard_map/ppermute | solution.py:345
  21.9 7.2 %collective-permute-start.7 = (f32[1,256,128]{2,1,0:T(8,128)S(1)}, f32[1,256,128]{2,1,0:T(8,128)S(1)}, u32[]{:S(2)}, u32[]{:S(2)}) collective-permute-start(f32[1,256,128]{2,1,0:T(8,128)S(1)} %shard_map.97.field_ref.refs_7_.refs_9_), channel_id=1, source_target_pairs={{0,16},{1,2},{2,1},{3,4},{4,3},{5,6},{6,5},{7,8},{8,7},{9,10},{10,... | collective-permute-start | bytes 393224 | tf_op jit(solution)/shard_map/ppermute | solution.py:344
  23.6 7.3 %collective-permute-start.20 = (f32[1,256,128]{2,1,0:T(8,128)S(1)}, f32[1,256,128]{2,1,0:T(8,128)S(1)}, u32[]{:S(2)}, u32[]{:S(2)}) collective-permute-start(f32[1,256,128]{2,1,0:T(8,128)S(1)} %shard_map.102.refs_2_.refs_0_), channel_id=1, source_target_pairs={{0,1},{1,0},{2,3},{3,2},{4,5},{5,4},{6,7},{7,6},{8,9},{9,8},{10,11... | collective-permute-start | bytes 393224 | tf_op jit(solution)/shard_map/ppermute | solution.py:345
  23.7 8.7 %collective-permute-start.21 = (f32[1,256,128]{2,1,0:T(8,128)S(1)}, f32[1,256,128]{2,1,0:T(8,128)S(1)}, u32[]{:S(2)}, u32[]{:S(2)}) collective-permute-start(f32[1,256,128]{2,1,0:T(8,128)S(1)} %shard_map.102.refs_2_.refs_0_), channel_id=1, source_target_pairs={{0,16},{1,2},{2,1},{3,4},{4,3},{5,6},{6,5},{7,8},{8,7},{9,10},{10,... | collective-permute-start | bytes 393224 | tf_op jit(solution)/shard_map/ppermute | solution.py:344
  24.9 8.0 %collective-permute-start.14 = (f32[1,256,128]{2,1,0:T(8,128)S(1)}, f32[1,256,128]{2,1,0:T(8,128)S(1)}, u32[]{:S(2)}, u32[]{:S(2)}) collective-permute-start(f32[1,256,128]{2,1,0:T(8,128)S(1)} %shard_map.100.refs_5_.field_ref.refs_6_), channel_id=1, source_target_pairs={{0,16},{1,2},{2,1},{3,4},{4,3},{5,6},{6,5},{7,8},{8,7},{9,10},{10,... | collective-permute-start | bytes 393224 | tf_op jit(solution)/shard_map/ppermute | solution.py:344
  26.1 6.7 %collective-permute-start.15 = (f32[1,256,128]{2,1,0:T(8,128)S(1)}, f32[1,256,128]{2,1,0:T(8,128)S(1)}, u32[]{:S(2)}, u32[]{:S(2)}) collective-permute-start(f32[1,256,128]{2,1,0:T(8,128)S(1)} %shard_map.100.refs_5_.field_ref.refs_6_), channel_id=1, source_target_pairs={{0,1},{1,0},{2,3},{3,2},{4,5},{5,4},{6,7},{7,6},{8,9},{9,8},{10,11... | collective-permute-start | bytes 393224 | tf_op jit(solution)/shard_map/ppermute | solution.py:345
  29.3 5.0 %collective-permute-start.8 = (f32[1,256,128]{2,1,0:T(8,128)S(1)}, f32[1,256,128]{2,1,0:T(8,128)S(1)}, u32[]{:S(2)}, u32[]{:S(2)}) collective-permute-start(f32[1,256,128]{2,1,0:T(8,128)S(1)} %shard_map.98.refs_8_.field_ref.refs_10_), channel_id=1, source_target_pairs={{0,16},{1,2},{2,1},{3,4},{4,3},{5,6},{6,5},{7,8},{8,7},{9,10},{10,... | collective-permute-start | bytes 393224 | tf_op jit(solution)/shard_map/ppermute | solution.py:344
  30.9 3.5 %collective-permute-start.9 = (f32[1,256,128]{2,1,0:T(8,128)S(1)}, f32[1,256,128]{2,1,0:T(8,128)S(1)}, u32[]{:S(2)}, u32[]{:S(2)}) collective-permute-start(f32[1,256,128]{2,1,0:T(8,128)S(1)} %shard_map.98.refs_8_.field_ref.refs_10_), channel_id=1, source_target_pairs={{0,1},{1,0},{2,3},{3,2},{4,5},{5,4},{6,7},{7,6},{8,9},{9,8},{10,11... | collective-permute-start | bytes 393224 | tf_op jit(solution)/shard_map/ppermute | solution.py:345

commit v13 on v11

--- a/solution.py
+++ b/solution.py
@@ -53,12 +53,21 @@
 
 def unfold(matrix_ref, far_ref, out_ref):
     layers = far_ref.shape[2]
-    for at in range(far_ref.shape[0]):
-        pieces = jnp.concatenate(split3(far_ref[at]), axis=1)
-        moved = jnp.dot(matrix_ref[...], pieces, preferred_element_type=jnp.float32)
-        out_ref[at] = (
-            moved[:, :layers] + moved[:, layers : 2 * layers] + moved[:, 2 * layers :]
-        )
+    tile = lax.axis_index("tile")
+    folded = jnp.logical_or(tile == 0, tile == lax.axis_size("tile") - 1)
+
+    @pl.when(folded)
+    def _():
+        for at in range(far_ref.shape[0]):
+            pieces = jnp.concatenate(split3(far_ref[at]), axis=1)
+            moved = jnp.dot(matrix_ref[...], pieces, preferred_element_type=jnp.float32)
+            out_ref[at] = (
+                moved[:, :layers] + moved[:, layers : 2 * layers] + moved[:, 2 * layers :]
+            )
+
+    @pl.when(jnp.logical_not(folded))
+    def _():
+        out_ref[...] = far_ref[...]
 
 
 def local_kernel(

time: 50.5 us -> 50.2 us (level)
  Pallas kernels: 8.42 us -> 9.57 us
  starting transfers between devices: 26.7 us -> 25.6 us
    pallas_call x14, Pallas kernels: 8.42 us -> 9.57 us  [call(): pl.pallas_call(kernel, out_shape=outs, in_specs=[pl.BlockSpec(memory_spac...]
    ppermute x11, starting transfers between devices: 9.96 us -> 8.89 us  [exchange(): near = lax.ppermute(value, NAMES, beside)]
  transfers between devices with their start and end apart: 22 -> 22, of which waited for: 0 -> 0; matrix products, arithmetic and copies ran while one was open for 0% -> 0% of each run, Pallas kernels for 13% -> 16%
where the time goes in v13:
time: 50.2 us; the launch traced here: 50.1 us
  starting transfers between devices  25.6 us (51%)
  blocking collectives  14.1 us (28%)
  Pallas kernels  9.57 us (19%)
  between operations  0.74 us (1%)
    ppermute x11, starting transfers between devices, exchange(): far = lax.ppermute(value, NAMES, across)  16.7 us
    all_to_all x1, blocking collectives, body(): moments = lax.all_to_all(moments, NAMES, 0, 0)  14.1 us
    pallas_call x14, Pallas kernels, call(): pl.pallas_call(kernel, out_shape=outs, in_specs=[pl.BlockSpec(memory_spac...  9.57 us
    ppermute x11, starting transfers between devices, exchange(): near = lax.ppermute(value, NAMES, beside)  8.89 us
  transfers between devices with their start and end apart: 22, of which 0 were waited for; matrix products, arithmetic and copies ran while one was open for 0% of the time, Pallas kernels for 16%

profile of v13, /device:TPU:0, one launch (start us, length us, event | category | flops | bytes accessed | tf_op | source)
XLA Modules:
  0.0 50.1 jit_solution(8373907465105879487)
XLA Ops:
  0.6 3.0 %collective-permute-start.2 = (f32[1,256,128]{2,1,0:T(8,128)}, f32[1,256,128]{2,1,0:T(8,128)S(1)}, u32[]{:S(2)}, u32[]{:S(2)}) collective-permute-start(f32[1,256,128]{2,1,0:T(8,128)} %bitcast.20), channel_id=1, source_target_pairs={{0,16},{1,2},{2,1},{3,4},{4,3},{5,6},{6,5},{7,8},{8,7},{9,10},{10,... | collective-permute-start | bytes 393224 | tf_op jit(solution)/shard_map/ppermute | solution.py:352
  3.6 0.1 collective-permute-start.3
  3.8 1.7 %shard_map.94 = (f32[256,128]{1,0:T(8,128)S(1)}, f32[4,256,128]{2,1,0:T(8,128)S(1)}, f32[256,128]{1,0:T(8,128)S(1)}, f32[3,256,128]{2,1,0:T(8,128)S(1)}, f32[256...) custom-call(f32[256,128]{1,0:T(8,128)} %bitcast.18, ...), custom_call_target="tpu_custom_call" | custom-call | tf_op jit(solution)/shard_map/pallas_call | solution.py:324
  5.4 0.4 collective-permute-start
  5.9 1.2 %collective-permute-start.1 = (f32[1,256,128]{2,1,0:T(8,128)S(1)}, f32[1,256,128]{2,1,0:T(8,128)S(1)}, u32[]{:S(2)}, u32[]{:S(2)}) collective-permute-start(f32[1,256,128]{2,1,0:T(8,128)S(1)} %bitcast.15), channel_id=1, source_target_pairs={{0,16},{1,2},{2,1},{3,4},{4,3},{5,6},{6,5},{7,8},{8,7},{9,10},{10,... | collective-permute-start | bytes 393224 | tf_op jit(solution)/shard_map/ppermute | solution.py:352
  7.1 0.0 collective-permute-done.2.far_ref
  7.1 0.3 shard_map.95
  7.4 0.2 collective-permute-start.16
  7.6 1.7 %collective-permute-start.17 = (f32[1,256,128]{2,1,0:T(8,128)S(1)}, f32[1,256,128]{2,1,0:T(8,128)S(1)}, u32[]{:S(2)}, u32[]{:S(2)}) collective-permute-start(f32[1,256,128]{2,1,0:T(8,128)S(1)} %get-tuple-element.41.field_ref.refs_0_), channel_id=1, source_target_pairs={{0,16},{1,2},{2,1},{3,4},{4,3},{5,6},{6,5},{7,8},{8,7},{9,10},{10,... | collective-permute-start | bytes 393224 | tf_op jit(solution)/shard_map/ppermute | solution.py:352
  9.3 0.7 %collective-permute-start.10 = (f32[1,256,128]{2,1,0:T(8,128)S(1)}, f32[1,256,128]{2,1,0:T(8,128)S(1)}, u32[]{:S(2)}, u32[]{:S(2)}) collective-permute-start(f32[1,256,128]{2,1,0:T(8,128)S(1)} %get-tuple-element.40.field_ref.refs_3_.refs_4_), channel_id=1, source_target_pairs={{0,1},{1,0},{2,3},{3,2},{4,5},{5,4},{6,7},{7,6},{8,9},{9,8},{10,11... | collective-permute-start | bytes 393224 | tf_op jit(solution)/shard_map/ppermute | solution.py:353
  10.1 0.0 collective-permute-done.near_ref
  10.1 1.5 %collective-permute-start.11 = (f32[1,256,128]{2,1,0:T(8,128)S(1)}, f32[1,256,128]{2,1,0:T(8,128)S(1)}, u32[]{:S(2)}, u32[]{:S(2)}) collective-permute-start(f32[1,256,128]{2,1,0:T(8,128)S(1)} %get-tuple-element.40.field_ref.refs_3_.refs_4_), channel_id=1, source_target_pairs={{0,16},{1,2},{2,1},{3,4},{4,3},{5,6},{6,5},{7,8},{8,7},{9,10},{10,... | collective-permute-start | bytes 393224 | tf_op jit(solution)/shard_map/ppermute | solution.py:352
  11.5 0.9 %shard_map.96 = (f32[256,128]{1,0:T(8,128)}, f32[1,256,128]{2,1,0:T(8,128)S(1)}) custom-call(f32[1,256,128]{2,1,0:T(8,128)S(1)} %collective-permute-done.near_ref, f32[1,256,128]{2,1,0:T(8,128)S(1)} %collective-permute-done.1.far_ref, f32[3,256,128]{2,1,0:T(8,128)S(1)} %get-tuple-element.30.right_ref, f32[256,128]{1,0:T(8,128)S(1)} %get-tuple-element.31.part_ref, ...), custom_call_target="tpu_custom_call" | custom-call | tf_op jit(solution)/shard_map/pallas_call | solution.py:324
  12.5 1.2 %collective-permute-start.5 = (f32[1,256,128]{2,1,0:T(8,128)S(1)}, f32[1,256,128]{2,1,0:T(8,128)S(1)}, u32[]{:S(2)}, u32[]{:S(2)}) collective-permute-start(f32[1,256,128]{2,1,0:T(8,128)S(1)} %get-tuple-element.38.field_ref.refs_6_.refs_8_), channel_id=1, source_target_pairs={{0,16},{1,2},{2,1},{3,4},{4,3},{5,6},{6,5},{7,8},{8,7},{9,10},{10,... | collective-permute-start | bytes 393224 | tf_op jit(solution)/shard_map/ppermute | solution.py:352
  13.7 0.4 shard_map.101.field_ref.refs_1_
  14.1 0.2 collective-permute-start.18
  14.3 0.0 collective-permute-done.10.near_ref
  14.3 1.5 %collective-permute-start.19 = (f32[1,256,128]{2,1,0:T(8,128)S(1)}, f32[1,256,128]{2,1,0:T(8,128)S(1)}, u32[]{:S(2)}, u32[]{:S(2)}) collective-permute-start(f32[1,256,128]{2,1,0:T(8,128)S(1)} %shard_map.101.field_ref.refs_1_), channel_id=1, source_target_pairs={{0,16},{1,2},{2,1},{3,4},{4,3},{5,6},{6,5},{7,8},{8,7},{9,10},{10,... | collective-permute-start | bytes 393224 | tf_op jit(solution)/shard_map/ppermute | solution.py:352
  15.8 0.0 collective-permute-done.11.far_ref
  15.8 0.4 shard_map.99.field_ref.refs_4_.refs_5_
  16.2 1.7 %collective-permute-start.12 = (f32[1,256,128]{2,1,0:T(8,128)S(1)}, f32[1,256,128]{2,1,0:T(8,128)S(1)}, u32[]{:S(2)}, u32[]{:S(2)}) collective-permute-start(f32[1,256,128]{2,1,0:T(8,128)S(1)} %shard_map.99.field_ref.refs_4_.refs_5_), channel_id=1, source_target_pairs={{0,1},{1,0},{2,3},{3,2},{4,5},{5,4},{6,7},{7,6},{8,9},{9,8},{10,11... | collective-permute-start | bytes 393224 | tf_op jit(solution)/shard_map/ppermute | solution.py:353
  17.9 0.0 collective-permute-done.4.near_ref
  17.9 1.5 %collective-permute-start.13 = (f32[1,256,128]{2,1,0:T(8,128)S(1)}, f32[1,256,128]{2,1,0:T(8,128)S(1)}, u32[]{:S(2)}, u32[]{:S(2)}) collective-permute-start(f32[1,256,128]{2,1,0:T(8,128)S(1)} %shard_map.99.field_ref.refs_4_.refs_5_), channel_id=1, source_target_pairs={{0,16},{1,2},{2,1},{3,4},{4,3},{5,6},{6,5},{7,8},{8,7},{9,10},{10,... | collective-permute-start | bytes 393224 | tf_op jit(solution)/shard_map/ppermute | solution.py:352
  19.4 0.0 collective-permute-done.5.far_ref
  19.4 0.4 shard_map.97.field_ref.refs_7_.refs_9_
  19.8 0.9 %collective-permute-start.6 = (f32[1,256,128]{2,1,0:T(8,128)S(1)}, f32[1,256,128]{2,1,0:T(8,128)S(1)}, u32[]{:S(2)}, u32[]{:S(2)}) collective-permute-start(f32[1,256,128]{2,1,0:T(8,128)S(1)} %shard_map.97.field_ref.refs_7_.refs_9_), channel_id=1, source_target_pairs={{0,1},{1,0},{2,3},{3,2},{4,5},{5,4},{6,7},{7,6},{8,9},{9,8},{10,11... | collective-permute-start | bytes 393224 | tf_op jit(solution)/shard_map/ppermute | solution.py:353
  20.7 0.0 collective-permute-done.18.near_ref
  20.7 1.5 %collective-permute-start.7 = (f32[1,256,128]{2,1,0:T(8,128)S(1)}, f32[1,256,128]{2,1,0:T(8,128)S(1)}, u32[]{:S(2)}, u32[]{:S(2)}) collective-permute-start(f32[1,256,128]{2,1,0:T(8,128)S(1)} %shard_map.97.field_ref.refs_7_.refs_9_), channel_id=1, source_target_pairs={{0,16},{1,2},{2,1},{3,4},{4,3},{5,6},{6,5},{7,8},{8,7},{9,10},{10,... | collective-permute-start | bytes 393224 | tf_op jit(solution)/shard_map/ppermute | solution.py:352
  22.2 0.0 collective-permute-done.19.far_ref
  22.2 0.4 shard_map.102.refs_2_.refs_0_
  22.6 0.9 %collective-permute-start.20 = (f32[1,256,128]{2,1,0:T(8,128)S(1)}, f32[1,256,128]{2,1,0:T(8,128)S(1)}, u32[]{:S(2)}, u32[]{:S(2)}) collective-permute-start(f32[1,256,128]{2,1,0:T(8,128)S(1)} %shard_map.102.refs_2_.refs_0_), channel_id=1, source_target_pairs={{0,1},{1,0},{2,3},{3,2},{4,5},{5,4},{6,7},{7,6},{8,9},{9,8},{10,11... | collective-permute-start | bytes 393224 | tf_op jit(solution)/shard_map/ppermute | solution.py:353
  23.5 0.0 collective-permute-done.12.near_ref
  23.5 1.5 %collective-permute-start.21 = (f32[1,256,128]{2,1,0:T(8,128)S(1)}, f32[1,256,128]{2,1,0:T(8,128)S(1)}, u32[]{:S(2)}, u32[]{:S(2)}) collective-permute-start(f32[1,256,128]{2,1,0:T(8,128)S(1)} %shard_map.102.refs_2_.refs_0_), channel_id=1, source_target_pairs={{0,16},{1,2},{2,1},{3,4},{4,3},{5,6},{6,5},{7,8},{8,7},{9,10},{10,... | collective-permute-start | bytes 393224 | tf_op jit(solution)/shard_map/ppermute | solution.py:352
  25.0 0.4 shard_map.100.refs_5_.field_ref.refs_6_
  25.4 0.6 %collective-permute-start.14 = (f32[1,256,128]{2,1,0:T(8,128)S(1)}, f32[1,256,128]{2,1,0:T(8,128)S(1)}, u32[]{:S(2)}, u32[]{:S(2)}) collective-permute-start(f32[1,256,128]{2,1,0:T(8,128)S(1)} %shard_map.100.refs_5_.field_ref.refs_6_), channel_id=1, source_target_pairs={{0,16},{1,2},{2,1},{3,4},{4,3},{5,6},{6,5},{7,8},{8,7},{9,10},{10,... | collective-permute-start | bytes 393224 | tf_op jit(solution)/shard_map/ppermute | solution.py:352
  26.0 1.4 %collective-permute-start.15 = (f32[1,256,128]{2,1,0:T(8,128)S(1)}, f32[1,256,128]{2,1,0:T(8,128)S(1)}, u32[]{:S(2)}, u32[]{:S(2)}) collective-permute-start(f32[1,256,128]{2,1,0:T(8,128)S(1)} %shard_map.100.refs_5_.field_ref.refs_6_), channel_id=1, source_target_pairs={{0,1},{1,0},{2,3},{3,2},{4,5},{5,4},{6,7},{7,6},{8,9},{9,8},{10,11... | collective-permute-start | bytes 393224 | tf_op jit(solution)/shard_map/ppermute | solution.py:353
  27.4 0.4 shard_map.98.refs_8_.field_ref.refs_10_
  27.8 1.6 %collective-permute-start.8 = (f32[1,256,128]{2,1,0:T(8,128)S(1)}, f32[1,256,128]{2,1,0:T(8,128)S(1)}, u32[]{:S(2)}, u32[]{:S(2)}) collective-permute-start(f32[1,256,128]{2,1,0:T(8,128)S(1)} %shard_map.98.refs_8_.field_ref.refs_10_), channel_id=1, source_target_pairs={{0,16},{1,2},{2,1},{3,4},{4,3},{5,6},{6,5},{7,8},{8,7},{9,10},{10,... | collective-permute-start | bytes 393224 | tf_op jit(solution)/shard_map/ppermute | solution.py:352
  29.4 2.3 %collective-permute-start.9 = (f32[1,256,128]{2,1,0:T(8,128)S(1)}, f32[1,256,128]{2,1,0:T(8,128)S(1)}, u32[]{:S(2)}, u32[]{:S(2)}) collective-permute-start(f32[1,256,128]{2,1,0:T(8,128)S(1)} %shard_map.98.refs_8_.field_ref.refs_10_), channel_id=1, source_target_pairs={{0,1},{1,0},{2,3},{3,2},{4,5},{5,4},{6,7},{7,6},{8,9},{9,8},{10,11... | collective-permute-start | bytes 393224 | tf_op jit(solution)/shard_map/ppermute | solution.py:353
  31.6 1.5 %shard_map.103 = (f32[8,128]{1,0:T(8,128)S(1)}, f32[5,3,256,128]{3,2,1,0:T(8,128)S(1)}, f32[5,3,256,128]{3,2,1,0:T(8,128)S(1)}) custom-call(f32[256,128]{1,0:T(8,128)S(1)} %get-tuple-element.42.diagonal_ref, f32[1,256,128]{2,1,0:T(8,128)S(1)} %get-tuple-element.41.field_ref.refs_0_, f32[1,256,128]{2,1,0:T(8,128)S(1)} %shard_map.101.field_ref.refs_1_, ...), custom_call_target="tpu_custom_call" | custom-call | tf_op jit(solution)/shard_map/pallas_call | solution.py:324
  33.1 0.0 collective-permute-done.21.far_ref
  33.1 0.5 %shard_map.104 = (f32[1,256,128]{2,1,0:T(8,128)S(1)}, f32[8,128]{1,0:T(8,128)S(1)}) custom-call(f32[1,256,128]{2,1,0:T(8,128)S(1)} %collective-permute-done.20.near_ref, f32[1,256,128]{2,1,0:T(8,128)S(1)} %collective-permute-done.21.far_ref, f32[1,256,128]{2,1,0:T(8,128)S(1)} %shard_map.102.refs_2_.refs_0_, ...), custom_call_target="tpu_custom_call" | custom-call | tf_op jit(solution)/shard_map/pallas_call | solution.py:324
  33.7 0.0 collective-permute-done.14.far_ref
  33.7 0.0 collective-permute-done.15.near_ref
  33.7 0.5 %shard_map.105 = (f32[1,256,128]{2,1,0:T(8,128)S(1)}, f32[8,128]{1,0:T(8,128)S(1)}) custom-call(f32[1,256,128]{2,1,0:T(8,128)S(1)} %collective-permute-done.14.far_ref, f32[1,256,128]{2,1,0:T(8,128)S(1)} %collective-permute-done.15.near_ref, f32[1,256,128]{2,1,0:T(8,128)S(1)} %shard_map.100.refs_5_.field_ref.refs_6_, ...), custom_call_target="tpu_custom_call" | custom-call | tf_op jit(solution)/shard_map/pallas_call | solution.py:324
  34.2 0.6 %shard_map.106 = (f32[1,256,128]{2,1,0:T(8,128)S(1)}, f32[32,1,128]{2,1,0:T(1,128)S(1)}) custom-call(f32[1,256,128]{2,1,0:T(8,128)S(1)} %collective-permute-done.8.far_ref, f32[1,256,128]{2,1,0:T(8,128)S(1)} %collective-permute-done.9.near_ref, f32[1,256,128]{2,1,0:T(8,128)S(1)} %shard_map.98.refs_8_.field_ref.refs_10_, ...), custom_call_target="tpu_custom_call" | custom-call | tf_op jit(solution)/shard_map/pallas_call | solution.py:324
  34.8 14.1 %all_to_all.5.moments_ref = f32[32,1,128]{2,1,0:T(1,128)S(1)} all-to-all(f32[32,1,128]{2,1,0:T(1,128)S(1)} %get-tuple-element.48), channel_id=1, replica_groups=mesh['diamond'=2,'tile'=16] {'diamond','tile'}, dimensions={0} | all-to-all | bytes 32768 | tf_op jit(solution)/shard_map/all_to_all | solution.py:403
  48.9 1.2 %shard_map.107 = (f32[3,256,128]{2,1,0:T(8,128)}, f32[3,256,128]{2,1,0:T(8,128)}) custom-call(f32[32,1,128]{2,1,0:T(1,128)S(1)} %all_to_all.5.moments_ref, f32[256,128]{1,0:T(8,128)S(1)} %get-tuple-element.42.diagonal_ref, f32[1,256,128]{2,1,0:T(8,128)S(1)} %get-tuple-element.41.field_ref.refs_0_, f32[1,256,128]{2,1,0:T(8,128)S(1)} %shard_map.101.field_ref.refs_1_, ...), custom_call_target="tpu_custom_call" | custom-call | tf_op jit(solution)/shard_map/pallas_call | solution.py:324
  (11 shorter events, 0.0 us)
Async XLA Ops:
  0.6 6.4 %collective-permute-start.2 = (f32[1,256,128]{2,1,0:T(8,128)}, f32[1,256,128]{2,1,0:T(8,128)S(1)}, u32[]{:S(2)}, u32[]{:S(2)}) collective-permute-start(f32[1,256,128]{2,1,0:T(8,128)} %bitcast.20), channel_id=1, source_target_pairs={{0,16},{1,2},{2,1},{3,4},{4,3},{5,6},{6,5},{7,8},{8,7},{9,10},{10,... | collective-permute-start | bytes 393224 | tf_op jit(solution)/shard_map/ppermute | solution.py:352
  3.6 3.4 %collective-permute-start.3 = (f32[1,256,128]{2,1,0:T(8,128)}, f32[1,256,128]{2,1,0:T(8,128)S(1)}, u32[]{:S(2)}, u32[]{:S(2)}) collective-permute-start(f32[1,256,128]{2,1,0:T(8,128)} %bitcast.21), channel_id=1, source_target_pairs={{0,1},{1,0},{2,3},{3,2},{4,5},{5,4},{6,7},{7,6},{8,9},{9,8},{10,11... | collective-permute-start | bytes 393224 | tf_op jit(solution)/shard_map/ppermute | solution.py:353
  5.4 4.6 %collective-permute-start = (f32[1,256,128]{2,1,0:T(8,128)S(1)}, f32[1,256,128]{2,1,0:T(8,128)S(1)}, u32[]{:S(2)}, u32[]{:S(2)}) collective-permute-start(f32[1,256,128]{2,1,0:T(8,128)S(1)} %bitcast.14), channel_id=1, source_target_pairs={{0,1},{1,0},{2,3},{3,2},{4,5},{5,4},{6,7},{7,6},{8,9},{9,8},{10,11... | collective-permute-start | bytes 393224 | tf_op jit(solution)/shard_map/ppermute | solution.py:353
  5.9 5.7 %collective-permute-start.1 = (f32[1,256,128]{2,1,0:T(8,128)S(1)}, f32[1,256,128]{2,1,0:T(8,128)S(1)}, u32[]{:S(2)}, u32[]{:S(2)}) collective-permute-start(f32[1,256,128]{2,1,0:T(8,128)S(1)} %bitcast.15), channel_id=1, source_target_pairs={{0,16},{1,2},{2,1},{3,4},{4,3},{5,6},{6,5},{7,8},{8,7},{9,10},{10,... | collective-permute-start | bytes 393224 | tf_op jit(solution)/shard_map/ppermute | solution.py:352
  7.4 5.1 %collective-permute-start.16 = (f32[1,256,128]{2,1,0:T(8,128)S(1)}, f32[1,256,128]{2,1,0:T(8,128)S(1)}, u32[]{:S(2)}, u32[]{:S(2)}) collective-permute-start(f32[1,256,128]{2,1,0:T(8,128)S(1)} %get-tuple-element.41.field_ref.refs_0_), channel_id=1, source_target_pairs={{0,1},{1,0},{2,3},{3,2},{4,5},{5,4},{6,7},{7,6},{8,9},{9,8},{10,11... | collective-permute-start | bytes 393224 | tf_op jit(solution)/shard_map/ppermute | solution.py:353
  7.6 6.1 %collective-permute-start.17 = (f32[1,256,128]{2,1,0:T(8,128)S(1)}, f32[1,256,128]{2,1,0:T(8,128)S(1)}, u32[]{:S(2)}, u32[]{:S(2)}) collective-permute-start(f32[1,256,128]{2,1,0:T(8,128)S(1)} %get-tuple-element.41.field_ref.refs_0_), channel_id=1, source_target_pairs={{0,16},{1,2},{2,1},{3,4},{4,3},{5,6},{6,5},{7,8},{8,7},{9,10},{10,... | collective-permute-start | bytes 393224 | tf_op jit(solution)/shard_map/ppermute | solution.py:352
  9.3 5.0 %collective-permute-start.10 = (f32[1,256,128]{2,1,0:T(8,128)S(1)}, f32[1,256,128]{2,1,0:T(8,128)S(1)}, u32[]{:S(2)}, u32[]{:S(2)}) collective-permute-start(f32[1,256,128]{2,1,0:T(8,128)S(1)} %get-tuple-element.40.field_ref.refs_3_.refs_4_), channel_id=1, source_target_pairs={{0,1},{1,0},{2,3},{3,2},{4,5},{5,4},{6,7},{7,6},{8,9},{9,8},{10,11... | collective-permute-start | bytes 393224 | tf_op jit(solution)/shard_map/ppermute | solution.py:353
  10.1 5.7 %collective-permute-start.11 = (f32[1,256,128]{2,1,0:T(8,128)S(1)}, f32[1,256,128]{2,1,0:T(8,128)S(1)}, u32[]{:S(2)}, u32[]{:S(2)}) collective-permute-start(f32[1,256,128]{2,1,0:T(8,128)S(1)} %get-tuple-element.40.field_ref.refs_3_.refs_4_), channel_id=1, source_target_pairs={{0,16},{1,2},{2,1},{3,4},{4,3},{5,6},{6,5},{7,8},{8,7},{9,10},{10,... | collective-permute-start | bytes 393224 | tf_op jit(solution)/shard_map/ppermute | solution.py:352
  12.5 5.4 %collective-permute-start.4 = (f32[1,256,128]{2,1,0:T(8,128)S(1)}, f32[1,256,128]{2,1,0:T(8,128)S(1)}, u32[]{:S(2)}, u32[]{:S(2)}) collective-permute-start(f32[1,256,128]{2,1,0:T(8,128)S(1)} %get-tuple-element.38.field_ref.refs_6_.refs_8_), channel_id=1, source_target_pairs={{0,1},{1,0},{2,3},{3,2},{4,5},{5,4},{6,7},{7,6},{8,9},{9,8},{10,11... | collective-permute-start | bytes 393224 | tf_op jit(solution)/shard_map/ppermute | solution.py:353
  12.5 6.9 %collective-permute-start.5 = (f32[1,256,128]{2,1,0:T(8,128)S(1)}, f32[1,256,128]{2,1,0:T(8,128)S(1)}, u32[]{:S(2)}, u32[]{:S(2)}) collective-permute-start(f32[1,256,128]{2,1,0:T(8,128)S(1)} %get-tuple-element.38.field_ref.refs_6_.refs_8_), channel_id=1, source_target_pairs={{0,16},{1,2},{2,1},{3,4},{4,3},{5,6},{6,5},{7,8},{8,7},{9,10},{10,... | collective-permute-start | bytes 393224 | tf_op jit(solution)/shard_map/ppermute | solution.py:352
  14.1 6.6 %collective-permute-start.18 = (f32[1,256,128]{2,1,0:T(8,128)S(1)}, f32[1,256,128]{2,1,0:T(8,128)S(1)}, u32[]{:S(2)}, u32[]{:S(2)}) collective-permute-start(f32[1,256,128]{2,1,0:T(8,128)S(1)} %shard_map.101.field_ref.refs_1_), channel_id=1, source_target_pairs={{0,1},{1,0},{2,3},{3,2},{4,5},{5,4},{6,7},{7,6},{8,9},{9,8},{10,11... | collective-permute-start | bytes 393224 | tf_op jit(solution)/shard_map/ppermute | solution.py:353
  14.3 7.9 %collective-permute-start.19 = (f32[1,256,128]{2,1,0:T(8,128)S(1)}, f32[1,256,128]{2,1,0:T(8,128)S(1)}, u32[]{:S(2)}, u32[]{:S(2)}) collective-permute-start(f32[1,256,128]{2,1,0:T(8,128)S(1)} %shard_map.101.field_ref.refs_1_), channel_id=1, source_target_pairs={{0,16},{1,2},{2,1},{3,4},{4,3},{5,6},{6,5},{7,8},{8,7},{9,10},{10,... | collective-permute-start | bytes 393224 | tf_op jit(solution)/shard_map/ppermute | solution.py:352
  16.2 7.4 %collective-permute-start.12 = (f32[1,256,128]{2,1,0:T(8,128)S(1)}, f32[1,256,128]{2,1,0:T(8,128)S(1)}, u32[]{:S(2)}, u32[]{:S(2)}) collective-permute-start(f32[1,256,128]{2,1,0:T(8,128)S(1)} %shard_map.99.field_ref.refs_4_.refs_5_), channel_id=1, source_target_pairs={{0,1},{1,0},{2,3},{3,2},{4,5},{5,4},{6,7},{7,6},{8,9},{9,8},{10,11... | collective-permute-start | bytes 393224 | tf_op jit(solution)/shard_map/ppermute | solution.py:353
  17.9 7.1 %collective-permute-start.13 = (f32[1,256,128]{2,1,0:T(8,128)S(1)}, f32[1,256,128]{2,1,0:T(8,128)S(1)}, u32[]{:S(2)}, u32[]{:S(2)}) collective-permute-start(f32[1,256,128]{2,1,0:T(8,128)S(1)} %shard_map.99.field_ref.refs_4_.refs_5_), channel_id=1, source_target_pairs={{0,16},{1,2},{2,1},{3,4},{4,3},{5,6},{6,5},{7,8},{8,7},{9,10},{10,... | collective-permute-start | bytes 393224 | tf_op jit(solution)/shard_map/ppermute | solution.py:352
  19.8 6.2 %collective-permute-start.6 = (f32[1,256,128]{2,1,0:T(8,128)S(1)}, f32[1,256,128]{2,1,0:T(8,128)S(1)}, u32[]{:S(2)}, u32[]{:S(2)}) collective-permute-start(f32[1,256,128]{2,1,0:T(8,128)S(1)} %shard_map.97.field_ref.refs_7_.refs_9_), channel_id=1, source_target_pairs={{0,1},{1,0},{2,3},{3,2},{4,5},{5,4},{6,7},{7,6},{8,9},{9,8},{10,11... | collective-permute-start | bytes 393224 | tf_op jit(solution)/shard_map/ppermute | solution.py:353
  20.7 6.7 %collective-permute-start.7 = (f32[1,256,128]{2,1,0:T(8,128)S(1)}, f32[1,256,128]{2,1,0:T(8,128)S(1)}, u32[]{:S(2)}, u32[]{:S(2)}) collective-permute-start(f32[1,256,128]{2,1,0:T(8,128)S(1)} %shard_map.97.field_ref.refs_7_.refs_9_), channel_id=1, source_target_pairs={{0,16},{1,2},{2,1},{3,4},{4,3},{5,6},{6,5},{7,8},{8,7},{9,10},{10,... | collective-permute-start | bytes 393224 | tf_op jit(solution)/shard_map/ppermute | solution.py:352
  22.6 6.8 %collective-permute-start.20 = (f32[1,256,128]{2,1,0:T(8,128)S(1)}, f32[1,256,128]{2,1,0:T(8,128)S(1)}, u32[]{:S(2)}, u32[]{:S(2)}) collective-permute-start(f32[1,256,128]{2,1,0:T(8,128)S(1)} %shard_map.102.refs_2_.refs_0_), channel_id=1, source_target_pairs={{0,1},{1,0},{2,3},{3,2},{4,5},{5,4},{6,7},{7,6},{8,9},{9,8},{10,11... | collective-permute-start | bytes 393224 | tf_op jit(solution)/shard_map/ppermute | solution.py:353
  23.5 9.6 %collective-permute-start.21 = (f32[1,256,128]{2,1,0:T(8,128)S(1)}, f32[1,256,128]{2,1,0:T(8,128)S(1)}, u32[]{:S(2)}, u32[]{:S(2)}) collective-permute-start(f32[1,256,128]{2,1,0:T(8,128)S(1)} %shard_map.102.refs_2_.refs_0_), channel_id=1, source_target_pairs={{0,16},{1,2},{2,1},{3,4},{4,3},{5,6},{6,5},{7,8},{8,7},{9,10},{10,... | collective-permute-start | bytes 393224 | tf_op jit(solution)/shard_map/ppermute | solution.py:352
  25.4 8.3 %collective-permute-start.14 = (f32[1,256,128]{2,1,0:T(8,128)S(1)}, f32[1,256,128]{2,1,0:T(8,128)S(1)}, u32[]{:S(2)}, u32[]{:S(2)}) collective-permute-start(f32[1,256,128]{2,1,0:T(8,128)S(1)} %shard_map.100.refs_5_.field_ref.refs_6_), channel_id=1, source_target_pairs={{0,16},{1,2},{2,1},{3,4},{4,3},{5,6},{6,5},{7,8},{8,7},{9,10},{10,... | collective-permute-start | bytes 393224 | tf_op jit(solution)/shard_map/ppermute | solution.py:352
  26.0 7.7 %collective-permute-start.15 = (f32[1,256,128]{2,1,0:T(8,128)S(1)}, f32[1,256,128]{2,1,0:T(8,128)S(1)}, u32[]{:S(2)}, u32[]{:S(2)}) collective-permute-start(f32[1,256,128]{2,1,0:T(8,128)S(1)} %shard_map.100.refs_5_.field_ref.refs_6_), channel_id=1, source_target_pairs={{0,1},{1,0},{2,3},{3,2},{4,5},{5,4},{6,7},{7,6},{8,9},{9,8},{10,11... | collective-permute-start | bytes 393224 | tf_op jit(solution)/shard_map/ppermute | solution.py:353
  27.8 6.4 %collective-permute-start.8 = (f32[1,256,128]{2,1,0:T(8,128)S(1)}, f32[1,256,128]{2,1,0:T(8,128)S(1)}, u32[]{:S(2)}, u32[]{:S(2)}) collective-permute-start(f32[1,256,128]{2,1,0:T(8,128)S(1)} %shard_map.98.refs_8_.field_ref.refs_10_), channel_id=1, source_target_pairs={{0,16},{1,2},{2,1},{3,4},{4,3},{5,6},{6,5},{7,8},{8,7},{9,10},{10,... | collective-permute-start | bytes 393224 | tf_op jit(solution)/shard_map/ppermute | solution.py:352
  29.4 4.9 %collective-permute-start.9 = (f32[1,256,128]{2,1,0:T(8,128)S(1)}, f32[1,256,128]{2,1,0:T(8,128)S(1)}, u32[]{:S(2)}, u32[]{:S(2)}) collective-permute-start(f32[1,256,128]{2,1,0:T(8,128)S(1)} %shard_map.98.refs_8_.field_ref.refs_10_), channel_id=1, source_target_pairs={{0,1},{1,0},{2,3},{3,2},{4,5},{5,4},{6,7},{7,6},{8,9},{9,8},{10,11... | collective-permute-start | bytes 393224 | tf_op jit(solution)/shard_map/ppermute | solution.py:353
